TPU v7x, 512 devices: a whole 4x4x16 slice. The times are simulated.
512 devices in a mesh: depth: 32 (over z, core), lat: 16 (over y, x).
Axes of the slice: x: 4, y: 4, z: 16, core: 2. Of those that a mesh axis runs over, the one named last changes fastest.
Arguments:
- inv_diag: bfloat16 [32, 1024, 1024], P('depth', 'lat'), may hold values from -1.3 to 1.3
- couple: bfloat16 [32, 1024, 1024], P('depth', None, 'lat'), may hold values from -1 to 1
- arrow: bfloat16 [32, 1024, 1024], P('depth', None, 'lat'), may hold values from -6 to 6
- corner: bfloat16 [1024, 1024], replicated, may hold values from -2 to 2, as said below
- band_offset: int32 [32], P('depth'), may hold values from -8 to 8, as said below
Outputs:
- cross_cov: float32 [32, 1024, 1024], P('depth', 'lat')
Inputs may be any that keep to these rules, and one draw needn't show every extreme that they name: `band_offset`: each layer's band lies at this shift; both ends of the range occur in every draw. `corner`: Symmetric.
All inputs are finite; a program needn't handle non-finite values.
Results may differ from a plain program's by a relative error of at most 0.035.
Values may be sent and summed in bfloat16 or wider, within the bound.
No kernel may reach another device: no remote copies, remote signals or barrier semaphores. Data moves between devices by JAX's collectives and lax.ppermute only.
A program may use at most 64 MiB of HBM per device.

v0:
```python
import jax
import jax.numpy as jnp
from jax import lax
from jax.sharding import PartitionSpec as P

HALF = 512


def passed_along(value, axis, steps):
    count = lax.axis_size(axis)
    leading, last = (max(0, -steps), min(count, count - steps))
    return lax.ppermute(value, axis, [(source, source + steps) for source in range(leading, last)])


def body(inv_diag, couple, arrow, corner, band_offset):
    lat_index = lax.axis_index("lat")
    lat_count = lax.axis_size("lat")
    depth_count = lax.axis_size("depth")
    g_rows = inv_diag[0]
    b_cols = couple[0]
    a_cols = arrow[0]
    width = g_rows.shape[1]
    share = g_rows.shape[0]
    arrow_share = a_cols.shape[0] // lat_count
    offset = band_offset[0]
    rows = lax.broadcasted_iota(jnp.int32, b_cols.shape, 0)
    cols = lax.broadcasted_iota(jnp.int32, b_cols.shape, 1) + lat_index * share
    keep = jnp.abs(cols - rows - offset) <= HALF
    banded = jnp.where(keep, b_cols, jnp.zeros_like(b_cols))
    slab = corner
    panel = jnp.dot(slab, a_cols, preferred_element_type=jnp.float32).astype(jnp.bfloat16)
    bias = -lax.psum_scatter(
        jnp.dot(panel, g_rows, preferred_element_type=jnp.float32).astype(jnp.bfloat16),
        "lat",
        scatter_dimension=0,
        tiled=True,
    ).astype(jnp.float32)
    slab = banded
    map_rows = (
        -lax.psum_scatter(
            jnp.dot(slab, g_rows, preferred_element_type=jnp.float32).astype(jnp.bfloat16),
            "lat",
            scatter_dimension=0,
            tiled=True,
        ).astype(jnp.float32)
    ).astype(jnp.bfloat16)
    levels = (depth_count - 1).bit_length()
    for level in range(levels):
        span = 1 << level
        final = level == levels - 1
        if final:
            bias_partner = passed_along(bias.astype(jnp.bfloat16), "depth", -span).astype(
                bias.dtype
            )
        else:
            map_partner, bias_partner = (
                passed_along(
                    map_rows.astype(jnp.float32).astype(jnp.bfloat16), "depth", -span
                ).astype(jnp.float32),
                passed_along(bias.astype(jnp.bfloat16), "depth", -span).astype(bias.dtype),
            )
            map_partner = map_partner.astype(jnp.bfloat16)
        empty_bias = jnp.zeros((arrow_share, width), jnp.float32)
        empty_map = jnp.zeros((share, width), jnp.float32)
        if final:
            new_bias = empty_bias + jnp.dot(
                bias_partner,
                lax.all_gather(map_rows, "lat", axis=0, tiled=True).astype(jnp.float32),
                precision=lax.Precision.HIGHEST,
            )
        else:
            add_piece = lax.all_gather(map_rows, "lat", axis=0, tiled=True)
            bias_total = (empty_bias, empty_map)[0] + jnp.dot(
                bias_partner, add_piece.astype(jnp.float32), precision=lax.Precision.HIGHEST
            )
            map_total = jnp.dot(map_partner, add_piece, preferred_element_type=jnp.float32)
            new_bias = bias_total
            new_map = map_total
        bias = new_bias + bias
        if not final:
            map_rows = new_map.astype(jnp.bfloat16)
    return bias[None]


def solution(mesh):
    placed = (
        P("depth", "lat", None),
        P("depth", None, "lat"),
        P("depth", None, "lat"),
        P(),
        P("depth"),
    )
    return jax.shard_map(
        body, mesh=mesh, in_specs=placed, out_specs=P("depth", "lat", None), check_vma=False
    )
```

profile of v0, /device:TPU:1, one launch (start us, length us, event | category | flops | bytes accessed | tf_op | source)
XLA Modules:
  0.0 524.1 jit_solution(11151712663046441418)
XLA Ops:
  6.5 0.0 copy-start
  6.5 0.0 reduce-scatter.5.cloned.1.call-start
  7.4 3.1 convolution_convert_fusion
  10.5 0.0 reduce-scatter.5.cloned.1.call-update
  10.5 0.0 all-gather.6.cloned.1.call-start
  10.6 94.3 %reduce-scatter.5.cloned.1.call-done = bf16[64,1024]{1,0:T(8,128)(2,1)} async-done(((bf16[1024,1024]{1,0:T(8,128)(2,1)}), bf16[64,1024]{1,0:T(8,128)(2,1)}) %reduce-scatter.5.cloned.1.call-update) | async-done | bytes 131088 | tf_op jit(solution)/shard_map/reduce_scatter | solution.py:40
  104.9 1.6 negate_convert_fusion
  106.5 0.0 all-gather.6.cloned.1.call-update
  106.5 0.0 all-gather.8.cloned.1.call-start
  106.5 4.2 collective-permute-start.2
  110.8 4.0 collective-permute-done.2
  114.8 54.0 %all-gather.6.cloned.1.call-done = bf16[1024,1024]{1,0:T(8,128)(2,1)} async-done(((bf16[64,1024]{1,0:T(8,128)(2,1)}), bf16[1024,1024]{1,0:T(8,128)(2,1)}) %all-gather.6.cloned.1.call-update) | async-done | bytes 2097168 | tf_op jit(solution)/shard_map/all_gather | solution.py:72
  168.8 2.7 convolution_convert_fusion.6
  171.5 0.0 all-gather.8.cloned.1.call-update
  171.5 0.0 copy-start.4
  171.6 0.0 copy-start.6
  171.6 0.0 all-gather.10.cloned.1.call-start
  171.6 1.4 collective-permute-start.4
  173.1 4.6 collective-permute-done.4
  177.7 54.3 %all-gather.8.cloned.1.call-done = bf16[1024,1024]{1,0:T(8,128)(2,1)} async-done(((bf16[64,1024]{1,0:T(8,128)(2,1)}), bf16[1024,1024]{1,0:T(8,128)(2,1)}) %all-gather.8.cloned.1.call-update) | async-done | bytes 2097168 | tf_op jit(solution)/shard_map/all_gather | solution.py:72
  232.0 2.7 convolution_convert_fusion.5
  234.7 0.0 all-gather.10.cloned.1.call-update
  234.7 0.0 all-gather.12.cloned.1.call-start
  234.8 1.3 collective-permute-start.6
  236.1 7.5 %collective-permute-done.6 = bf16[64,1024]{1,0:T(8,128)(2,1)S(1)} collective-permute-done((bf16[64,1024]{1,0:T(8,128)(2,1)}, bf16[64,1024]{1,0:T(8,128)(2,1)S(1)}, u32[]{:S(2)}, u32[]{:S(2)}) %collective-permute-start.6) | collective-permute-done | bytes 131104 | tf_op jit(solution)/shard_map/ppermute | solution.py:12
  243.6 51.5 %all-gather.10.cloned.1.call-done = bf16[1024,1024]{1,0:T(8,128)(2,1)} async-done(((bf16[64,1024]{1,0:T(8,128)(2,1)}), bf16[1024,1024]{1,0:T(8,128)(2,1)}) %all-gather.10.cloned.1.call-update) | async-done | bytes 2097168 | tf_op jit(solution)/shard_map/all_gather | solution.py:72
  295.0 2.7 convolution_convert_fusion.4
  297.8 0.0 all-gather.12.cloned.1.call-update
  297.8 0.0 reduce-scatter.3.cloned.1.call-start
  297.8 0.0 copy-done
  297.9 0.0 copy-done.4
  297.9 0.0 copy-done.6
  297.9 3.5 convolution_convert_fusion.1
  301.4 0.0 reduce-scatter.3.cloned.1.call-update
  301.4 0.0 all-gather.14.cloned.1.call-start
  301.5 0.8 copy-done.5
  302.3 1.3 collective-permute-start.8
  303.6 13.3 %collective-permute-done.8 = bf16[64,1024]{1,0:T(8,128)(2,1)S(1)} collective-permute-done((bf16[64,1024]{1,0:T(8,128)(2,1)S(1)}, bf16[64,1024]{1,0:T(8,128)(2,1)S(1)}, u32[]{:S(2)}, u32[]{:S(2)}) %collective-permute-start.8) | collective-permute-done | bytes 131104 | tf_op jit(solution)/shard_map/ppermute | solution.py:12
  316.8 41.2 %all-gather.12.cloned.1.call-done = bf16[1024,1024]{1,0:T(8,128)(2,1)} async-done(((bf16[64,1024]{1,0:T(8,128)(2,1)}), bf16[1024,1024]{1,0:T(8,128)(2,1)}) %all-gather.12.cloned.1.call-update) | async-done | bytes 2097168 | tf_op jit(solution)/shard_map/all_gather | solution.py:72
  358.1 2.7 convolution_convert_fusion.3
  360.8 0.0 all-gather.14.cloned.1.call-update
  360.8 90.2 %reduce-scatter.3.cloned.1.call-done = bf16[64,1024]{1,0:T(8,128)(2,1)} async-done(((bf16[1024,1024]{1,0:T(8,128)(2,1)}), bf16[64,1024]{1,0:T(8,128)(2,1)}) %reduce-scatter.3.cloned.1.call-update) | async-done | bytes 131088 | tf_op jit(solution)/shard_map/reduce_scatter | solution.py:32
  451.0 1.1 fusion.1
  452.1 4.2 collective-permute-start
  456.3 3.8 collective-permute-done
  460.1 2.1 fusion.15
  462.2 0.0 copy-start.2
  462.2 1.4 collective-permute-start.1
  463.7 4.5 collective-permute-done.1
  468.2 0.0 copy-done.1
  468.2 0.5 fusion.16
  468.7 0.0 copy-start.3
  468.7 1.4 collective-permute-start.3
  470.1 8.2 %collective-permute-done.3 = bf16[64,1024]{1,0:T(8,128)(2,1)S(1)} collective-permute-done((bf16[64,1024]{1,0:T(8,128)(2,1)S(1)}, bf16[64,1024]{1,0:T(8,128)(2,1)S(1)}, u32[]{:S(2)}, u32[]{:S(2)}) %collective-permute-start.3) | collective-permute-done | bytes 131104 | tf_op jit(solution)/shard_map/ppermute | solution.py:12
  478.3 0.0 copy-done.2
  478.3 0.5 fusion.17
  478.8 1.3 collective-permute-start.5
  480.1 17.7 %collective-permute-done.5 = bf16[64,1024]{1,0:T(8,128)(2,1)S(1)} collective-permute-done((bf16[64,1024]{1,0:T(8,128)(2,1)S(1)}, bf16[64,1024]{1,0:T(8,128)(2,1)S(1)}, u32[]{:S(2)}, u32[]{:S(2)}) %collective-permute-start.5) | collective-permute-done | bytes 131104 | tf_op jit(solution)/shard_map/ppermute | solution.py:12
  497.8 0.0 copy-done.3
  497.8 0.5 fusion.18
  498.3 1.3 collective-permute-start.7
  499.6 14.1 %collective-permute-done.7 = bf16[64,1024]{1,0:T(8,128)(2,1)S(1)} collective-permute-done((bf16[64,1024]{1,0:T(8,128)(2,1)S(1)}, bf16[64,1024]{1,0:T(8,128)(2,1)S(1)}, u32[]{:S(2)}, u32[]{:S(2)}) %collective-permute-start.7) | collective-permute-done | bytes 131104 | tf_op jit(solution)/shard_map/ppermute | solution.py:12
  513.7 0.8 all-gather.14.cloned.1.call-done
  514.5 2.8 fusion
  (3 shorter events, 0.0 us)
Async XLA Ops:
  6.5 291.3 %copy-start = (bf16[1024,1024]{1,0:T(8,128)(2,1)S(1)}, bf16[1024,1024]{1,0:T(8,128)(2,1)}, u32[]{:S(2)}) copy-start(bf16[1024,1024]{1,0:T(8,128)(2,1)} %param.8) | copy-start | bytes 6291460
  6.5 98.4 %reduce-scatter.5.cloned.1.call-start = ((), (), s32[]{:S(2)}) async-start(), calls=%async_computation.3 | async-start | bytes 2228224 | tf_op jit(solution)/shard_map/reduce_scatter | solution.py:40
  10.5 158.3 %all-gather.6.cloned.1.call-start = ((), (), s32[]{:S(2)}) async-start(), calls=%async_computation.4 | async-start | bytes 2228224 | tf_op jit(solution)/shard_map/all_gather | solution.py:72
  106.5 125.5 %all-gather.8.cloned.1.call-start = ((), (), s32[]{:S(2)}) async-start(), calls=%async_computation.5 | async-start | bytes 2228224 | tf_op jit(solution)/shard_map/all_gather | solution.py:72
  106.5 8.2 %collective-permute-start.2 = (bf16[64,1024]{1,0:T(8,128)(2,1)}, bf16[64,1024]{1,0:T(8,128)(2,1)S(1)}, u32[]{:S(2)}, u32[]{:S(2)}) collective-permute-start(bf16[64,1024]{1,0:T(8,128)(2,1)} %negate_convert_fusion), channel_id=1, source_target_pairs={{16,0},{32,16},{48,32},{64,48},{80,64},{96,80},{112,96},{128,112},... | collective-permute-start | bytes 393224 | tf_op jit(solution)/shard_map/ppermute | solution.py:12
  171.5 126.3 %copy-start.4 = (bf16[1,64,1024]{2,1,0:T(8,128)(2,1)S(1)}, bf16[1,64,1024]{2,1,0:T(8,128)(2,1)}, u32[]{:S(2)}) copy-start(bf16[1,64,1024]{2,1,0:T(8,128)(2,1)} %param.5) | copy-start | bytes 393220
  171.6 126.3 %copy-start.6 = (bf16[1,1024,64]{1,2,0:T(8,128)(2,1)S(1)}, bf16[1,1024,64]{1,2,0:T(8,128)(2,1)}, u32[]{:S(2)}) copy-start(bf16[1,1024,64]{1,2,0:T(8,128)(2,1)} %param.7) | copy-start | bytes 393220
  171.6 123.5 %all-gather.10.cloned.1.call-start = ((), (), s32[]{:S(2)}) async-start(), calls=%async_computation.6 | async-start | bytes 2228224 | tf_op jit(solution)/shard_map/all_gather | solution.py:72
  171.6 6.1 %collective-permute-start.4 = (bf16[64,1024]{1,0:T(8,128)(2,1)}, bf16[64,1024]{1,0:T(8,128)(2,1)S(1)}, u32[]{:S(2)}, u32[]{:S(2)}) collective-permute-start(bf16[64,1024]{1,0:T(8,128)(2,1)} %convolution_convert_fusion.6), channel_id=1, source_target_pairs={{32,0},{48,16},{64,32},{80,48},{96,64},{112,80},{128,96},{144,112}... | collective-permute-start | bytes 393224 | tf_op jit(solution)/shard_map/ppermute | solution.py:12
  234.7 123.3 %all-gather.12.cloned.1.call-start = ((), (), s32[]{:S(2)}) async-start(), calls=%async_computation.7 | async-start | bytes 2228224 | tf_op jit(solution)/shard_map/all_gather | solution.py:72
  234.8 8.8 %collective-permute-start.6 = (bf16[64,1024]{1,0:T(8,128)(2,1)}, bf16[64,1024]{1,0:T(8,128)(2,1)S(1)}, u32[]{:S(2)}, u32[]{:S(2)}) collective-permute-start(bf16[64,1024]{1,0:T(8,128)(2,1)} %convolution_convert_fusion.5), channel_id=1, source_target_pairs={{64,0},{80,16},{96,32},{112,48},{128,64},{144,80},{160,96},{176,11... | collective-permute-start | bytes 393224 | tf_op jit(solution)/shard_map/ppermute | solution.py:12
  297.8 153.2 %reduce-scatter.3.cloned.1.call-start = ((), (), s32[]{:S(2)}) async-start(), calls=%async_computation.2 | async-start | bytes 2228224 | tf_op jit(solution)/shard_map/reduce_scatter | solution.py:32
  301.4 0.9 copy-start.5
  301.4 213.1 %all-gather.14.cloned.1.call-start = ((), (), s32[]{:S(2)}) async-start(), calls=%async_computation.8 | async-start | bytes 2228224 | tf_op jit(solution)/shard_map/all_gather | solution.py:68
  302.3 14.5 %collective-permute-start.8 = (bf16[64,1024]{1,0:T(8,128)(2,1)S(1)}, bf16[64,1024]{1,0:T(8,128)(2,1)S(1)}, u32[]{:S(2)}, u32[]{:S(2)}) collective-permute-start(bf16[64,1024]{1,0:T(8,128)(2,1)S(1)} %copy-done.5), channel_id=1, source_target_pairs={{128,0},{144,16},{160,32},{176,48},{192,64},{208,80},{224,96},{240... | collective-permute-start | bytes 393224 | tf_op jit(solution)/shard_map/ppermute | solution.py:12
  451.0 17.2 %copy-start.1 = (bf16[1024,1024]{1,0:T(8,128)(2,1)S(1)}, bf16[1024,1024]{1,0:T(8,128)(2,1)}, u32[]{:S(2)}) copy-start(bf16[1024,1024]{1,0:T(8,128)(2,1)} %all-gather.8.cloned.1.call-done) | copy-start | bytes 6291460
  452.1 8.0 %collective-permute-start = (bf16[64,1024]{1,0:T(8,128)(2,1)S(1)}, bf16[64,1024]{1,0:T(8,128)(2,1)S(1)}, u32[]{:S(2)}, u32[]{:S(2)}) collective-permute-start(bf16[64,1024]{1,0:T(8,128)(2,1)S(1)} %fusion.1), channel_id=1, source_target_pairs={{16,0},{32,16},{48,32},{64,48},{80,64},{96,80},{112,96},{128,112},... | collective-permute-start | bytes 393224 | tf_op jit(solution)/shard_map/ppermute | solution.py:12
  462.2 16.1 %copy-start.2 = (bf16[1024,1024]{1,0:T(8,128)(2,1)S(1)}, bf16[1024,1024]{1,0:T(8,128)(2,1)}, u32[]{:S(2)}) copy-start(bf16[1024,1024]{1,0:T(8,128)(2,1)} %all-gather.10.cloned.1.call-done) | copy-start | bytes 6291460
  462.2 6.0 %collective-permute-start.1 = (bf16[64,1024]{1,0:T(8,128)(2,1)S(1)}, bf16[64,1024]{1,0:T(8,128)(2,1)S(1)}, u32[]{:S(2)}, u32[]{:S(2)}) collective-permute-start(bf16[64,1024]{1,0:T(8,128)(2,1)S(1)} %get-tuple-element.5), channel_id=1, source_target_pairs={{32,0},{48,16},{64,32},{80,48},{96,64},{112,80},{128,96},{144,112}... | collective-permute-start | bytes 393224 | tf_op jit(solution)/shard_map/ppermute | solution.py:12
  468.7 29.1 %copy-start.3 = (bf16[1024,1024]{1,0:T(8,128)(2,1)S(1)}, bf16[1024,1024]{1,0:T(8,128)(2,1)}, u32[]{:S(2)}) copy-start(bf16[1024,1024]{1,0:T(8,128)(2,1)} %all-gather.12.cloned.1.call-done) | copy-start | bytes 6291460
  468.7 9.6 %collective-permute-start.3 = (bf16[64,1024]{1,0:T(8,128)(2,1)S(1)}, bf16[64,1024]{1,0:T(8,128)(2,1)S(1)}, u32[]{:S(2)}, u32[]{:S(2)}) collective-permute-start(bf16[64,1024]{1,0:T(8,128)(2,1)S(1)} %get-tuple-element.7), channel_id=1, source_target_pairs={{64,0},{80,16},{96,32},{112,48},{128,64},{144,80},{160,96},{176,11... | collective-permute-start | bytes 393224 | tf_op jit(solution)/shard_map/ppermute | solution.py:12
  478.8 19.0 %collective-permute-start.5 = (bf16[64,1024]{1,0:T(8,128)(2,1)S(1)}, bf16[64,1024]{1,0:T(8,128)(2,1)S(1)}, u32[]{:S(2)}, u32[]{:S(2)}) collective-permute-start(bf16[64,1024]{1,0:T(8,128)(2,1)S(1)} %get-tuple-element.9), channel_id=1, source_target_pairs={{128,0},{144,16},{160,32},{176,48},{192,64},{208,80},{224,96},{240... | collective-permute-start | bytes 393224 | tf_op jit(solution)/shard_map/ppermute | solution.py:12
  498.3 15.4 %collective-permute-start.7 = (bf16[64,1024]{1,0:T(8,128)(2,1)S(1)}, bf16[64,1024]{1,0:T(8,128)(2,1)S(1)}, u32[]{:S(2)}, u32[]{:S(2)}) collective-permute-start(bf16[64,1024]{1,0:T(8,128)(2,1)S(1)} %get-tuple-element.11), channel_id=1, source_target_pairs={{256,0},{272,16},{288,32},{304,48},{320,64},{336,80},{352,96},{368... | collective-permute-start | bytes 393224 | tf_op jit(solution)/shard_map/ppermute | solution.py:12
Sparse Core Ops, SparseCore 0:
  11.5 93.3 reduce-scatter.4
  108.3 60.4 all-gather.5
  172.3 59.6 all-gather.7
  235.3 59.6 all-gather.9
  298.3 59.6 all-gather.11
  362.6 88.3 reduce-scatter.2
  454.0 60.4 all-gather.13
where the time goes:
time: 528 us; the launch traced here: 524 us
  waiting for transfers between devices  464 us (88%)
  matrix products  23.9 us (5%)
  starting transfers between devices  18.1 us (3%)
  between operations  14.5 us (3%)
    all_gather x4, waiting for transfers between devices, body(): add_piece = lax.all_gather(map_rows, 'lat', axis=0, tiled=True)  201 us
    reduce_scatter x1, waiting for transfers between devices, body(): lax.psum_scatter(jnp.dot(slab, g_rows, preferred_element_type=jnp.float32...  94.3 us
    reduce_scatter x1, waiting for transfers between devices, body(): lax.psum_scatter(jnp.dot(panel, g_rows, preferred_element_type=jnp.float3...  90.2 us
    ppermute x9, waiting for transfers between devices, passed_along(): lax.ppermute(value, axis, [(source, source + steps) for source in range(l...  77.7 us
    ppermute x9, starting transfers between devices, passed_along(): lax.ppermute(value, axis, [(source, source + steps) for source in range(l...  17.9 us
    dot_general x4, matrix products, body(): jnp.dot(map_partner, add_piece, preferred_element_type=jnp.float32)  10.9 us
  transfers between devices with their start and end apart: 16, of which 16 were waited for; matrix products, arithmetic and copies ran while one was open for 2% of the time, Pallas kernels for 0%

commit v1 on v0

v1 whole, which is shorter than its diff:
```python
import jax
import jax.numpy as jnp
from jax import lax
from jax.sharding import PartitionSpec as P

HALF = 512
BOTH = ("depth", "lat")
F32 = jnp.float32
BF16 = jnp.bfloat16


def groups(depth_count, side, flipped):
    lists = []
    for d in range(depth_count):
        by_row = (d % 2 == 0) != flipped
        for a in range(side):
            cells = [a * side + b if by_row else b * side + a for b in range(side)]
            lists.append([d * side * side + cell for cell in cells])
    return lists


def gather_one(value, axis_groups, side):
    spread = jnp.broadcast_to(value[None], (side,) + value.shape)
    return lax.all_to_all(spread, BOTH, 0, 0, axis_index_groups=axis_groups)


def gather_two(value, depth_count, side):
    first = gather_one(value, groups(depth_count, side, False), side)
    return gather_one(first, groups(depth_count, side, True), side)


def mm(a, b):
    return jnp.dot(a, b, preferred_element_type=F32)


def splits(chips):
    top = (chips * 6 + 15) // 16
    mid = (chips - top + 1) // 2
    return [top, mid, chips - top - mid]


def body(inv_diag, couple, arrow, corner, band_offset):
    depth_count = lax.axis_size("depth")
    lat_count = lax.axis_size("lat")
    side = 4
    depth = lax.axis_index("depth")
    lat = lax.axis_index("lat")
    core = depth % 2
    chip = depth // 2
    chips = depth_count // 2
    g_rows = inv_diag[0]
    share, width = g_rows.shape
    offset = band_offset[0]
    rows = lax.broadcasted_iota(jnp.int32, couple.shape[1:], 0)
    cols = lax.broadcasted_iota(jnp.int32, couple.shape[1:], 1) + lat * share
    keep = jnp.abs(cols - rows - offset) <= HALF
    banded_t = jnp.where(keep, couple[0], jnp.zeros_like(couple[0])).T
    panel = mm(corner, arrow[0]).astype(BF16)
    panel_rows = lax.all_to_all(
        panel.reshape(lat_count, share, share), "lat", 0, 0
    )
    pair = jnp.stack([g_rows, banded_t])
    both = gather_two(pair, depth_count, side)
    g_all = both[:, :, 0].reshape(width, width)
    b_all = both[:, :, 1].reshape(width, width)
    step = -lax.dot_general(
        b_all, g_all, (((0,), (0,)), ((), ())), preferred_element_type=F32
    )
    step = step.astype(BF16)
    p4 = panel_rows.reshape(side, side, share, share)
    p4 = jnp.where(core == 0, p4, jnp.swapaxes(p4, 0, 1))
    p_flat = jnp.transpose(p4, (2, 0, 1, 3)).reshape(share, width)
    bias = -mm(p_flat, g_all)
    sent = jnp.concatenate([step, bias.astype(BF16)])
    swap = [(d, d ^ 1) for d in range(depth_count)]
    got = lax.ppermute(sent, "depth", swap)
    step_odd = jnp.where(core == 1, step, got[:width])
    step_even = jnp.where(core == 0, step, got[:width])
    couple_two = mm(step_odd, step_even).astype(BF16)
    bias_other = got[width:].astype(F32)
    zero = jnp.zeros((share, width), F32)
    add_odd = jnp.where(core == 1, bias, zero)
    add_even = jnp.where(core == 1, mm(bias.astype(BF16), step_even) + bias_other, zero)
    sizes = splits(chips)
    tops, bottoms, top = [], [], chips - 1
    for size in sizes:
        tops.append(top)
        bottoms.append(top - size + 1)
        top -= size
    at_top = (chip == tops[0]) | (chip == tops[1]) | (chip == tops[2])
    r = lax.broadcasted_iota(jnp.int32, (share, width), 0) + lat * share
    c = lax.broadcasted_iota(jnp.int32, (share, width), 1)
    start = (r == c) & at_top & (core == 0)
    v_in = jnp.where(start, 1.0, 0.0).astype(BF16)
    v_even = mm(v_in, couple_two) + add_even
    for hop in range(1, max(sizes)):
        pairs = []
        for block_top, size in zip(tops, sizes):
            if hop < size:
                source, target = block_top - hop + 1, block_top - hop
                pairs += [(2 * source + k, 2 * target + k) for k in range(2)]
        v_in = v_in + lax.ppermute(v_even.astype(BF16), "depth", pairs)
        v_even = mm(v_in, couple_two) + add_even
    v_odd = mm(v_in, step_odd) + add_odd
    mine = jnp.where(core == 0, v_even, v_odd)
    other = lax.ppermute(
        jnp.where(core == 0, v_odd, v_even).astype(BF16), "depth", swap
    )
    map_rows = jnp.where(core == 0, mine.astype(BF16), other)
    own_bias = jnp.where(core == 0, other.astype(F32), mine)
    entry = jnp.zeros((share, width), BF16)
    for target in range(bottoms[1], tops[1] + 1):
        entry = entry + lax.ppermute(
            own_bias.astype(BF16), "depth", [(2 * bottoms[0], 2 * target)]
        )
    maps = gather_two(map_rows, depth_count, side)
    maps = jnp.where(core == 0, maps, jnp.swapaxes(maps, 0, 1)).reshape(width, width)
    middle = mm(entry, maps) + own_bias
    last = jnp.zeros((share, width), BF16)
    for target in range(bottoms[2], tops[2] + 1):
        last = last + lax.ppermute(
            middle.astype(BF16), "depth", [(2 * bottoms[1], 2 * target)]
        )
    entry = entry + last
    entry_odd = lax.ppermute(
        entry, "depth", [(2 * k, 2 * k + 1) for k in range(chips)]
    )
    entry = jnp.where(core == 0, entry, entry_odd)
    return (mm(entry, maps) + own_bias)[None]


def solution(mesh):
    placed = (
        P("depth", "lat", None),
        P("depth", None, "lat"),
        P("depth", None, "lat"),
        P(),
        P("depth"),
    )
    return jax.shard_map(
        body, mesh=mesh, in_specs=placed, out_specs=P("depth", "lat", None), check_vma=False
    )
```

time: 528 us -> 188 us (0.36)
  waiting for transfers between devices: 464 us -> 92.2 us
  starting transfers between devices: 18.1 us -> 46.8 us
  between operations: 14.5 us -> 1.33 us
  local copies, waits for them, and re-layouts: 0.86 us -> 11.4 us
  blocking collectives: 0 us -> 9.63 us
    all_gather x5 -> x0, waiting for transfers between devices: 202 us -> none  [the longest x4 201 us: body(): add_piece = lax.all_gather(map_rows, 'lat', axis=0, tiled=True)]
    reduce_scatter x2 -> x0, waiting for transfers between devices: 185 us -> none  [the longest x1 94.3 us: body(): lax.psum_scatter(jnp.dot(slab, g_rows, preferred_element_type=jnp.float32...]
    all_to_all x0 -> x4, waiting for transfers between devices: none -> 51.9 us  [the longest x3 46.3 us: gather_one(): return lax.all_to_all(spread, BOTH, 0, 0, axis_index_groups=axis_groups)]
    ppermute x9 -> x18, waiting for transfers between devices: 77.7 us -> 40.3 us  [the longest x1 18.6 us: body(): lax.ppermute(entry, 'depth', [(2 * k, 2 * k + 1) for k in range(chips)])]
    all_to_all x0 -> x4, starting transfers between devices: none -> 19.1 us  [the longest x3 14.3 us: gather_one(): return lax.all_to_all(spread, BOTH, 0, 0, axis_index_groups=axis_groups)]
    ppermute x9 -> x18, starting transfers between devices: 17.9 us -> 27.7 us  [the longest x1 9.12 us: body(): got = lax.ppermute(sent, 'depth', swap)]
    all_to_all x0 -> x1, blocking collectives: none -> 9.63 us  [gather_one(): return lax.all_to_all(spread, BOTH, 0, 0, axis_index_groups=axis_groups)]
    broadcast_in_dim x0 -> x4, local copies, waits for them, and re-layouts: none -> 5.32 us  [gather_one(): spread = jnp.broadcast_to(value[None], (side,) + value.shape)]
  transfers between devices with their start and end apart: 16 -> 22, of which waited for: 16 -> 8; matrix products, arithmetic and copies ran while one was open for 2% -> 2% of each run, Pallas kernels for 0% -> 0%
where the time goes in v1:
time: 188 us; the launch traced here: 187 us
  waiting for transfers between devices  92.2 us (49%)
  starting transfers between devices  46.8 us (25%)
  matrix products  19.4 us (10%)
  local copies, waits for them, and re-layouts  11.4 us (6%)
  blocking collectives  9.63 us (5%)
  other arithmetic  6.58 us (4%)
    all_to_all x3, waiting for transfers between devices, gather_one(): return lax.all_to_all(spread, BOTH, 0, 0, axis_index_groups=axis_groups)  46.3 us
    ppermute x1, waiting for transfers between devices, body(): lax.ppermute(entry, 'depth', [(2 * k, 2 * k + 1) for k in range(chips)])  18.6 us
    ppermute x5, waiting for transfers between devices, body(): v_in = v_in + lax.ppermute(v_even.astype(BF16), 'depth', pairs)  16.5 us
    dot_general x13, matrix products, mm(): return jnp.dot(a, b, preferred_element_type=F32)  14.8 us
    all_to_all x3, starting transfers between devices, gather_one(): return lax.all_to_all(spread, BOTH, 0, 0, axis_index_groups=axis_groups)  14.3 us
    all_to_all x1, blocking collectives, gather_one(): return lax.all_to_all(spread, BOTH, 0, 0, axis_index_groups=axis_groups)  9.63 us
    ppermute x1, starting transfers between devices, body(): got = lax.ppermute(sent, 'depth', swap)  9.12 us
    ppermute x1, starting transfers between devices, body(): lax.ppermute(jnp.where(core == 0, v_odd, v_even).astype(BF16), 'depth', s...  6.67 us
  transfers between devices with their start and end apart: 22, of which 8 were waited for; matrix products, arithmetic and copies ran while one was open for 2% of the time, Pallas kernels for 0%

profile of v1, /device:TPU:1, one launch (start us, length us, event | category | flops | bytes accessed | tf_op | source)
XLA Modules:
  0.0 187.3 jit_solution(559885806413689366)
XLA Ops:
  0.8 0.0 copy-start.4
  0.8 1.1 fusion.15
  1.9 0.9 pad_maximum_fusion.1
  2.9 1.1 broadcast_in_dim.42
  4.0 5.0 %all-to-all-start = ((bf16[4,2,64,1024]{3,2,1,0:T(8,128)(2,1)}), bf16[4,2,64,1024]{3,2,1,0:T(8,128)(2,1)S(1)}, u32[]{:S(2)}, u32[]{:S(2)}) async-start(bf16[4,2,64,1024]{3,2,1,0:T(8,128)(2,1)} %broadcast_in_dim.42), calls=%async_computation | async-start | bytes 2097152 | tf_op jit(solution)/shard_map/all_to_all | solution.py:24
  9.0 0.8 convolution_convert_fusion.1
  9.7 0.2 copy.22
  9.9 0.9 reshape.29
  10.8 7.9 %all-to-all-done = bf16[4,2,64,1024]{3,2,1,0:T(8,128)(2,1)S(1)} async-done(((bf16[4,2,64,1024]{3,2,1,0:T(8,128)(2,1)}), bf16[4,2,64,1024]{3,2,1,0:T(8,128)(2,1)S(1)}, u32[]{:S(2)}, u32[]{:S(2)}) %all-to-all-start) | async-done | bytes 1048608 | tf_op jit(solution)/shard_map/all_to_all | solution.py:24
  18.7 1.0 copy-done.1
  19.7 4.8 %all-to-all-start.2 = ((bf16[16,2,2048]{2,1,0:T(2,128)(2,1)}), bf16[16,2,2048]{2,1,0:T(2,128)(2,1)S(1)}, u32[]{:S(2)}, u32[]{:S(2)}) async-start(bf16[16,2,2048]{2,1,0:T(2,128)(2,1)} %reshape.29), calls=%async_computation.2 | async-start | bytes 262144 | tf_op jit(solution)/shard_map/all_to_all | solution.py:59
  24.5 1.3 copy.14
  25.8 5.5 %all-to-all-done.2 = bf16[16,2,2048]{2,1,0:T(2,128)(2,1)S(1)} async-done(((bf16[16,2,2048]{2,1,0:T(2,128)(2,1)}), bf16[16,2,2048]{2,1,0:T(2,128)(2,1)S(1)}, u32[]{:S(2)}, u32[]{:S(2)}) %all-to-all-start.2) | async-done | bytes 131104 | tf_op jit(solution)/shard_map/all_to_all | solution.py:59
  31.3 2.6 %broadcast_in_dim.43 = bf16[4,4,2,64,1024]{4,3,1,2,0:T(8,128)(2,1)} broadcast(bf16[4,2,64,1024]{3,2,0,1:T(8,128)(2,1)S(1)} %copy.14), dimensions={1,2,3,4} | broadcast | bytes 5242880 | tf_op jit(solution)/shard_map/broadcast_in_dim | solution.py:23
  33.9 4.8 %all-to-all-start.1 = ((bf16[4,4,2,64,1024]{4,3,1,2,0:T(8,128)(2,1)}), bf16[4,4,2,64,1024]{4,3,1,2,0:T(8,128)(2,1)}, u32[]{:S(2)}, u32[]{:S(2)}) async-start(bf16[4,4,2,64,1024]{4,3,1,2,0:T(8,128)(2,1)} %broadcast_in_dim.43), calls=%async_computation.1 | async-start | bytes 8388608 | tf_op jit(solution)/shard_map/all_to_all | solution.py:24
  38.7 0.2 reshape.30
  39.0 0.2 copy.19
  39.2 0.2 reshape.26
  39.4 26.3 %all-to-all-done.1 = bf16[4,4,2,64,1024]{4,3,1,2,0:T(8,128)(2,1)} async-done(((bf16[4,4,2,64,1024]{4,3,1,2,0:T(8,128)(2,1)}), bf16[4,4,2,64,1024]{4,3,1,2,0:T(8,128)(2,1)}, u32[]{:S(2)}, u32[]{:S(2)}) %all-to-all-start.1) | async-done | bytes 4194336 | tf_op jit(solution)/shard_map/all_to_all | solution.py:24
  65.7 1.8 slice.18
  67.4 0.5 fusion.34
  67.9 4.6 %fusion = bf16[1024,1024]{1,0:T(8,128)(2,1)S(1)} fusion(bf16[4,4,2,64,1024]{4,3,1,2,0:T(8,128)(2,1)} %all-to-all-done.1), kind=kOutput, calls=%fused_computation.1 | convolution fusion | flops 2149580800 | bytes 6291456 | tf_op jit(solution)/shard_map/dot_general | solution.py:66
  72.5 1.7 pad_maximum_fusion
  74.3 0.3 copy-done.2
  74.6 9.1 %collective-permute-start = (bf16[1088,1024]{1,0:T(8,128)(2,1)}, bf16[1088,1024]{1,0:T(8,128)(2,1)}, u32[]{:S(2)}, u32[]{:S(2)}) collective-permute-start(bf16[1088,1024]{1,0:T(8,128)(2,1)} %pad_maximum_fusion), channel_id=1, source_target_pairs={{0,16},{16,0},{32,48},{48,32},{64,80},{80,64},{96,112},{112,96},{1... | collective-permute-start | bytes 6684680 | tf_op jit(solution)/shard_map/ppermute | solution.py:76
  83.8 4.3 %collective-permute-done = bf16[1088,1024]{1,0:T(8,128)(2,1)} collective-permute-done((bf16[1088,1024]{1,0:T(8,128)(2,1)}, bf16[1088,1024]{1,0:T(8,128)(2,1)}, u32[]{:S(2)}, u32[]{:S(2)}) %collective-permute-start) | collective-permute-done | bytes 2228256 | tf_op jit(solution)/shard_map/ppermute | solution.py:76
  88.0 2.1 %fusion.3 = f32[64,1024]{1,0:T(8,128)S(1)} fusion(bf16[64,1024]{1,0:T(8,128)(2,1)S(1)} %get-tuple-element.7, bf16[1024,1024]{1,0:T(8,128)(2,1)} %copy-done.2, pred[]{:T(512)S(6)} %eq.14, bf16[1088,1024]{1,0:T(8,128)(2,1)} %collective-permute-done, pred[]{:T(512)S(6)} %eq.35), kind=kOutput, calls=%fused_computation.19 | convolution fusion | flops 135462912 | bytes 4718594 | tf_op jit(solution)/shard_map/dot_general | solution.py:33
  90.1 4.6 %convolution_convert_fusion = bf16[1024,1024]{1,0:T(8,128)(2,1)S(1)} fusion(bf16[1024,1024]{1,0:T(8,128)(2,1)S(1)} %copy-done.3, pred[]{:T(512)S(6)} %eq.35, bf16[1088,1024]{1,0:T(8,128)(2,1)} %collective-permute-done, pred[]{:T(512)S(6)} %eq.14), kind=kOutput, calls=%fused_computation.8 | convolution fusion | flops 2150629376 | bytes 10485762 | tf_op jit(solution)/shard_map/dot_general | solution.py:33
  94.7 0.5 fusion.4
  95.2 0.7 collective-permute-start.1
  95.9 0.6 fusion.5
  96.5 0.7 collective-permute-start.2
  97.1 0.5 fusion.6
  97.7 0.7 collective-permute-start.3
  98.4 0.2 fusion.30
  98.6 0.5 fusion.7
  99.1 1.3 collective-permute-start.4
  100.4 16.5 %collective-permute-done.4 = bf16[64,1024]{1,0:T(8,128)(2,1)S(1)} collective-permute-done((bf16[64,1024]{1,0:T(8,128)(2,1)S(1)}, bf16[64,1024]{1,0:T(8,128)(2,1)S(1)}, u32[]{:S(2)}, u32[]{:S(2)}) %collective-permute-start.4) | collective-permute-done | bytes 131104 | tf_op jit(solution)/shard_map/ppermute | solution.py:102
  116.9 0.5 fusion.8
  117.4 0.7 collective-permute-start.5
  118.1 0.5 convolution_add_fusion.2
  118.6 2.1 %select_convert_fusion = (bf16[64,1024]{1,0:T(8,128)(2,1)S(1)}, f32[64,1024]{1,0:T(8,128)S(1)}) fusion(f32[64,1024]{1,0:T(8,128)S(1)} %convolution_add_fusion.2, pred[]{:T(512)S(6)} %eq.14, f32[64,1024]{1,0:T(8,128)S(1)} %get-tuple-element.8, pred[]{:T(512)S(6)} %eq.35, bf16[1024,1024]{1,0:T(8,128)(2,1)S(1)} %copy-done.3, ...), kind=kOutput, calls=%fused_computation.33 | convolution fusion | flops 135528448 | bytes 5375488 | tf_op jit(solution)/shard_map/dot_general | solution.py:33
  120.7 6.7 %collective-permute-start.6 = (bf16[64,1024]{1,0:T(8,128)(2,1)S(1)}, bf16[64,1024]{1,0:T(8,128)(2,1)S(1)}, u32[]{:S(2)}, u32[]{:S(2)}) collective-permute-start(bf16[64,1024]{1,0:T(8,128)(2,1)S(1)} %get-tuple-element.9), channel_id=1, source_target_pairs={{0,16},{16,0},{32,48},{48,32},{64,80},{80,64},{96,112},{112,96},{1... | collective-permute-start | bytes 393224 | tf_op jit(solution)/shard_map/ppermute | solution.py:106
  127.4 1.0 collective-permute-done.6
  128.4 0.1 broadcast_in_dim.44
  128.5 9.6 %all_to_all.25 = bf16[4,64,1024]{2,1,0:T(8,128)(2,1)S(1)} all-to-all(bf16[4,64,1024]{2,1,0:T(8,128)(2,1)S(1)} %broadcast_in_dim.44), channel_id=1, replica_groups={{0,1,2,3},{4,5,6,7},{8,9,10,11},{12,13,14,15},{16,20,24,28},{17,21,25,2..., dimensions={0} | all-to-all | bytes 1048576 | tf_op jit(solution)/shard_map/all_to_all | solution.py:24
  138.1 1.6 broadcast_in_dim.45
  139.7 4.4 %all-to-all-start.4 = ((bf16[4,4,64,1024]{3,2,1,0:T(8,128)(2,1)}), bf16[4,4,64,1024]{3,2,1,0:T(8,128)(2,1)}, u32[]{:S(2)}, u32[]{:S(2)}) async-start(bf16[4,4,64,1024]{3,2,1,0:T(8,128)(2,1)} %broadcast_in_dim.45), calls=%async_computation.4 | async-start | bytes 4194304 | tf_op jit(solution)/shard_map/all_to_all | solution.py:24
  144.2 0.7 collective-permute-start.11
  144.9 0.7 collective-permute-start.10
  145.5 0.7 collective-permute-start.9
  146.2 0.7 collective-permute-start.8
  146.9 0.7 collective-permute-start.7
  147.7 12.2 %all-to-all-done.4 = bf16[4,4,64,1024]{3,2,1,0:T(8,128)(2,1)} async-done(((bf16[4,4,64,1024]{3,2,1,0:T(8,128)(2,1)}), bf16[4,4,64,1024]{3,2,1,0:T(8,128)(2,1)}, u32[]{:S(2)}, u32[]{:S(2)}) %all-to-all-start.4) | async-done | bytes 2097184 | tf_op jit(solution)/shard_map/all_to_all | solution.py:24
  159.8 2.4 %bitcast_select_fusion = bf16[4,4,64,1024]{3,2,1,0:T(8,128)(2,1)S(1)} fusion(bf16[4,4,64,1024]{3,2,1,0:T(8,128)(2,1)} %all-to-all-done.4, pred[]{:T(512)S(6)} %eq.14), kind=kLoop, calls=%fused_computation.5 | loop fusion | flops 1048576 | bytes 4194305 | tf_op jit(solution)/shard_map/jit(_where)/select_n | solution.py:117
  162.3 0.5 fusion.9
  162.8 0.7 collective-permute-start.16
  163.5 0.7 collective-permute-start.15
  164.1 0.7 collective-permute-start.14
  164.8 0.7 collective-permute-start.13
  165.5 0.7 collective-permute-start.12
  166.3 1.3 collective-permute-start.17
  167.6 18.6 %collective-permute-done.17 = bf16[64,1024]{1,0:T(8,128)(2,1)S(1)} collective-permute-done((bf16[64,1024]{1,0:T(8,128)(2,1)S(1)}, bf16[64,1024]{1,0:T(8,128)(2,1)S(1)}, u32[]{:S(2)}, u32[]{:S(2)}) %collective-permute-start.17) | collective-permute-done | bytes 131104 | tf_op jit(solution)/shard_map/ppermute | solution.py:125
  186.1 1.2 fusion.2
  (28 shorter events, 0.3 us)
Async XLA Ops:
  0.0 9.0 %copy-start = (bf16[1024,1024]{1,0:T(8,128)(2,1)S(1)}, bf16[1024,1024]{1,0:T(8,128)(2,1)}, u32[]{:S(2)}) copy-start(bf16[1024,1024]{1,0:T(8,128)(2,1)} %param.8) | copy-start | bytes 6291460
  0.8 8.2 %copy-start.4 = (bf16[1,1024,64]{1,2,0:T(8,128)(2,1)S(1)}, bf16[1,1024,64]{1,2,0:T(8,128)(2,1)}, u32[]{:S(2)}) copy-start(bf16[1,1024,64]{1,2,0:T(8,128)(2,1)} %param.7) | copy-start | bytes 393220
  4.0 14.8 %all-to-all-start = ((bf16[4,2,64,1024]{3,2,1,0:T(8,128)(2,1)}), bf16[4,2,64,1024]{3,2,1,0:T(8,128)(2,1)S(1)}, u32[]{:S(2)}, u32[]{:S(2)}) async-start(bf16[4,2,64,1024]{3,2,1,0:T(8,128)(2,1)} %broadcast_in_dim.42), calls=%async_computation | async-start | bytes 2097152 | tf_op jit(solution)/shard_map/all_to_all | solution.py:24
  18.7 1.0 copy-start.1
  19.7 11.6 %all-to-all-start.2 = ((bf16[16,2,2048]{2,1,0:T(2,128)(2,1)}), bf16[16,2,2048]{2,1,0:T(2,128)(2,1)S(1)}, u32[]{:S(2)}, u32[]{:S(2)}) async-start(bf16[16,2,2048]{2,1,0:T(2,128)(2,1)} %reshape.29), calls=%async_computation.2 | async-start | bytes 262144 | tf_op jit(solution)/shard_map/all_to_all | solution.py:59
  33.9 31.8 %all-to-all-start.1 = ((bf16[4,4,2,64,1024]{4,3,1,2,0:T(8,128)(2,1)}), bf16[4,4,2,64,1024]{4,3,1,2,0:T(8,128)(2,1)}, u32[]{:S(2)}, u32[]{:S(2)}) async-start(bf16[4,4,2,64,1024]{4,3,1,2,0:T(8,128)(2,1)} %broadcast_in_dim.43), calls=%async_computation.1 | async-start | bytes 8388608 | tf_op jit(solution)/shard_map/all_to_all | solution.py:24
  72.5 2.0 %copy-start.2 = (bf16[1024,1024]{1,0:T(8,128)(2,1)}, bf16[1024,1024]{1,0:T(8,128)(2,1)S(1)}, u32[]{:S(2)}) copy-start(bf16[1024,1024]{1,0:T(8,128)(2,1)S(1)} %fusion) | copy-start | bytes 6291460
  74.6 13.4 %collective-permute-start = (bf16[1088,1024]{1,0:T(8,128)(2,1)}, bf16[1088,1024]{1,0:T(8,128)(2,1)}, u32[]{:S(2)}, u32[]{:S(2)}) collective-permute-start(bf16[1088,1024]{1,0:T(8,128)(2,1)} %pad_maximum_fusion), channel_id=1, source_target_pairs={{0,16},{16,0},{32,48},{48,32},{64,80},{80,64},{96,112},{112,96},{1... | collective-permute-start | bytes 6684680 | tf_op jit(solution)/shard_map/ppermute | solution.py:76
  83.7 6.4 %copy-start.3 = (bf16[1024,1024]{1,0:T(8,128)(2,1)S(1)}, bf16[1024,1024]{1,0:T(8,128)(2,1)}, u32[]{:S(2)}) copy-start(bf16[1024,1024]{1,0:T(8,128)(2,1)} %copy-done.2) | copy-start | bytes 6291460
  95.2 0.7 collective-permute-start.1
  96.5 0.7 collective-permute-start.2
  97.7 0.7 collective-permute-start.3
  99.1 17.8 %collective-permute-start.4 = (bf16[64,1024]{1,0:T(8,128)(2,1)S(1)}, bf16[64,1024]{1,0:T(8,128)(2,1)S(1)}, u32[]{:S(2)}, u32[]{:S(2)}) collective-permute-start(bf16[64,1024]{1,0:T(8,128)(2,1)S(1)} %fusion.7), channel_id=1, source_target_pairs={{384,352},{400,368},{192,160},{208,176},{32,0},{48,16},{385,353},{... | collective-permute-start | bytes 393224 | tf_op jit(solution)/shard_map/ppermute | solution.py:102
  117.4 0.7 collective-permute-start.5
  120.7 7.6 %collective-permute-start.6 = (bf16[64,1024]{1,0:T(8,128)(2,1)S(1)}, bf16[64,1024]{1,0:T(8,128)(2,1)S(1)}, u32[]{:S(2)}, u32[]{:S(2)}) collective-permute-start(bf16[64,1024]{1,0:T(8,128)(2,1)S(1)} %get-tuple-element.9), channel_id=1, source_target_pairs={{0,16},{16,0},{32,48},{48,32},{64,80},{80,64},{96,112},{112,96},{1... | collective-permute-start | bytes 393224 | tf_op jit(solution)/shard_map/ppermute | solution.py:106
  139.7 20.2 %all-to-all-start.4 = ((bf16[4,4,64,1024]{3,2,1,0:T(8,128)(2,1)}), bf16[4,4,64,1024]{3,2,1,0:T(8,128)(2,1)}, u32[]{:S(2)}, u32[]{:S(2)}) async-start(bf16[4,4,64,1024]{3,2,1,0:T(8,128)(2,1)} %broadcast_in_dim.45), calls=%async_computation.4 | async-start | bytes 4194304 | tf_op jit(solution)/shard_map/all_to_all | solution.py:24
  144.2 3.4 %collective-permute-start.11 = (bf16[64,1024]{1,0:T(8,128)(2,1)S(1)}, bf16[64,1024]{1,0:T(8,128)(2,1)S(1)}, u32[]{:S(2)}, u32[]{:S(2)}) collective-permute-start(bf16[64,1024]{1,0:T(8,128)(2,1)S(1)} %get-tuple-element.5), channel_id=1, source_target_pairs={{320,288},{321,289},{322,290},{323,291},{324,292},{325,293},{326,2... | collective-permute-start | bytes 393224 | tf_op jit(solution)/shard_map/ppermute | solution.py:113
  144.9 2.7 %collective-permute-start.10 = (bf16[64,1024]{1,0:T(8,128)(2,1)S(1)}, bf16[64,1024]{1,0:T(8,128)(2,1)S(1)}, u32[]{:S(2)}, u32[]{:S(2)}) collective-permute-start(bf16[64,1024]{1,0:T(8,128)(2,1)S(1)} %get-tuple-element.5), channel_id=1, source_target_pairs={{320,256},{321,257},{322,258},{323,259},{324,260},{325,261},{326,2... | collective-permute-start | bytes 393224 | tf_op jit(solution)/shard_map/ppermute | solution.py:113
  145.5 2.1 %collective-permute-start.9 = (bf16[64,1024]{1,0:T(8,128)(2,1)S(1)}, bf16[64,1024]{1,0:T(8,128)(2,1)S(1)}, u32[]{:S(2)}, u32[]{:S(2)}) collective-permute-start(bf16[64,1024]{1,0:T(8,128)(2,1)S(1)} %get-tuple-element.5), channel_id=1, source_target_pairs={{320,224},{321,225},{322,226},{323,227},{324,228},{325,229},{326,2... | collective-permute-start | bytes 393224 | tf_op jit(solution)/shard_map/ppermute | solution.py:113
  146.2 1.4 collective-permute-start.8
  146.9 0.7 collective-permute-start.7
  162.8 3.4 %collective-permute-start.16 = (bf16[64,1024]{1,0:T(8,128)(2,1)S(1)}, bf16[64,1024]{1,0:T(8,128)(2,1)S(1)}, u32[]{:S(2)}, u32[]{:S(2)}) collective-permute-start(bf16[64,1024]{1,0:T(8,128)(2,1)S(1)} %fusion.9), channel_id=1, source_target_pairs={{160,128},{161,129},{162,130},{163,131},{164,132},{165,133},{166,1... | collective-permute-start | bytes 393224 | tf_op jit(solution)/shard_map/ppermute | solution.py:121
  163.5 2.7 %collective-permute-start.15 = (bf16[64,1024]{1,0:T(8,128)(2,1)S(1)}, bf16[64,1024]{1,0:T(8,128)(2,1)S(1)}, u32[]{:S(2)}, u32[]{:S(2)}) collective-permute-start(bf16[64,1024]{1,0:T(8,128)(2,1)S(1)} %fusion.9), channel_id=1, source_target_pairs={{160,96},{161,97},{162,98},{163,99},{164,100},{165,101},{166,102},... | collective-permute-start | bytes 393224 | tf_op jit(solution)/shard_map/ppermute | solution.py:121
  164.1 2.1 %collective-permute-start.14 = (bf16[64,1024]{1,0:T(8,128)(2,1)S(1)}, bf16[64,1024]{1,0:T(8,128)(2,1)S(1)}, u32[]{:S(2)}, u32[]{:S(2)}) collective-permute-start(bf16[64,1024]{1,0:T(8,128)(2,1)S(1)} %fusion.9), channel_id=1, source_target_pairs={{160,64},{161,65},{162,66},{163,67},{164,68},{165,69},{166,70},{16... | collective-permute-start | bytes 393224 | tf_op jit(solution)/shard_map/ppermute | solution.py:121
  164.8 1.4 collective-permute-start.13
  165.5 0.7 collective-permute-start.12
  166.3 19.9 %collective-permute-start.17 = (bf16[64,1024]{1,0:T(8,128)(2,1)S(1)}, bf16[64,1024]{1,0:T(8,128)(2,1)S(1)}, u32[]{:S(2)}, u32[]{:S(2)}) collective-permute-start(bf16[64,1024]{1,0:T(8,128)(2,1)S(1)} %add_add_fusion), channel_id=1, source_target_pairs={{0,16},{32,48},{64,80},{96,112},{128,144},{160,176},{192,208},{224... | collective-permute-start | bytes 393224 | tf_op jit(solution)/shard_map/ppermute | solution.py:125

commit v2 on v1

v2 whole, which is shorter than its diff:
```python
import jax
import jax.numpy as jnp
from jax import lax
from jax.sharding import PartitionSpec as P

HALF = 512
BOTH = ("depth", "lat")
F32 = jnp.float32
BF16 = jnp.bfloat16


def groups(depth_count, side, flipped):
    lists = []
    for d in range(depth_count):
        by_row = (d % 2 == 0) != flipped
        for a in range(side):
            cells = [a * side + b if by_row else b * side + a for b in range(side)]
            lists.append([d * side * side + cell for cell in cells])
    return lists


def gather_one(value, axis_groups, side):
    spread = jnp.broadcast_to(value[None], (side,) + value.shape)
    return lax.all_to_all(spread, BOTH, 0, 0, axis_index_groups=axis_groups)


def gather_two(value, depth_count, side):
    first = gather_one(value, groups(depth_count, side, False), side)
    return gather_one(first, groups(depth_count, side, True), side)


def mm(a, b):
    return jnp.dot(a, b, preferred_element_type=F32)


def body(inv_diag, couple, arrow, corner, band_offset):
    depth_count = lax.axis_size("depth")
    lat_count = lax.axis_size("lat")
    side = 4
    depth = lax.axis_index("depth")
    lat = lax.axis_index("lat")
    core = depth % 2
    chips = depth_count // 2
    g_rows = inv_diag[0]
    share, width = g_rows.shape
    offset = band_offset[0]
    rows = lax.broadcasted_iota(jnp.int32, couple.shape[1:], 0)
    cols = lax.broadcasted_iota(jnp.int32, couple.shape[1:], 1) + lat * share
    keep = jnp.abs(cols - rows - offset) <= HALF
    banded_t = jnp.where(keep, couple[0], jnp.zeros_like(couple[0])).T
    panel = mm(corner, arrow[0]).astype(BF16)
    panel_rows = lax.all_to_all(
        panel.reshape(lat_count, share, share), "lat", 0, 0
    )
    pair = jnp.stack([g_rows, banded_t])
    both = gather_two(pair, depth_count, side)
    g_all = both[:, :, 0].reshape(width, width)
    b_all = both[:, :, 1].reshape(width, width)
    step = -lax.dot_general(
        b_all, g_all, (((0,), (0,)), ((), ())), preferred_element_type=F32
    )
    step = step.astype(BF16)
    p4 = panel_rows.reshape(side, side, share, share)
    p4 = jnp.where(core == 0, p4, jnp.swapaxes(p4, 0, 1))
    p_flat = jnp.transpose(p4, (2, 0, 1, 3)).reshape(share, width)
    bias = -mm(p_flat, g_all)
    half = share // 2
    swap = [(d, d ^ 1) for d in range(depth_count)]
    mates = [[d * lat_count + q, (d + 1) * lat_count + q] for d in range(0, depth_count, 2) for q in range(lat_count)]
    two = lax.all_to_all(
        jnp.broadcast_to(step[None], (2,) + step.shape), BOTH, 0, 0, axis_index_groups=mates
    )
    step_even, step_odd = two[0], two[1]
    low = core == 0
    kept = jnp.where(low, bias[:half], bias[half:])
    got = lax.ppermute(jnp.where(low, bias[half:], bias[:half]), "depth", swap)
    bias_even = jnp.where(low, kept, got)
    bias_odd = jnp.where(low, got, kept)
    entry = jnp.zeros((half, width), BF16)
    for hop in range(chips):
        if hop:
            source = chips - hop
            pairs = [(2 * source + k, 2 * source - 2 + k) for k in range(2)]
            entry = entry + lax.ppermute(x_even.astype(BF16), "depth", pairs)
        x_odd = mm(entry, step_odd) + bias_odd
        x_even = mm(x_odd.astype(BF16), step_even) + bias_even
    mine = jnp.where(low, x_even, x_odd)
    other = lax.ppermute(jnp.where(low, x_odd, x_even), "depth", swap)
    return jnp.where(low, jnp.concatenate([mine, other]), jnp.concatenate([other, mine]))[None]


def solution(mesh):
    placed = (
        P("depth", "lat", None),
        P("depth", None, "lat"),
        P("depth", None, "lat"),
        P(),
        P("depth"),
    )
    return jax.shard_map(
        body, mesh=mesh, in_specs=placed, out_specs=P("depth", "lat", None), check_vma=False
    )
```

time: 188 us -> 226 us (1.20)
  matrix products: 19.4 us -> 55.9 us
  blocking collectives: 9.63 us -> 0 us
  starting transfers between devices: 46.8 us -> 55.7 us
  waiting for transfers between devices: 92.2 us -> 96.8 us
  other arithmetic: 6.58 us -> 3.07 us
    dot_general x13 -> x19, matrix products: 14.8 us -> 51.2 us  [mm(): return jnp.dot(a, b, preferred_element_type=F32)]
    ppermute x18 -> x17, waiting for transfers between devices: 40.3 us -> 53 us  [the longest x15 52.1 us: body(): entry = entry + lax.ppermute(x_even.astype(BF16), 'depth', pairs)]
    all_to_all x3 -> x2, waiting for transfers between devices: 46.3 us -> 34.2 us  [gather_one(): return lax.all_to_all(spread, BOTH, 0, 0, axis_index_groups=axis_groups)]
    all_to_all x1 -> x0, blocking collectives: 9.63 us -> none  [gather_one(): return lax.all_to_all(spread, BOTH, 0, 0, axis_index_groups=axis_groups)]
    ppermute x18 -> x17, starting transfers between devices: 27.7 us -> 35.5 us  [the longest x1 15.6 us: body(): other = lax.ppermute(jnp.where(low, x_odd, x_even), 'depth', swap)]
    all_to_all x0 -> x1, starting transfers between devices: none -> 5.6 us  [body(): lax.all_to_all(jnp.broadcast_to(step[None], (2,) + step.shape), BOTH, 0,...]
    all_to_all x3 -> x2, starting transfers between devices: 14.3 us -> 9.87 us  [gather_one(): return lax.all_to_all(spread, BOTH, 0, 0, axis_index_groups=axis_groups)]
    all_to_all x0 -> x1, waiting for transfers between devices: none -> 4.1 us  [body(): lax.all_to_all(jnp.broadcast_to(step[None], (2,) + step.shape), BOTH, 0,...]
  transfers between devices with their start and end apart: 22 -> 21, of which waited for: 8 -> 6; matrix products, arithmetic and copies ran while one was open for 2% -> 5% of each run, Pallas kernels for 0% -> 0%
where the time goes in v2:
time: 226 us; the launch traced here: 225 us
  waiting for transfers between devices  96.8 us (43%)
  matrix products  55.9 us (25%)
  starting transfers between devices  55.7 us (25%)
  local copies, waits for them, and re-layouts  12 us (5%)
  other arithmetic  3.07 us (1%)
    ppermute x15, waiting for transfers between devices, body(): entry = entry + lax.ppermute(x_even.astype(BF16), 'depth', pairs)  52.1 us
    dot_general x19, matrix products, mm(): return jnp.dot(a, b, preferred_element_type=F32)  51.2 us
    all_to_all x2, waiting for transfers between devices, gather_one(): return lax.all_to_all(spread, BOTH, 0, 0, axis_index_groups=axis_groups)  34.2 us
    ppermute x1, starting transfers between devices, body(): other = lax.ppermute(jnp.where(low, x_odd, x_even), 'depth', swap)  15.6 us
    ppermute x15, starting transfers between devices, body(): entry = entry + lax.ppermute(x_even.astype(BF16), 'depth', pairs)  10.8 us
    all_to_all x2, starting transfers between devices, gather_one(): return lax.all_to_all(spread, BOTH, 0, 0, axis_index_groups=axis_groups)  9.87 us
    ppermute x1, starting transfers between devices, body(): got = lax.ppermute(jnp.where(low, bias[half:], bias[:half]), 'depth', swap)  9.13 us
    all_to_all x1, starting transfers between devices, body(): lax.all_to_all(jnp.broadcast_to(step[None], (2,) + step.shape), BOTH, 0,...  5.6 us
  transfers between devices with their start and end apart: 21, of which 6 were waited for; matrix products, arithmetic and copies ran while one was open for 5% of the time, Pallas kernels for 0%

profile of v2, /device:TPU:1, one launch (start us, length us, event | category | flops | bytes accessed | tf_op | source)
XLA Modules:
  0.0 224.9 jit_solution(11081384735893231564)
XLA Ops:
  0.8 0.0 copy-start.2
  0.8 1.1 fusion.34
  1.9 0.9 pad_maximum_fusion
  2.9 1.1 broadcast_in_dim.12
  4.0 5.0 %all-to-all-start = ((bf16[4,2,64,1024]{3,2,1,0:T(8,128)(2,1)}), bf16[4,2,64,1024]{3,2,1,0:T(8,128)(2,1)S(1)}, u32[]{:S(2)}, u32[]{:S(2)}) async-start(bf16[4,2,64,1024]{3,2,1,0:T(8,128)(2,1)} %broadcast_in_dim.12), calls=%async_computation | async-start | bytes 2097152 | tf_op jit(solution)/shard_map/all_to_all | solution.py:24
  9.0 0.8 convolution_convert_fusion
  9.7 0.2 copy.18
  9.9 0.9 reshape.79
  10.8 7.9 %all-to-all-done = bf16[4,2,64,1024]{3,2,1,0:T(8,128)(2,1)S(1)} async-done(((bf16[4,2,64,1024]{3,2,1,0:T(8,128)(2,1)}), bf16[4,2,64,1024]{3,2,1,0:T(8,128)(2,1)S(1)}, u32[]{:S(2)}, u32[]{:S(2)}) %all-to-all-start) | async-done | bytes 1048608 | tf_op jit(solution)/shard_map/all_to_all | solution.py:24
  18.7 1.0 copy-done.1
  19.7 4.8 %all-to-all-start.3 = ((bf16[16,2,2048]{2,1,0:T(2,128)(2,1)}), bf16[16,2,2048]{2,1,0:T(2,128)(2,1)S(1)}, u32[]{:S(2)}, u32[]{:S(2)}) async-start(bf16[16,2,2048]{2,1,0:T(2,128)(2,1)} %reshape.79), calls=%async_computation.3 | async-start | bytes 262144 | tf_op jit(solution)/shard_map/all_to_all | solution.py:52
  24.5 1.3 copy.11
  25.8 5.5 %all-to-all-done.3 = bf16[16,2,2048]{2,1,0:T(2,128)(2,1)S(1)} async-done(((bf16[16,2,2048]{2,1,0:T(2,128)(2,1)}), bf16[16,2,2048]{2,1,0:T(2,128)(2,1)S(1)}, u32[]{:S(2)}, u32[]{:S(2)}) %all-to-all-start.3) | async-done | bytes 131104 | tf_op jit(solution)/shard_map/all_to_all | solution.py:52
  31.3 2.6 %broadcast_in_dim.13 = bf16[4,4,2,64,1024]{4,3,1,2,0:T(8,128)(2,1)} broadcast(bf16[4,2,64,1024]{3,2,0,1:T(8,128)(2,1)S(1)} %copy.11), dimensions={1,2,3,4} | broadcast | bytes 5242880 | tf_op jit(solution)/shard_map/broadcast_in_dim | solution.py:23
  33.9 4.9 %all-to-all-start.1 = ((bf16[4,4,2,64,1024]{4,3,1,2,0:T(8,128)(2,1)}), bf16[4,4,2,64,1024]{4,3,1,2,0:T(8,128)(2,1)}, u32[]{:S(2)}, u32[]{:S(2)}) async-start(bf16[4,4,2,64,1024]{4,3,1,2,0:T(8,128)(2,1)} %broadcast_in_dim.13), calls=%async_computation.1 | async-start | bytes 8388608 | tf_op jit(solution)/shard_map/all_to_all | solution.py:24
  38.8 0.2 reshape.80
  39.0 0.2 copy.16
  39.2 0.2 reshape.77
  39.4 26.3 %all-to-all-done.1 = bf16[4,4,2,64,1024]{4,3,1,2,0:T(8,128)(2,1)} async-done(((bf16[4,4,2,64,1024]{4,3,1,2,0:T(8,128)(2,1)}), bf16[4,4,2,64,1024]{4,3,1,2,0:T(8,128)(2,1)}, u32[]{:S(2)}, u32[]{:S(2)}) %all-to-all-start.1) | async-done | bytes 4194336 | tf_op jit(solution)/shard_map/all_to_all | solution.py:24
  65.7 1.8 slice.27
  67.5 0.5 convolution_negate_fusion
  68.0 9.1 %collective-permute-start = (f32[32,1024]{1,0:T(8,128)S(1)}, f32[32,1024]{1,0:T(8,128)S(1)}, u32[]{:S(2)}, u32[]{:S(2)}) collective-permute-start(f32[32,1024]{1,0:T(8,128)S(1)} %slice_select_fusion.1), channel_id=1, source_target_pairs={{0,16},{16,0},{32,48},{48,32},{64,80},{80,64},{96,112},{112,96},{1... | collective-permute-start | bytes 393224 | tf_op jit(solution)/shard_map/ppermute | solution.py:76
  77.1 4.6 %fusion = bf16[1024,1024]{1,0:T(8,128)(2,1)S(1)} fusion(bf16[4,4,2,64,1024]{4,3,1,2,0:T(8,128)(2,1)} %all-to-all-done.1), kind=kOutput, calls=%fused_computation.1 | convolution fusion | flops 2149580800 | bytes 6291456 | tf_op jit(solution)/shard_map/dot_general | solution.py:59
  81.8 2.6 %broadcast_in_dim.14 = bf16[2,1024,1024]{2,1,0:T(8,128)(2,1)} broadcast(bf16[1024,1024]{1,0:T(8,128)(2,1)S(1)} %fusion), dimensions={1,2} | broadcast | bytes 6291456 | tf_op jit(solution)/shard_map/broadcast_in_dim | solution.py:71
  84.3 5.6 %all-to-all-start.2 = ((bf16[2,1024,1024]{2,1,0:T(8,128)(2,1)}), bf16[2,1024,1024]{2,1,0:T(8,128)(2,1)}, u32[]{:S(2)}, u32[]{:S(2)}) async-start(bf16[2,1024,1024]{2,1,0:T(8,128)(2,1)} %broadcast_in_dim.14), calls=%async_computation.2 | async-start | bytes 8388608 | tf_op jit(solution)/shard_map/all_to_all | solution.py:70
  89.9 0.0 collective-permute-done
  89.9 4.1 %all-to-all-done.2 = bf16[2,1024,1024]{2,1,0:T(8,128)(2,1)} async-done(((bf16[2,1024,1024]{2,1,0:T(8,128)(2,1)}), bf16[2,1024,1024]{2,1,0:T(8,128)(2,1)}, u32[]{:S(2)}, u32[]{:S(2)}) %all-to-all-start.2) | async-done | bytes 4194336 | tf_op jit(solution)/shard_map/all_to_all | solution.py:70
  94.0 3.1 %fusion.3 = bf16[32,1024]{1,0:T(8,128)(2,1)S(1)} fusion(f32[32,1024]{1,0:T(8,128)S(1)} %get-tuple-element.5, f32[32,1024]{1,0:T(8,128)S(1)} %get-tuple-element.6, bf16[2,1024,1024]{2,1,0:T(8,128)(2,1)} %all-to-all-done.2), kind=kOutput, calls=%fused_computation.41 | convolution fusion | flops 134348800 | bytes 4521984 | tf_op jit(solution)/shard_map/dot_general | solution.py:33
  97.1 0.7 collective-permute-start.1
  97.8 3.1 %fusion.5 = bf16[32,1024]{1,0:T(8,128)(2,1)S(1)} fusion(f32[32,1024]{1,0:T(8,128)S(1)} %get-tuple-element.5, f32[32,1024]{1,0:T(8,128)S(1)} %get-tuple-element.6, bf16[32,1024]{1,0:T(8,128)(2,1)S(1)} %collective-permute-done.1, bf16[2,1024,1024]{2,1,0:T(8,128)(2,1)} %all-to-all-done.2), kind=kOutput, calls=%fused_computation.43 | convolution fusion | flops 134348800 | bytes 4587520 | tf_op jit(solution)/shard_map/dot_general | solution.py:33
  100.9 0.7 collective-permute-start.2
  101.6 3.1 %fusion.7 = bf16[32,1024]{1,0:T(8,128)(2,1)S(1)} fusion(f32[32,1024]{1,0:T(8,128)S(1)} %get-tuple-element.5, f32[32,1024]{1,0:T(8,128)S(1)} %get-tuple-element.6, bf16[32,1024]{1,0:T(8,128)(2,1)S(1)} %add.156, bf16[2,1024,1024]{2,1,0:T(8,128)(2,1)} %all-to-all-done.2), kind=kOutput, calls=%fused_computation.45 | convolution fusion | flops 134348800 | bytes 4587520 | tf_op jit(solution)/shard_map/dot_general | solution.py:33
  104.6 0.7 collective-permute-start.3
  105.3 0.0 collective-permute-done.3
  105.3 3.1 %fusion.9 = bf16[32,1024]{1,0:T(8,128)(2,1)S(1)} fusion(f32[32,1024]{1,0:T(8,128)S(1)} %get-tuple-element.5, f32[32,1024]{1,0:T(8,128)S(1)} %get-tuple-element.6, bf16[32,1024]{1,0:T(8,128)(2,1)S(1)} %add.159, bf16[2,1024,1024]{2,1,0:T(8,128)(2,1)} %all-to-all-done.2), kind=kOutput, calls=%fused_computation.47 | convolution fusion | flops 134348800 | bytes 4587520 | tf_op jit(solution)/shard_map/dot_general | solution.py:33
  108.4 0.7 collective-permute-start.4
  109.1 3.1 %fusion.11 = bf16[32,1024]{1,0:T(8,128)(2,1)S(1)} fusion(f32[32,1024]{1,0:T(8,128)S(1)} %get-tuple-element.5, f32[32,1024]{1,0:T(8,128)S(1)} %get-tuple-element.6, bf16[32,1024]{1,0:T(8,128)(2,1)S(1)} %add.162, bf16[2,1024,1024]{2,1,0:T(8,128)(2,1)} %all-to-all-done.2), kind=kOutput, calls=%fused_computation.49 | convolution fusion | flops 134348800 | bytes 4587520 | tf_op jit(solution)/shard_map/dot_general | solution.py:33
  112.2 0.7 collective-permute-start.5
  112.9 3.1 %fusion.13 = bf16[32,1024]{1,0:T(8,128)(2,1)S(1)} fusion(f32[32,1024]{1,0:T(8,128)S(1)} %get-tuple-element.5, f32[32,1024]{1,0:T(8,128)S(1)} %get-tuple-element.6, bf16[32,1024]{1,0:T(8,128)(2,1)S(1)} %add.165, bf16[2,1024,1024]{2,1,0:T(8,128)(2,1)} %all-to-all-done.2), kind=kOutput, calls=%fused_computation.51 | convolution fusion | flops 134348800 | bytes 4587520 | tf_op jit(solution)/shard_map/dot_general | solution.py:33
  116.0 0.7 collective-permute-start.6
  116.7 3.1 %fusion.15 = bf16[32,1024]{1,0:T(8,128)(2,1)S(1)} fusion(f32[32,1024]{1,0:T(8,128)S(1)} %get-tuple-element.5, f32[32,1024]{1,0:T(8,128)S(1)} %get-tuple-element.6, bf16[32,1024]{1,0:T(8,128)(2,1)S(1)} %add.168, bf16[2,1024,1024]{2,1,0:T(8,128)(2,1)} %all-to-all-done.2), kind=kOutput, calls=%fused_computation.53 | convolution fusion | flops 134348800 | bytes 4587520 | tf_op jit(solution)/shard_map/dot_general | solution.py:33
  119.7 0.7 collective-permute-start.7
  120.5 3.1 %fusion.17 = bf16[32,1024]{1,0:T(8,128)(2,1)S(1)} fusion(f32[32,1024]{1,0:T(8,128)S(1)} %get-tuple-element.5, f32[32,1024]{1,0:T(8,128)S(1)} %get-tuple-element.6, bf16[32,1024]{1,0:T(8,128)(2,1)S(1)} %add.171, bf16[2,1024,1024]{2,1,0:T(8,128)(2,1)} %all-to-all-done.2), kind=kOutput, calls=%fused_computation.55 | convolution fusion | flops 134348800 | bytes 4587520 | tf_op jit(solution)/shard_map/dot_general | solution.py:33
  123.5 0.8 collective-permute-start.8
  124.4 3.1 %fusion.19 = bf16[32,1024]{1,0:T(8,128)(2,1)S(1)} fusion(f32[32,1024]{1,0:T(8,128)S(1)} %get-tuple-element.5, f32[32,1024]{1,0:T(8,128)S(1)} %get-tuple-element.6, bf16[32,1024]{1,0:T(8,128)(2,1)S(1)} %add.174, bf16[2,1024,1024]{2,1,0:T(8,128)(2,1)} %all-to-all-done.2), kind=kOutput, calls=%fused_computation.57 | convolution fusion | flops 134348800 | bytes 4587520 | tf_op jit(solution)/shard_map/dot_general | solution.py:33
  127.5 0.7 collective-permute-start.9
  128.2 3.1 %fusion.21 = bf16[32,1024]{1,0:T(8,128)(2,1)S(1)} fusion(f32[32,1024]{1,0:T(8,128)S(1)} %get-tuple-element.5, f32[32,1024]{1,0:T(8,128)S(1)} %get-tuple-element.6, bf16[32,1024]{1,0:T(8,128)(2,1)S(1)} %add.177, bf16[2,1024,1024]{2,1,0:T(8,128)(2,1)} %all-to-all-done.2), kind=kOutput, calls=%fused_computation.59 | convolution fusion | flops 134348800 | bytes 4587520 | tf_op jit(solution)/shard_map/dot_general | solution.py:33
  131.3 0.7 collective-permute-start.10
  132.0 3.1 %fusion.23 = bf16[32,1024]{1,0:T(8,128)(2,1)S(1)} fusion(f32[32,1024]{1,0:T(8,128)S(1)} %get-tuple-element.5, f32[32,1024]{1,0:T(8,128)S(1)} %get-tuple-element.6, bf16[32,1024]{1,0:T(8,128)(2,1)S(1)} %add.180, bf16[2,1024,1024]{2,1,0:T(8,128)(2,1)} %all-to-all-done.2), kind=kOutput, calls=%fused_computation.61 | convolution fusion | flops 134348800 | bytes 4587520 | tf_op jit(solution)/shard_map/dot_general | solution.py:33
  135.0 0.7 collective-permute-start.11
  135.8 3.1 %fusion.25 = bf16[32,1024]{1,0:T(8,128)(2,1)S(1)} fusion(f32[32,1024]{1,0:T(8,128)S(1)} %get-tuple-element.5, f32[32,1024]{1,0:T(8,128)S(1)} %get-tuple-element.6, bf16[32,1024]{1,0:T(8,128)(2,1)S(1)} %add.183, bf16[2,1024,1024]{2,1,0:T(8,128)(2,1)} %all-to-all-done.2), kind=kOutput, calls=%fused_computation.63 | convolution fusion | flops 134348800 | bytes 4587520 | tf_op jit(solution)/shard_map/dot_general | solution.py:33
  138.8 0.7 collective-permute-start.12
  139.5 3.1 %fusion.27 = bf16[32,1024]{1,0:T(8,128)(2,1)S(1)} fusion(f32[32,1024]{1,0:T(8,128)S(1)} %get-tuple-element.5, f32[32,1024]{1,0:T(8,128)S(1)} %get-tuple-element.6, bf16[32,1024]{1,0:T(8,128)(2,1)S(1)} %add.186, bf16[2,1024,1024]{2,1,0:T(8,128)(2,1)} %all-to-all-done.2), kind=kOutput, calls=%fused_computation.65 | convolution fusion | flops 134348800 | bytes 4587520 | tf_op jit(solution)/shard_map/dot_general | solution.py:33
  142.6 0.7 collective-permute-start.13
  143.3 3.1 %fusion.29 = bf16[32,1024]{1,0:T(8,128)(2,1)S(1)} fusion(f32[32,1024]{1,0:T(8,128)S(1)} %get-tuple-element.5, f32[32,1024]{1,0:T(8,128)S(1)} %get-tuple-element.6, bf16[32,1024]{1,0:T(8,128)(2,1)S(1)} %add.189, bf16[2,1024,1024]{2,1,0:T(8,128)(2,1)} %all-to-all-done.2), kind=kOutput, calls=%fused_computation.67 | convolution fusion | flops 134348800 | bytes 4587520 | tf_op jit(solution)/shard_map/dot_general | solution.py:33
  146.4 0.7 collective-permute-start.14
  147.1 3.1 %fusion.31 = bf16[32,1024]{1,0:T(8,128)(2,1)S(1)} fusion(f32[32,1024]{1,0:T(8,128)S(1)} %get-tuple-element.5, f32[32,1024]{1,0:T(8,128)S(1)} %get-tuple-element.6, bf16[32,1024]{1,0:T(8,128)(2,1)S(1)} %add.192, bf16[2,1024,1024]{2,1,0:T(8,128)(2,1)} %all-to-all-done.2), kind=kOutput, calls=%fused_computation.69 | convolution fusion | flops 134348800 | bytes 4587520 | tf_op jit(solution)/shard_map/dot_general | solution.py:33
  150.2 1.3 collective-permute-start.15
  151.5 52.0 %collective-permute-done.15 = bf16[32,1024]{1,0:T(8,128)(2,1)S(1)} collective-permute-done((bf16[32,1024]{1,0:T(8,128)(2,1)S(1)}, bf16[32,1024]{1,0:T(8,128)(2,1)S(1)}, u32[]{:S(2)}, u32[]{:S(2)}) %collective-permute-start.15) | collective-permute-done | bytes 65568 | tf_op jit(solution)/shard_map/ppermute | solution.py:84
  203.5 2.0 convolution_add_fusion.1
  205.5 2.1 select_bitcast_fusion
  207.6 15.6 %collective-permute-start.16 = (f32[32,1024]{1,0:T(8,128)S(1)}, f32[32,1024]{1,0:T(8,128)S(1)}, u32[]{:S(2)}, u32[]{:S(2)}) collective-permute-start(f32[32,1024]{1,0:T(8,128)S(1)} %get-tuple-element.8), channel_id=1, source_target_pairs={{0,16},{16,0},{32,48},{48,32},{64,80},{80,64},{96,112},{112,96},{1... | collective-permute-start | bytes 393224 | tf_op jit(solution)/shard_map/ppermute | solution.py:88
  223.2 1.0 collective-permute-done.16
  224.2 0.7 maximum_select_fusion
  (34 shorter events, 0.4 us)
Async XLA Ops:
  0.0 9.0 %copy-start = (bf16[1024,1024]{1,0:T(8,128)(2,1)S(1)}, bf16[1024,1024]{1,0:T(8,128)(2,1)}, u32[]{:S(2)}) copy-start(bf16[1024,1024]{1,0:T(8,128)(2,1)} %param.8) | copy-start | bytes 6291460
  0.8 8.2 %copy-start.2 = (bf16[1,1024,64]{1,2,0:T(8,128)(2,1)S(1)}, bf16[1,1024,64]{1,2,0:T(8,128)(2,1)}, u32[]{:S(2)}) copy-start(bf16[1,1024,64]{1,2,0:T(8,128)(2,1)} %param.7) | copy-start | bytes 393220
  4.0 14.8 %all-to-all-start = ((bf16[4,2,64,1024]{3,2,1,0:T(8,128)(2,1)}), bf16[4,2,64,1024]{3,2,1,0:T(8,128)(2,1)S(1)}, u32[]{:S(2)}, u32[]{:S(2)}) async-start(bf16[4,2,64,1024]{3,2,1,0:T(8,128)(2,1)} %broadcast_in_dim.12), calls=%async_computation | async-start | bytes 2097152 | tf_op jit(solution)/shard_map/all_to_all | solution.py:24
  18.7 1.0 copy-start.1
  19.7 11.6 %all-to-all-start.3 = ((bf16[16,2,2048]{2,1,0:T(2,128)(2,1)}), bf16[16,2,2048]{2,1,0:T(2,128)(2,1)S(1)}, u32[]{:S(2)}, u32[]{:S(2)}) async-start(bf16[16,2,2048]{2,1,0:T(2,128)(2,1)} %reshape.79), calls=%async_computation.3 | async-start | bytes 262144 | tf_op jit(solution)/shard_map/all_to_all | solution.py:52
  33.9 31.8 %all-to-all-start.1 = ((bf16[4,4,2,64,1024]{4,3,1,2,0:T(8,128)(2,1)}), bf16[4,4,2,64,1024]{4,3,1,2,0:T(8,128)(2,1)}, u32[]{:S(2)}, u32[]{:S(2)}) async-start(bf16[4,4,2,64,1024]{4,3,1,2,0:T(8,128)(2,1)} %broadcast_in_dim.13), calls=%async_computation.1 | async-start | bytes 8388608 | tf_op jit(solution)/shard_map/all_to_all | solution.py:24
  68.0 21.9 %collective-permute-start = (f32[32,1024]{1,0:T(8,128)S(1)}, f32[32,1024]{1,0:T(8,128)S(1)}, u32[]{:S(2)}, u32[]{:S(2)}) collective-permute-start(f32[32,1024]{1,0:T(8,128)S(1)} %slice_select_fusion.1), channel_id=1, source_target_pairs={{0,16},{16,0},{32,48},{48,32},{64,80},{80,64},{96,112},{112,96},{1... | collective-permute-start | bytes 393224 | tf_op jit(solution)/shard_map/ppermute | solution.py:76
  84.3 9.7 %all-to-all-start.2 = ((bf16[2,1024,1024]{2,1,0:T(8,128)(2,1)}), bf16[2,1024,1024]{2,1,0:T(8,128)(2,1)}, u32[]{:S(2)}, u32[]{:S(2)}) async-start(bf16[2,1024,1024]{2,1,0:T(8,128)(2,1)} %broadcast_in_dim.14), calls=%async_computation.2 | async-start | bytes 8388608 | tf_op jit(solution)/shard_map/all_to_all | solution.py:70
  97.1 0.7 collective-permute-start.1
  100.9 0.7 collective-permute-start.2
  104.6 0.7 collective-permute-start.3
  108.4 0.7 collective-permute-start.4
  112.2 0.7 collective-permute-start.5
  116.0 0.7 collective-permute-start.6
  119.7 0.7 collective-permute-start.7
  123.5 0.9 collective-permute-start.8
  127.5 0.7 collective-permute-start.9
  131.3 0.7 collective-permute-start.10
  135.0 0.7 collective-permute-start.11
  138.8 0.7 collective-permute-start.12
  142.6 0.7 collective-permute-start.13
  146.4 0.7 collective-permute-start.14
  150.2 53.3 %collective-permute-start.15 = (bf16[32,1024]{1,0:T(8,128)(2,1)S(1)}, bf16[32,1024]{1,0:T(8,128)(2,1)S(1)}, u32[]{:S(2)}, u32[]{:S(2)}) collective-permute-start(bf16[32,1024]{1,0:T(8,128)(2,1)S(1)} %fusion.31), channel_id=1, source_target_pairs={{32,0},{48,16},{33,1},{49,17},{34,2},{50,18},{35,3},{51,19},{36,4}... | collective-permute-start | bytes 196616 | tf_op jit(solution)/shard_map/ppermute | solution.py:84
  207.6 16.6 %collective-permute-start.16 = (f32[32,1024]{1,0:T(8,128)S(1)}, f32[32,1024]{1,0:T(8,128)S(1)}, u32[]{:S(2)}, u32[]{:S(2)}) collective-permute-start(f32[32,1024]{1,0:T(8,128)S(1)} %get-tuple-element.8), channel_id=1, source_target_pairs={{0,16},{16,0},{32,48},{48,32},{64,80},{80,64},{96,112},{112,96},{1... | collective-permute-start | bytes 393224 | tf_op jit(solution)/shard_map/ppermute | solution.py:88

commit v3 on v2

v3 whole, which is shorter than its diff:
```python
import jax
import jax.numpy as jnp
from jax import lax
from jax.experimental import pallas as pl
from jax.experimental.pallas import tpu as pltpu
from jax.sharding import PartitionSpec as P

HALF = 512
BOTH = ("depth", "lat")
F32 = jnp.float32
BF16 = jnp.bfloat16


def groups(depth_count, side, flipped):
    lists = []
    for d in range(depth_count):
        by_row = (d % 2 == 0) != flipped
        for a in range(side):
            cells = [a * side + b if by_row else b * side + a for b in range(side)]
            lists.append([d * side * side + cell for cell in cells])
    return lists


def gather_one(value, axis_groups, side):
    spread = jnp.broadcast_to(value[None], (side,) + value.shape)
    return lax.all_to_all(spread, BOTH, 0, 0, axis_index_groups=axis_groups)


def gather_two(value, depth_count, side):
    first = gather_one(value, groups(depth_count, side, False), side)
    return gather_one(first, groups(depth_count, side, True), side)


def mm(a, b):
    return jnp.dot(a, b, preferred_element_type=F32)


def around(base, side):
    return [(base + shift) % side for shift in (0, -1, 1, 2)]


def ring_moves(depths, side, flipped, shift):
    pairs = []
    for d in depths:
        by_x = (d % 2 == 0) != flipped
        for y in range(side):
            for x in range(side):
                ty, tx = (y, (x + shift) % side) if by_x else ((y + shift) % side, x)
                pairs.append(((d * side + y) * side + x, (d * side + ty) * side + tx))
    return pairs


def ring_gather(value, depths, side, flipped):
    return [value] + [
        lax.ppermute(value, BOTH, ring_moves(depths, side, flipped, shift))
        for shift in (1, -1, 2)
    ]


def sent_down(value, chip_pairs):
    return lax.ppermute(value, "depth", [(2 * a + 1, 2 * b + 1) for a, b in chip_pairs])


def place_kernel(order, a, b, c, d, out):
    count = out.shape[0] // 16
    for g, block in enumerate((a, b, c, d)):
        for f in range(4):
            start = pl.multiple_of(order[4 * g + f] * count, count)
            out[pl.ds(start, count), :] = block[f * count : (f + 1) * count, :]


def place(order, blocks):
    rows, width = blocks[0].shape
    return pl.pallas_call(
        place_kernel,
        out_shape=jax.ShapeDtypeStruct((4 * rows, width), blocks[0].dtype),
        in_specs=[pl.BlockSpec(memory_space=pltpu.SMEM)]
        + [pl.BlockSpec(memory_space=pltpu.VMEM)] * 4,
        out_specs=pl.BlockSpec(memory_space=pltpu.VMEM),
        compiler_params=pltpu.CompilerParams(vmem_limit_bytes=16 * 1024 * 1024),
    )(order, *blocks)


def body(inv_diag, couple, arrow, corner, band_offset):
    depth_count = lax.axis_size("depth")
    lat_count = lax.axis_size("lat")
    side = 4
    depth = lax.axis_index("depth")
    lat = lax.axis_index("lat")
    core = depth % 2
    chip = depth // 2
    chips = depth_count // 2
    g_rows = inv_diag[0]
    share, width = g_rows.shape
    offset = band_offset[0]
    rows = lax.broadcasted_iota(jnp.int32, couple.shape[1:], 0)
    cols = lax.broadcasted_iota(jnp.int32, couple.shape[1:], 1) + lat * share
    keep = jnp.abs(cols - rows - offset) <= HALF
    banded_t = jnp.where(keep, couple[0], jnp.zeros_like(couple[0])).T
    panel = mm(corner, arrow[0]).astype(BF16)
    pair = jnp.stack([g_rows, banded_t])
    both = gather_two(pair, depth_count, side)
    panel, both = lax.optimization_barrier((panel, both))
    panel_rows = lax.all_to_all(
        panel.reshape(lat_count, share, share), "lat", 0, 0
    )
    g_all = both[:, :, 0].reshape(width, width)
    b_all = both[:, :, 1].reshape(width, width)
    step = -lax.dot_general(
        b_all, g_all, (((0,), (0,)), ((), ())), preferred_element_type=F32
    )
    step = step.astype(BF16)
    p4 = panel_rows.reshape(side, side, share, share)
    p4 = jnp.where(core == 0, p4, jnp.swapaxes(p4, 0, 1))
    p_flat = jnp.transpose(p4, (2, 0, 1, 3)).reshape(share, width)
    bias = -mm(p_flat, g_all)
    low = core == 0
    swap = [(d, d ^ 1) for d in range(depth_count)]
    up = [(2 * k, 2 * k + 1) for k in range(chips)]
    got = lax.ppermute(step, "depth", swap)
    step_odd = jnp.where(low, got, step)
    step_even = jnp.where(low, step, got)
    product = mm(step_odd, step_even).astype(BF16)
    bias_other = lax.ppermute(bias, "depth", up)
    zero = jnp.zeros((share, width), F32)
    add_odd = jnp.where(low, zero, bias)
    add_even = jnp.where(low, zero, mm(bias.astype(BF16), got) + bias_other)
    lower = (chips * 6) // 16
    tops = [chips - 1, lower - 1]
    sizes = [chips - lower, lower]
    row = lax.broadcasted_iota(jnp.int32, (share, width), 0) + lat * share
    col = lax.broadcasted_iota(jnp.int32, (share, width), 1)
    start = (row == col) & ((chip == tops[0]) | (chip == tops[1])) & low
    v_in = jnp.where(start, 1.0, 0.0).astype(BF16)
    v_even = mm(v_in, product) + add_even
    for hop in range(1, max(sizes)):
        pairs = []
        for block_top, size in zip(tops, sizes):
            if hop < size:
                source = block_top - hop + 1
                pairs += [(2 * source + k, 2 * source - 2 + k) for k in range(2)]
        v_in = v_in + lax.ppermute(v_even.astype(BF16), "depth", pairs)
        v_even = mm(v_in, product) + add_even
    v_odd = jnp.where(low, mm(v_in, got), mm(v_in, step)) + add_odd
    mine = jnp.where(low, v_even, v_odd)
    other = lax.ppermute(jnp.where(low, v_odd, v_even).astype(BF16), "depth", swap)
    map_rows = jnp.where(low, mine.astype(BF16), other)
    own_bias = jnp.where(low, other.astype(F32), mine)
    depths = range(2 * lower)
    ring = jnp.concatenate(ring_gather(map_rows, depths, side, False))
    edge = v_even.astype(BF16)
    near, far = lower - 1, lower // 2 - 1
    entry = sent_down(edge, [(lower, near)]) + sent_down(edge, [(lower, far)])
    relayed = sent_down(entry, [(near, near - 1), (far, far - 1)])
    last = [(source, source - 2) for source, low_end in ((near, far), (far, -1)) if source - 2 > low_end]
    entry = entry + relayed + sent_down(entry, last)
    y, x = lat // side, lat % side
    order = jnp.stack(
        [
            jnp.where(low, side * b + a, side * a + b)
            for b in around(jnp.where(low, y, x), side)
            for a in around(jnp.where(low, x, y), side)
        ]
    )
    maps = place(order, ring_gather(ring, depths, side, True))
    entry_even = lax.ppermute(
        entry, "depth", [(2 * k + 1, 2 * k) for k in range(lower)]
    )
    entry = jnp.where(low, entry_even, entry)
    return (mm(entry, maps) + own_bias)[None]


def solution(mesh):
    placed = (
        P("depth", "lat", None),
        P("depth", None, "lat"),
        P("depth", None, "lat"),
        P(),
        P("depth"),
    )
    return jax.shard_map(
        body, mesh=mesh, in_specs=placed, out_specs=P("depth", "lat", None), check_vma=False
    )
```

time: 226 us -> 177 us (0.78)
  waiting for transfers between devices: 96.8 us -> 66.1 us
  matrix products: 55.9 us -> 26.7 us
  blocking collectives: 0 us -> 14.9 us
  local copies, waits for them, and re-layouts: 12 us -> 8.74 us
    dot_general x19 -> x17, matrix products: 51.2 us -> 20.8 us  [mm(): return jnp.dot(a, b, preferred_element_type=F32)]
    ppermute x17 -> x23, waiting for transfers between devices: 53 us -> 36.9 us  [the longest x9 20.3 us: body(): v_in = v_in + lax.ppermute(v_even.astype(BF16), 'depth', pairs)]
    all_to_all x0 -> x1, blocking collectives: none -> 14.9 us  [gather_one(): return lax.all_to_all(spread, BOTH, 0, 0, axis_index_groups=axis_groups)]
    ppermute x17 -> x23, starting transfers between devices: 35.5 us -> 45.5 us  [the longest x6 16.3 us: ring_gather(): lax.ppermute(value, BOTH, ring_moves(depths, side, flipped, shift))]
    all_to_all x2 -> x1, waiting for transfers between devices: 34.2 us -> 26.2 us  [gather_one(): return lax.all_to_all(spread, BOTH, 0, 0, axis_index_groups=axis_groups)]
    all_to_all x1 -> x0, starting transfers between devices: 5.6 us -> none  [body(): lax.all_to_all(jnp.broadcast_to(step[None], (2,) + step.shape), BOTH, 0,...]
    all_to_all x2 -> x1, starting transfers between devices: 9.87 us -> 4.98 us  [gather_one(): return lax.all_to_all(spread, BOTH, 0, 0, axis_index_groups=axis_groups)]
    all_to_all x1 -> x0, waiting for transfers between devices: 4.1 us -> none  [body(): lax.all_to_all(jnp.broadcast_to(step[None], (2,) + step.shape), BOTH, 0,...]
  transfers between devices with their start and end apart: 21 -> 25, of which waited for: 6 -> 6; matrix products, arithmetic and copies ran while one was open for 5% -> 8% of each run, Pallas kernels for 0% -> 1%
where the time goes in v3:
time: 177 us; the launch traced here: 176 us
  waiting for transfers between devices  66.1 us (37%)
  starting transfers between devices  53.9 us (30%)
  matrix products  26.7 us (15%)
  blocking collectives  14.9 us (8%)
  local copies, waits for them, and re-layouts  8.74 us (5%)
  other arithmetic  3.17 us (2%)
    all_to_all x1, waiting for transfers between devices, gather_one(): return lax.all_to_all(spread, BOTH, 0, 0, axis_index_groups=axis_groups)  26.2 us
    dot_general x17, matrix products, mm(): return jnp.dot(a, b, preferred_element_type=F32)  20.8 us
    ppermute x9, waiting for transfers between devices, body(): v_in = v_in + lax.ppermute(v_even.astype(BF16), 'depth', pairs)  20.3 us
    ppermute x6, starting transfers between devices, ring_gather(): lax.ppermute(value, BOTH, ring_moves(depths, side, flipped, shift))  16.3 us
    all_to_all x1, blocking collectives, gather_one(): return lax.all_to_all(spread, BOTH, 0, 0, axis_index_groups=axis_groups)  14.9 us
    ppermute x4, waiting for transfers between devices, sent_down(): lax.ppermute(value, 'depth', [(2 * a + 1, 2 * b + 1) for a, b in chip_pai...  12 us
    ppermute x1, starting transfers between devices, body(): got = lax.ppermute(step, 'depth', swap)  8.09 us
    ppermute x1, starting transfers between devices, body(): lax.ppermute(jnp.where(low, v_odd, v_even).astype(BF16), 'depth', swap)  7.67 us
  transfers between devices with their start and end apart: 25, of which 6 were waited for; matrix products, arithmetic and copies ran while one was open for 8% of the time, Pallas kernels for 1%

profile of v3, /device:TPU:1, one launch (start us, length us, event | category | flops | bytes accessed | tf_op | source)
XLA Modules:
  0.0 176.4 jit_solution(10951245026919510413)
XLA Ops:
  0.8 1.0 fusion.28
  1.9 0.9 pad_maximum_fusion.1
  2.8 0.1 broadcast_in_dim.30
  2.9 14.9 %all_to_all.15 = bf16[4,2,64,1024]{3,2,1,0:T(8,128)(2,1)S(1)} all-to-all(bf16[4,2,64,1024]{3,2,1,0:T(8,128)(2,1)S(1)} %broadcast_in_dim.30), channel_id=1, replica_groups={{0,1,2,3},{4,5,6,7},{8,9,10,11},{12,13,14,15},{16,20,24,28},{17,21,25,2..., dimensions={0} | all-to-all | bytes 2097152 | tf_op jit(solution)/shard_map/all_to_all | solution.py:26
  17.9 2.6 %broadcast_in_dim.31 = bf16[4,4,2,64,1024]{4,3,1,2,0:T(8,128)(2,1)} broadcast(bf16[4,2,64,1024]{3,2,0,1:T(8,128)(2,1)S(1)} %copy.11), dimensions={1,2,3,4} | broadcast | bytes 5242880 | tf_op jit(solution)/shard_map/broadcast_in_dim | solution.py:25
  20.5 5.0 %all-to-all-start.1 = ((bf16[4,4,2,64,1024]{4,3,1,2,0:T(8,128)(2,1)}), bf16[4,4,2,64,1024]{4,3,1,2,0:T(8,128)(2,1)}, u32[]{:S(2)}, u32[]{:S(2)}) async-start(bf16[4,4,2,64,1024]{4,3,1,2,0:T(8,128)(2,1)} %broadcast_in_dim.31), calls=%async_computation.1 | async-start | bytes 8388608 | tf_op jit(solution)/shard_map/all_to_all | solution.py:26
  25.5 0.8 convolution_convert_fusion
  26.2 26.2 %all-to-all-done.1 = bf16[4,4,2,64,1024]{4,3,1,2,0:T(8,128)(2,1)} async-done(((bf16[4,4,2,64,1024]{4,3,1,2,0:T(8,128)(2,1)}), bf16[4,4,2,64,1024]{4,3,1,2,0:T(8,128)(2,1)}, u32[]{:S(2)}, u32[]{:S(2)}) %all-to-all-start.1) | async-done | bytes 4194336 | tf_op jit(solution)/shard_map/all_to_all | solution.py:26
  52.4 6.0 %fusion = bf16[1024,1024]{1,0:T(8,128)(2,1)} fusion(bf16[4,4,2,64,1024]{4,3,1,2,0:T(8,128)(2,1)} %all-to-all-done.1), kind=kOutput, calls=%fused_computation.1 | convolution fusion | flops 2149580800 | bytes 6291456 | tf_op jit(solution)/shard_map/dot_general | solution.py:109
  58.4 8.1 %collective-permute-start = (bf16[1024,1024]{1,0:T(8,128)(2,1)}, bf16[1024,1024]{1,0:T(8,128)(2,1)}, u32[]{:S(2)}, u32[]{:S(2)}) collective-permute-start(bf16[1024,1024]{1,0:T(8,128)(2,1)} %fusion), channel_id=1, source_target_pairs={{0,16},{16,0},{32,48},{48,32},{64,80},{80,64},{96,112},{112,96},{1... | collective-permute-start | bytes 6291464 | tf_op jit(solution)/shard_map/ppermute | solution.py:120
  66.5 0.2 copy.18
  66.7 0.9 reshape.23
  67.6 3.5 %all-to-all-start.2 = ((bf16[16,2,2048]{2,1,0:T(2,128)(2,1)}), bf16[16,2,2048]{2,1,0:T(2,128)(2,1)S(1)}, u32[]{:S(2)}, u32[]{:S(2)}) async-start(bf16[16,2,2048]{2,1,0:T(2,128)(2,1)} %reshape.23), calls=%async_computation.2 | async-start | bytes 262144 | tf_op jit(solution)/shard_map/all_to_all | solution.py:104
  71.1 2.6 %copy.12 = bf16[4,4,2,64,1024]{4,3,1,0,2:T(8,128)(2,1)S(1)} copy(bf16[4,4,2,64,1024]{4,3,1,2,0:T(8,128)(2,1)} %all-to-all-done.1) | data formatting | bytes 8388608 | tf_op jit(solution)/shard_map/optimization_barrier | solution.py:103
  73.7 1.5 slice.9
  75.3 3.1 %all-to-all-done.2 = bf16[16,2,2048]{2,1,0:T(2,128)(2,1)S(1)} async-done(((bf16[16,2,2048]{2,1,0:T(2,128)(2,1)}), bf16[16,2,2048]{2,1,0:T(2,128)(2,1)S(1)}, u32[]{:S(2)}, u32[]{:S(2)}) %all-to-all-start.2) | async-done | bytes 131104 | tf_op jit(solution)/shard_map/all_to_all | solution.py:104
  78.3 0.2 reshape.24
  78.6 0.2 copy.16
  78.8 0.2 reshape.21
  79.0 2.1 %convolution_negate_fusion = f32[64,1024]{1,0:T(8,128)S(1)} fusion(bf16[64,1024]{1,0:T(8,128)(2,1)S(1)} %reshape.21, bf16[1024,1024]{1,0:T(8,128)(2,1)} %bitcast.73), kind=kOutput, calls=%fused_computation.25 | convolution fusion | flops 134283264 | bytes 2490368 | tf_op jit(solution)/shard_map/dot_general | solution.py:35
  81.1 1.3 collective-permute-start.1
  82.4 4.6 %fusion.6 = bf16[1024,1024]{1,0:T(8,128)(2,1)S(1)} fusion(bf16[1024,1024]{1,0:T(8,128)(2,1)} %fusion, bf16[1024,1024]{1,0:T(8,128)(2,1)} %collective-permute-done, pred[]{:T(512)S(6)} %eq.36), kind=kOutput, calls=%fused_computation.8 | convolution fusion | flops 2150629376 | bytes 6291457 | tf_op jit(solution)/shard_map/dot_general | solution.py:35
  87.0 2.1 %fusion.13 = f32[64,1024]{1,0:T(8,128)S(1)} fusion(f32[64,1024]{1,0:T(8,128)S(1)} %collective-permute-done.1, bf16[1024,1024]{1,0:T(8,128)(2,1)} %collective-permute-done, f32[64,1024]{1,0:T(8,128)S(1)} %convolution_negate_fusion, pred[]{:T(512)S(6)} %eq.36), kind=kOutput, calls=%fused_computation.23 | convolution fusion | flops 134414336 | bytes 2883585 | tf_op jit(solution)/shard_map/dot_general | solution.py:35
  89.1 0.5 fusion.14
  89.6 0.7 collective-permute-start.2
  90.3 0.5 fusion.15
  90.8 0.7 collective-permute-start.3
  91.5 0.5 fusion.16
  92.1 0.7 collective-permute-start.4
  92.8 0.2 fusion.46
  92.9 0.5 fusion.17
  93.4 0.7 collective-permute-start.5
  94.2 0.5 fusion.18
  94.7 1.3 collective-permute-start.6
  96.0 20.2 %collective-permute-done.6 = bf16[64,1024]{1,0:T(8,128)(2,1)S(1)} collective-permute-done((bf16[64,1024]{1,0:T(8,128)(2,1)S(1)}, bf16[64,1024]{1,0:T(8,128)(2,1)S(1)}, u32[]{:S(2)}, u32[]{:S(2)}) %collective-permute-start.6) | collective-permute-done | bytes 131104 | tf_op jit(solution)/shard_map/ppermute | solution.py:142
  116.2 0.5 fusion.19
  116.7 0.7 collective-permute-start.7
  117.5 0.5 fusion.20
  118.0 0.7 collective-permute-start.8
  118.7 0.5 fusion.21
  119.2 0.7 collective-permute-start.9
  119.9 0.5 fusion.22
  120.4 0.8 collective-permute-start.10
  121.3 0.5 fusion.49
  121.8 2.1 %fusion.42 = f32[64,1024]{1,0:T(8,128)S(1)} fusion(bf16[1024,1024]{1,0:T(8,128)(2,1)} %fusion, bf16[64,1024]{1,0:T(8,128)(2,1)S(1)} %add.272, bf16[64,1024]{1,0:T(8,128)(2,1)S(1)} %collective-permute-done.10), kind=kOutput, calls=%fused_computation.65 | convolution fusion | flops 134283264 | bytes 2621440 | tf_op jit(solution)/shard_map/dot_general | solution.py:35
  123.8 2.1 %select_convert_fusion = (bf16[64,1024]{1,0:T(8,128)(2,1)S(1)}, f32[64,1024]{1,0:T(8,128)S(1)}) fusion(f32[64,1024]{1,0:T(8,128)S(1)} %get-tuple-element.12, pred[]{:T(512)S(6)} %eq.36, f32[64,1024]{1,0:T(8,128)S(1)} %convolution_negate_fusion, f32[64,1024]{1,0:T(8,128)S(1)} %fusion.42, bf16[1024,1024]{1,0:T(8,128)(2,1)} %collective-permute-done, ...), kind=kOutput, calls=%fused_computation.40 | convolution fusion | flops 134545408 | bytes 3538945 | tf_op jit(solution)/shard_map/dot_general | solution.py:35
  125.9 7.7 %collective-permute-start.16 = (bf16[64,1024]{1,0:T(8,128)(2,1)S(1)}, bf16[64,1024]{1,0:T(8,128)(2,1)S(1)}, u32[]{:S(2)}, u32[]{:S(2)}) collective-permute-start(bf16[64,1024]{1,0:T(8,128)(2,1)S(1)} %get-tuple-element.9), channel_id=1, source_target_pairs={{0,16},{16,0},{32,48},{48,32},{64,80},{80,64},{96,112},{112,96},{1... | collective-permute-start | bytes 393224 | tf_op jit(solution)/shard_map/ppermute | solution.py:146
  133.6 1.0 collective-permute-done.16
  134.6 2.3 %collective-permute-start.19 = (bf16[64,1024]{1,0:T(8,128)(2,1)S(1)}, bf16[64,1024]{1,0:T(8,128)(2,1)S(1)}, u32[]{:S(2)}, u32[]{:S(2)}) collective-permute-start(bf16[64,1024]{1,0:T(8,128)(2,1)S(1)} %convert_select_fusion), channel_id=1, source_target_pairs={{0,2},{1,3},{2,0},{3,1},{4,6},{5,7},{6,4},{7,5},{8,10},{9,11},{10,... | collective-permute-start | bytes 393224 | tf_op jit(solution)/shard_map/ppermute | solution.py:55
  136.9 3.5 %collective-permute-start.18 = (bf16[64,1024]{1,0:T(8,128)(2,1)S(1)}, bf16[64,1024]{1,0:T(8,128)(2,1)S(1)}, u32[]{:S(2)}, u32[]{:S(2)}) collective-permute-start(bf16[64,1024]{1,0:T(8,128)(2,1)S(1)} %convert_select_fusion), channel_id=1, source_target_pairs={{0,3},{1,0},{2,1},{3,2},{4,7},{5,4},{6,5},{7,6},{8,11},{9,8},{10,9... | collective-permute-start | bytes 393224 | tf_op jit(solution)/shard_map/ppermute | solution.py:55
  140.5 1.9 %collective-permute-start.17 = (bf16[64,1024]{1,0:T(8,128)(2,1)S(1)}, bf16[64,1024]{1,0:T(8,128)(2,1)S(1)}, u32[]{:S(2)}, u32[]{:S(2)}) collective-permute-start(bf16[64,1024]{1,0:T(8,128)(2,1)S(1)} %convert_select_fusion), channel_id=1, source_target_pairs={{0,1},{1,2},{2,3},{3,0},{4,5},{5,6},{6,7},{7,4},{8,9},{9,10},{10,1... | collective-permute-start | bytes 393224 | tf_op jit(solution)/shard_map/ppermute | solution.py:55
  142.4 0.7 collective-permute-start.12
  143.1 0.7 collective-permute-start.11
  143.8 3.6 %collective-permute-done.17 = bf16[64,1024]{1,0:T(8,128)(2,1)S(1)} collective-permute-done((bf16[64,1024]{1,0:T(8,128)(2,1)S(1)}, bf16[64,1024]{1,0:T(8,128)(2,1)S(1)}, u32[]{:S(2)}, u32[]{:S(2)}) %collective-permute-start.17) | collective-permute-done | bytes 131104 | tf_op jit(solution)/shard_map/ppermute | solution.py:55
  147.4 3.3 %collective-permute-start.22 = (bf16[256,1024]{1,0:T(8,128)(2,1)S(1)}, bf16[256,1024]{1,0:T(8,128)(2,1)S(1)}, u32[]{:S(2)}, u32[]{:S(2)}) collective-permute-start(bf16[256,1024]{1,0:T(8,128)(2,1)S(1)} %pad_maximum_fusion.a), channel_id=1, source_target_pairs={{0,8},{1,9},{2,10},{3,11},{4,12},{5,13},{6,14},{7,15},{8,0},{9,1},... | collective-permute-start | bytes 1572872 | tf_op jit(solution)/shard_map/ppermute | solution.py:55
  150.8 3.2 %collective-permute-start.21 = (bf16[256,1024]{1,0:T(8,128)(2,1)S(1)}, bf16[256,1024]{1,0:T(8,128)(2,1)}, u32[]{:S(2)}, u32[]{:S(2)}) collective-permute-start(bf16[256,1024]{1,0:T(8,128)(2,1)S(1)} %pad_maximum_fusion.a), channel_id=1, source_target_pairs={{0,12},{1,13},{2,14},{3,15},{4,0},{5,1},{6,2},{7,3},{8,4},{9,5},{1... | collective-permute-start | bytes 1572872 | tf_op jit(solution)/shard_map/ppermute | solution.py:55
  154.0 2.1 %collective-permute-start.20 = (bf16[256,1024]{1,0:T(8,128)(2,1)S(1)}, bf16[256,1024]{1,0:T(8,128)(2,1)}, u32[]{:S(2)}, u32[]{:S(2)}) collective-permute-start(bf16[256,1024]{1,0:T(8,128)(2,1)S(1)} %pad_maximum_fusion.a), channel_id=1, source_target_pairs={{0,4},{1,5},{2,6},{3,7},{4,8},{5,9},{6,10},{7,11},{8,12},{9,13},{1... | collective-permute-start | bytes 1572872 | tf_op jit(solution)/shard_map/ppermute | solution.py:55
  156.1 1.3 collective-permute-start.14
  157.4 0.7 collective-permute-start.13
  158.1 12.0 %collective-permute-done.14 = bf16[64,1024]{1,0:T(8,128)(2,1)S(1)} collective-permute-done((bf16[64,1024]{1,0:T(8,128)(2,1)S(1)}, bf16[64,1024]{1,0:T(8,128)(2,1)S(1)}, u32[]{:S(2)}, u32[]{:S(2)}) %collective-permute-start.14) | collective-permute-done | bytes 131104 | tf_op jit(solution)/shard_map/ppermute | solution.py:61
  170.1 0.7 add_add_fusion
  170.8 1.9 %collective-permute-start.15 = (bf16[64,1024]{1,0:T(8,128)(2,1)}, bf16[64,1024]{1,0:T(8,128)(2,1)}, u32[]{:S(2)}, u32[]{:S(2)}) collective-permute-start(bf16[64,1024]{1,0:T(8,128)(2,1)} %add_add_fusion), channel_id=1, source_target_pairs={{16,0},{48,32},{80,64},{112,96},{144,128},{176,160},{17,1},{49,33}... | collective-permute-start | bytes 393224 | tf_op jit(solution)/shard_map/ppermute | solution.py:166
  172.8 1.4 shard_map.55
  174.3 2.1 %fusion.11 = f32[1,64,1024]{2,1,0:T(8,128)} fusion(bf16[1024,1024]{1,0:T(8,128)(2,1)S(1)} %shard_map.55, bf16[64,1024]{1,0:T(8,128)(2,1)S(1)} %collective-permute-done.16, bf16[64,1024]{1,0:T(8,128)(2,1)} %collective-permute-done.15, bf16[64,1024]{1,0:T(8,128)(2,1)} %add_add_fusion, pred[]{:T(512)S(6)} %eq.36, f32[64,1024]{1,0:T(8,128)S(1)} %get-tuple-element.12, ...), kind=kOutput, calls=%fused_computation.10 | convolution fusion | flops 134545408 | bytes 3276801 | tf_op jit(solution)/shard_map/dot_general | solution.py:35
  (39 shorter events, 0.6 us)
Async XLA Ops:
  0.0 25.4 %copy-start = (bf16[1024,1024]{1,0:T(8,128)(2,1)S(1)}, bf16[1024,1024]{1,0:T(8,128)(2,1)}, u32[]{:S(2)}) copy-start(bf16[1024,1024]{1,0:T(8,128)(2,1)} %param.8) | copy-start | bytes 6291460
  20.5 5.0 %copy-start.3 = (bf16[1,1024,64]{1,2,0:T(8,128)(2,1)S(1)}, bf16[1,1024,64]{1,2,0:T(8,128)(2,1)}, u32[]{:S(2)}) copy-start(bf16[1,1024,64]{1,2,0:T(8,128)(2,1)} %param.7) | copy-start | bytes 393220
  20.5 31.9 %all-to-all-start.1 = ((bf16[4,4,2,64,1024]{4,3,1,2,0:T(8,128)(2,1)}), bf16[4,4,2,64,1024]{4,3,1,2,0:T(8,128)(2,1)}, u32[]{:S(2)}, u32[]{:S(2)}) async-start(bf16[4,4,2,64,1024]{4,3,1,2,0:T(8,128)(2,1)} %broadcast_in_dim.31), calls=%async_computation.1 | async-start | bytes 8388608 | tf_op jit(solution)/shard_map/all_to_all | solution.py:26
  58.4 24.0 %collective-permute-start = (bf16[1024,1024]{1,0:T(8,128)(2,1)}, bf16[1024,1024]{1,0:T(8,128)(2,1)}, u32[]{:S(2)}, u32[]{:S(2)}) collective-permute-start(bf16[1024,1024]{1,0:T(8,128)(2,1)} %fusion), channel_id=1, source_target_pairs={{0,16},{16,0},{32,48},{48,32},{64,80},{80,64},{96,112},{112,96},{1... | collective-permute-start | bytes 6291464 | tf_op jit(solution)/shard_map/ppermute | solution.py:120
  67.6 10.8 %all-to-all-start.2 = ((bf16[16,2,2048]{2,1,0:T(2,128)(2,1)}), bf16[16,2,2048]{2,1,0:T(2,128)(2,1)S(1)}, u32[]{:S(2)}, u32[]{:S(2)}) async-start(bf16[16,2,2048]{2,1,0:T(2,128)(2,1)} %reshape.23), calls=%async_computation.2 | async-start | bytes 262144 | tf_op jit(solution)/shard_map/all_to_all | solution.py:104
  81.1 5.9 %collective-permute-start.1 = (f32[64,1024]{1,0:T(8,128)S(1)}, f32[64,1024]{1,0:T(8,128)S(1)}, u32[]{:S(2)}, u32[]{:S(2)}) collective-permute-start(f32[64,1024]{1,0:T(8,128)S(1)} %convolution_negate_fusion), channel_id=1, source_target_pairs={{0,16},{32,48},{64,80},{96,112},{128,144},{160,176},{192,208},{224... | collective-permute-start | bytes 786440 | tf_op jit(solution)/shard_map/ppermute | solution.py:124
  89.6 0.7 collective-permute-start.2
  90.8 0.7 collective-permute-start.3
  92.1 0.7 collective-permute-start.4
  93.4 0.7 collective-permute-start.5
  94.7 21.5 %collective-permute-start.6 = (bf16[64,1024]{1,0:T(8,128)(2,1)S(1)}, bf16[64,1024]{1,0:T(8,128)(2,1)S(1)}, u32[]{:S(2)}, u32[]{:S(2)}) collective-permute-start(bf16[64,1024]{1,0:T(8,128)(2,1)S(1)} %fusion.18), channel_id=1, source_target_pairs={{352,320},{368,336},{32,0},{48,16},{353,321},{369,337},{33,1},{49,... | collective-permute-start | bytes 393224 | tf_op jit(solution)/shard_map/ppermute | solution.py:142
  116.7 0.7 collective-permute-start.7
  118.0 0.7 collective-permute-start.8
  119.2 0.7 collective-permute-start.9
  120.4 0.9 collective-permute-start.10
  125.9 17.8 %copy-start.1 = (f32[64,1024]{1,0:T(8,128)}, f32[64,1024]{1,0:T(8,128)S(1)}, u32[]{:S(2)}) copy-start(f32[64,1024]{1,0:T(8,128)S(1)} %get-tuple-element.10) | copy-start | bytes 786436
  125.9 8.6 %collective-permute-start.16 = (bf16[64,1024]{1,0:T(8,128)(2,1)S(1)}, bf16[64,1024]{1,0:T(8,128)(2,1)S(1)}, u32[]{:S(2)}, u32[]{:S(2)}) collective-permute-start(bf16[64,1024]{1,0:T(8,128)(2,1)S(1)} %get-tuple-element.9), channel_id=1, source_target_pairs={{0,16},{16,0},{32,48},{48,32},{64,80},{80,64},{96,112},{112,96},{1... | collective-permute-start | bytes 393224 | tf_op jit(solution)/shard_map/ppermute | solution.py:146
  134.6 9.1 %collective-permute-start.19 = (bf16[64,1024]{1,0:T(8,128)(2,1)S(1)}, bf16[64,1024]{1,0:T(8,128)(2,1)S(1)}, u32[]{:S(2)}, u32[]{:S(2)}) collective-permute-start(bf16[64,1024]{1,0:T(8,128)(2,1)S(1)} %convert_select_fusion), channel_id=1, source_target_pairs={{0,2},{1,3},{2,0},{3,1},{4,6},{5,7},{6,4},{7,5},{8,10},{9,11},{10,... | collective-permute-start | bytes 393224 | tf_op jit(solution)/shard_map/ppermute | solution.py:55
  136.9 6.9 %collective-permute-start.18 = (bf16[64,1024]{1,0:T(8,128)(2,1)S(1)}, bf16[64,1024]{1,0:T(8,128)(2,1)S(1)}, u32[]{:S(2)}, u32[]{:S(2)}) collective-permute-start(bf16[64,1024]{1,0:T(8,128)(2,1)S(1)} %convert_select_fusion), channel_id=1, source_target_pairs={{0,3},{1,0},{2,1},{3,2},{4,7},{5,4},{6,5},{7,6},{8,11},{9,8},{10,9... | collective-permute-start | bytes 393224 | tf_op jit(solution)/shard_map/ppermute | solution.py:55
  140.5 6.9 %collective-permute-start.17 = (bf16[64,1024]{1,0:T(8,128)(2,1)S(1)}, bf16[64,1024]{1,0:T(8,128)(2,1)S(1)}, u32[]{:S(2)}, u32[]{:S(2)}) collective-permute-start(bf16[64,1024]{1,0:T(8,128)(2,1)S(1)} %convert_select_fusion), channel_id=1, source_target_pairs={{0,1},{1,2},{2,3},{3,0},{4,5},{5,6},{6,7},{7,4},{8,9},{9,10},{10,1... | collective-permute-start | bytes 393224 | tf_op jit(solution)/shard_map/ppermute | solution.py:55
  142.4 13.7 %collective-permute-start.12 = (bf16[64,1024]{1,0:T(8,128)(2,1)S(1)}, bf16[64,1024]{1,0:T(8,128)(2,1)S(1)}, u32[]{:S(2)}, u32[]{:S(2)}) collective-permute-start(bf16[64,1024]{1,0:T(8,128)(2,1)S(1)} %get-tuple-element.11), channel_id=1, source_target_pairs={{208,80},{209,81},{210,82},{211,83},{212,84},{213,85},{214,86},{21... | collective-permute-start | bytes 393224 | tf_op jit(solution)/shard_map/ppermute | solution.py:61
  143.1 13.0 %collective-permute-start.11 = (bf16[64,1024]{1,0:T(8,128)(2,1)S(1)}, bf16[64,1024]{1,0:T(8,128)(2,1)S(1)}, u32[]{:S(2)}, u32[]{:S(2)}) collective-permute-start(bf16[64,1024]{1,0:T(8,128)(2,1)S(1)} %get-tuple-element.11), channel_id=1, source_target_pairs={{208,176},{209,177},{210,178},{211,179},{212,180},{213,181},{214,1... | collective-permute-start | bytes 393224 | tf_op jit(solution)/shard_map/ppermute | solution.py:61
  147.4 25.4 %collective-permute-start.22 = (bf16[256,1024]{1,0:T(8,128)(2,1)S(1)}, bf16[256,1024]{1,0:T(8,128)(2,1)S(1)}, u32[]{:S(2)}, u32[]{:S(2)}) collective-permute-start(bf16[256,1024]{1,0:T(8,128)(2,1)S(1)} %pad_maximum_fusion.a), channel_id=1, source_target_pairs={{0,8},{1,9},{2,10},{3,11},{4,12},{5,13},{6,14},{7,15},{8,0},{9,1},... | collective-permute-start | bytes 1572872 | tf_op jit(solution)/shard_map/ppermute | solution.py:55
  150.8 22.1 %collective-permute-start.21 = (bf16[256,1024]{1,0:T(8,128)(2,1)S(1)}, bf16[256,1024]{1,0:T(8,128)(2,1)}, u32[]{:S(2)}, u32[]{:S(2)}) collective-permute-start(bf16[256,1024]{1,0:T(8,128)(2,1)S(1)} %pad_maximum_fusion.a), channel_id=1, source_target_pairs={{0,12},{1,13},{2,14},{3,15},{4,0},{5,1},{6,2},{7,3},{8,4},{9,5},{1... | collective-permute-start | bytes 1572872 | tf_op jit(solution)/shard_map/ppermute | solution.py:55
  154.0 18.9 %collective-permute-start.20 = (bf16[256,1024]{1,0:T(8,128)(2,1)S(1)}, bf16[256,1024]{1,0:T(8,128)(2,1)}, u32[]{:S(2)}, u32[]{:S(2)}) collective-permute-start(bf16[256,1024]{1,0:T(8,128)(2,1)S(1)} %pad_maximum_fusion.a), channel_id=1, source_target_pairs={{0,4},{1,5},{2,6},{3,7},{4,8},{5,9},{6,10},{7,11},{8,12},{9,13},{1... | collective-permute-start | bytes 1572872 | tf_op jit(solution)/shard_map/ppermute | solution.py:55
  156.1 14.0 %collective-permute-start.14 = (bf16[64,1024]{1,0:T(8,128)(2,1)S(1)}, bf16[64,1024]{1,0:T(8,128)(2,1)S(1)}, u32[]{:S(2)}, u32[]{:S(2)}) collective-permute-start(bf16[64,1024]{1,0:T(8,128)(2,1)S(1)} %add.276), channel_id=1, source_target_pairs={{176,112},{80,16},{177,113},{81,17},{178,114},{82,18},{179,115},{8... | collective-permute-start | bytes 393224 | tf_op jit(solution)/shard_map/ppermute | solution.py:61
  157.4 12.7 %collective-permute-start.13 = (bf16[64,1024]{1,0:T(8,128)(2,1)S(1)}, bf16[64,1024]{1,0:T(8,128)(2,1)S(1)}, u32[]{:S(2)}, u32[]{:S(2)}) collective-permute-start(bf16[64,1024]{1,0:T(8,128)(2,1)S(1)} %add.276), channel_id=1, source_target_pairs={{176,144},{80,48},{177,145},{81,49},{178,146},{82,50},{179,147},{8... | collective-permute-start | bytes 393224 | tf_op jit(solution)/shard_map/ppermute | solution.py:61
  170.8 3.5 %collective-permute-start.15 = (bf16[64,1024]{1,0:T(8,128)(2,1)}, bf16[64,1024]{1,0:T(8,128)(2,1)}, u32[]{:S(2)}, u32[]{:S(2)}) collective-permute-start(bf16[64,1024]{1,0:T(8,128)(2,1)} %add_add_fusion), channel_id=1, source_target_pairs={{16,0},{48,32},{80,64},{112,96},{144,128},{176,160},{17,1},{49,33}... | collective-permute-start | bytes 393224 | tf_op jit(solution)/shard_map/ppermute | solution.py:166
  172.8 1.5 copy-start.2

commit v4 on v3

v4 whole, which is shorter than its diff:
```python
import jax
import jax.numpy as jnp
from jax import lax
from jax.experimental import pallas as pl
from jax.experimental.pallas import tpu as pltpu
from jax.sharding import PartitionSpec as P

HALF = 512
BOTH = ("depth", "lat")
F32 = jnp.float32
BF16 = jnp.bfloat16
SIDE = 4
VMEM = pl.BlockSpec(memory_space=pltpu.VMEM)
SMEM = pl.BlockSpec(memory_space=pltpu.SMEM)
PARAMS = pltpu.CompilerParams(vmem_limit_bytes=32 * 1024 * 1024)


def mm(a, b):
    return jnp.dot(a, b, preferred_element_type=F32)


def around(base):
    return [(base + shift) % SIDE for shift in (0, -1, 1, 2)]


def ring_moves(depths, flipped, shift):
    pairs = []
    for d in depths:
        by_x = (d % 2 == 0) != flipped
        for y in range(SIDE):
            for x in range(SIDE):
                ty, tx = (y, (x + shift) % SIDE) if by_x else ((y + shift) % SIDE, x)
                pairs.append(((d * SIDE + y) * SIDE + x, (d * SIDE + ty) * SIDE + tx))
    return pairs


def ring_gather(value, depths, flipped):
    return [value] + [
        lax.ppermute(value, BOTH, ring_moves(depths, flipped, shift))
        for shift in (1, -1, 2)
    ]


def sent_down(value, chip_pairs):
    return lax.ppermute(value, "depth", [(2 * a + 1, 2 * b + 1) for a, b in chip_pairs])


def place_kernel(order, a, b, c, d, out):
    count = out.shape[0] // 16
    for g, block in enumerate((a, b, c, d)):
        for f in range(4):
            start = pl.multiple_of(order[4 * g + f] * count, count)
            out[pl.ds(start, count), :] = block[f * count : (f + 1) * count, :]


def place(order, blocks):
    rows, width = blocks[0].shape
    return pl.pallas_call(
        place_kernel,
        out_shape=jax.ShapeDtypeStruct((4 * rows, width), blocks[0].dtype),
        in_specs=[SMEM] + [VMEM] * 4,
        out_specs=VMEM,
        compiler_params=PARAMS,
    )(order, *blocks)


def pack_kernel(a, b, c, d, out):
    count = a.shape[1]
    wide = out.shape[1]
    for f, block in enumerate((a, b, c, d)):
        out[0, f * count : (f + 1) * count, :] = block[0]
    for m in range(a.shape[2] // wide):
        cut = slice(m * wide, (m + 1) * wide)
        turned = jnp.concatenate([block[1, :, cut] for block in (a, b, c, d)])
        out[1, :, cut] = turned.T


def pack(blocks):
    two, count, width = blocks[0].shape
    return pl.pallas_call(
        pack_kernel,
        out_shape=jax.ShapeDtypeStruct((two, 4 * count, width), BF16),
        in_specs=[VMEM] * 4,
        out_specs=VMEM,
        compiler_params=PARAMS,
    )(*blocks)


def step_kernel(panel, a, b, c, d, step, bias):
    wide = a.shape[1]
    right = jnp.concatenate([block[0] for block in (a, b, c, d)])
    for m in range(step.shape[0] // wide):
        cut = slice(m * wide, (m + 1) * wide)
        left = jnp.concatenate([block[1, :, cut] for block in (a, b, c, d)], axis=1)
        step[cut, :] = (-mm(left, right)).astype(BF16)
    bias[...] = -mm(panel[...], right)


def step_terms(panel, blocks):
    width = blocks[0].shape[2]
    return pl.pallas_call(
        step_kernel,
        out_shape=[
            jax.ShapeDtypeStruct((width, width), BF16),
            jax.ShapeDtypeStruct(panel.shape, F32),
        ],
        in_specs=[VMEM] * 5,
        out_specs=[VMEM, VMEM],
        compiler_params=PARAMS,
        cost_estimate=pl.CostEstimate(flops=2 * width**3, bytes_accessed=6 * width**2, transcendentals=0),
    )(panel, *blocks)


def product_kernel(core, own, got, bias, bias_got, product, odd, add_even):
    cut = 256
    width = own.shape[0]

    def fill(first, second):
        for m in range(width // cut):
            rows = slice(m * cut, (m + 1) * cut)
            product[rows, :] = mm(first[rows, :], second[...]).astype(BF16)
        odd[...] = first[...]

    @pl.when(core[0] == 0)
    def _():
        fill(got, own)
        add_even[...] = jnp.zeros_like(add_even)

    @pl.when(core[0] != 0)
    def _():
        fill(own, got)
        add_even[...] = mm(bias[...].astype(BF16), got[...]) + bias_got[...]


def products(core, own, got, bias, bias_got):
    width = own.shape[0]
    return pl.pallas_call(
        product_kernel,
        out_shape=[
            jax.ShapeDtypeStruct(own.shape, BF16),
            jax.ShapeDtypeStruct(own.shape, BF16),
            jax.ShapeDtypeStruct(bias.shape, F32),
        ],
        in_specs=[SMEM] + [VMEM] * 4,
        out_specs=[VMEM] * 3,
        compiler_params=PARAMS,
        cost_estimate=pl.CostEstimate(flops=2 * width**3, bytes_accessed=6 * width**2, transcendentals=0),
    )(core.reshape(1), own, got, bias, bias_got)


def body(inv_diag, couple, arrow, corner, band_offset):
    depth_count = lax.axis_size("depth")
    lat_count = lax.axis_size("lat")
    depth = lax.axis_index("depth")
    lat = lax.axis_index("lat")
    core = depth % 2
    chip = depth // 2
    chips = depth_count // 2
    low = core == 0
    y, x = lat // SIDE, lat % SIDE
    order = [
        jnp.where(low, SIDE * b + a, SIDE * a + b)
        for b in around(jnp.where(low, y, x))
        for a in around(jnp.where(low, x, y))
    ]
    g_rows = inv_diag[0]
    share, width = g_rows.shape
    cells = couple[0].T
    row = lax.broadcasted_iota(jnp.int32, cells.shape, 0) + lat * share
    col = lax.broadcasted_iota(jnp.int32, cells.shape, 1)
    keep = jnp.abs(row - col - band_offset[0]) <= HALF
    pair = jnp.stack([g_rows, jnp.where(keep, cells, jnp.zeros_like(cells))])
    panel = mm(corner, arrow[0]).astype(BF16)
    panel_rows = lax.all_to_all(panel.reshape(lat_count, share, share), "lat", 0, 0)
    everyone = range(depth_count)
    first = pack(ring_gather(pair, everyone, False))
    blocks = ring_gather(first, everyone, True)
    panel_cut = jnp.concatenate(
        [lax.dynamic_index_in_dim(panel_rows, q, 0, False) for q in order], axis=1
    )
    step, bias = step_terms(panel_cut, blocks)
    swap = [(d, d ^ 1) for d in range(depth_count)]
    got = lax.ppermute(step, "depth", swap)
    bias_got = lax.ppermute(bias, "depth", [(2 * k, 2 * k + 1) for k in range(chips)])
    product, step_odd, add_even = products(core, step, got, bias, bias_got)
    add_odd = jnp.where(low, jnp.zeros_like(bias), bias)
    lower = (chips * 6) // 16
    tops = [chips - 1, lower - 1]
    sizes = [chips - lower, lower]
    start = (row == col) & ((chip == tops[0]) | (chip == tops[1])) & low
    v_in = jnp.where(start, 1.0, 0.0).astype(BF16)
    v_even = mm(v_in, product) + add_even
    for hop in range(1, max(sizes)):
        pairs = []
        for block_top, size in zip(tops, sizes):
            if hop < size:
                source = block_top - hop + 1
                pairs += [(2 * source + k, 2 * source - 2 + k) for k in range(2)]
        v_in = v_in + lax.ppermute(v_even.astype(BF16), "depth", pairs)
        v_even = mm(v_in, product) + add_even
    edge = v_even.astype(BF16)
    v_odd = mm(v_in, step_odd) + add_odd
    other = lax.ppermute(
        jnp.where(low, v_odd.astype(BF16), edge), "depth", swap[: 2 * lower]
    )
    map_rows = jnp.where(low, edge, other)
    depths = range(2 * lower)
    ring = jnp.concatenate(ring_gather(map_rows, depths, False))
    near, far = lower - 1, lower // 2 - 1
    entry = sent_down(edge, [(lower, near)]) + sent_down(edge, [(lower, far)])
    relayed = sent_down(entry, [(near, near - 1), (far, far - 1)])
    last = [(source, source - 2) for source, low_end in ((near, far), (far, -1)) if source - 2 > low_end]
    entry = entry + relayed + sent_down(entry, last)
    maps = place(jnp.stack(order), ring_gather(ring, depths, True))
    below = chip < lower
    across = lax.ppermute(
        jnp.where(below, entry, edge), "depth", [(2 * k + 1, 2 * k) for k in range(chips)]
    )
    zero = jnp.zeros_like(entry)
    enter = jnp.where(below, jnp.where(low, across, entry), zero)
    own = jnp.where(low, jnp.where(below, other, across).astype(F32), v_odd)
    return (mm(enter, maps) + own)[None]


def solution(mesh):
    placed = (
        P("depth", "lat", None),
        P("depth", None, "lat"),
        P("depth", None, "lat"),
        P(),
        P("depth"),
    )
    return jax.shard_map(
        body, mesh=mesh, in_specs=placed, out_specs=P("depth", "lat", None), check_vma=False
    )
```

time: 177 us -> 178 us (level)
  matrix products: 26.7 us -> 8.32 us
  blocking collectives: 14.9 us -> 0 us
  waiting for transfers between devices: 66.1 us -> 80.3 us
  starting transfers between devices: 53.9 us -> 67.9 us
  Pallas kernels: 1.39 us -> 12 us
  local copies, waits for them, and re-layouts: 8.74 us -> 3.18 us
    all_to_all x1 -> x0, waiting for transfers between devices: 26.2 us -> none  [gather_one(): return lax.all_to_all(spread, BOTH, 0, 0, axis_index_groups=axis_groups)]
    ppermute x9 -> x15, starting transfers between devices: 27.2 us -> 47.1 us  [the longest x12 37.9 us: ring_gather(): lax.ppermute(value, BOTH, ring_moves(depths, flipped, shift))]
    ppermute x9 -> x15, waiting for transfers between devices: 4.59 us -> 21.2 us  [the longest x12 18.5 us: ring_gather(): lax.ppermute(value, BOTH, ring_moves(depths, flipped, shift))]
    all_to_all x1 -> x0, blocking collectives: 14.9 us -> none  [gather_one(): return lax.all_to_all(spread, BOTH, 0, 0, axis_index_groups=axis_groups)]
    dot_general x17 -> x13, matrix products: 20.8 us -> 8.32 us  [mm(): return jnp.dot(a, b, preferred_element_type=F32)]
    all_to_all x1, waiting for transfers between devices: 3.08 us -> 14.3 us  [body(): lax.all_to_all(panel.reshape(lat_count, share, share), 'lat', 0, 0)]
    pallas_call x0 -> x3, Pallas kernels: none -> 10.7 us  [the longest x1 5.58 us: step_terms(): pl.pallas_call(step_kernel, out_shape=[jax.ShapeDtypeStruct((width, width...]
    ppermute x4, waiting for transfers between devices: 12 us -> 20.6 us  [sent_down(): lax.ppermute(value, 'depth', [(2 * a + 1, 2 * b + 1) for a, b in chip_pai...]
  transfers between devices with their start and end apart: 25 -> 30, of which waited for: 6 -> 12; matrix products, arithmetic and copies ran while one was open for 8% -> 2% of each run, Pallas kernels for 1% -> 1%
where the time goes in v4:
time: 178 us; the launch traced here: 177 us
  waiting for transfers between devices  80.3 us (45%)
  starting transfers between devices  67.9 us (38%)
  Pallas kernels  12 us (7%)
  matrix products  8.32 us (5%)
  local copies, waits for them, and re-layouts  3.18 us (2%)
  other arithmetic  3.12 us (2%)
  between operations  1.8 us (1%)
    ppermute x12, starting transfers between devices, ring_gather(): lax.ppermute(value, BOTH, ring_moves(depths, flipped, shift))  37.9 us
    ppermute x9, waiting for transfers between devices, body(): v_in = v_in + lax.ppermute(v_even.astype(BF16), 'depth', pairs)  24.1 us
    ppermute x4, waiting for transfers between devices, sent_down(): lax.ppermute(value, 'depth', [(2 * a + 1, 2 * b + 1) for a, b in chip_pai...  20.6 us
    ppermute x12, waiting for transfers between devices, ring_gather(): lax.ppermute(value, BOTH, ring_moves(depths, flipped, shift))  18.5 us
    all_to_all x1, waiting for transfers between devices, body(): lax.all_to_all(panel.reshape(lat_count, share, share), 'lat', 0, 0)  14.3 us
    dot_general x13, matrix products, mm(): return jnp.dot(a, b, preferred_element_type=F32)  8.32 us
    ppermute x1, starting transfers between devices, body(): got = lax.ppermute(step, 'depth', swap)  7.03 us
    ppermute x9, starting transfers between devices, body(): v_in = v_in + lax.ppermute(v_even.astype(BF16), 'depth', pairs)  6.82 us
  transfers between devices with their start and end apart: 30, of which 12 were waited for; matrix products, arithmetic and copies ran while one was open for 2% of the time, Pallas kernels for 1%

profile of v4, /device:TPU:1, one launch (start us, length us, event | category | flops | bytes accessed | tf_op | source)
XLA Modules:
  0.0 176.6 jit_solution(16669277598166424634)
XLA Ops:
  0.8 1.0 fusion.15
  1.9 0.9 pad_maximum_fusion.1.a
  2.8 5.7 %collective-permute-start.2 = (bf16[2,64,1024]{2,1,0:T(8,128)(2,1)S(1)}, bf16[2,64,1024]{2,1,0:T(8,128)(2,1)S(1)}, u32[]{:S(2)}, u32[]{:S(2)}) collective-permute-start(bf16[2,64,1024]{2,1,0:T(8,128)(2,1)S(1)} %pad_maximum_fusion.1.a), channel_id=1, source_target_pairs={{0,2},{1,3},{2,0},{3,1},{4,6},{5,7},{6,4},{7,5},{8,10},{9,11},{10,... | collective-permute-start | bytes 786440 | tf_op jit(solution)/shard_map/ppermute | solution.py:39
  8.5 2.7 %collective-permute-start.1 = (bf16[2,64,1024]{2,1,0:T(8,128)(2,1)S(1)}, bf16[2,64,1024]{2,1,0:T(8,128)(2,1)S(1)}, u32[]{:S(2)}, u32[]{:S(2)}) collective-permute-start(bf16[2,64,1024]{2,1,0:T(8,128)(2,1)S(1)} %pad_maximum_fusion.1.a), channel_id=1, source_target_pairs={{0,3},{1,0},{2,1},{3,2},{4,7},{5,4},{6,5},{7,6},{8,11},{9,8},{10,9... | collective-permute-start | bytes 786440 | tf_op jit(solution)/shard_map/ppermute | solution.py:39
  11.2 2.6 %collective-permute-start = (bf16[2,64,1024]{2,1,0:T(8,128)(2,1)S(1)}, bf16[2,64,1024]{2,1,0:T(8,128)(2,1)S(1)}, u32[]{:S(2)}, u32[]{:S(2)}) collective-permute-start(bf16[2,64,1024]{2,1,0:T(8,128)(2,1)S(1)} %pad_maximum_fusion.1.a), channel_id=1, source_target_pairs={{0,1},{1,2},{2,3},{3,0},{4,5},{5,6},{6,7},{7,4},{8,9},{9,10},{10,1... | collective-permute-start | bytes 786440 | tf_op jit(solution)/shard_map/ppermute | solution.py:39
  13.8 1.8 %collective-permute-done.1.c = bf16[2,64,1024]{2,1,0:T(8,128)(2,1)S(1)} collective-permute-done((bf16[2,64,1024]{2,1,0:T(8,128)(2,1)S(1)}, bf16[2,64,1024]{2,1,0:T(8,128)(2,1)S(1)}, u32[]{:S(2)}, u32[]{:S(2)}) %collective-permute-start.1) | collective-permute-done | bytes 262176 | tf_op jit(solution)/shard_map/ppermute | solution.py:39
  15.6 3.9 %collective-permute-done.b = bf16[2,64,1024]{2,1,0:T(8,128)(2,1)S(1)} collective-permute-done((bf16[2,64,1024]{2,1,0:T(8,128)(2,1)S(1)}, bf16[2,64,1024]{2,1,0:T(8,128)(2,1)S(1)}, u32[]{:S(2)}, u32[]{:S(2)}) %collective-permute-start) | collective-permute-done | bytes 262176 | tf_op jit(solution)/shard_map/ppermute | solution.py:39
  19.7 4.7 %collective-permute-start.5 = (bf16[2,256,1024]{2,1,0:T(8,128)(2,1)S(1)}, bf16[2,256,1024]{2,1,0:T(8,128)(2,1)}, u32[]{:S(2)}, u32[]{:S(2)}) collective-permute-start(bf16[2,256,1024]{2,1,0:T(8,128)(2,1)S(1)} %shard_map.55.a), channel_id=1, source_target_pairs={{0,8},{1,9},{2,10},{3,11},{4,12},{5,13},{6,14},{7,15},{8,0},{9,1},... | collective-permute-start | bytes 3145736 | tf_op jit(solution)/shard_map/ppermute | solution.py:39
  24.4 2.8 %collective-permute-start.4 = (bf16[2,256,1024]{2,1,0:T(8,128)(2,1)S(1)}, bf16[2,256,1024]{2,1,0:T(8,128)(2,1)}, u32[]{:S(2)}, u32[]{:S(2)}) collective-permute-start(bf16[2,256,1024]{2,1,0:T(8,128)(2,1)S(1)} %shard_map.55.a), channel_id=1, source_target_pairs={{0,12},{1,13},{2,14},{3,15},{4,0},{5,1},{6,2},{7,3},{8,4},{9,5},{1... | collective-permute-start | bytes 3145736 | tf_op jit(solution)/shard_map/ppermute | solution.py:39
  27.1 2.5 %collective-permute-start.3 = (bf16[2,256,1024]{2,1,0:T(8,128)(2,1)S(1)}, bf16[2,256,1024]{2,1,0:T(8,128)(2,1)}, u32[]{:S(2)}, u32[]{:S(2)}) collective-permute-start(bf16[2,256,1024]{2,1,0:T(8,128)(2,1)S(1)} %shard_map.55.a), channel_id=1, source_target_pairs={{0,4},{1,5},{2,6},{3,7},{4,8},{5,9},{6,10},{7,11},{8,12},{9,13},{1... | collective-permute-start | bytes 3145736 | tf_op jit(solution)/shard_map/ppermute | solution.py:39
  29.7 0.8 convolution_convert_fusion
  30.6 0.9 reshape.8
  31.5 3.7 %all-to-all-start = ((bf16[16,2,2048]{2,1,0:T(2,128)(2,1)}), bf16[16,2,2048]{2,1,0:T(2,128)(2,1)S(1)}, u32[]{:S(2)}, u32[]{:S(2)}) async-start(bf16[16,2,2048]{2,1,0:T(2,128)(2,1)} %reshape.8), calls=%async_computation | async-start | bytes 262144 | tf_op jit(solution)/shard_map/all_to_all | solution.py:174
  35.5 14.3 %all-to-all-done = bf16[16,2,2048]{2,1,0:T(2,128)(2,1)S(1)} async-done(((bf16[16,2,2048]{2,1,0:T(2,128)(2,1)}), bf16[16,2,2048]{2,1,0:T(2,128)(2,1)S(1)}, u32[]{:S(2)}, u32[]{:S(2)}) %all-to-all-start) | async-done | bytes 131104 | tf_op jit(solution)/shard_map/all_to_all | solution.py:174
  49.8 0.2 reshape.9
  50.0 0.7 dynamic-slice_bitcast_fusion
  50.8 1.0 concatenate.6.panel
  51.9 5.6 %shard_map.56 = (bf16[1024,1024]{1,0:T(8,128)(2,1)}, f32[64,1024]{1,0:T(8,128)S(1)}) custom-call(bf16[64,1024]{1,0:T(8,128)(2,1)S(1)} %concatenate.6.panel, bf16[2,256,1024]{2,1,0:T(8,128)(2,1)S(1)} %shard_map.55.a, bf16[2,256,1024]{2,1,0:T(8,128)(2,1)} %collective-permute-done.3.b, bf16[2,256,1024]{2,1,0:T(8,128)(2,1)} %collective-permute-done.4.c, ...), custom_call_target="tpu_custom_call" | custom-call | flops 2147483648 | bytes 6291456 | tf_op jit(solution)/shard_map/pallas_call | solution.py:101
  57.4 7.0 %collective-permute-start.6 = (bf16[1024,1024]{1,0:T(8,128)(2,1)}, bf16[1024,1024]{1,0:T(8,128)(2,1)}, u32[]{:S(2)}, u32[]{:S(2)}) collective-permute-start(bf16[1024,1024]{1,0:T(8,128)(2,1)} %get-tuple-element.10.own), channel_id=1, source_target_pairs={{0,16},{16,0},{32,48},{48,32},{64,80},{80,64},{96,112},{112,96},{1... | collective-permute-start | bytes 6291464 | tf_op jit(solution)/shard_map/ppermute | solution.py:183
  64.5 1.3 collective-permute-start.7
  65.8 2.7 %collective-permute-done.7.bias_got = f32[64,1024]{1,0:T(8,128)S(1)} collective-permute-done((f32[64,1024]{1,0:T(8,128)S(1)}, f32[64,1024]{1,0:T(8,128)S(1)}, u32[]{:S(2)}, u32[]{:S(2)}) %collective-permute-start.7) | collective-permute-done | bytes 262176 | tf_op jit(solution)/shard_map/ppermute | solution.py:184
  68.6 4.9 %shard_map.57 = (bf16[1024,1024]{1,0:T(8,128)(2,1)S(1)}, bf16[1024,1024]{1,0:T(8,128)(2,1)S(1)}, f32[64,1024]{1,0:T(8,128)S(1)}) custom-call(s32[1]{0:T(128)} %bitcast.core, bf16[1024,1024]{1,0:T(8,128)(2,1)} %get-tuple-element.10.own, bf16[1024,1024]{1,0:T(8,128)(2,1)} %collective-permute-done.6.got, f32[64,1024]{1,0:T(8,128)S(1)} %get-tuple-element.11.bias, ...), custom_call_target="tpu_custom_call" | custom-call | flops 2147483648 | bytes 6291456 | tf_op jit(solution)/shard_map/pallas_call | solution.py:137
  73.5 0.5 fusion.1
  74.0 0.7 collective-permute-start.8
  74.7 0.6 fusion.2
  75.3 0.7 collective-permute-start.9
  76.0 0.5 fusion.3
  76.5 0.7 collective-permute-start.10
  77.4 0.5 fusion.4
  77.9 0.7 collective-permute-start.11
  78.6 0.5 fusion.5
  79.1 1.3 collective-permute-start.12
  80.4 24.1 %collective-permute-done.12 = bf16[64,1024]{1,0:T(8,128)(2,1)S(1)} collective-permute-done((bf16[64,1024]{1,0:T(8,128)(2,1)S(1)}, bf16[64,1024]{1,0:T(8,128)(2,1)S(1)}, u32[]{:S(2)}, u32[]{:S(2)}) %collective-permute-start.12) | collective-permute-done | bytes 131104 | tf_op jit(solution)/shard_map/ppermute | solution.py:199
  104.5 0.5 fusion.6
  105.0 0.7 collective-permute-start.13
  105.8 0.5 fusion.7
  106.2 0.7 collective-permute-start.14
  107.0 0.5 fusion.8
  107.5 0.8 collective-permute-start.15
  108.4 0.5 fusion.9
  108.9 0.7 collective-permute-start.16
  109.6 0.5 convolution_add_fusion.1
  110.1 0.5 convert_select_fusion
  110.6 0.7 collective-permute-start.18
  111.2 0.7 collective-permute-start.17
  111.9 6.0 %collective-permute-start.22 = (bf16[64,1024]{1,0:T(8,128)(2,1)S(1)}, bf16[64,1024]{1,0:T(8,128)(2,1)S(1)}, u32[]{:S(2)}, u32[]{:S(2)}) collective-permute-start(bf16[64,1024]{1,0:T(8,128)(2,1)S(1)} %get-tuple-element.33), channel_id=1, source_target_pairs={{0,16},{16,0},{32,48},{48,32},{64,80},{80,64},{96,112},{112,96},{1... | collective-permute-start | bytes 393224 | tf_op jit(solution)/shard_map/ppermute | solution.py:203
  118.0 1.3 collective-permute-start.20
  119.3 0.7 collective-permute-start.19
  119.9 20.5 %collective-permute-done.20 = bf16[64,1024]{1,0:T(8,128)(2,1)S(1)} collective-permute-done((bf16[64,1024]{1,0:T(8,128)(2,1)S(1)}, bf16[64,1024]{1,0:T(8,128)(2,1)S(1)}, u32[]{:S(2)}, u32[]{:S(2)}) %collective-permute-start.20) | collective-permute-done | bytes 131104 | tf_op jit(solution)/shard_map/ppermute | solution.py:45
  140.5 0.7 broadcast_select_fusion.1
  141.2 4.5 %collective-permute-start.25 = (bf16[64,1024]{1,0:T(8,128)(2,1)S(1)}, bf16[64,1024]{1,0:T(8,128)(2,1)S(1)}, u32[]{:S(2)}, u32[]{:S(2)}) collective-permute-start(bf16[64,1024]{1,0:T(8,128)(2,1)S(1)} %get-tuple-element.32), channel_id=1, source_target_pairs={{0,2},{1,3},{2,0},{3,1},{4,6},{5,7},{6,4},{7,5},{8,10},{9,11},{10,... | collective-permute-start | bytes 393224 | tf_op jit(solution)/shard_map/ppermute | solution.py:39
  145.7 2.7 %collective-permute-start.24 = (bf16[64,1024]{1,0:T(8,128)(2,1)S(1)}, bf16[64,1024]{1,0:T(8,128)(2,1)S(1)}, u32[]{:S(2)}, u32[]{:S(2)}) collective-permute-start(bf16[64,1024]{1,0:T(8,128)(2,1)S(1)} %get-tuple-element.32), channel_id=1, source_target_pairs={{0,3},{1,0},{2,1},{3,2},{4,7},{5,4},{6,5},{7,6},{8,11},{9,8},{10,9... | collective-permute-start | bytes 393224 | tf_op jit(solution)/shard_map/ppermute | solution.py:39
  148.4 2.6 %collective-permute-start.23 = (bf16[64,1024]{1,0:T(8,128)(2,1)S(1)}, bf16[64,1024]{1,0:T(8,128)(2,1)S(1)}, u32[]{:S(2)}, u32[]{:S(2)}) collective-permute-start(bf16[64,1024]{1,0:T(8,128)(2,1)S(1)} %get-tuple-element.32), channel_id=1, source_target_pairs={{0,1},{1,2},{2,3},{3,0},{4,5},{5,6},{6,7},{7,4},{8,9},{9,10},{10,1... | collective-permute-start | bytes 393224 | tf_op jit(solution)/shard_map/ppermute | solution.py:39
  151.0 2.3 %collective-permute-done.24 = bf16[64,1024]{1,0:T(8,128)(2,1)S(1)} collective-permute-done((bf16[64,1024]{1,0:T(8,128)(2,1)S(1)}, bf16[64,1024]{1,0:T(8,128)(2,1)S(1)}, u32[]{:S(2)}, u32[]{:S(2)}) %collective-permute-start.24) | collective-permute-done | bytes 131104 | tf_op jit(solution)/shard_map/ppermute | solution.py:39
  153.3 2.7 %collective-permute-done.23 = bf16[64,1024]{1,0:T(8,128)(2,1)S(1)} collective-permute-done((bf16[64,1024]{1,0:T(8,128)(2,1)S(1)}, bf16[64,1024]{1,0:T(8,128)(2,1)S(1)}, u32[]{:S(2)}, u32[]{:S(2)}) %collective-permute-start.23) | collective-permute-done | bytes 131104 | tf_op jit(solution)/shard_map/ppermute | solution.py:39
  156.0 2.0 %collective-permute-start.28 = (bf16[256,1024]{1,0:T(8,128)(2,1)S(1)}, bf16[256,1024]{1,0:T(8,128)(2,1)S(1)}, u32[]{:S(2)}, u32[]{:S(2)}) collective-permute-start(bf16[256,1024]{1,0:T(8,128)(2,1)S(1)} %pad_maximum_fusion.a), channel_id=1, source_target_pairs={{0,8},{1,9},{2,10},{3,11},{4,12},{5,13},{6,14},{7,15},{8,0},{9,1},... | collective-permute-start | bytes 1572872 | tf_op jit(solution)/shard_map/ppermute | solution.py:39
  158.0 3.4 %collective-permute-start.27 = (bf16[256,1024]{1,0:T(8,128)(2,1)S(1)}, bf16[256,1024]{1,0:T(8,128)(2,1)}, u32[]{:S(2)}, u32[]{:S(2)}) collective-permute-start(bf16[256,1024]{1,0:T(8,128)(2,1)S(1)} %pad_maximum_fusion.a), channel_id=1, source_target_pairs={{0,12},{1,13},{2,14},{3,15},{4,0},{5,1},{6,2},{7,3},{8,4},{9,5},{1... | collective-permute-start | bytes 1572872 | tf_op jit(solution)/shard_map/ppermute | solution.py:39
  161.3 1.9 %collective-permute-start.26 = (bf16[256,1024]{1,0:T(8,128)(2,1)S(1)}, bf16[256,1024]{1,0:T(8,128)(2,1)}, u32[]{:S(2)}, u32[]{:S(2)}) collective-permute-start(bf16[256,1024]{1,0:T(8,128)(2,1)S(1)} %pad_maximum_fusion.a), channel_id=1, source_target_pairs={{0,4},{1,5},{2,6},{3,7},{4,8},{5,9},{6,10},{7,11},{8,12},{9,13},{1... | collective-permute-start | bytes 1572872 | tf_op jit(solution)/shard_map/ppermute | solution.py:39
  163.3 1.9 %collective-permute-start.21 = (bf16[64,1024]{1,0:T(8,128)(2,1)}, bf16[64,1024]{1,0:T(8,128)(2,1)}, u32[]{:S(2)}, u32[]{:S(2)}) collective-permute-start(bf16[64,1024]{1,0:T(8,128)(2,1)} %get-tuple-element.31), channel_id=1, source_target_pairs={{16,0},{48,32},{80,64},{112,96},{144,128},{176,160},{208,192},{240... | collective-permute-start | bytes 393224 | tf_op jit(solution)/shard_map/ppermute | solution.py:216
  165.3 2.2 %collective-permute-done.28.d = bf16[256,1024]{1,0:T(8,128)(2,1)S(1)} collective-permute-done((bf16[256,1024]{1,0:T(8,128)(2,1)S(1)}, bf16[256,1024]{1,0:T(8,128)(2,1)S(1)}, u32[]{:S(2)}, u32[]{:S(2)}) %collective-permute-start.28) | collective-permute-done | bytes 524320 | tf_op jit(solution)/shard_map/ppermute | solution.py:39
  167.5 3.2 %collective-permute-done.27.c = bf16[256,1024]{1,0:T(8,128)(2,1)} collective-permute-done((bf16[256,1024]{1,0:T(8,128)(2,1)S(1)}, bf16[256,1024]{1,0:T(8,128)(2,1)}, u32[]{:S(2)}, u32[]{:S(2)}) %collective-permute-start.27) | collective-permute-done | bytes 524320 | tf_op jit(solution)/shard_map/ppermute | solution.py:39
  170.7 2.4 %collective-permute-done.26.b = bf16[256,1024]{1,0:T(8,128)(2,1)} collective-permute-done((bf16[256,1024]{1,0:T(8,128)(2,1)S(1)}, bf16[256,1024]{1,0:T(8,128)(2,1)}, u32[]{:S(2)}, u32[]{:S(2)}) %collective-permute-start.26) | collective-permute-done | bytes 524320 | tf_op jit(solution)/shard_map/ppermute | solution.py:39
  173.1 1.3 shard_map.58
  174.5 2.1 %fusion = f32[1,64,1024]{2,1,0:T(8,128)} fusion(bf16[1024,1024]{1,0:T(8,128)(2,1)S(1)} %shard_map.58, f32[64,1024]{1,0:T(8,128)S(1)} %copy-done.2, bf16[64,1024]{1,0:T(8,128)(2,1)S(1)} %collective-permute-done.22, bf16[64,1024]{1,0:T(8,128)(2,1)} %collective-permute-done.21, pred[]{:T(512)S(6)} %eq.35, pred[]{:T(512)S(6)} %lt.118, ...), kind=kOutput, calls=%fused_computation.1 | convolution fusion | flops 134742016 | bytes 3276802 | tf_op jit(solution)/shard_map/dot_general | solution.py:19
  (47 shorter events, 1.1 us)
Async XLA Ops:
  0.0 29.7 %copy-start = (bf16[1024,1024]{1,0:T(8,128)(2,1)S(1)}, bf16[1024,1024]{1,0:T(8,128)(2,1)}, u32[]{:S(2)}) copy-start(bf16[1024,1024]{1,0:T(8,128)(2,1)} %param.8) | copy-start | bytes 6291460
  0.0 29.7 %copy-start.5 = (bf16[1,1024,64]{1,2,0:T(8,128)(2,1)S(1)}, bf16[1,1024,64]{1,2,0:T(8,128)(2,1)}, u32[]{:S(2)}) copy-start(bf16[1,1024,64]{1,2,0:T(8,128)(2,1)} %param.7) | copy-start | bytes 393220
  0.8 14.8 %copy-start.6 = (s32[64]{0:T(128)}, s32[64]{0:T(128)S(1)}, u32[]{:S(2)}) copy-start(s32[64]{0:T(128)S(1)} %iota_add_fusion) | copy-start | bytes 772
  2.8 11.0 %collective-permute-start.2 = (bf16[2,64,1024]{2,1,0:T(8,128)(2,1)S(1)}, bf16[2,64,1024]{2,1,0:T(8,128)(2,1)S(1)}, u32[]{:S(2)}, u32[]{:S(2)}) collective-permute-start(bf16[2,64,1024]{2,1,0:T(8,128)(2,1)S(1)} %pad_maximum_fusion.1.a), channel_id=1, source_target_pairs={{0,2},{1,3},{2,0},{3,1},{4,6},{5,7},{6,4},{7,5},{8,10},{9,11},{10,... | collective-permute-start | bytes 786440 | tf_op jit(solution)/shard_map/ppermute | solution.py:39
  8.5 7.1 %collective-permute-start.1 = (bf16[2,64,1024]{2,1,0:T(8,128)(2,1)S(1)}, bf16[2,64,1024]{2,1,0:T(8,128)(2,1)S(1)}, u32[]{:S(2)}, u32[]{:S(2)}) collective-permute-start(bf16[2,64,1024]{2,1,0:T(8,128)(2,1)S(1)} %pad_maximum_fusion.1.a), channel_id=1, source_target_pairs={{0,3},{1,0},{2,1},{3,2},{4,7},{5,4},{6,5},{7,6},{8,11},{9,8},{10,9... | collective-permute-start | bytes 786440 | tf_op jit(solution)/shard_map/ppermute | solution.py:39
  11.2 8.3 %collective-permute-start = (bf16[2,64,1024]{2,1,0:T(8,128)(2,1)S(1)}, bf16[2,64,1024]{2,1,0:T(8,128)(2,1)S(1)}, u32[]{:S(2)}, u32[]{:S(2)}) collective-permute-start(bf16[2,64,1024]{2,1,0:T(8,128)(2,1)S(1)} %pad_maximum_fusion.1.a), channel_id=1, source_target_pairs={{0,1},{1,2},{2,3},{3,0},{4,5},{5,6},{6,7},{7,4},{8,9},{9,10},{10,1... | collective-permute-start | bytes 786440 | tf_op jit(solution)/shard_map/ppermute | solution.py:39
  19.7 32.1 %collective-permute-start.5 = (bf16[2,256,1024]{2,1,0:T(8,128)(2,1)S(1)}, bf16[2,256,1024]{2,1,0:T(8,128)(2,1)}, u32[]{:S(2)}, u32[]{:S(2)}) collective-permute-start(bf16[2,256,1024]{2,1,0:T(8,128)(2,1)S(1)} %shard_map.55.a), channel_id=1, source_target_pairs={{0,8},{1,9},{2,10},{3,11},{4,12},{5,13},{6,14},{7,15},{8,0},{9,1},... | collective-permute-start | bytes 3145736 | tf_op jit(solution)/shard_map/ppermute | solution.py:39
  24.4 27.5 %collective-permute-start.4 = (bf16[2,256,1024]{2,1,0:T(8,128)(2,1)S(1)}, bf16[2,256,1024]{2,1,0:T(8,128)(2,1)}, u32[]{:S(2)}, u32[]{:S(2)}) collective-permute-start(bf16[2,256,1024]{2,1,0:T(8,128)(2,1)S(1)} %shard_map.55.a), channel_id=1, source_target_pairs={{0,12},{1,13},{2,14},{3,15},{4,0},{5,1},{6,2},{7,3},{8,4},{9,5},{1... | collective-permute-start | bytes 3145736 | tf_op jit(solution)/shard_map/ppermute | solution.py:39
  27.1 24.7 %collective-permute-start.3 = (bf16[2,256,1024]{2,1,0:T(8,128)(2,1)S(1)}, bf16[2,256,1024]{2,1,0:T(8,128)(2,1)}, u32[]{:S(2)}, u32[]{:S(2)}) collective-permute-start(bf16[2,256,1024]{2,1,0:T(8,128)(2,1)S(1)} %shard_map.55.a), channel_id=1, source_target_pairs={{0,4},{1,5},{2,6},{3,7},{4,8},{5,9},{6,10},{7,11},{8,12},{9,13},{1... | collective-permute-start | bytes 3145736 | tf_op jit(solution)/shard_map/ppermute | solution.py:39
  31.5 18.3 %all-to-all-start = ((bf16[16,2,2048]{2,1,0:T(2,128)(2,1)}), bf16[16,2,2048]{2,1,0:T(2,128)(2,1)S(1)}, u32[]{:S(2)}, u32[]{:S(2)}) async-start(bf16[16,2,2048]{2,1,0:T(2,128)(2,1)} %reshape.8), calls=%async_computation | async-start | bytes 262144 | tf_op jit(solution)/shard_map/all_to_all | solution.py:174
  57.4 11.1 %collective-permute-start.6 = (bf16[1024,1024]{1,0:T(8,128)(2,1)}, bf16[1024,1024]{1,0:T(8,128)(2,1)}, u32[]{:S(2)}, u32[]{:S(2)}) collective-permute-start(bf16[1024,1024]{1,0:T(8,128)(2,1)} %get-tuple-element.10.own), channel_id=1, source_target_pairs={{0,16},{16,0},{32,48},{48,32},{64,80},{80,64},{96,112},{112,96},{1... | collective-permute-start | bytes 6291464 | tf_op jit(solution)/shard_map/ppermute | solution.py:183
  64.5 4.0 %collective-permute-start.7 = (f32[64,1024]{1,0:T(8,128)S(1)}, f32[64,1024]{1,0:T(8,128)S(1)}, u32[]{:S(2)}, u32[]{:S(2)}) collective-permute-start(f32[64,1024]{1,0:T(8,128)S(1)} %get-tuple-element.11.bias), channel_id=1, source_target_pairs={{0,16},{32,48},{64,80},{96,112},{128,144},{160,176},{192,208},{224... | collective-permute-start | bytes 786440 | tf_op jit(solution)/shard_map/ppermute | solution.py:184
  68.6 4.9 %copy-start.7 = (s32[64]{0:T(128)S(1)}, s32[64]{0:T(128)}, u32[]{:S(2)}) copy-start(s32[64]{0:T(128)} %copy-done.6) | copy-start | bytes 772
  74.0 0.7 collective-permute-start.8
  75.3 0.7 collective-permute-start.9
  76.5 0.7 collective-permute-start.10
  77.9 0.7 collective-permute-start.11
  79.1 25.4 %collective-permute-start.12 = (bf16[64,1024]{1,0:T(8,128)(2,1)S(1)}, bf16[64,1024]{1,0:T(8,128)(2,1)S(1)}, u32[]{:S(2)}, u32[]{:S(2)}) collective-permute-start(bf16[64,1024]{1,0:T(8,128)(2,1)S(1)} %fusion.5), channel_id=1, source_target_pairs={{352,320},{368,336},{32,0},{48,16},{353,321},{369,337},{33,1},{49,... | collective-permute-start | bytes 393224 | tf_op jit(solution)/shard_map/ppermute | solution.py:199
  105.0 0.7 collective-permute-start.13
  106.2 0.7 collective-permute-start.14
  107.5 0.9 collective-permute-start.15
  108.9 0.7 collective-permute-start.16
  110.0 31.2 %copy-start.1 = (f32[64,1024]{1,0:T(8,128)}, f32[64,1024]{1,0:T(8,128)S(1)}, u32[]{:S(2)}) copy-start(f32[64,1024]{1,0:T(8,128)S(1)} %convolution_add_fusion.1) | copy-start | bytes 786436
  110.6 7.3 %collective-permute-start.18 = (bf16[64,1024]{1,0:T(8,128)(2,1)S(1)}, bf16[64,1024]{1,0:T(8,128)(2,1)S(1)}, u32[]{:S(2)}, u32[]{:S(2)}) collective-permute-start(bf16[64,1024]{1,0:T(8,128)(2,1)S(1)} %get-tuple-element.34), channel_id=1, source_target_pairs={{208,80},{209,81},{210,82},{211,83},{212,84},{213,85},{214,86},{21... | collective-permute-start | bytes 393224 | tf_op jit(solution)/shard_map/ppermute | solution.py:45
  111.2 6.7 %collective-permute-start.17 = (bf16[64,1024]{1,0:T(8,128)(2,1)S(1)}, bf16[64,1024]{1,0:T(8,128)(2,1)S(1)}, u32[]{:S(2)}, u32[]{:S(2)}) collective-permute-start(bf16[64,1024]{1,0:T(8,128)(2,1)S(1)} %get-tuple-element.34), channel_id=1, source_target_pairs={{208,176},{209,177},{210,178},{211,179},{212,180},{213,181},{214,1... | collective-permute-start | bytes 393224 | tf_op jit(solution)/shard_map/ppermute | solution.py:45
  111.9 8.0 %collective-permute-start.22 = (bf16[64,1024]{1,0:T(8,128)(2,1)S(1)}, bf16[64,1024]{1,0:T(8,128)(2,1)S(1)}, u32[]{:S(2)}, u32[]{:S(2)}) collective-permute-start(bf16[64,1024]{1,0:T(8,128)(2,1)S(1)} %get-tuple-element.33), channel_id=1, source_target_pairs={{0,16},{16,0},{32,48},{48,32},{64,80},{80,64},{96,112},{112,96},{1... | collective-permute-start | bytes 393224 | tf_op jit(solution)/shard_map/ppermute | solution.py:203
  118.0 22.5 %collective-permute-start.20 = (bf16[64,1024]{1,0:T(8,128)(2,1)S(1)}, bf16[64,1024]{1,0:T(8,128)(2,1)S(1)}, u32[]{:S(2)}, u32[]{:S(2)}) collective-permute-start(bf16[64,1024]{1,0:T(8,128)(2,1)S(1)} %add.381), channel_id=1, source_target_pairs={{176,112},{80,16},{177,113},{81,17},{178,114},{82,18},{179,115},{8... | collective-permute-start | bytes 393224 | tf_op jit(solution)/shard_map/ppermute | solution.py:45
  119.3 21.2 %collective-permute-start.19 = (bf16[64,1024]{1,0:T(8,128)(2,1)S(1)}, bf16[64,1024]{1,0:T(8,128)(2,1)S(1)}, u32[]{:S(2)}, u32[]{:S(2)}) collective-permute-start(bf16[64,1024]{1,0:T(8,128)(2,1)S(1)} %add.381), channel_id=1, source_target_pairs={{176,144},{80,48},{177,145},{81,49},{178,146},{82,50},{179,147},{8... | collective-permute-start | bytes 393224 | tf_op jit(solution)/shard_map/ppermute | solution.py:45
  140.5 12.8 %copy-start.3 = (bf16[64,1024]{1,0:T(8,128)(2,1)}, bf16[64,1024]{1,0:T(8,128)(2,1)S(1)}, u32[]{:S(2)}) copy-start(bf16[64,1024]{1,0:T(8,128)(2,1)S(1)} %collective-permute-done.19) | copy-start | bytes 393220
  141.2 9.8 %collective-permute-start.25 = (bf16[64,1024]{1,0:T(8,128)(2,1)S(1)}, bf16[64,1024]{1,0:T(8,128)(2,1)S(1)}, u32[]{:S(2)}, u32[]{:S(2)}) collective-permute-start(bf16[64,1024]{1,0:T(8,128)(2,1)S(1)} %get-tuple-element.32), channel_id=1, source_target_pairs={{0,2},{1,3},{2,0},{3,1},{4,6},{5,7},{6,4},{7,5},{8,10},{9,11},{10,... | collective-permute-start | bytes 393224 | tf_op jit(solution)/shard_map/ppermute | solution.py:39
  145.7 7.6 %collective-permute-start.24 = (bf16[64,1024]{1,0:T(8,128)(2,1)S(1)}, bf16[64,1024]{1,0:T(8,128)(2,1)S(1)}, u32[]{:S(2)}, u32[]{:S(2)}) collective-permute-start(bf16[64,1024]{1,0:T(8,128)(2,1)S(1)} %get-tuple-element.32), channel_id=1, source_target_pairs={{0,3},{1,0},{2,1},{3,2},{4,7},{5,4},{6,5},{7,6},{8,11},{9,8},{10,9... | collective-permute-start | bytes 393224 | tf_op jit(solution)/shard_map/ppermute | solution.py:39
  148.4 7.5 %collective-permute-start.23 = (bf16[64,1024]{1,0:T(8,128)(2,1)S(1)}, bf16[64,1024]{1,0:T(8,128)(2,1)S(1)}, u32[]{:S(2)}, u32[]{:S(2)}) collective-permute-start(bf16[64,1024]{1,0:T(8,128)(2,1)S(1)} %get-tuple-element.32), channel_id=1, source_target_pairs={{0,1},{1,2},{2,3},{3,0},{4,5},{5,6},{6,7},{7,4},{8,9},{9,10},{10,1... | collective-permute-start | bytes 393224 | tf_op jit(solution)/shard_map/ppermute | solution.py:39
  156.0 11.5 %collective-permute-start.28 = (bf16[256,1024]{1,0:T(8,128)(2,1)S(1)}, bf16[256,1024]{1,0:T(8,128)(2,1)S(1)}, u32[]{:S(2)}, u32[]{:S(2)}) collective-permute-start(bf16[256,1024]{1,0:T(8,128)(2,1)S(1)} %pad_maximum_fusion.a), channel_id=1, source_target_pairs={{0,8},{1,9},{2,10},{3,11},{4,12},{5,13},{6,14},{7,15},{8,0},{9,1},... | collective-permute-start | bytes 1572872 | tf_op jit(solution)/shard_map/ppermute | solution.py:39
  158.0 12.8 %collective-permute-start.27 = (bf16[256,1024]{1,0:T(8,128)(2,1)S(1)}, bf16[256,1024]{1,0:T(8,128)(2,1)}, u32[]{:S(2)}, u32[]{:S(2)}) collective-permute-start(bf16[256,1024]{1,0:T(8,128)(2,1)S(1)} %pad_maximum_fusion.a), channel_id=1, source_target_pairs={{0,12},{1,13},{2,14},{3,15},{4,0},{5,1},{6,2},{7,3},{8,4},{9,5},{1... | collective-permute-start | bytes 1572872 | tf_op jit(solution)/shard_map/ppermute | solution.py:39
  161.3 11.8 %collective-permute-start.26 = (bf16[256,1024]{1,0:T(8,128)(2,1)S(1)}, bf16[256,1024]{1,0:T(8,128)(2,1)}, u32[]{:S(2)}, u32[]{:S(2)}) collective-permute-start(bf16[256,1024]{1,0:T(8,128)(2,1)S(1)} %pad_maximum_fusion.a), channel_id=1, source_target_pairs={{0,4},{1,5},{2,6},{3,7},{4,8},{5,9},{6,10},{7,11},{8,12},{9,13},{1... | collective-permute-start | bytes 1572872 | tf_op jit(solution)/shard_map/ppermute | solution.py:39
  163.3 11.2 %collective-permute-start.21 = (bf16[64,1024]{1,0:T(8,128)(2,1)}, bf16[64,1024]{1,0:T(8,128)(2,1)}, u32[]{:S(2)}, u32[]{:S(2)}) collective-permute-start(bf16[64,1024]{1,0:T(8,128)(2,1)} %get-tuple-element.31), channel_id=1, source_target_pairs={{16,0},{48,32},{80,64},{112,96},{144,128},{176,160},{208,192},{240... | collective-permute-start | bytes 393224 | tf_op jit(solution)/shard_map/ppermute | solution.py:216
  165.3 9.2 %copy-start.2 = (f32[64,1024]{1,0:T(8,128)S(1)}, f32[64,1024]{1,0:T(8,128)}, u32[]{:S(2)}) copy-start(f32[64,1024]{1,0:T(8,128)} %copy-done.1) | copy-start | bytes 786436
  165.3 9.2 %copy-start.4 = (bf16[64,1024]{1,0:T(8,128)(2,1)S(1)}, bf16[64,1024]{1,0:T(8,128)(2,1)}, u32[]{:S(2)}) copy-start(bf16[64,1024]{1,0:T(8,128)(2,1)} %copy-done.3) | copy-start | bytes 393220

commit v5 on v4

--- a/solution.py
+++ b/solution.py
@@ -146,6 +146,19 @@
         compiler_params=PARAMS,
         cost_estimate=pl.CostEstimate(flops=2 * width**3, bytes_accessed=6 * width**2, transcendentals=0),
     )(core.reshape(1), own, got, bias, bias_got)
+
+
+def join_kernel(a, b, ready, out):
+    out[...] = a[...] + b[...]
+
+
+def joined(a, b, ready):
+    return pl.pallas_call(
+        join_kernel,
+        out_shape=jax.ShapeDtypeStruct(a.shape, a.dtype),
+        in_specs=[VMEM, VMEM, pl.BlockSpec(memory_space=pl.ANY)],
+        out_specs=VMEM,
+    )(a, b, ready)
 
 
 def body(inv_diag, couple, arrow, corner, band_offset):
@@ -207,7 +220,7 @@
     depths = range(2 * lower)
     ring = jnp.concatenate(ring_gather(map_rows, depths, False))
     near, far = lower - 1, lower // 2 - 1
-    entry = sent_down(edge, [(lower, near)]) + sent_down(edge, [(lower, far)])
+    entry = joined(sent_down(edge, [(lower, near)]), sent_down(edge, [(lower, far)]), ring)
     relayed = sent_down(entry, [(near, near - 1), (far, far - 1)])
     last = [(source, source - 2) for source, low_end in ((near, far), (far, -1)) if source - 2 > low_end]
     entry = entry + relayed + sent_down(entry, last)

time: 178 us -> 158 us (0.89)
  waiting for transfers between devices: 80.3 us -> 54.9 us
    ppermute x4, waiting for transfers between devices: 20.6 us -> 4.61 us  [sent_down(): lax.ppermute(value, 'depth', [(2 * a + 1, 2 * b + 1) for a, b in chip_pai...]
    ppermute x12, waiting for transfers between devices: 18.5 us -> 8.15 us  [ring_gather(): lax.ppermute(value, BOTH, ring_moves(depths, flipped, shift))]
  transfers between devices with their start and end apart: 30 -> 30, of which waited for: 12 -> 9; matrix products, arithmetic and copies ran while one was open for 2% -> 4% of each run, Pallas kernels for 1% -> 2%
where the time goes in v5:
time: 158 us; the launch traced here: 157 us
  starting transfers between devices  69.4 us (44%)
  waiting for transfers between devices  54.9 us (35%)
  Pallas kernels  13.7 us (9%)
  matrix products  8.37 us (5%)
  local copies, waits for them, and re-layouts  4.83 us (3%)
  other arithmetic  4.06 us (3%)
  between operations  1.8 us (1%)
    ppermute x12, starting transfers between devices, ring_gather(): lax.ppermute(value, BOTH, ring_moves(depths, flipped, shift))  38.1 us
    ppermute x9, waiting for transfers between devices, body(): v_in = v_in + lax.ppermute(v_even.astype(BF16), 'depth', pairs)  24.1 us
    all_to_all x1, waiting for transfers between devices, body(): lax.all_to_all(panel.reshape(lat_count, share, share), 'lat', 0, 0)  14.3 us
    dot_general x13, matrix products, mm(): return jnp.dot(a, b, preferred_element_type=F32)  8.37 us
    ppermute x12, waiting for transfers between devices, ring_gather(): lax.ppermute(value, BOTH, ring_moves(depths, flipped, shift))  8.15 us
    ppermute x1, starting transfers between devices, body(): got = lax.ppermute(step, 'depth', swap)  7.03 us
    ppermute x9, starting transfers between devices, body(): v_in = v_in + lax.ppermute(v_even.astype(BF16), 'depth', pairs)  6.82 us
    ppermute x1, starting transfers between devices, body(): lax.ppermute(jnp.where(low, v_odd.astype(BF16), edge), 'depth', swap[:2 *...  5.98 us
  transfers between devices with their start and end apart: 30, of which 9 were waited for; matrix products, arithmetic and copies ran while one was open for 4% of the time, Pallas kernels for 2%

profile of v5, /device:TPU:1, one launch (start us, length us, event | category | flops | bytes accessed | tf_op | source)
XLA Modules:
  0.0 157.1 jit_solution(3805267339682545342)
XLA Ops:
  0.8 1.0 fusion.15
  1.9 0.9 pad_maximum_fusion.1.a
  2.8 5.7 %collective-permute-start.2 = (bf16[2,64,1024]{2,1,0:T(8,128)(2,1)S(1)}, bf16[2,64,1024]{2,1,0:T(8,128)(2,1)S(1)}, u32[]{:S(2)}, u32[]{:S(2)}) collective-permute-start(bf16[2,64,1024]{2,1,0:T(8,128)(2,1)S(1)} %pad_maximum_fusion.1.a), channel_id=1, source_target_pairs={{0,2},{1,3},{2,0},{3,1},{4,6},{5,7},{6,4},{7,5},{8,10},{9,11},{10,... | collective-permute-start | bytes 786440 | tf_op jit(solution)/shard_map/ppermute | solution.py:39
  8.5 2.7 %collective-permute-start.1 = (bf16[2,64,1024]{2,1,0:T(8,128)(2,1)S(1)}, bf16[2,64,1024]{2,1,0:T(8,128)(2,1)S(1)}, u32[]{:S(2)}, u32[]{:S(2)}) collective-permute-start(bf16[2,64,1024]{2,1,0:T(8,128)(2,1)S(1)} %pad_maximum_fusion.1.a), channel_id=1, source_target_pairs={{0,3},{1,0},{2,1},{3,2},{4,7},{5,4},{6,5},{7,6},{8,11},{9,8},{10,9... | collective-permute-start | bytes 786440 | tf_op jit(solution)/shard_map/ppermute | solution.py:39
  11.2 2.6 %collective-permute-start = (bf16[2,64,1024]{2,1,0:T(8,128)(2,1)S(1)}, bf16[2,64,1024]{2,1,0:T(8,128)(2,1)S(1)}, u32[]{:S(2)}, u32[]{:S(2)}) collective-permute-start(bf16[2,64,1024]{2,1,0:T(8,128)(2,1)S(1)} %pad_maximum_fusion.1.a), channel_id=1, source_target_pairs={{0,1},{1,2},{2,3},{3,0},{4,5},{5,6},{6,7},{7,4},{8,9},{9,10},{10,1... | collective-permute-start | bytes 786440 | tf_op jit(solution)/shard_map/ppermute | solution.py:39
  13.8 1.8 %collective-permute-done.1.c = bf16[2,64,1024]{2,1,0:T(8,128)(2,1)S(1)} collective-permute-done((bf16[2,64,1024]{2,1,0:T(8,128)(2,1)S(1)}, bf16[2,64,1024]{2,1,0:T(8,128)(2,1)S(1)}, u32[]{:S(2)}, u32[]{:S(2)}) %collective-permute-start.1) | collective-permute-done | bytes 262176 | tf_op jit(solution)/shard_map/ppermute | solution.py:39
  15.6 3.9 %collective-permute-done.b = bf16[2,64,1024]{2,1,0:T(8,128)(2,1)S(1)} collective-permute-done((bf16[2,64,1024]{2,1,0:T(8,128)(2,1)S(1)}, bf16[2,64,1024]{2,1,0:T(8,128)(2,1)S(1)}, u32[]{:S(2)}, u32[]{:S(2)}) %collective-permute-start) | collective-permute-done | bytes 262176 | tf_op jit(solution)/shard_map/ppermute | solution.py:39
  19.7 4.7 %collective-permute-start.5 = (bf16[2,256,1024]{2,1,0:T(8,128)(2,1)S(1)}, bf16[2,256,1024]{2,1,0:T(8,128)(2,1)}, u32[]{:S(2)}, u32[]{:S(2)}) collective-permute-start(bf16[2,256,1024]{2,1,0:T(8,128)(2,1)S(1)} %shard_map.55.a), channel_id=1, source_target_pairs={{0,8},{1,9},{2,10},{3,11},{4,12},{5,13},{6,14},{7,15},{8,0},{9,1},... | collective-permute-start | bytes 3145736 | tf_op jit(solution)/shard_map/ppermute | solution.py:39
  24.4 2.8 %collective-permute-start.4 = (bf16[2,256,1024]{2,1,0:T(8,128)(2,1)S(1)}, bf16[2,256,1024]{2,1,0:T(8,128)(2,1)}, u32[]{:S(2)}, u32[]{:S(2)}) collective-permute-start(bf16[2,256,1024]{2,1,0:T(8,128)(2,1)S(1)} %shard_map.55.a), channel_id=1, source_target_pairs={{0,12},{1,13},{2,14},{3,15},{4,0},{5,1},{6,2},{7,3},{8,4},{9,5},{1... | collective-permute-start | bytes 3145736 | tf_op jit(solution)/shard_map/ppermute | solution.py:39
  27.1 2.5 %collective-permute-start.3 = (bf16[2,256,1024]{2,1,0:T(8,128)(2,1)S(1)}, bf16[2,256,1024]{2,1,0:T(8,128)(2,1)}, u32[]{:S(2)}, u32[]{:S(2)}) collective-permute-start(bf16[2,256,1024]{2,1,0:T(8,128)(2,1)S(1)} %shard_map.55.a), channel_id=1, source_target_pairs={{0,4},{1,5},{2,6},{3,7},{4,8},{5,9},{6,10},{7,11},{8,12},{9,13},{1... | collective-permute-start | bytes 3145736 | tf_op jit(solution)/shard_map/ppermute | solution.py:39
  29.7 0.8 convolution_convert_fusion
  30.6 0.9 reshape.8
  31.5 3.7 %all-to-all-start = ((bf16[16,2,2048]{2,1,0:T(2,128)(2,1)}), bf16[16,2,2048]{2,1,0:T(2,128)(2,1)S(1)}, u32[]{:S(2)}, u32[]{:S(2)}) async-start(bf16[16,2,2048]{2,1,0:T(2,128)(2,1)} %reshape.8), calls=%async_computation | async-start | bytes 262144 | tf_op jit(solution)/shard_map/all_to_all | solution.py:187
  35.5 14.3 %all-to-all-done = bf16[16,2,2048]{2,1,0:T(2,128)(2,1)S(1)} async-done(((bf16[16,2,2048]{2,1,0:T(2,128)(2,1)}), bf16[16,2,2048]{2,1,0:T(2,128)(2,1)S(1)}, u32[]{:S(2)}, u32[]{:S(2)}) %all-to-all-start) | async-done | bytes 131104 | tf_op jit(solution)/shard_map/all_to_all | solution.py:187
  49.8 0.2 reshape.9
  50.0 0.7 dynamic-slice_bitcast_fusion
  50.8 1.0 concatenate.6.panel
  51.9 5.6 %shard_map.56 = (bf16[1024,1024]{1,0:T(8,128)(2,1)}, f32[64,1024]{1,0:T(8,128)S(1)}) custom-call(bf16[64,1024]{1,0:T(8,128)(2,1)S(1)} %concatenate.6.panel, bf16[2,256,1024]{2,1,0:T(8,128)(2,1)S(1)} %shard_map.55.a, bf16[2,256,1024]{2,1,0:T(8,128)(2,1)} %collective-permute-done.3.b, bf16[2,256,1024]{2,1,0:T(8,128)(2,1)} %collective-permute-done.4.c, ...), custom_call_target="tpu_custom_call" | custom-call | flops 2147483648 | bytes 6291456 | tf_op jit(solution)/shard_map/pallas_call | solution.py:101
  57.4 7.0 %collective-permute-start.6 = (bf16[1024,1024]{1,0:T(8,128)(2,1)}, bf16[1024,1024]{1,0:T(8,128)(2,1)}, u32[]{:S(2)}, u32[]{:S(2)}) collective-permute-start(bf16[1024,1024]{1,0:T(8,128)(2,1)} %get-tuple-element.10.own), channel_id=1, source_target_pairs={{0,16},{16,0},{32,48},{48,32},{64,80},{80,64},{96,112},{112,96},{1... | collective-permute-start | bytes 6291464 | tf_op jit(solution)/shard_map/ppermute | solution.py:196
  64.5 1.3 collective-permute-start.7
  65.8 2.7 %collective-permute-done.7.bias_got = f32[64,1024]{1,0:T(8,128)S(1)} collective-permute-done((f32[64,1024]{1,0:T(8,128)S(1)}, f32[64,1024]{1,0:T(8,128)S(1)}, u32[]{:S(2)}, u32[]{:S(2)}) %collective-permute-start.7) | collective-permute-done | bytes 262176 | tf_op jit(solution)/shard_map/ppermute | solution.py:197
  68.6 4.9 %shard_map.57 = (bf16[1024,1024]{1,0:T(8,128)(2,1)S(1)}, bf16[1024,1024]{1,0:T(8,128)(2,1)S(1)}, f32[64,1024]{1,0:T(8,128)S(1)}) custom-call(s32[1]{0:T(128)} %bitcast.core, bf16[1024,1024]{1,0:T(8,128)(2,1)} %get-tuple-element.10.own, bf16[1024,1024]{1,0:T(8,128)(2,1)} %collective-permute-done.6.got, f32[64,1024]{1,0:T(8,128)S(1)} %get-tuple-element.11.bias, ...), custom_call_target="tpu_custom_call" | custom-call | flops 2147483648 | bytes 6291456 | tf_op jit(solution)/shard_map/pallas_call | solution.py:137
  73.5 0.5 fusion.1
  74.0 0.7 collective-permute-start.8
  74.7 0.5 fusion.2
  75.3 0.7 collective-permute-start.9
  76.0 0.5 fusion.3
  76.5 0.7 collective-permute-start.10
  77.4 0.5 fusion.4
  77.9 0.7 collective-permute-start.11
  78.6 0.5 fusion.5
  79.1 1.3 collective-permute-start.12
  80.4 24.1 %collective-permute-done.12 = bf16[64,1024]{1,0:T(8,128)(2,1)S(1)} collective-permute-done((bf16[64,1024]{1,0:T(8,128)(2,1)S(1)}, bf16[64,1024]{1,0:T(8,128)(2,1)S(1)}, u32[]{:S(2)}, u32[]{:S(2)}) %collective-permute-start.12) | collective-permute-done | bytes 131104 | tf_op jit(solution)/shard_map/ppermute | solution.py:212
  104.5 0.5 fusion.6
  105.0 0.7 collective-permute-start.13
  105.7 0.5 fusion.7
  106.2 0.7 collective-permute-start.14
  107.0 0.5 fusion.8
  107.4 0.8 collective-permute-start.15
  108.4 0.5 fusion.9
  108.8 0.7 collective-permute-start.16
  109.5 0.5 convolution_add_fusion.1
  110.0 0.5 convert_select_fusion
  110.5 6.0 %collective-permute-start.19 = (bf16[64,1024]{1,0:T(8,128)(2,1)S(1)}, bf16[64,1024]{1,0:T(8,128)(2,1)S(1)}, u32[]{:S(2)}, u32[]{:S(2)}) collective-permute-start(bf16[64,1024]{1,0:T(8,128)(2,1)S(1)} %get-tuple-element.31), channel_id=1, source_target_pairs={{0,16},{16,0},{32,48},{48,32},{64,80},{80,64},{96,112},{112,96},{1... | collective-permute-start | bytes 393224 | tf_op jit(solution)/shard_map/ppermute | solution.py:216
  116.5 1.0 collective-permute-done.19
  117.5 4.5 %collective-permute-start.22 = (bf16[64,1024]{1,0:T(8,128)(2,1)S(1)}, bf16[64,1024]{1,0:T(8,128)(2,1)S(1)}, u32[]{:S(2)}, u32[]{:S(2)}) collective-permute-start(bf16[64,1024]{1,0:T(8,128)(2,1)S(1)} %broadcast_select_fusion), channel_id=1, source_target_pairs={{0,2},{1,3},{2,0},{3,1},{4,6},{5,7},{6,4},{7,5},{8,10},{9,11},{10,... | collective-permute-start | bytes 393224 | tf_op jit(solution)/shard_map/ppermute | solution.py:39
  122.0 2.7 %collective-permute-start.21 = (bf16[64,1024]{1,0:T(8,128)(2,1)S(1)}, bf16[64,1024]{1,0:T(8,128)(2,1)S(1)}, u32[]{:S(2)}, u32[]{:S(2)}) collective-permute-start(bf16[64,1024]{1,0:T(8,128)(2,1)S(1)} %broadcast_select_fusion), channel_id=1, source_target_pairs={{0,3},{1,0},{2,1},{3,2},{4,7},{5,4},{6,5},{7,6},{8,11},{9,8},{10,9... | collective-permute-start | bytes 393224 | tf_op jit(solution)/shard_map/ppermute | solution.py:39
  124.7 2.6 %collective-permute-start.20 = (bf16[64,1024]{1,0:T(8,128)(2,1)S(1)}, bf16[64,1024]{1,0:T(8,128)(2,1)S(1)}, u32[]{:S(2)}, u32[]{:S(2)}) collective-permute-start(bf16[64,1024]{1,0:T(8,128)(2,1)S(1)} %broadcast_select_fusion), channel_id=1, source_target_pairs={{0,1},{1,2},{2,3},{3,0},{4,5},{5,6},{6,7},{7,4},{8,9},{9,10},{10,1... | collective-permute-start | bytes 393224 | tf_op jit(solution)/shard_map/ppermute | solution.py:39
  127.3 0.7 collective-permute-start.18
  128.0 1.3 collective-permute-start.17
  129.3 2.4 %collective-permute-done.20 = bf16[64,1024]{1,0:T(8,128)(2,1)S(1)} collective-permute-done((bf16[64,1024]{1,0:T(8,128)(2,1)S(1)}, bf16[64,1024]{1,0:T(8,128)(2,1)S(1)}, u32[]{:S(2)}, u32[]{:S(2)}) %collective-permute-start.20) | collective-permute-done | bytes 131104 | tf_op jit(solution)/shard_map/ppermute | solution.py:39
  131.8 1.9 %collective-permute-start.28 = (bf16[256,1024]{1,0:T(8,128)(2,1)S(1)}, bf16[256,1024]{1,0:T(8,128)(2,1)S(1)}, u32[]{:S(2)}, u32[]{:S(2)}) collective-permute-start(bf16[256,1024]{1,0:T(8,128)(2,1)S(1)} %pad_maximum_fusion.ready.a), channel_id=1, source_target_pairs={{0,8},{1,9},{2,10},{3,11},{4,12},{5,13},{6,14},{7,15},{8,0},{9,1},... | collective-permute-start | bytes 1572872 | tf_op jit(solution)/shard_map/ppermute | solution.py:39
  133.7 3.6 %collective-permute-start.27 = (bf16[256,1024]{1,0:T(8,128)(2,1)S(1)}, bf16[256,1024]{1,0:T(8,128)(2,1)}, u32[]{:S(2)}, u32[]{:S(2)}) collective-permute-start(bf16[256,1024]{1,0:T(8,128)(2,1)S(1)} %pad_maximum_fusion.ready.a), channel_id=1, source_target_pairs={{0,12},{1,13},{2,14},{3,15},{4,0},{5,1},{6,2},{7,3},{8,4},{9,5},{1... | collective-permute-start | bytes 1572872 | tf_op jit(solution)/shard_map/ppermute | solution.py:39
  137.3 1.9 %collective-permute-start.26 = (bf16[256,1024]{1,0:T(8,128)(2,1)S(1)}, bf16[256,1024]{1,0:T(8,128)(2,1)}, u32[]{:S(2)}, u32[]{:S(2)}) collective-permute-start(bf16[256,1024]{1,0:T(8,128)(2,1)S(1)} %pad_maximum_fusion.ready.a), channel_id=1, source_target_pairs={{0,4},{1,5},{2,6},{3,7},{4,8},{5,9},{6,10},{7,11},{8,12},{9,13},{1... | collective-permute-start | bytes 1572872 | tf_op jit(solution)/shard_map/ppermute | solution.py:39
  139.3 0.6 copy-done.7
  139.9 1.6 %shard_map.58 = bf16[64,1024]{1,0:T(8,128)(2,1)} custom-call(bf16[64,1024]{1,0:T(8,128)(2,1)} %collective-permute-done.17.a, bf16[64,1024]{1,0:T(8,128)(2,1)} %copy-done.7, bf16[256,1024]{1,0:T(8,128)(2,1)} %copy-done.1), custom_call_target="tpu_custom_call" | custom-call | tf_op jit(solution)/shard_map/pallas_call | solution.py:156
  141.5 1.3 collective-permute-start.24
  142.8 1.3 collective-permute-start.23
  144.1 4.6 %collective-permute-done.24 = bf16[64,1024]{1,0:T(8,128)(2,1)S(1)} collective-permute-done((bf16[64,1024]{1,0:T(8,128)(2,1)}, bf16[64,1024]{1,0:T(8,128)(2,1)S(1)}, u32[]{:S(2)}, u32[]{:S(2)}) %collective-permute-start.24) | collective-permute-done | bytes 131104 | tf_op jit(solution)/shard_map/ppermute | solution.py:45
  148.7 1.7 %broadcast_select_fusion.1 = bf16[64,1024]{1,0:T(8,128)(2,1)} fusion(bf16[64,1024]{1,0:T(8,128)(2,1)S(1)} %get-tuple-element.32, pred[]{:T(512)S(6)} %lt.118, bf16[64,1024]{1,0:T(8,128)(2,1)S(1)} %collective-permute-done.24, bf16[64,1024]{1,0:T(8,128)(2,1)} %shard_map.58, bf16[64,1024]{1,0:T(8,128)(2,1)} %collective-permute-done.23), kind=kLoop, calls=%fused_computation.47 | loop fusion | flops 196608 | bytes 655361 | tf_op jit(solution)/shard_map/jit(_where)/select_n | solution.py:230
  150.4 1.9 %collective-permute-start.25 = (bf16[64,1024]{1,0:T(8,128)(2,1)}, bf16[64,1024]{1,0:T(8,128)(2,1)}, u32[]{:S(2)}, u32[]{:S(2)}) collective-permute-start(bf16[64,1024]{1,0:T(8,128)(2,1)} %broadcast_select_fusion.1), channel_id=1, source_target_pairs={{16,0},{48,32},{80,64},{112,96},{144,128},{176,160},{208,192},{240... | collective-permute-start | bytes 393224 | tf_op jit(solution)/shard_map/ppermute | solution.py:229
  152.5 1.0 copy-done.2
  153.5 1.4 shard_map.59
  154.9 2.1 %fusion = f32[1,64,1024]{2,1,0:T(8,128)} fusion(bf16[1024,1024]{1,0:T(8,128)(2,1)S(1)} %shard_map.59, f32[64,1024]{1,0:T(8,128)S(1)} %copy-done.4, bf16[64,1024]{1,0:T(8,128)(2,1)S(1)} %collective-permute-done.19, bf16[64,1024]{1,0:T(8,128)(2,1)} %collective-permute-done.25, pred[]{:T(512)S(6)} %eq.35, pred[]{:T(512)S(6)} %lt.118, ...), kind=kOutput, calls=%fused_computation.1 | convolution fusion | flops 134742016 | bytes 3276802 | tf_op jit(solution)/shard_map/dot_general | solution.py:19
  (52 shorter events, 1.1 us)
Async XLA Ops:
  0.0 29.7 %copy-start = (bf16[1024,1024]{1,0:T(8,128)(2,1)S(1)}, bf16[1024,1024]{1,0:T(8,128)(2,1)}, u32[]{:S(2)}) copy-start(bf16[1024,1024]{1,0:T(8,128)(2,1)} %param.8) | copy-start | bytes 6291460
  0.0 29.7 %copy-start.6 = (bf16[1,1024,64]{1,2,0:T(8,128)(2,1)S(1)}, bf16[1,1024,64]{1,2,0:T(8,128)(2,1)}, u32[]{:S(2)}) copy-start(bf16[1,1024,64]{1,2,0:T(8,128)(2,1)} %param.7) | copy-start | bytes 393220
  0.8 14.8 %copy-start.8 = (s32[64]{0:T(128)}, s32[64]{0:T(128)S(1)}, u32[]{:S(2)}) copy-start(s32[64]{0:T(128)S(1)} %iota_add_fusion) | copy-start | bytes 772
  2.8 11.0 %collective-permute-start.2 = (bf16[2,64,1024]{2,1,0:T(8,128)(2,1)S(1)}, bf16[2,64,1024]{2,1,0:T(8,128)(2,1)S(1)}, u32[]{:S(2)}, u32[]{:S(2)}) collective-permute-start(bf16[2,64,1024]{2,1,0:T(8,128)(2,1)S(1)} %pad_maximum_fusion.1.a), channel_id=1, source_target_pairs={{0,2},{1,3},{2,0},{3,1},{4,6},{5,7},{6,4},{7,5},{8,10},{9,11},{10,... | collective-permute-start | bytes 786440 | tf_op jit(solution)/shard_map/ppermute | solution.py:39
  8.5 7.1 %collective-permute-start.1 = (bf16[2,64,1024]{2,1,0:T(8,128)(2,1)S(1)}, bf16[2,64,1024]{2,1,0:T(8,128)(2,1)S(1)}, u32[]{:S(2)}, u32[]{:S(2)}) collective-permute-start(bf16[2,64,1024]{2,1,0:T(8,128)(2,1)S(1)} %pad_maximum_fusion.1.a), channel_id=1, source_target_pairs={{0,3},{1,0},{2,1},{3,2},{4,7},{5,4},{6,5},{7,6},{8,11},{9,8},{10,9... | collective-permute-start | bytes 786440 | tf_op jit(solution)/shard_map/ppermute | solution.py:39
  11.2 8.3 %collective-permute-start = (bf16[2,64,1024]{2,1,0:T(8,128)(2,1)S(1)}, bf16[2,64,1024]{2,1,0:T(8,128)(2,1)S(1)}, u32[]{:S(2)}, u32[]{:S(2)}) collective-permute-start(bf16[2,64,1024]{2,1,0:T(8,128)(2,1)S(1)} %pad_maximum_fusion.1.a), channel_id=1, source_target_pairs={{0,1},{1,2},{2,3},{3,0},{4,5},{5,6},{6,7},{7,4},{8,9},{9,10},{10,1... | collective-permute-start | bytes 786440 | tf_op jit(solution)/shard_map/ppermute | solution.py:39
  19.7 32.1 %collective-permute-start.5 = (bf16[2,256,1024]{2,1,0:T(8,128)(2,1)S(1)}, bf16[2,256,1024]{2,1,0:T(8,128)(2,1)}, u32[]{:S(2)}, u32[]{:S(2)}) collective-permute-start(bf16[2,256,1024]{2,1,0:T(8,128)(2,1)S(1)} %shard_map.55.a), channel_id=1, source_target_pairs={{0,8},{1,9},{2,10},{3,11},{4,12},{5,13},{6,14},{7,15},{8,0},{9,1},... | collective-permute-start | bytes 3145736 | tf_op jit(solution)/shard_map/ppermute | solution.py:39
  24.4 27.5 %collective-permute-start.4 = (bf16[2,256,1024]{2,1,0:T(8,128)(2,1)S(1)}, bf16[2,256,1024]{2,1,0:T(8,128)(2,1)}, u32[]{:S(2)}, u32[]{:S(2)}) collective-permute-start(bf16[2,256,1024]{2,1,0:T(8,128)(2,1)S(1)} %shard_map.55.a), channel_id=1, source_target_pairs={{0,12},{1,13},{2,14},{3,15},{4,0},{5,1},{6,2},{7,3},{8,4},{9,5},{1... | collective-permute-start | bytes 3145736 | tf_op jit(solution)/shard_map/ppermute | solution.py:39
  27.1 24.7 %collective-permute-start.3 = (bf16[2,256,1024]{2,1,0:T(8,128)(2,1)S(1)}, bf16[2,256,1024]{2,1,0:T(8,128)(2,1)}, u32[]{:S(2)}, u32[]{:S(2)}) collective-permute-start(bf16[2,256,1024]{2,1,0:T(8,128)(2,1)S(1)} %shard_map.55.a), channel_id=1, source_target_pairs={{0,4},{1,5},{2,6},{3,7},{4,8},{5,9},{6,10},{7,11},{8,12},{9,13},{1... | collective-permute-start | bytes 3145736 | tf_op jit(solution)/shard_map/ppermute | solution.py:39
  31.5 18.3 %all-to-all-start = ((bf16[16,2,2048]{2,1,0:T(2,128)(2,1)}), bf16[16,2,2048]{2,1,0:T(2,128)(2,1)S(1)}, u32[]{:S(2)}, u32[]{:S(2)}) async-start(bf16[16,2,2048]{2,1,0:T(2,128)(2,1)} %reshape.8), calls=%async_computation | async-start | bytes 262144 | tf_op jit(solution)/shard_map/all_to_all | solution.py:187
  57.4 11.1 %collective-permute-start.6 = (bf16[1024,1024]{1,0:T(8,128)(2,1)}, bf16[1024,1024]{1,0:T(8,128)(2,1)}, u32[]{:S(2)}, u32[]{:S(2)}) collective-permute-start(bf16[1024,1024]{1,0:T(8,128)(2,1)} %get-tuple-element.10.own), channel_id=1, source_target_pairs={{0,16},{16,0},{32,48},{48,32},{64,80},{80,64},{96,112},{112,96},{1... | collective-permute-start | bytes 6291464 | tf_op jit(solution)/shard_map/ppermute | solution.py:196
  64.5 4.0 %collective-permute-start.7 = (f32[64,1024]{1,0:T(8,128)S(1)}, f32[64,1024]{1,0:T(8,128)S(1)}, u32[]{:S(2)}, u32[]{:S(2)}) collective-permute-start(f32[64,1024]{1,0:T(8,128)S(1)} %get-tuple-element.11.bias), channel_id=1, source_target_pairs={{0,16},{32,48},{64,80},{96,112},{128,144},{160,176},{192,208},{224... | collective-permute-start | bytes 786440 | tf_op jit(solution)/shard_map/ppermute | solution.py:197
  68.6 4.9 %copy-start.9 = (s32[64]{0:T(128)S(1)}, s32[64]{0:T(128)}, u32[]{:S(2)}) copy-start(s32[64]{0:T(128)} %copy-done.8) | copy-start | bytes 772
  74.0 0.7 collective-permute-start.8
  75.3 0.7 collective-permute-start.9
  76.5 0.7 collective-permute-start.10
  77.9 0.7 collective-permute-start.11
  79.1 25.4 %collective-permute-start.12 = (bf16[64,1024]{1,0:T(8,128)(2,1)S(1)}, bf16[64,1024]{1,0:T(8,128)(2,1)S(1)}, u32[]{:S(2)}, u32[]{:S(2)}) collective-permute-start(bf16[64,1024]{1,0:T(8,128)(2,1)S(1)} %fusion.5), channel_id=1, source_target_pairs={{352,320},{368,336},{32,0},{48,16},{353,321},{369,337},{33,1},{49,... | collective-permute-start | bytes 393224 | tf_op jit(solution)/shard_map/ppermute | solution.py:212
  105.0 0.7 collective-permute-start.13
  106.2 0.7 collective-permute-start.14
  107.4 0.9 collective-permute-start.15
  108.8 0.7 collective-permute-start.16
  110.0 19.3 %copy-start.3 = (f32[64,1024]{1,0:T(8,128)}, f32[64,1024]{1,0:T(8,128)S(1)}, u32[]{:S(2)}) copy-start(f32[64,1024]{1,0:T(8,128)S(1)} %convolution_add_fusion.1) | copy-start | bytes 786436
  110.5 6.9 %collective-permute-start.19 = (bf16[64,1024]{1,0:T(8,128)(2,1)S(1)}, bf16[64,1024]{1,0:T(8,128)(2,1)S(1)}, u32[]{:S(2)}, u32[]{:S(2)}) collective-permute-start(bf16[64,1024]{1,0:T(8,128)(2,1)S(1)} %get-tuple-element.31), channel_id=1, source_target_pairs={{0,16},{16,0},{32,48},{48,32},{64,80},{80,64},{96,112},{112,96},{1... | collective-permute-start | bytes 393224 | tf_op jit(solution)/shard_map/ppermute | solution.py:216
  117.5 11.8 %collective-permute-start.22 = (bf16[64,1024]{1,0:T(8,128)(2,1)S(1)}, bf16[64,1024]{1,0:T(8,128)(2,1)S(1)}, u32[]{:S(2)}, u32[]{:S(2)}) collective-permute-start(bf16[64,1024]{1,0:T(8,128)(2,1)S(1)} %broadcast_select_fusion), channel_id=1, source_target_pairs={{0,2},{1,3},{2,0},{3,1},{4,6},{5,7},{6,4},{7,5},{8,10},{9,11},{10,... | collective-permute-start | bytes 393224 | tf_op jit(solution)/shard_map/ppermute | solution.py:39
  122.0 7.3 %collective-permute-start.21 = (bf16[64,1024]{1,0:T(8,128)(2,1)S(1)}, bf16[64,1024]{1,0:T(8,128)(2,1)S(1)}, u32[]{:S(2)}, u32[]{:S(2)}) collective-permute-start(bf16[64,1024]{1,0:T(8,128)(2,1)S(1)} %broadcast_select_fusion), channel_id=1, source_target_pairs={{0,3},{1,0},{2,1},{3,2},{4,7},{5,4},{6,5},{7,6},{8,11},{9,8},{10,9... | collective-permute-start | bytes 393224 | tf_op jit(solution)/shard_map/ppermute | solution.py:39
  124.7 7.0 %collective-permute-start.20 = (bf16[64,1024]{1,0:T(8,128)(2,1)S(1)}, bf16[64,1024]{1,0:T(8,128)(2,1)S(1)}, u32[]{:S(2)}, u32[]{:S(2)}) collective-permute-start(bf16[64,1024]{1,0:T(8,128)(2,1)S(1)} %broadcast_select_fusion), channel_id=1, source_target_pairs={{0,1},{1,2},{2,3},{3,0},{4,5},{5,6},{6,7},{7,4},{8,9},{9,10},{10,1... | collective-permute-start | bytes 393224 | tf_op jit(solution)/shard_map/ppermute | solution.py:39
  127.3 12.0 %collective-permute-start.18 = (bf16[64,1024]{1,0:T(8,128)(2,1)S(1)}, bf16[64,1024]{1,0:T(8,128)(2,1)S(1)}, u32[]{:S(2)}, u32[]{:S(2)}) collective-permute-start(bf16[64,1024]{1,0:T(8,128)(2,1)S(1)} %get-tuple-element.32), channel_id=1, source_target_pairs={{208,80},{209,81},{210,82},{211,83},{212,84},{213,85},{214,86},{21... | collective-permute-start | bytes 393224 | tf_op jit(solution)/shard_map/ppermute | solution.py:45
  128.0 11.3 %collective-permute-start.17 = (bf16[64,1024]{1,0:T(8,128)(2,1)S(1)}, bf16[64,1024]{1,0:T(8,128)(2,1)}, u32[]{:S(2)}, u32[]{:S(2)}) collective-permute-start(bf16[64,1024]{1,0:T(8,128)(2,1)S(1)} %get-tuple-element.32), channel_id=1, source_target_pairs={{208,176},{209,177},{210,178},{211,179},{212,180},{213,181},{214,1... | collective-permute-start | bytes 393224 | tf_op jit(solution)/shard_map/ppermute | solution.py:45
  131.8 7.5 %copy-start.1 = (bf16[256,1024]{1,0:T(8,128)(2,1)}, bf16[256,1024]{1,0:T(8,128)(2,1)S(1)}, u32[]{:S(2)}) copy-start(bf16[256,1024]{1,0:T(8,128)(2,1)S(1)} %pad_maximum_fusion.ready.a) | copy-start | bytes 1572868
  131.8 20.7 %collective-permute-start.28 = (bf16[256,1024]{1,0:T(8,128)(2,1)S(1)}, bf16[256,1024]{1,0:T(8,128)(2,1)S(1)}, u32[]{:S(2)}, u32[]{:S(2)}) collective-permute-start(bf16[256,1024]{1,0:T(8,128)(2,1)S(1)} %pad_maximum_fusion.ready.a), channel_id=1, source_target_pairs={{0,8},{1,9},{2,10},{3,11},{4,12},{5,13},{6,14},{7,15},{8,0},{9,1},... | collective-permute-start | bytes 1572872 | tf_op jit(solution)/shard_map/ppermute | solution.py:39
  133.7 18.7 %collective-permute-start.27 = (bf16[256,1024]{1,0:T(8,128)(2,1)S(1)}, bf16[256,1024]{1,0:T(8,128)(2,1)}, u32[]{:S(2)}, u32[]{:S(2)}) collective-permute-start(bf16[256,1024]{1,0:T(8,128)(2,1)S(1)} %pad_maximum_fusion.ready.a), channel_id=1, source_target_pairs={{0,12},{1,13},{2,14},{3,15},{4,0},{5,1},{6,2},{7,3},{8,4},{9,5},{1... | collective-permute-start | bytes 1572872 | tf_op jit(solution)/shard_map/ppermute | solution.py:39
  137.3 15.1 %collective-permute-start.26 = (bf16[256,1024]{1,0:T(8,128)(2,1)S(1)}, bf16[256,1024]{1,0:T(8,128)(2,1)}, u32[]{:S(2)}, u32[]{:S(2)}) collective-permute-start(bf16[256,1024]{1,0:T(8,128)(2,1)S(1)} %pad_maximum_fusion.ready.a), channel_id=1, source_target_pairs={{0,4},{1,5},{2,6},{3,7},{4,8},{5,9},{6,10},{7,11},{8,12},{9,13},{1... | collective-permute-start | bytes 1572872 | tf_op jit(solution)/shard_map/ppermute | solution.py:39
  139.3 0.6 copy-start.7
  141.5 7.2 %collective-permute-start.24 = (bf16[64,1024]{1,0:T(8,128)(2,1)}, bf16[64,1024]{1,0:T(8,128)(2,1)S(1)}, u32[]{:S(2)}, u32[]{:S(2)}) collective-permute-start(bf16[64,1024]{1,0:T(8,128)(2,1)} %shard_map.58), channel_id=1, source_target_pairs={{176,112},{80,16},{177,113},{81,17},{178,114},{82,18},{179,115},{8... | collective-permute-start | bytes 393224 | tf_op jit(solution)/shard_map/ppermute | solution.py:45
  142.8 5.9 %collective-permute-start.23 = (bf16[64,1024]{1,0:T(8,128)(2,1)}, bf16[64,1024]{1,0:T(8,128)(2,1)}, u32[]{:S(2)}, u32[]{:S(2)}) collective-permute-start(bf16[64,1024]{1,0:T(8,128)(2,1)} %shard_map.58), channel_id=1, source_target_pairs={{176,144},{80,48},{177,145},{81,49},{178,146},{82,50},{179,147},{8... | collective-permute-start | bytes 393224 | tf_op jit(solution)/shard_map/ppermute | solution.py:45
  150.4 4.5 %collective-permute-start.25 = (bf16[64,1024]{1,0:T(8,128)(2,1)}, bf16[64,1024]{1,0:T(8,128)(2,1)}, u32[]{:S(2)}, u32[]{:S(2)}) collective-permute-start(bf16[64,1024]{1,0:T(8,128)(2,1)} %broadcast_select_fusion.1), channel_id=1, source_target_pairs={{16,0},{48,32},{80,64},{112,96},{144,128},{176,160},{208,192},{240... | collective-permute-start | bytes 393224 | tf_op jit(solution)/shard_map/ppermute | solution.py:229
  152.5 1.0 copy-start.2
  153.5 1.4 copy-start.4
  153.5 1.4 copy-start.5

commit v6 on v5

--- a/solution.py
+++ b/solution.py
@@ -12,7 +12,9 @@
 SIDE = 4
 VMEM = pl.BlockSpec(memory_space=pltpu.VMEM)
 SMEM = pl.BlockSpec(memory_space=pltpu.SMEM)
-PARAMS = pltpu.CompilerParams(vmem_limit_bytes=32 * 1024 * 1024)
+MIB = 1024 * 1024
+PARAMS = pltpu.CompilerParams(vmem_limit_bytes=16 * MIB)
+SMALL = pltpu.CompilerParams(vmem_limit_bytes=4 * MIB)
 
 
 def mm(a, b):
@@ -156,9 +158,60 @@
     return pl.pallas_call(
         join_kernel,
         out_shape=jax.ShapeDtypeStruct(a.shape, a.dtype),
-        in_specs=[VMEM, VMEM, pl.BlockSpec(memory_space=pl.ANY)],
-        out_specs=VMEM,
+        in_specs=[VMEM, VMEM, VMEM],
+        out_specs=VMEM,
+        compiler_params=SMALL,
     )(a, b, ready)
+
+
+def settle_kernel(flags, entry, relayed, last, edge, out):
+    @pl.when(flags[1] != 0)
+    def _():
+        out[...] = entry[...] + relayed[...] + last[...]
+
+    @pl.when(flags[1] == 0)
+    def _():
+        out[...] = edge[...]
+
+
+def settled(flags, entry, relayed, last, edge):
+    return pl.pallas_call(
+        settle_kernel,
+        out_shape=jax.ShapeDtypeStruct(entry.shape, entry.dtype),
+        in_specs=[SMEM] + [VMEM] * 4,
+        out_specs=VMEM,
+        compiler_params=SMALL,
+    )(flags, entry, relayed, last, edge)
+
+
+def close_kernel(flags, maps, entry, across, other, v_odd, out):
+    low, below = flags[0] != 0, flags[1] != 0
+
+    @pl.when(low & below)
+    def _():
+        out[...] = mm(across[...], maps[...]) + other[...].astype(F32)
+
+    @pl.when(low & jnp.logical_not(below))
+    def _():
+        out[...] = across[...].astype(F32)
+
+    @pl.when(jnp.logical_not(low) & below)
+    def _():
+        out[...] = mm(entry[...], maps[...]) + v_odd[...]
+
+    @pl.when(jnp.logical_not(low) & jnp.logical_not(below))
+    def _():
+        out[...] = v_odd[...]
+
+
+def closed(flags, maps, entry, across, other, v_odd):
+    return pl.pallas_call(
+        close_kernel,
+        out_shape=jax.ShapeDtypeStruct(entry.shape, F32),
+        in_specs=[SMEM] + [VMEM] * 5,
+        out_specs=VMEM,
+        compiler_params=PARAMS,
+    )(flags, maps, entry, across, other, v_odd)
 
 
 def body(inv_diag, couple, arrow, corner, band_offset):
@@ -197,7 +250,7 @@
     bias_got = lax.ppermute(bias, "depth", [(2 * k, 2 * k + 1) for k in range(chips)])
     product, step_odd, add_even = products(core, step, got, bias, bias_got)
     add_odd = jnp.where(low, jnp.zeros_like(bias), bias)
-    lower = (chips * 6) // 16
+    lower = (chips * 5) // 16
     tops = [chips - 1, lower - 1]
     sizes = [chips - lower, lower]
     start = (row == col) & ((chip == tops[0]) | (chip == tops[1])) & low
@@ -205,10 +258,10 @@
     v_even = mm(v_in, product) + add_even
     for hop in range(1, max(sizes)):
         pairs = []
-        for block_top, size in zip(tops, sizes):
+        for block_top, size, cores in zip(tops, sizes, ((1,), (0, 1))):
             if hop < size:
                 source = block_top - hop + 1
-                pairs += [(2 * source + k, 2 * source - 2 + k) for k in range(2)]
+                pairs += [(2 * source + k, 2 * source - 2 + k) for k in cores]
         v_in = v_in + lax.ppermute(v_even.astype(BF16), "depth", pairs)
         v_even = mm(v_in, product) + add_even
     edge = v_even.astype(BF16)
@@ -223,16 +276,13 @@
     entry = joined(sent_down(edge, [(lower, near)]), sent_down(edge, [(lower, far)]), ring)
     relayed = sent_down(entry, [(near, near - 1), (far, far - 1)])
     last = [(source, source - 2) for source, low_end in ((near, far), (far, -1)) if source - 2 > low_end]
-    entry = entry + relayed + sent_down(entry, last)
+    last = sent_down(entry, last)
     maps = place(jnp.stack(order), ring_gather(ring, depths, True))
     below = chip < lower
-    across = lax.ppermute(
-        jnp.where(below, entry, edge), "depth", [(2 * k + 1, 2 * k) for k in range(chips)]
-    )
-    zero = jnp.zeros_like(entry)
-    enter = jnp.where(below, jnp.where(low, across, entry), zero)
-    own = jnp.where(low, jnp.where(below, other, across).astype(F32), v_odd)
-    return (mm(enter, maps) + own)[None]
+    flags = jnp.stack([low, below]).astype(jnp.int32)
+    entry = settled(flags, entry, relayed, last, edge)
+    across = lax.ppermute(entry, "depth", [(2 * k + 1, 2 * k) for k in range(chips)])
+    return closed(flags, maps, entry, across, other, v_odd)[None]
 
 
 def solution(mesh):

time: 158 us -> 160 us (1.013)
  waiting for transfers between devices: 54.9 us -> 59.8 us
  Pallas kernels: 13.7 us -> 16.6 us
  local copies, waits for them, and re-layouts: 4.83 us -> 3.17 us
    ppermute x4, waiting for transfers between devices: 4.61 us -> 12 us  [sent_down(): lax.ppermute(value, 'depth', [(2 * a + 1, 2 * b + 1) for a, b in chip_pai...]
    ppermute x9 -> x10, waiting for transfers between devices: 24.1 us -> 19.5 us  [body(): v_in = v_in + lax.ppermute(v_even.astype(BF16), 'depth', pairs)]
    pallas_call x0 -> x2, Pallas kernels: none -> 3.9 us  [the longest x1 2.18 us: closed(): pl.pallas_call(close_kernel, out_shape=jax.ShapeDtypeStruct(entry.shape,...]
    ppermute x12, waiting for transfers between devices: 8.15 us -> 10.1 us  [ring_gather(): lax.ppermute(value, BOTH, ring_moves(depths, flipped, shift))]
    unnamed x22 -> x14, local copies, waits for them, and re-layouts: 2.8 us -> 1.13 us
    select_n x1 -> x0, other arithmetic: 1.66 us -> none  [body(): jnp.where(below, entry, edge)]
    ppermute x9 -> x10, starting transfers between devices: 6.82 us -> 7.49 us  [body(): v_in = v_in + lax.ppermute(v_even.astype(BF16), 'depth', pairs)]
  transfers between devices with their start and end apart: 30 -> 31, of which waited for: 9 -> 10; matrix products, arithmetic and copies ran while one was open for 4% -> 2% of each run, Pallas kernels for 2% -> 2%
where the time goes in v6:
time: 160 us; the launch traced here: 159 us
  starting transfers between devices  68.5 us (43%)
  waiting for transfers between devices  59.8 us (37%)
  Pallas kernels  16.6 us (10%)
  matrix products  6.87 us (4%)
  local copies, waits for them, and re-layouts  3.17 us (2%)
  other arithmetic  2.51 us (2%)
  between operations  1.79 us (1%)
    ppermute x12, starting transfers between devices, ring_gather(): lax.ppermute(value, BOTH, ring_moves(depths, flipped, shift))  38.1 us
    ppermute x10, waiting for transfers between devices, body(): v_in = v_in + lax.ppermute(v_even.astype(BF16), 'depth', pairs)  19.5 us
    all_to_all x1, waiting for transfers between devices, body(): lax.all_to_all(panel.reshape(lat_count, share, share), 'lat', 0, 0)  14.3 us
    ppermute x4, waiting for transfers between devices, sent_down(): lax.ppermute(value, 'depth', [(2 * a + 1, 2 * b + 1) for a, b in chip_pai...  12 us
    ppermute x12, waiting for transfers between devices, ring_gather(): lax.ppermute(value, BOTH, ring_moves(depths, flipped, shift))  10.1 us
    ppermute x10, starting transfers between devices, body(): v_in = v_in + lax.ppermute(v_even.astype(BF16), 'depth', pairs)  7.49 us
    ppermute x1, starting transfers between devices, body(): got = lax.ppermute(step, 'depth', swap)  7.03 us
    dot_general x13, matrix products, mm(): return jnp.dot(a, b, preferred_element_type=F32)  6.87 us
  transfers between devices with their start and end apart: 31, of which 10 were waited for; matrix products, arithmetic and copies ran while one was open for 2% of the time, Pallas kernels for 2%

profile of v6, /device:TPU:1, one launch (start us, length us, event | category | flops | bytes accessed | tf_op | source)
XLA Modules:
  0.0 159.3 jit_solution(15604488061789920872)
XLA Ops:
  0.8 1.0 fusion.15
  1.9 0.9 pad_maximum_fusion.1.a
  2.8 5.7 %collective-permute-start.2 = (bf16[2,64,1024]{2,1,0:T(8,128)(2,1)S(1)}, bf16[2,64,1024]{2,1,0:T(8,128)(2,1)S(1)}, u32[]{:S(2)}, u32[]{:S(2)}) collective-permute-start(bf16[2,64,1024]{2,1,0:T(8,128)(2,1)S(1)} %pad_maximum_fusion.1.a), channel_id=1, source_target_pairs={{0,2},{1,3},{2,0},{3,1},{4,6},{5,7},{6,4},{7,5},{8,10},{9,11},{10,... | collective-permute-start | bytes 786440 | tf_op jit(solution)/shard_map/ppermute | solution.py:41
  8.5 2.7 %collective-permute-start.1 = (bf16[2,64,1024]{2,1,0:T(8,128)(2,1)S(1)}, bf16[2,64,1024]{2,1,0:T(8,128)(2,1)S(1)}, u32[]{:S(2)}, u32[]{:S(2)}) collective-permute-start(bf16[2,64,1024]{2,1,0:T(8,128)(2,1)S(1)} %pad_maximum_fusion.1.a), channel_id=1, source_target_pairs={{0,3},{1,0},{2,1},{3,2},{4,7},{5,4},{6,5},{7,6},{8,11},{9,8},{10,9... | collective-permute-start | bytes 786440 | tf_op jit(solution)/shard_map/ppermute | solution.py:41
  11.2 2.6 %collective-permute-start = (bf16[2,64,1024]{2,1,0:T(8,128)(2,1)S(1)}, bf16[2,64,1024]{2,1,0:T(8,128)(2,1)S(1)}, u32[]{:S(2)}, u32[]{:S(2)}) collective-permute-start(bf16[2,64,1024]{2,1,0:T(8,128)(2,1)S(1)} %pad_maximum_fusion.1.a), channel_id=1, source_target_pairs={{0,1},{1,2},{2,3},{3,0},{4,5},{5,6},{6,7},{7,4},{8,9},{9,10},{10,1... | collective-permute-start | bytes 786440 | tf_op jit(solution)/shard_map/ppermute | solution.py:41
  13.8 1.8 %collective-permute-done.1.c = bf16[2,64,1024]{2,1,0:T(8,128)(2,1)S(1)} collective-permute-done((bf16[2,64,1024]{2,1,0:T(8,128)(2,1)S(1)}, bf16[2,64,1024]{2,1,0:T(8,128)(2,1)S(1)}, u32[]{:S(2)}, u32[]{:S(2)}) %collective-permute-start.1) | collective-permute-done | bytes 262176 | tf_op jit(solution)/shard_map/ppermute | solution.py:41
  15.6 3.9 %collective-permute-done.b = bf16[2,64,1024]{2,1,0:T(8,128)(2,1)S(1)} collective-permute-done((bf16[2,64,1024]{2,1,0:T(8,128)(2,1)S(1)}, bf16[2,64,1024]{2,1,0:T(8,128)(2,1)S(1)}, u32[]{:S(2)}, u32[]{:S(2)}) %collective-permute-start) | collective-permute-done | bytes 262176 | tf_op jit(solution)/shard_map/ppermute | solution.py:41
  19.7 4.7 %collective-permute-start.5 = (bf16[2,256,1024]{2,1,0:T(8,128)(2,1)S(1)}, bf16[2,256,1024]{2,1,0:T(8,128)(2,1)}, u32[]{:S(2)}, u32[]{:S(2)}) collective-permute-start(bf16[2,256,1024]{2,1,0:T(8,128)(2,1)S(1)} %shard_map.55.a), channel_id=1, source_target_pairs={{0,8},{1,9},{2,10},{3,11},{4,12},{5,13},{6,14},{7,15},{8,0},{9,1},... | collective-permute-start | bytes 3145736 | tf_op jit(solution)/shard_map/ppermute | solution.py:41
  24.4 2.8 %collective-permute-start.4 = (bf16[2,256,1024]{2,1,0:T(8,128)(2,1)S(1)}, bf16[2,256,1024]{2,1,0:T(8,128)(2,1)}, u32[]{:S(2)}, u32[]{:S(2)}) collective-permute-start(bf16[2,256,1024]{2,1,0:T(8,128)(2,1)S(1)} %shard_map.55.a), channel_id=1, source_target_pairs={{0,12},{1,13},{2,14},{3,15},{4,0},{5,1},{6,2},{7,3},{8,4},{9,5},{1... | collective-permute-start | bytes 3145736 | tf_op jit(solution)/shard_map/ppermute | solution.py:41
  27.1 2.5 %collective-permute-start.3 = (bf16[2,256,1024]{2,1,0:T(8,128)(2,1)S(1)}, bf16[2,256,1024]{2,1,0:T(8,128)(2,1)}, u32[]{:S(2)}, u32[]{:S(2)}) collective-permute-start(bf16[2,256,1024]{2,1,0:T(8,128)(2,1)S(1)} %shard_map.55.a), channel_id=1, source_target_pairs={{0,4},{1,5},{2,6},{3,7},{4,8},{5,9},{6,10},{7,11},{8,12},{9,13},{1... | collective-permute-start | bytes 3145736 | tf_op jit(solution)/shard_map/ppermute | solution.py:41
  29.7 0.8 convolution_convert_fusion
  30.6 0.9 reshape.8
  31.5 3.7 %all-to-all-start = ((bf16[16,2,2048]{2,1,0:T(2,128)(2,1)}), bf16[16,2,2048]{2,1,0:T(2,128)(2,1)S(1)}, u32[]{:S(2)}, u32[]{:S(2)}) async-start(bf16[16,2,2048]{2,1,0:T(2,128)(2,1)} %reshape.8), calls=%async_computation | async-start | bytes 262144 | tf_op jit(solution)/shard_map/all_to_all | solution.py:240
  35.5 14.3 %all-to-all-done = bf16[16,2,2048]{2,1,0:T(2,128)(2,1)S(1)} async-done(((bf16[16,2,2048]{2,1,0:T(2,128)(2,1)}), bf16[16,2,2048]{2,1,0:T(2,128)(2,1)S(1)}, u32[]{:S(2)}, u32[]{:S(2)}) %all-to-all-start) | async-done | bytes 131104 | tf_op jit(solution)/shard_map/all_to_all | solution.py:240
  50.0 0.7 dynamic-slice_bitcast_fusion
  50.8 1.0 concatenate.6.panel
  51.9 5.6 %shard_map.56 = (bf16[1024,1024]{1,0:T(8,128)(2,1)}, f32[64,1024]{1,0:T(8,128)S(1)}) custom-call(bf16[64,1024]{1,0:T(8,128)(2,1)S(1)} %concatenate.6.panel, bf16[2,256,1024]{2,1,0:T(8,128)(2,1)S(1)} %shard_map.55.a, bf16[2,256,1024]{2,1,0:T(8,128)(2,1)} %collective-permute-done.3.b, bf16[2,256,1024]{2,1,0:T(8,128)(2,1)} %collective-permute-done.4.c, ...), custom_call_target="tpu_custom_call" | custom-call | flops 2147483648 | bytes 6291456 | tf_op jit(solution)/shard_map/pallas_call | solution.py:103
  57.4 7.0 %collective-permute-start.6 = (bf16[1024,1024]{1,0:T(8,128)(2,1)}, bf16[1024,1024]{1,0:T(8,128)(2,1)}, u32[]{:S(2)}, u32[]{:S(2)}) collective-permute-start(bf16[1024,1024]{1,0:T(8,128)(2,1)} %get-tuple-element.10.own), channel_id=1, source_target_pairs={{0,16},{16,0},{32,48},{48,32},{64,80},{80,64},{96,112},{112,96},{1... | collective-permute-start | bytes 6291464 | tf_op jit(solution)/shard_map/ppermute | solution.py:249
  64.5 1.3 collective-permute-start.7
  65.8 2.7 %collective-permute-done.7.bias_got = f32[64,1024]{1,0:T(8,128)S(1)} collective-permute-done((f32[64,1024]{1,0:T(8,128)S(1)}, f32[64,1024]{1,0:T(8,128)S(1)}, u32[]{:S(2)}, u32[]{:S(2)}) %collective-permute-start.7) | collective-permute-done | bytes 262176 | tf_op jit(solution)/shard_map/ppermute | solution.py:250
  68.6 4.9 %shard_map.57 = (bf16[1024,1024]{1,0:T(8,128)(2,1)S(1)}, bf16[1024,1024]{1,0:T(8,128)(2,1)S(1)}, f32[64,1024]{1,0:T(8,128)S(1)}) custom-call(s32[1]{0:T(128)} %bitcast.18.core, bf16[1024,1024]{1,0:T(8,128)(2,1)} %get-tuple-element.10.own, bf16[1024,1024]{1,0:T(8,128)(2,1)} %collective-permute-done.6.got, f32[64,1024]{1,0:T(8,128)S(1)} %get-tuple-element.11.bias, ...), custom_call_target="tpu_custom_call" | custom-call | flops 2147483648 | bytes 6291456 | tf_op jit(solution)/shard_map/pallas_call | solution.py:139
  73.5 0.5 fusion
  74.0 0.7 collective-permute-start.8
  74.7 0.6 fusion.1
  75.3 0.7 collective-permute-start.9
  76.0 0.6 fusion.2
  76.5 0.7 collective-permute-start.10
  77.4 0.5 fusion.3
  77.9 1.3 collective-permute-start.11
  79.2 19.5 %collective-permute-done.11 = bf16[64,1024]{1,0:T(8,128)(2,1)S(1)} collective-permute-done((bf16[64,1024]{1,0:T(8,128)(2,1)S(1)}, bf16[64,1024]{1,0:T(8,128)(2,1)S(1)}, u32[]{:S(2)}, u32[]{:S(2)}) %collective-permute-start.11) | collective-permute-done | bytes 131104 | tf_op jit(solution)/shard_map/ppermute | solution.py:265
  98.8 0.5 fusion.4
  99.3 0.7 collective-permute-start.12
  100.0 0.5 fusion.5
  100.5 0.7 collective-permute-start.13
  101.2 0.5 fusion.6
  101.7 0.7 collective-permute-start.14
  102.5 0.5 fusion.7
  103.0 0.8 collective-permute-start.15
  103.9 0.5 fusion.8
  104.4 0.7 collective-permute-start.16
  105.1 0.5 fusion.9
  105.6 0.7 collective-permute-start.17
  106.3 0.5 convolution_add_fusion.v_odd
  106.8 0.5 convert_select_fusion
  107.3 5.1 %collective-permute-start.18 = (bf16[64,1024]{1,0:T(8,128)(2,1)S(1)}, bf16[64,1024]{1,0:T(8,128)(2,1)S(1)}, u32[]{:S(2)}, u32[]{:S(2)}) collective-permute-start(bf16[64,1024]{1,0:T(8,128)(2,1)S(1)} %get-tuple-element.31), channel_id=1, source_target_pairs={{0,16},{16,0},{32,48},{48,32},{64,80},{80,64},{96,112},{112,96},{1... | collective-permute-start | bytes 393224 | tf_op jit(solution)/shard_map/ppermute | solution.py:269
  112.4 1.0 collective-permute-done.18.other
  113.4 4.5 %collective-permute-start.21 = (bf16[64,1024]{1,0:T(8,128)(2,1)S(1)}, bf16[64,1024]{1,0:T(8,128)(2,1)S(1)}, u32[]{:S(2)}, u32[]{:S(2)}) collective-permute-start(bf16[64,1024]{1,0:T(8,128)(2,1)S(1)} %broadcast_select_fusion), channel_id=1, source_target_pairs={{0,2},{1,3},{2,0},{3,1},{4,6},{5,7},{6,4},{7,5},{8,10},{9,11},{10,... | collective-permute-start | bytes 393224 | tf_op jit(solution)/shard_map/ppermute | solution.py:41
  117.9 2.7 %collective-permute-start.20 = (bf16[64,1024]{1,0:T(8,128)(2,1)S(1)}, bf16[64,1024]{1,0:T(8,128)(2,1)S(1)}, u32[]{:S(2)}, u32[]{:S(2)}) collective-permute-start(bf16[64,1024]{1,0:T(8,128)(2,1)S(1)} %broadcast_select_fusion), channel_id=1, source_target_pairs={{0,3},{1,0},{2,1},{3,2},{4,7},{5,4},{6,5},{7,6},{8,11},{9,8},{10,9... | collective-permute-start | bytes 393224 | tf_op jit(solution)/shard_map/ppermute | solution.py:41
  120.6 2.6 %collective-permute-start.19 = (bf16[64,1024]{1,0:T(8,128)(2,1)S(1)}, bf16[64,1024]{1,0:T(8,128)(2,1)S(1)}, u32[]{:S(2)}, u32[]{:S(2)}) collective-permute-start(bf16[64,1024]{1,0:T(8,128)(2,1)S(1)} %broadcast_select_fusion), channel_id=1, source_target_pairs={{0,1},{1,2},{2,3},{3,0},{4,5},{5,6},{6,7},{7,4},{8,9},{9,10},{10,1... | collective-permute-start | bytes 393224 | tf_op jit(solution)/shard_map/ppermute | solution.py:41
  123.2 0.4 collective-permute-done.20
  123.6 4.0 %collective-permute-done.19 = bf16[64,1024]{1,0:T(8,128)(2,1)S(1)} collective-permute-done((bf16[64,1024]{1,0:T(8,128)(2,1)S(1)}, bf16[64,1024]{1,0:T(8,128)(2,1)S(1)}, u32[]{:S(2)}, u32[]{:S(2)}) %collective-permute-start.19) | collective-permute-done | bytes 131104 | tf_op jit(solution)/shard_map/ppermute | solution.py:41
  127.7 1.9 %collective-permute-start.24 = (bf16[256,1024]{1,0:T(8,128)(2,1)S(1)}, bf16[256,1024]{1,0:T(8,128)(2,1)S(1)}, u32[]{:S(2)}, u32[]{:S(2)}) collective-permute-start(bf16[256,1024]{1,0:T(8,128)(2,1)S(1)} %pad_maximum_fusion.a.ready), channel_id=1, source_target_pairs={{0,8},{1,9},{2,10},{3,11},{4,12},{5,13},{6,14},{7,15},{8,0},{9,1},... | collective-permute-start | bytes 1572872 | tf_op jit(solution)/shard_map/ppermute | solution.py:41
  129.6 3.6 %collective-permute-start.23 = (bf16[256,1024]{1,0:T(8,128)(2,1)S(1)}, bf16[256,1024]{1,0:T(8,128)(2,1)}, u32[]{:S(2)}, u32[]{:S(2)}) collective-permute-start(bf16[256,1024]{1,0:T(8,128)(2,1)S(1)} %pad_maximum_fusion.a.ready), channel_id=1, source_target_pairs={{0,12},{1,13},{2,14},{3,15},{4,0},{5,1},{6,2},{7,3},{8,4},{9,5},{1... | collective-permute-start | bytes 1572872 | tf_op jit(solution)/shard_map/ppermute | solution.py:41
  133.2 1.9 %collective-permute-start.22 = (bf16[256,1024]{1,0:T(8,128)(2,1)S(1)}, bf16[256,1024]{1,0:T(8,128)(2,1)}, u32[]{:S(2)}, u32[]{:S(2)}) collective-permute-start(bf16[256,1024]{1,0:T(8,128)(2,1)S(1)} %pad_maximum_fusion.a.ready), channel_id=1, source_target_pairs={{0,4},{1,5},{2,6},{3,7},{4,8},{5,9},{6,10},{7,11},{8,12},{9,13},{1... | collective-permute-start | bytes 1572872 | tf_op jit(solution)/shard_map/ppermute | solution.py:41
  135.1 0.7 collective-permute-start.26
  135.8 0.7 collective-permute-start.25
  136.5 0.7 shard_map.59.entry
  137.2 1.3 collective-permute-start.28
  138.5 1.3 collective-permute-start.27
  139.9 12.0 %collective-permute-done.27.relayed = bf16[64,1024]{1,0:T(8,128)(2,1)} collective-permute-done((bf16[64,1024]{1,0:T(8,128)(2,1)}, bf16[64,1024]{1,0:T(8,128)(2,1)}, u32[]{:S(2)}, u32[]{:S(2)}) %collective-permute-start.27) | collective-permute-done | bytes 131104 | tf_op jit(solution)/shard_map/ppermute | solution.py:47
  151.9 1.7 %shard_map.60.entry = bf16[64,1024]{1,0:T(8,128)(2,1)} custom-call(s32[2]{0:T(128)S(1)} %add_convert_fusion.flags, bf16[64,1024]{1,0:T(8,128)(2,1)} %shard_map.59.entry, bf16[64,1024]{1,0:T(8,128)(2,1)} %collective-permute-done.27.relayed, bf16[64,1024]{1,0:T(8,128)(2,1)} %collective-permute-done.28.last, bf16[64,1024]{1,0:T(8,128)(2,1)S(1)} %get-tuple-element.32.edge), custom_call_target="tpu_custom_call" | custom-call | tf_op jit(solution)/shard_map/pallas_call | solution.py:178
  153.6 1.9 %collective-permute-start.29 = (bf16[64,1024]{1,0:T(8,128)(2,1)}, bf16[64,1024]{1,0:T(8,128)(2,1)}, u32[]{:S(2)}, u32[]{:S(2)}) collective-permute-start(bf16[64,1024]{1,0:T(8,128)(2,1)} %shard_map.60.entry), channel_id=1, source_target_pairs={{16,0},{48,32},{80,64},{112,96},{144,128},{176,160},{208,192},{240... | collective-permute-start | bytes 393224 | tf_op jit(solution)/shard_map/ppermute | solution.py:284
  155.7 1.4 shard_map.58.maps
  157.1 2.2 %shard_map.61 = f32[64,1024]{1,0:T(8,128)} custom-call(s32[2]{0:T(128)S(1)} %add_convert_fusion.flags, bf16[1024,1024]{1,0:T(8,128)(2,1)S(1)} %shard_map.58.maps, bf16[64,1024]{1,0:T(8,128)(2,1)} %shard_map.60.entry, bf16[64,1024]{1,0:T(8,128)(2,1)} %collective-permute-done.29.across, bf16[64,1024]{1,0:T(8,128)(2,1)S(1)} %copy-done.2, ...), custom_call_target="tpu_custom_call" | custom-call | tf_op jit(solution)/shard_map/pallas_call | solution.py:208
  (49 shorter events, 1.4 us)
Async XLA Ops:
  0.0 29.7 %copy-start = (bf16[1024,1024]{1,0:T(8,128)(2,1)S(1)}, bf16[1024,1024]{1,0:T(8,128)(2,1)}, u32[]{:S(2)}) copy-start(bf16[1024,1024]{1,0:T(8,128)(2,1)} %param.8) | copy-start | bytes 6291460
  0.0 29.7 %copy-start.3 = (bf16[1,1024,64]{1,2,0:T(8,128)(2,1)S(1)}, bf16[1,1024,64]{1,2,0:T(8,128)(2,1)}, u32[]{:S(2)}) copy-start(bf16[1,1024,64]{1,2,0:T(8,128)(2,1)} %param.7) | copy-start | bytes 393220
  0.8 14.8 %copy-start.4 = (s32[64]{0:T(128)}, s32[64]{0:T(128)S(1)}, u32[]{:S(2)}) copy-start(s32[64]{0:T(128)S(1)} %iota_add_fusion) | copy-start | bytes 772
  2.8 11.0 %collective-permute-start.2 = (bf16[2,64,1024]{2,1,0:T(8,128)(2,1)S(1)}, bf16[2,64,1024]{2,1,0:T(8,128)(2,1)S(1)}, u32[]{:S(2)}, u32[]{:S(2)}) collective-permute-start(bf16[2,64,1024]{2,1,0:T(8,128)(2,1)S(1)} %pad_maximum_fusion.1.a), channel_id=1, source_target_pairs={{0,2},{1,3},{2,0},{3,1},{4,6},{5,7},{6,4},{7,5},{8,10},{9,11},{10,... | collective-permute-start | bytes 786440 | tf_op jit(solution)/shard_map/ppermute | solution.py:41
  8.5 7.1 %collective-permute-start.1 = (bf16[2,64,1024]{2,1,0:T(8,128)(2,1)S(1)}, bf16[2,64,1024]{2,1,0:T(8,128)(2,1)S(1)}, u32[]{:S(2)}, u32[]{:S(2)}) collective-permute-start(bf16[2,64,1024]{2,1,0:T(8,128)(2,1)S(1)} %pad_maximum_fusion.1.a), channel_id=1, source_target_pairs={{0,3},{1,0},{2,1},{3,2},{4,7},{5,4},{6,5},{7,6},{8,11},{9,8},{10,9... | collective-permute-start | bytes 786440 | tf_op jit(solution)/shard_map/ppermute | solution.py:41
  11.2 8.3 %collective-permute-start = (bf16[2,64,1024]{2,1,0:T(8,128)(2,1)S(1)}, bf16[2,64,1024]{2,1,0:T(8,128)(2,1)S(1)}, u32[]{:S(2)}, u32[]{:S(2)}) collective-permute-start(bf16[2,64,1024]{2,1,0:T(8,128)(2,1)S(1)} %pad_maximum_fusion.1.a), channel_id=1, source_target_pairs={{0,1},{1,2},{2,3},{3,0},{4,5},{5,6},{6,7},{7,4},{8,9},{9,10},{10,1... | collective-permute-start | bytes 786440 | tf_op jit(solution)/shard_map/ppermute | solution.py:41
  19.7 32.1 %collective-permute-start.5 = (bf16[2,256,1024]{2,1,0:T(8,128)(2,1)S(1)}, bf16[2,256,1024]{2,1,0:T(8,128)(2,1)}, u32[]{:S(2)}, u32[]{:S(2)}) collective-permute-start(bf16[2,256,1024]{2,1,0:T(8,128)(2,1)S(1)} %shard_map.55.a), channel_id=1, source_target_pairs={{0,8},{1,9},{2,10},{3,11},{4,12},{5,13},{6,14},{7,15},{8,0},{9,1},... | collective-permute-start | bytes 3145736 | tf_op jit(solution)/shard_map/ppermute | solution.py:41
  24.4 27.5 %collective-permute-start.4 = (bf16[2,256,1024]{2,1,0:T(8,128)(2,1)S(1)}, bf16[2,256,1024]{2,1,0:T(8,128)(2,1)}, u32[]{:S(2)}, u32[]{:S(2)}) collective-permute-start(bf16[2,256,1024]{2,1,0:T(8,128)(2,1)S(1)} %shard_map.55.a), channel_id=1, source_target_pairs={{0,12},{1,13},{2,14},{3,15},{4,0},{5,1},{6,2},{7,3},{8,4},{9,5},{1... | collective-permute-start | bytes 3145736 | tf_op jit(solution)/shard_map/ppermute | solution.py:41
  27.1 24.7 %collective-permute-start.3 = (bf16[2,256,1024]{2,1,0:T(8,128)(2,1)S(1)}, bf16[2,256,1024]{2,1,0:T(8,128)(2,1)}, u32[]{:S(2)}, u32[]{:S(2)}) collective-permute-start(bf16[2,256,1024]{2,1,0:T(8,128)(2,1)S(1)} %shard_map.55.a), channel_id=1, source_target_pairs={{0,4},{1,5},{2,6},{3,7},{4,8},{5,9},{6,10},{7,11},{8,12},{9,13},{1... | collective-permute-start | bytes 3145736 | tf_op jit(solution)/shard_map/ppermute | solution.py:41
  31.5 18.3 %all-to-all-start = ((bf16[16,2,2048]{2,1,0:T(2,128)(2,1)}), bf16[16,2,2048]{2,1,0:T(2,128)(2,1)S(1)}, u32[]{:S(2)}, u32[]{:S(2)}) async-start(bf16[16,2,2048]{2,1,0:T(2,128)(2,1)} %reshape.8), calls=%async_computation | async-start | bytes 262144 | tf_op jit(solution)/shard_map/all_to_all | solution.py:240
  57.4 11.1 %collective-permute-start.6 = (bf16[1024,1024]{1,0:T(8,128)(2,1)}, bf16[1024,1024]{1,0:T(8,128)(2,1)}, u32[]{:S(2)}, u32[]{:S(2)}) collective-permute-start(bf16[1024,1024]{1,0:T(8,128)(2,1)} %get-tuple-element.10.own), channel_id=1, source_target_pairs={{0,16},{16,0},{32,48},{48,32},{64,80},{80,64},{96,112},{112,96},{1... | collective-permute-start | bytes 6291464 | tf_op jit(solution)/shard_map/ppermute | solution.py:249
  64.5 4.0 %collective-permute-start.7 = (f32[64,1024]{1,0:T(8,128)S(1)}, f32[64,1024]{1,0:T(8,128)S(1)}, u32[]{:S(2)}, u32[]{:S(2)}) collective-permute-start(f32[64,1024]{1,0:T(8,128)S(1)} %get-tuple-element.11.bias), channel_id=1, source_target_pairs={{0,16},{32,48},{64,80},{96,112},{128,144},{160,176},{192,208},{224... | collective-permute-start | bytes 786440 | tf_op jit(solution)/shard_map/ppermute | solution.py:250
  68.6 4.9 %copy-start.5 = (s32[64]{0:T(128)S(1)}, s32[64]{0:T(128)}, u32[]{:S(2)}) copy-start(s32[64]{0:T(128)} %copy-done.4) | copy-start | bytes 772
  74.0 0.7 collective-permute-start.8
  75.3 0.7 collective-permute-start.9
  76.5 0.7 collective-permute-start.10
  77.9 20.8 %collective-permute-start.11 = (bf16[64,1024]{1,0:T(8,128)(2,1)S(1)}, bf16[64,1024]{1,0:T(8,128)(2,1)S(1)}, u32[]{:S(2)}, u32[]{:S(2)}) collective-permute-start(bf16[64,1024]{1,0:T(8,128)(2,1)S(1)} %fusion.3), channel_id=1, source_target_pairs={{400,368},{32,0},{48,16},{401,369},{33,1},{49,17},{402,370},{34,2}... | collective-permute-start | bytes 393224 | tf_op jit(solution)/shard_map/ppermute | solution.py:265
  99.3 0.7 collective-permute-start.12
  100.5 0.7 collective-permute-start.13
  101.7 0.7 collective-permute-start.14
  103.0 0.9 collective-permute-start.15
  104.4 0.7 collective-permute-start.16
  105.6 0.7 collective-permute-start.17
  107.3 6.1 %collective-permute-start.18 = (bf16[64,1024]{1,0:T(8,128)(2,1)S(1)}, bf16[64,1024]{1,0:T(8,128)(2,1)S(1)}, u32[]{:S(2)}, u32[]{:S(2)}) collective-permute-start(bf16[64,1024]{1,0:T(8,128)(2,1)S(1)} %get-tuple-element.31), channel_id=1, source_target_pairs={{0,16},{16,0},{32,48},{48,32},{64,80},{80,64},{96,112},{112,96},{1... | collective-permute-start | bytes 393224 | tf_op jit(solution)/shard_map/ppermute | solution.py:269
  113.4 10.2 %copy-start.1 = (bf16[64,1024]{1,0:T(8,128)(2,1)}, bf16[64,1024]{1,0:T(8,128)(2,1)S(1)}, u32[]{:S(2)}) copy-start(bf16[64,1024]{1,0:T(8,128)(2,1)S(1)} %collective-permute-done.18.other) | copy-start | bytes 393220
  113.4 9.8 %collective-permute-start.21 = (bf16[64,1024]{1,0:T(8,128)(2,1)S(1)}, bf16[64,1024]{1,0:T(8,128)(2,1)S(1)}, u32[]{:S(2)}, u32[]{:S(2)}) collective-permute-start(bf16[64,1024]{1,0:T(8,128)(2,1)S(1)} %broadcast_select_fusion), channel_id=1, source_target_pairs={{0,2},{1,3},{2,0},{3,1},{4,6},{5,7},{6,4},{7,5},{8,10},{9,11},{10,... | collective-permute-start | bytes 393224 | tf_op jit(solution)/shard_map/ppermute | solution.py:41
  117.9 5.7 %collective-permute-start.20 = (bf16[64,1024]{1,0:T(8,128)(2,1)S(1)}, bf16[64,1024]{1,0:T(8,128)(2,1)S(1)}, u32[]{:S(2)}, u32[]{:S(2)}) collective-permute-start(bf16[64,1024]{1,0:T(8,128)(2,1)S(1)} %broadcast_select_fusion), channel_id=1, source_target_pairs={{0,3},{1,0},{2,1},{3,2},{4,7},{5,4},{6,5},{7,6},{8,11},{9,8},{10,9... | collective-permute-start | bytes 393224 | tf_op jit(solution)/shard_map/ppermute | solution.py:41
  120.6 7.0 %collective-permute-start.19 = (bf16[64,1024]{1,0:T(8,128)(2,1)S(1)}, bf16[64,1024]{1,0:T(8,128)(2,1)S(1)}, u32[]{:S(2)}, u32[]{:S(2)}) collective-permute-start(bf16[64,1024]{1,0:T(8,128)(2,1)S(1)} %broadcast_select_fusion), channel_id=1, source_target_pairs={{0,1},{1,2},{2,3},{3,0},{4,5},{5,6},{6,7},{7,4},{8,9},{9,10},{10,1... | collective-permute-start | bytes 393224 | tf_op jit(solution)/shard_map/ppermute | solution.py:41
  127.7 28.0 %collective-permute-start.24 = (bf16[256,1024]{1,0:T(8,128)(2,1)S(1)}, bf16[256,1024]{1,0:T(8,128)(2,1)S(1)}, u32[]{:S(2)}, u32[]{:S(2)}) collective-permute-start(bf16[256,1024]{1,0:T(8,128)(2,1)S(1)} %pad_maximum_fusion.a.ready), channel_id=1, source_target_pairs={{0,8},{1,9},{2,10},{3,11},{4,12},{5,13},{6,14},{7,15},{8,0},{9,1},... | collective-permute-start | bytes 1572872 | tf_op jit(solution)/shard_map/ppermute | solution.py:41
  129.6 26.1 %collective-permute-start.23 = (bf16[256,1024]{1,0:T(8,128)(2,1)S(1)}, bf16[256,1024]{1,0:T(8,128)(2,1)}, u32[]{:S(2)}, u32[]{:S(2)}) collective-permute-start(bf16[256,1024]{1,0:T(8,128)(2,1)S(1)} %pad_maximum_fusion.a.ready), channel_id=1, source_target_pairs={{0,12},{1,13},{2,14},{3,15},{4,0},{5,1},{6,2},{7,3},{8,4},{9,5},{1... | collective-permute-start | bytes 1572872 | tf_op jit(solution)/shard_map/ppermute | solution.py:41
  133.2 22.4 %collective-permute-start.22 = (bf16[256,1024]{1,0:T(8,128)(2,1)S(1)}, bf16[256,1024]{1,0:T(8,128)(2,1)}, u32[]{:S(2)}, u32[]{:S(2)}) collective-permute-start(bf16[256,1024]{1,0:T(8,128)(2,1)S(1)} %pad_maximum_fusion.a.ready), channel_id=1, source_target_pairs={{0,4},{1,5},{2,6},{3,7},{4,8},{5,9},{6,10},{7,11},{8,12},{9,13},{1... | collective-permute-start | bytes 1572872 | tf_op jit(solution)/shard_map/ppermute | solution.py:41
  135.1 1.4 collective-permute-start.26
  135.8 0.7 collective-permute-start.25
  137.2 2.7 %collective-permute-start.28 = (bf16[64,1024]{1,0:T(8,128)(2,1)}, bf16[64,1024]{1,0:T(8,128)(2,1)}, u32[]{:S(2)}, u32[]{:S(2)}) collective-permute-start(bf16[64,1024]{1,0:T(8,128)(2,1)} %shard_map.59.entry), channel_id=1, source_target_pairs={{144,80},{145,81},{146,82},{147,83},{148,84},{149,85},{150,86},{15... | collective-permute-start | bytes 393224 | tf_op jit(solution)/shard_map/ppermute | solution.py:47
  138.5 13.4 %collective-permute-start.27 = (bf16[64,1024]{1,0:T(8,128)(2,1)}, bf16[64,1024]{1,0:T(8,128)(2,1)}, u32[]{:S(2)}, u32[]{:S(2)}) collective-permute-start(bf16[64,1024]{1,0:T(8,128)(2,1)} %shard_map.59.entry), channel_id=1, source_target_pairs={{144,112},{48,16},{145,113},{49,17},{146,114},{50,18},{147,115},{5... | collective-permute-start | bytes 393224 | tf_op jit(solution)/shard_map/ppermute | solution.py:47
  153.6 3.5 %collective-permute-start.29 = (bf16[64,1024]{1,0:T(8,128)(2,1)}, bf16[64,1024]{1,0:T(8,128)(2,1)}, u32[]{:S(2)}, u32[]{:S(2)}) collective-permute-start(bf16[64,1024]{1,0:T(8,128)(2,1)} %shard_map.60.entry), channel_id=1, source_target_pairs={{16,0},{48,32},{80,64},{112,96},{144,128},{176,160},{208,192},{240... | collective-permute-start | bytes 393224 | tf_op jit(solution)/shard_map/ppermute | solution.py:284
  155.6 1.4 copy-start.2

commit v7 on v6

--- a/solution.py
+++ b/solution.py
@@ -88,29 +88,79 @@
     )(*blocks)
 
 
-def step_kernel(panel, a, b, c, d, step, bias):
+def half_product(first, second, cut):
+    left = jnp.concatenate([first[1, :, cut], second[1, :, cut]], axis=1)
+    return mm(left, jnp.concatenate([first[0], second[0]]))
+
+
+def part_kernel(a, d, out, token):
+    token[...] = jnp.zeros_like(token)
     wide = a.shape[1]
-    right = jnp.concatenate([block[0] for block in (a, b, c, d)])
+    for m in range(out.shape[0] // wide):
+        cut = slice(m * wide, (m + 1) * wide)
+        out[cut, :] = half_product(a, d, cut).astype(BF16)
+
+
+def step_kernel(panel, part, b, c, a_right, d_right, step, bias):
+    wide = b.shape[1]
     for m in range(step.shape[0] // wide):
         cut = slice(m * wide, (m + 1) * wide)
-        left = jnp.concatenate([block[1, :, cut] for block in (a, b, c, d)], axis=1)
-        step[cut, :] = (-mm(left, right)).astype(BF16)
-    bias[...] = -mm(panel[...], right)
-
-
-def step_terms(panel, blocks):
-    width = blocks[0].shape[2]
+        step[cut, :] = (-(part[cut, :].astype(F32) + half_product(b, c, cut))).astype(BF16)
+    total = mm(panel[:, :wide], a_right[0])
+    for f, right in ((1, b), (2, c), (3, d_right)):
+        total = total + mm(panel[:, f * wide : (f + 1) * wide], right[0])
+    bias[...] = -total
+
+
+def cut_kernel(order, panel, ready, out):
+    share = panel.shape[2] // 2
+    for i in range(0, panel.shape[0], 2):
+        two = [panel[order[i]].astype(F32), panel[order[i + 1]].astype(F32)]
+        upper = jnp.concatenate([part[:, :share] for part in two], axis=1)
+        under = jnp.concatenate([part[:, share:] for part in two], axis=1)
+        both = jnp.concatenate([upper, under]).astype(BF16)
+        out[:, i * share : (i + 2) * share] = both
+
+
+def step_terms(order, panel, blocks):
+    a, b, c, d = blocks
+    two, wide, width = a.shape
+    cost = pl.CostEstimate(flops=width**3, bytes_accessed=6 * width**2, transcendentals=0)
+    part, token = pl.pallas_call(
+        part_kernel,
+        out_shape=[
+            jax.ShapeDtypeStruct((width, width), BF16),
+            jax.ShapeDtypeStruct((8, 128), F32),
+        ],
+        in_specs=[VMEM] * 2,
+        out_specs=[VMEM, VMEM],
+        compiler_params=PARAMS,
+        cost_estimate=cost,
+    )(a, d)
+    panel = pl.pallas_call(
+        cut_kernel,
+        out_shape=jax.ShapeDtypeStruct((2 * panel.shape[1], width), BF16),
+        in_specs=[SMEM, VMEM, VMEM],
+        out_specs=VMEM,
+        compiler_params=SMALL,
+    )(order, panel, token)
+
+    def whole(shape):
+        return pl.BlockSpec(shape, lambda i: (0,) * len(shape))
+
+    right = whole((1, wide, width))
     return pl.pallas_call(
         step_kernel,
         out_shape=[
             jax.ShapeDtypeStruct((width, width), BF16),
             jax.ShapeDtypeStruct(panel.shape, F32),
         ],
-        in_specs=[VMEM] * 5,
+        in_specs=[VMEM, VMEM, VMEM, VMEM, right, right],
         out_specs=[VMEM, VMEM],
-        compiler_params=PARAMS,
-        cost_estimate=pl.CostEstimate(flops=2 * width**3, bytes_accessed=6 * width**2, transcendentals=0),
-    )(panel, *blocks)
+        grid=(1,),
+        compiler_params=PARAMS,
+        cost_estimate=cost,
+    )(panel, part, b, c, a, d)
 
 
 def product_kernel(core, own, got, bias, bias_got, product, odd, add_even):
@@ -236,21 +286,20 @@
     col = lax.broadcasted_iota(jnp.int32, cells.shape, 1)
     keep = jnp.abs(row - col - band_offset[0]) <= HALF
     pair = jnp.stack([g_rows, jnp.where(keep, cells, jnp.zeros_like(cells))])
-    panel = mm(corner, arrow[0]).astype(BF16)
-    panel_rows = lax.all_to_all(panel.reshape(lat_count, share, share), "lat", 0, 0)
+    panel = mm(corner, arrow[0]).astype(BF16).reshape(lat_count, 2, share // 2, share)
+    panel = jnp.swapaxes(panel, 1, 2).reshape(lat_count, share // 2, 2 * share)
+    panel_rows = lax.all_to_all(panel, "lat", 0, 0)
     everyone = range(depth_count)
     first = pack(ring_gather(pair, everyone, False))
     blocks = ring_gather(first, everyone, True)
-    panel_cut = jnp.concatenate(
-        [lax.dynamic_index_in_dim(panel_rows, q, 0, False) for q in order], axis=1
-    )
-    step, bias = step_terms(panel_cut, blocks)
+    order = jnp.stack(order)
+    step, bias = step_terms(order, panel_rows, blocks)
     swap = [(d, d ^ 1) for d in range(depth_count)]
     got = lax.ppermute(step, "depth", swap)
     bias_got = lax.ppermute(bias, "depth", [(2 * k, 2 * k + 1) for k in range(chips)])
     product, step_odd, add_even = products(core, step, got, bias, bias_got)
     add_odd = jnp.where(low, jnp.zeros_like(bias), bias)
-    lower = (chips * 5) // 16
+    lower = (chips * 6) // 16
     tops = [chips - 1, lower - 1]
     sizes = [chips - lower, lower]
     start = (row == col) & ((chip == tops[0]) | (chip == tops[1])) & low
@@ -277,7 +326,7 @@
     relayed = sent_down(entry, [(near, near - 1), (far, far - 1)])
     last = [(source, source - 2) for source, low_end in ((near, far), (far, -1)) if source - 2 > low_end]
     last = sent_down(entry, last)
-    maps = place(jnp.stack(order), ring_gather(ring, depths, True))
+    maps = place(order, ring_gather(ring, depths, True))
     below = chip < lower
     flags = jnp.stack([low, below]).astype(jnp.int32)
     entry = settled(flags, entry, relayed, last, edge)

time: 160 us -> 155 us (0.969)
  waiting for transfers between devices: 59.8 us -> 51.7 us
  local copies, waits for them, and re-layouts: 3.17 us -> 5.96 us
    ppermute x4, waiting for transfers between devices: 12 us -> 5.02 us  [sent_down(): lax.ppermute(value, 'depth', [(2 * a + 1, 2 * b + 1) for a, b in chip_pai...]
    all_to_all x1, waiting for transfers between devices: 14.3 us -> 8.64 us  [body(): panel_rows = lax.all_to_all(panel, 'lat', 0, 0)]
    ppermute x10 -> x9, waiting for transfers between devices: 19.5 us -> 24.1 us  [body(): v_in = v_in + lax.ppermute(v_even.astype(BF16), 'depth', pairs)]
    pallas_call x0 -> x2, Pallas kernels: none -> 3.12 us  [the longest x1 2.48 us: step_terms(): pl.pallas_call(part_kernel, out_shape=[jax.ShapeDtypeStruct((width, width...]
    unnamed x14 -> x12, local copies, waits for them, and re-layouts: 1.13 us -> 2.95 us
    reshape x1, local copies, waits for them, and re-layouts: 0.17 us -> 1.8 us  [body(): panel = jnp.swapaxes(panel, 1, 2).reshape(lat_count, share // 2, 2 * share)]
    ppermute x10 -> x9, starting transfers between devices: 7.49 us -> 6.82 us  [body(): v_in = v_in + lax.ppermute(v_even.astype(BF16), 'depth', pairs)]
    dot_general x13 -> x12, matrix products: 6.87 us -> 6.37 us  [mm(): return jnp.dot(a, b, preferred_element_type=F32)]
  transfers between devices with their start and end apart: 31 -> 30, of which waited for: 10 -> 10; matrix products, arithmetic and copies ran while one was open for 2% -> 2% of each run, Pallas kernels for 2% -> 4%
where the time goes in v7:
time: 155 us; the launch traced here: 154 us
  starting transfers between devices  68.2 us (44%)
  waiting for transfers between devices  51.7 us (33%)
  Pallas kernels  17.5 us (11%)
  matrix products  6.37 us (4%)
  local copies, waits for them, and re-layouts  5.96 us (4%)
  other arithmetic  2.48 us (2%)
  between operations  1.65 us (1%)
    ppermute x12, starting transfers between devices, ring_gather(): lax.ppermute(value, BOTH, ring_moves(depths, flipped, shift))  38.1 us
    ppermute x9, waiting for transfers between devices, body(): v_in = v_in + lax.ppermute(v_even.astype(BF16), 'depth', pairs)  24.1 us
    ppermute x12, waiting for transfers between devices, ring_gather(): lax.ppermute(value, BOTH, ring_moves(depths, flipped, shift))  10.1 us
    all_to_all x1, waiting for transfers between devices, body(): panel_rows = lax.all_to_all(panel, 'lat', 0, 0)  8.64 us
    ppermute x1, starting transfers between devices, body(): got = lax.ppermute(step, 'depth', swap)  7.03 us
    ppermute x9, starting transfers between devices, body(): v_in = v_in + lax.ppermute(v_even.astype(BF16), 'depth', pairs)  6.82 us
    dot_general x12, matrix products, mm(): return jnp.dot(a, b, preferred_element_type=F32)  6.37 us
    ppermute x1, starting transfers between devices, body(): lax.ppermute(jnp.where(low, v_odd.astype(BF16), edge), 'depth', swap[:2 *...  5.97 us
  transfers between devices with their start and end apart: 30, of which 10 were waited for; matrix products, arithmetic and copies ran while one was open for 2% of the time, Pallas kernels for 4%

profile of v7, /device:TPU:1, one launch (start us, length us, event | category | flops | bytes accessed | tf_op | source)
XLA Modules:
  0.0 153.9 jit_solution(12697482914477487294)
XLA Ops:
  0.8 1.1 fusion.14
  1.9 0.9 pad_maximum_fusion.1.a
  2.8 5.7 %collective-permute-start.2 = (bf16[2,64,1024]{2,1,0:T(8,128)(2,1)S(1)}, bf16[2,64,1024]{2,1,0:T(8,128)(2,1)S(1)}, u32[]{:S(2)}, u32[]{:S(2)}) collective-permute-start(bf16[2,64,1024]{2,1,0:T(8,128)(2,1)S(1)} %pad_maximum_fusion.1.a), channel_id=1, source_target_pairs={{0,2},{1,3},{2,0},{3,1},{4,6},{5,7},{6,4},{7,5},{8,10},{9,11},{10,... | collective-permute-start | bytes 786440 | tf_op jit(solution)/shard_map/ppermute | solution.py:41
  8.5 2.7 %collective-permute-start.1 = (bf16[2,64,1024]{2,1,0:T(8,128)(2,1)S(1)}, bf16[2,64,1024]{2,1,0:T(8,128)(2,1)S(1)}, u32[]{:S(2)}, u32[]{:S(2)}) collective-permute-start(bf16[2,64,1024]{2,1,0:T(8,128)(2,1)S(1)} %pad_maximum_fusion.1.a), channel_id=1, source_target_pairs={{0,3},{1,0},{2,1},{3,2},{4,7},{5,4},{6,5},{7,6},{8,11},{9,8},{10,9... | collective-permute-start | bytes 786440 | tf_op jit(solution)/shard_map/ppermute | solution.py:41
  11.2 2.6 %collective-permute-start = (bf16[2,64,1024]{2,1,0:T(8,128)(2,1)S(1)}, bf16[2,64,1024]{2,1,0:T(8,128)(2,1)S(1)}, u32[]{:S(2)}, u32[]{:S(2)}) collective-permute-start(bf16[2,64,1024]{2,1,0:T(8,128)(2,1)S(1)} %pad_maximum_fusion.1.a), channel_id=1, source_target_pairs={{0,1},{1,2},{2,3},{3,0},{4,5},{5,6},{6,7},{7,4},{8,9},{9,10},{10,1... | collective-permute-start | bytes 786440 | tf_op jit(solution)/shard_map/ppermute | solution.py:41
  13.8 1.8 %collective-permute-done.1.c = bf16[2,64,1024]{2,1,0:T(8,128)(2,1)S(1)} collective-permute-done((bf16[2,64,1024]{2,1,0:T(8,128)(2,1)S(1)}, bf16[2,64,1024]{2,1,0:T(8,128)(2,1)S(1)}, u32[]{:S(2)}, u32[]{:S(2)}) %collective-permute-start.1) | collective-permute-done | bytes 262176 | tf_op jit(solution)/shard_map/ppermute | solution.py:41
  15.6 3.9 %collective-permute-done.b = bf16[2,64,1024]{2,1,0:T(8,128)(2,1)S(1)} collective-permute-done((bf16[2,64,1024]{2,1,0:T(8,128)(2,1)S(1)}, bf16[2,64,1024]{2,1,0:T(8,128)(2,1)S(1)}, u32[]{:S(2)}, u32[]{:S(2)}) %collective-permute-start) | collective-permute-done | bytes 262176 | tf_op jit(solution)/shard_map/ppermute | solution.py:41
  19.7 4.7 %collective-permute-start.3 = (bf16[2,256,1024]{2,1,0:T(8,128)(2,1)S(1)}, bf16[2,256,1024]{2,1,0:T(8,128)(2,1)}, u32[]{:S(2)}, u32[]{:S(2)}) collective-permute-start(bf16[2,256,1024]{2,1,0:T(8,128)(2,1)S(1)} %shard_map.55.a.a_right), channel_id=1, source_target_pairs={{0,8},{1,9},{2,10},{3,11},{4,12},{5,13},{6,14},{7,15},{8,0},{9,1},... | collective-permute-start | bytes 3145736 | tf_op jit(solution)/shard_map/ppermute | solution.py:41
  24.4 2.8 %collective-permute-start.5 = (bf16[2,256,1024]{2,1,0:T(8,128)(2,1)S(1)}, bf16[2,256,1024]{2,1,0:T(8,128)(2,1)}, u32[]{:S(2)}, u32[]{:S(2)}) collective-permute-start(bf16[2,256,1024]{2,1,0:T(8,128)(2,1)S(1)} %shard_map.55.a.a_right), channel_id=1, source_target_pairs={{0,12},{1,13},{2,14},{3,15},{4,0},{5,1},{6,2},{7,3},{8,4},{9,5},{1... | collective-permute-start | bytes 3145736 | tf_op jit(solution)/shard_map/ppermute | solution.py:41
  27.1 2.5 %collective-permute-start.4 = (bf16[2,256,1024]{2,1,0:T(8,128)(2,1)S(1)}, bf16[2,256,1024]{2,1,0:T(8,128)(2,1)}, u32[]{:S(2)}, u32[]{:S(2)}) collective-permute-start(bf16[2,256,1024]{2,1,0:T(8,128)(2,1)S(1)} %shard_map.55.a.a_right), channel_id=1, source_target_pairs={{0,4},{1,5},{2,6},{3,7},{4,8},{5,9},{6,10},{7,11},{8,12},{9,13},{1... | collective-permute-start | bytes 3145736 | tf_op jit(solution)/shard_map/ppermute | solution.py:41
  29.7 0.8 convolution_convert_fusion
  30.6 0.9 copy.8
  31.6 1.8 %reshape.11 = bf16[16,32,128]{2,1,0:T(8,128)(2,1)} reshape(bf16[16,32,2,64]{3,2,1,0:T(2,128)(2,1)} %copy.8) | data formatting | bytes 262144 | tf_op jit(solution)/shard_map/reshape | solution.py:290
  33.4 3.7 %all-to-all-start = ((bf16[16,32,128]{2,1,0:T(8,128)(2,1)}), bf16[16,32,128]{2,1,0:T(8,128)(2,1)S(1)}, u32[]{:S(2)}, u32[]{:S(2)}) async-start(bf16[16,32,128]{2,1,0:T(8,128)(2,1)} %reshape.11), calls=%async_computation | async-start | bytes 262144 | tf_op jit(solution)/shard_map/all_to_all | solution.py:291
  37.3 2.5 %shard_map.56 = (bf16[1024,1024]{1,0:T(8,128)(2,1)S(1)}, f32[8,128]{1,0:T(8,128)S(1)}) custom-call(bf16[2,256,1024]{2,1,0:T(8,128)(2,1)S(1)} %shard_map.55.a.a_right, bf16[2,256,1024]{2,1,0:T(8,128)(2,1)} %collective-permute-done.3.d.d_right), custom_call_target="tpu_custom_call" | custom-call | flops 1073741824 | bytes 6291456 | tf_op jit(solution)/shard_map/pallas_call | solution.py:129
  39.8 1.3 copy-done.1
  41.2 8.6 %all-to-all-done.panel = bf16[16,32,128]{2,1,0:T(8,128)(2,1)S(1)} async-done(((bf16[16,32,128]{2,1,0:T(8,128)(2,1)}), bf16[16,32,128]{2,1,0:T(8,128)(2,1)S(1)}, u32[]{:S(2)}, u32[]{:S(2)}) %all-to-all-start) | async-done | bytes 131104 | tf_op jit(solution)/shard_map/all_to_all | solution.py:291
  49.8 0.6 shard_map.57.panel
  50.5 1.6 %copy-done.2 = bf16[1024,1024]{1,0:T(8,128)(2,1)S(1)} copy-done((bf16[1024,1024]{1,0:T(8,128)(2,1)S(1)}, bf16[1024,1024]{1,0:T(8,128)(2,1)}, u32[]{:S(2)}) %copy-start.2) | copy-done | bytes 2097176
  52.1 4.5 %shard_map.58 = (bf16[1024,1024]{1,0:T(8,128)(2,1)}, f32[64,1024]{1,0:T(8,128)S(1)}) custom-call(bf16[64,1024]{1,0:T(8,128)(2,1)S(1)} %shard_map.57.panel, bf16[1024,1024]{1,0:T(8,128)(2,1)S(1)} %copy-done.2, bf16[2,256,1024]{2,1,0:T(8,128)(2,1)} %collective-permute-done.4.b, bf16[2,256,1024]{2,1,0:T(8,128)(2,1)} %collective-permute-done.5.c, ...), custom_call_target="tpu_custom_call" | custom-call | flops 1073741824 | bytes 6291456 | tf_op jit(solution)/shard_map/pallas_call | solution.py:152
  56.6 7.0 %collective-permute-start.6 = (bf16[1024,1024]{1,0:T(8,128)(2,1)}, bf16[1024,1024]{1,0:T(8,128)(2,1)}, u32[]{:S(2)}, u32[]{:S(2)}) collective-permute-start(bf16[1024,1024]{1,0:T(8,128)(2,1)} %get-tuple-element.14.own), channel_id=1, source_target_pairs={{0,16},{16,0},{32,48},{48,32},{64,80},{80,64},{96,112},{112,96},{1... | collective-permute-start | bytes 6291464 | tf_op jit(solution)/shard_map/ppermute | solution.py:298
  63.6 1.3 collective-permute-start.7
  64.9 2.7 %collective-permute-done.7.bias_got = f32[64,1024]{1,0:T(8,128)S(1)} collective-permute-done((f32[64,1024]{1,0:T(8,128)S(1)}, f32[64,1024]{1,0:T(8,128)S(1)}, u32[]{:S(2)}, u32[]{:S(2)}) %collective-permute-start.7) | collective-permute-done | bytes 262176 | tf_op jit(solution)/shard_map/ppermute | solution.py:299
  67.7 4.9 %shard_map.59 = (bf16[1024,1024]{1,0:T(8,128)(2,1)S(1)}, bf16[1024,1024]{1,0:T(8,128)(2,1)S(1)}, f32[64,1024]{1,0:T(8,128)S(1)}) custom-call(s32[1]{0:T(128)} %bitcast.18.core, bf16[1024,1024]{1,0:T(8,128)(2,1)} %get-tuple-element.14.own, bf16[1024,1024]{1,0:T(8,128)(2,1)} %collective-permute-done.6.got, f32[64,1024]{1,0:T(8,128)S(1)} %get-tuple-element.15.bias, ...), custom_call_target="tpu_custom_call" | custom-call | flops 2147483648 | bytes 6291456 | tf_op jit(solution)/shard_map/pallas_call | solution.py:189
  72.6 0.5 fusion
  73.2 0.7 collective-permute-start.8
  73.8 0.6 fusion.1
  74.4 0.7 collective-permute-start.9
  75.1 0.6 fusion.2
  75.7 0.7 collective-permute-start.10
  76.5 0.5 fusion.3
  77.0 0.7 collective-permute-start.11
  77.8 0.5 fusion.4
  78.3 1.3 collective-permute-start.12
  79.6 24.1 %collective-permute-done.12 = bf16[64,1024]{1,0:T(8,128)(2,1)S(1)} collective-permute-done((bf16[64,1024]{1,0:T(8,128)(2,1)S(1)}, bf16[64,1024]{1,0:T(8,128)(2,1)S(1)}, u32[]{:S(2)}, u32[]{:S(2)}) %collective-permute-start.12) | collective-permute-done | bytes 131104 | tf_op jit(solution)/shard_map/ppermute | solution.py:314
  103.7 0.5 fusion.5
  104.2 0.7 collective-permute-start.13
  104.9 0.5 fusion.6
  105.4 0.8 collective-permute-start.14
  106.3 0.5 fusion.7
  106.8 0.7 collective-permute-start.15
  107.6 0.5 fusion.8
  108.1 0.7 collective-permute-start.16
  108.7 0.5 convolution_add_fusion.v_odd
  109.3 0.5 convert_select_fusion
  109.8 6.0 %collective-permute-start.17 = (bf16[64,1024]{1,0:T(8,128)(2,1)S(1)}, bf16[64,1024]{1,0:T(8,128)(2,1)S(1)}, u32[]{:S(2)}, u32[]{:S(2)}) collective-permute-start(bf16[64,1024]{1,0:T(8,128)(2,1)S(1)} %get-tuple-element.19), channel_id=1, source_target_pairs={{0,16},{16,0},{32,48},{48,32},{64,80},{80,64},{96,112},{112,96},{1... | collective-permute-start | bytes 393224 | tf_op jit(solution)/shard_map/ppermute | solution.py:318
  115.7 1.0 collective-permute-done.17.other
  116.7 4.5 %collective-permute-start.20 = (bf16[64,1024]{1,0:T(8,128)(2,1)S(1)}, bf16[64,1024]{1,0:T(8,128)(2,1)S(1)}, u32[]{:S(2)}, u32[]{:S(2)}) collective-permute-start(bf16[64,1024]{1,0:T(8,128)(2,1)S(1)} %broadcast_select_fusion), channel_id=1, source_target_pairs={{0,2},{1,3},{2,0},{3,1},{4,6},{5,7},{6,4},{7,5},{8,10},{9,11},{10,... | collective-permute-start | bytes 393224 | tf_op jit(solution)/shard_map/ppermute | solution.py:41
  121.2 2.7 %collective-permute-start.19 = (bf16[64,1024]{1,0:T(8,128)(2,1)S(1)}, bf16[64,1024]{1,0:T(8,128)(2,1)S(1)}, u32[]{:S(2)}, u32[]{:S(2)}) collective-permute-start(bf16[64,1024]{1,0:T(8,128)(2,1)S(1)} %broadcast_select_fusion), channel_id=1, source_target_pairs={{0,3},{1,0},{2,1},{3,2},{4,7},{5,4},{6,5},{7,6},{8,11},{9,8},{10,9... | collective-permute-start | bytes 393224 | tf_op jit(solution)/shard_map/ppermute | solution.py:41
  124.0 2.6 %collective-permute-start.18 = (bf16[64,1024]{1,0:T(8,128)(2,1)S(1)}, bf16[64,1024]{1,0:T(8,128)(2,1)S(1)}, u32[]{:S(2)}, u32[]{:S(2)}) collective-permute-start(bf16[64,1024]{1,0:T(8,128)(2,1)S(1)} %broadcast_select_fusion), channel_id=1, source_target_pairs={{0,1},{1,2},{2,3},{3,0},{4,5},{5,6},{6,7},{7,4},{8,9},{9,10},{10,1... | collective-permute-start | bytes 393224 | tf_op jit(solution)/shard_map/ppermute | solution.py:41
  126.9 4.0 %collective-permute-done.18 = bf16[64,1024]{1,0:T(8,128)(2,1)S(1)} collective-permute-done((bf16[64,1024]{1,0:T(8,128)(2,1)S(1)}, bf16[64,1024]{1,0:T(8,128)(2,1)S(1)}, u32[]{:S(2)}, u32[]{:S(2)}) %collective-permute-start.18) | collective-permute-done | bytes 131104 | tf_op jit(solution)/shard_map/ppermute | solution.py:41
  131.0 1.9 %collective-permute-start.23 = (bf16[256,1024]{1,0:T(8,128)(2,1)S(1)}, bf16[256,1024]{1,0:T(8,128)(2,1)S(1)}, u32[]{:S(2)}, u32[]{:S(2)}) collective-permute-start(bf16[256,1024]{1,0:T(8,128)(2,1)S(1)} %pad_maximum_fusion.a.ready), channel_id=1, source_target_pairs={{0,8},{1,9},{2,10},{3,11},{4,12},{5,13},{6,14},{7,15},{8,0},{9,1},... | collective-permute-start | bytes 1572872 | tf_op jit(solution)/shard_map/ppermute | solution.py:41
  132.9 3.6 %collective-permute-start.22 = (bf16[256,1024]{1,0:T(8,128)(2,1)S(1)}, bf16[256,1024]{1,0:T(8,128)(2,1)}, u32[]{:S(2)}, u32[]{:S(2)}) collective-permute-start(bf16[256,1024]{1,0:T(8,128)(2,1)S(1)} %pad_maximum_fusion.a.ready), channel_id=1, source_target_pairs={{0,12},{1,13},{2,14},{3,15},{4,0},{5,1},{6,2},{7,3},{8,4},{9,5},{1... | collective-permute-start | bytes 1572872 | tf_op jit(solution)/shard_map/ppermute | solution.py:41
  136.5 1.9 %collective-permute-start.21 = (bf16[256,1024]{1,0:T(8,128)(2,1)S(1)}, bf16[256,1024]{1,0:T(8,128)(2,1)}, u32[]{:S(2)}, u32[]{:S(2)}) collective-permute-start(bf16[256,1024]{1,0:T(8,128)(2,1)S(1)} %pad_maximum_fusion.a.ready), channel_id=1, source_target_pairs={{0,4},{1,5},{2,6},{3,7},{4,8},{5,9},{6,10},{7,11},{8,12},{9,13},{1... | collective-permute-start | bytes 1572872 | tf_op jit(solution)/shard_map/ppermute | solution.py:41
  138.5 0.7 collective-permute-start.25
  139.2 0.7 collective-permute-start.24
  139.8 0.7 shard_map.61.entry
  140.5 1.3 collective-permute-start.27
  141.8 1.3 collective-permute-start.26
  143.2 5.0 %collective-permute-done.27.last = bf16[64,1024]{1,0:T(8,128)(2,1)} collective-permute-done((bf16[64,1024]{1,0:T(8,128)(2,1)}, bf16[64,1024]{1,0:T(8,128)(2,1)}, u32[]{:S(2)}, u32[]{:S(2)}) %collective-permute-start.27) | collective-permute-done | bytes 131104 | tf_op jit(solution)/shard_map/ppermute | solution.py:47
  148.2 1.1 shard_map.62.entry
  149.3 1.4 collective-permute-start.28
  150.8 1.4 shard_map.60.maps
  152.2 1.7 %shard_map.63 = f32[64,1024]{1,0:T(8,128)} custom-call(s32[2]{0:T(128)S(1)} %add_convert_fusion.flags, bf16[1024,1024]{1,0:T(8,128)(2,1)S(1)} %shard_map.60.maps, bf16[64,1024]{1,0:T(8,128)(2,1)S(1)} %shard_map.62.entry, bf16[64,1024]{1,0:T(8,128)(2,1)S(1)} %collective-permute-done.28.across, bf16[64,1024]{1,0:T(8,128)(2,1)S(1)} %copy-done.4, ...), custom_call_target="tpu_custom_call" | custom-call | tf_op jit(solution)/shard_map/pallas_call | solution.py:258
  (45 shorter events, 1.5 us)
Async XLA Ops:
  0.0 29.7 %copy-start = (bf16[1024,1024]{1,0:T(8,128)(2,1)S(1)}, bf16[1024,1024]{1,0:T(8,128)(2,1)}, u32[]{:S(2)}) copy-start(bf16[1024,1024]{1,0:T(8,128)(2,1)} %param.8) | copy-start | bytes 6291460
  0.0 29.7 %copy-start.5 = (bf16[1,1024,64]{1,2,0:T(8,128)(2,1)S(1)}, bf16[1,1024,64]{1,2,0:T(8,128)(2,1)}, u32[]{:S(2)}) copy-start(bf16[1,1024,64]{1,2,0:T(8,128)(2,1)} %param.7) | copy-start | bytes 393220
  2.8 11.0 %collective-permute-start.2 = (bf16[2,64,1024]{2,1,0:T(8,128)(2,1)S(1)}, bf16[2,64,1024]{2,1,0:T(8,128)(2,1)S(1)}, u32[]{:S(2)}, u32[]{:S(2)}) collective-permute-start(bf16[2,64,1024]{2,1,0:T(8,128)(2,1)S(1)} %pad_maximum_fusion.1.a), channel_id=1, source_target_pairs={{0,2},{1,3},{2,0},{3,1},{4,6},{5,7},{6,4},{7,5},{8,10},{9,11},{10,... | collective-permute-start | bytes 786440 | tf_op jit(solution)/shard_map/ppermute | solution.py:41
  8.5 7.1 %collective-permute-start.1 = (bf16[2,64,1024]{2,1,0:T(8,128)(2,1)S(1)}, bf16[2,64,1024]{2,1,0:T(8,128)(2,1)S(1)}, u32[]{:S(2)}, u32[]{:S(2)}) collective-permute-start(bf16[2,64,1024]{2,1,0:T(8,128)(2,1)S(1)} %pad_maximum_fusion.1.a), channel_id=1, source_target_pairs={{0,3},{1,0},{2,1},{3,2},{4,7},{5,4},{6,5},{7,6},{8,11},{9,8},{10,9... | collective-permute-start | bytes 786440 | tf_op jit(solution)/shard_map/ppermute | solution.py:41
  11.2 8.3 %collective-permute-start = (bf16[2,64,1024]{2,1,0:T(8,128)(2,1)S(1)}, bf16[2,64,1024]{2,1,0:T(8,128)(2,1)S(1)}, u32[]{:S(2)}, u32[]{:S(2)}) collective-permute-start(bf16[2,64,1024]{2,1,0:T(8,128)(2,1)S(1)} %pad_maximum_fusion.1.a), channel_id=1, source_target_pairs={{0,1},{1,2},{2,3},{3,0},{4,5},{5,6},{6,7},{7,4},{8,9},{9,10},{10,1... | collective-permute-start | bytes 786440 | tf_op jit(solution)/shard_map/ppermute | solution.py:41
  19.7 17.6 %collective-permute-start.3 = (bf16[2,256,1024]{2,1,0:T(8,128)(2,1)S(1)}, bf16[2,256,1024]{2,1,0:T(8,128)(2,1)}, u32[]{:S(2)}, u32[]{:S(2)}) collective-permute-start(bf16[2,256,1024]{2,1,0:T(8,128)(2,1)S(1)} %shard_map.55.a.a_right), channel_id=1, source_target_pairs={{0,8},{1,9},{2,10},{3,11},{4,12},{5,13},{6,14},{7,15},{8,0},{9,1},... | collective-permute-start | bytes 3145736 | tf_op jit(solution)/shard_map/ppermute | solution.py:41
  24.4 26.1 %collective-permute-start.5 = (bf16[2,256,1024]{2,1,0:T(8,128)(2,1)S(1)}, bf16[2,256,1024]{2,1,0:T(8,128)(2,1)}, u32[]{:S(2)}, u32[]{:S(2)}) collective-permute-start(bf16[2,256,1024]{2,1,0:T(8,128)(2,1)S(1)} %shard_map.55.a.a_right), channel_id=1, source_target_pairs={{0,12},{1,13},{2,14},{3,15},{4,0},{5,1},{6,2},{7,3},{8,4},{9,5},{1... | collective-permute-start | bytes 3145736 | tf_op jit(solution)/shard_map/ppermute | solution.py:41
  27.1 23.4 %collective-permute-start.4 = (bf16[2,256,1024]{2,1,0:T(8,128)(2,1)S(1)}, bf16[2,256,1024]{2,1,0:T(8,128)(2,1)}, u32[]{:S(2)}, u32[]{:S(2)}) collective-permute-start(bf16[2,256,1024]{2,1,0:T(8,128)(2,1)S(1)} %shard_map.55.a.a_right), channel_id=1, source_target_pairs={{0,4},{1,5},{2,6},{3,7},{4,8},{5,9},{6,10},{7,11},{8,12},{9,13},{1... | collective-permute-start | bytes 3145736 | tf_op jit(solution)/shard_map/ppermute | solution.py:41
  33.4 16.5 %all-to-all-start = ((bf16[16,32,128]{2,1,0:T(8,128)(2,1)}), bf16[16,32,128]{2,1,0:T(8,128)(2,1)S(1)}, u32[]{:S(2)}, u32[]{:S(2)}) async-start(bf16[16,32,128]{2,1,0:T(8,128)(2,1)} %reshape.11), calls=%async_computation | async-start | bytes 262144 | tf_op jit(solution)/shard_map/all_to_all | solution.py:291
  39.8 1.4 copy-start.1
  50.5 1.6 %copy-start.2 = (bf16[1024,1024]{1,0:T(8,128)(2,1)S(1)}, bf16[1024,1024]{1,0:T(8,128)(2,1)}, u32[]{:S(2)}) copy-start(bf16[1024,1024]{1,0:T(8,128)(2,1)} %copy-done.1) | copy-start | bytes 6291460
  56.6 11.1 %collective-permute-start.6 = (bf16[1024,1024]{1,0:T(8,128)(2,1)}, bf16[1024,1024]{1,0:T(8,128)(2,1)}, u32[]{:S(2)}, u32[]{:S(2)}) collective-permute-start(bf16[1024,1024]{1,0:T(8,128)(2,1)} %get-tuple-element.14.own), channel_id=1, source_target_pairs={{0,16},{16,0},{32,48},{48,32},{64,80},{80,64},{96,112},{112,96},{1... | collective-permute-start | bytes 6291464 | tf_op jit(solution)/shard_map/ppermute | solution.py:298
  63.6 4.0 %collective-permute-start.7 = (f32[64,1024]{1,0:T(8,128)S(1)}, f32[64,1024]{1,0:T(8,128)S(1)}, u32[]{:S(2)}, u32[]{:S(2)}) collective-permute-start(f32[64,1024]{1,0:T(8,128)S(1)} %get-tuple-element.15.bias), channel_id=1, source_target_pairs={{0,16},{32,48},{64,80},{96,112},{128,144},{160,176},{192,208},{224... | collective-permute-start | bytes 786440 | tf_op jit(solution)/shard_map/ppermute | solution.py:299
  73.2 0.7 collective-permute-start.8
  74.4 0.7 collective-permute-start.9
  75.7 0.7 collective-permute-start.10
  77.0 0.7 collective-permute-start.11
  78.3 25.4 %collective-permute-start.12 = (bf16[64,1024]{1,0:T(8,128)(2,1)S(1)}, bf16[64,1024]{1,0:T(8,128)(2,1)S(1)}, u32[]{:S(2)}, u32[]{:S(2)}) collective-permute-start(bf16[64,1024]{1,0:T(8,128)(2,1)S(1)} %fusion.4), channel_id=1, source_target_pairs={{368,336},{32,0},{48,16},{369,337},{33,1},{49,17},{370,338},{34,2}... | collective-permute-start | bytes 393224 | tf_op jit(solution)/shard_map/ppermute | solution.py:314
  104.2 0.7 collective-permute-start.13
  105.4 0.9 collective-permute-start.14
  106.8 0.7 collective-permute-start.15
  108.1 0.7 collective-permute-start.16
  109.8 6.9 %collective-permute-start.17 = (bf16[64,1024]{1,0:T(8,128)(2,1)S(1)}, bf16[64,1024]{1,0:T(8,128)(2,1)S(1)}, u32[]{:S(2)}, u32[]{:S(2)}) collective-permute-start(bf16[64,1024]{1,0:T(8,128)(2,1)S(1)} %get-tuple-element.19), channel_id=1, source_target_pairs={{0,16},{16,0},{32,48},{48,32},{64,80},{80,64},{96,112},{112,96},{1... | collective-permute-start | bytes 393224 | tf_op jit(solution)/shard_map/ppermute | solution.py:318
  116.7 10.2 %copy-start.3 = (bf16[64,1024]{1,0:T(8,128)(2,1)}, bf16[64,1024]{1,0:T(8,128)(2,1)S(1)}, u32[]{:S(2)}) copy-start(bf16[64,1024]{1,0:T(8,128)(2,1)S(1)} %collective-permute-done.17.other) | copy-start | bytes 393220
  116.7 9.8 %collective-permute-start.20 = (bf16[64,1024]{1,0:T(8,128)(2,1)S(1)}, bf16[64,1024]{1,0:T(8,128)(2,1)S(1)}, u32[]{:S(2)}, u32[]{:S(2)}) collective-permute-start(bf16[64,1024]{1,0:T(8,128)(2,1)S(1)} %broadcast_select_fusion), channel_id=1, source_target_pairs={{0,2},{1,3},{2,0},{3,1},{4,6},{5,7},{6,4},{7,5},{8,10},{9,11},{10,... | collective-permute-start | bytes 393224 | tf_op jit(solution)/shard_map/ppermute | solution.py:41
  121.2 5.7 %collective-permute-start.19 = (bf16[64,1024]{1,0:T(8,128)(2,1)S(1)}, bf16[64,1024]{1,0:T(8,128)(2,1)S(1)}, u32[]{:S(2)}, u32[]{:S(2)}) collective-permute-start(bf16[64,1024]{1,0:T(8,128)(2,1)S(1)} %broadcast_select_fusion), channel_id=1, source_target_pairs={{0,3},{1,0},{2,1},{3,2},{4,7},{5,4},{6,5},{7,6},{8,11},{9,8},{10,9... | collective-permute-start | bytes 393224 | tf_op jit(solution)/shard_map/ppermute | solution.py:41
  124.0 7.0 %collective-permute-start.18 = (bf16[64,1024]{1,0:T(8,128)(2,1)S(1)}, bf16[64,1024]{1,0:T(8,128)(2,1)S(1)}, u32[]{:S(2)}, u32[]{:S(2)}) collective-permute-start(bf16[64,1024]{1,0:T(8,128)(2,1)S(1)} %broadcast_select_fusion), channel_id=1, source_target_pairs={{0,1},{1,2},{2,3},{3,0},{4,5},{5,6},{6,7},{7,4},{8,9},{9,10},{10,1... | collective-permute-start | bytes 393224 | tf_op jit(solution)/shard_map/ppermute | solution.py:41
  131.0 19.8 %collective-permute-start.23 = (bf16[256,1024]{1,0:T(8,128)(2,1)S(1)}, bf16[256,1024]{1,0:T(8,128)(2,1)S(1)}, u32[]{:S(2)}, u32[]{:S(2)}) collective-permute-start(bf16[256,1024]{1,0:T(8,128)(2,1)S(1)} %pad_maximum_fusion.a.ready), channel_id=1, source_target_pairs={{0,8},{1,9},{2,10},{3,11},{4,12},{5,13},{6,14},{7,15},{8,0},{9,1},... | collective-permute-start | bytes 1572872 | tf_op jit(solution)/shard_map/ppermute | solution.py:41
  132.9 17.8 %collective-permute-start.22 = (bf16[256,1024]{1,0:T(8,128)(2,1)S(1)}, bf16[256,1024]{1,0:T(8,128)(2,1)}, u32[]{:S(2)}, u32[]{:S(2)}) collective-permute-start(bf16[256,1024]{1,0:T(8,128)(2,1)S(1)} %pad_maximum_fusion.a.ready), channel_id=1, source_target_pairs={{0,12},{1,13},{2,14},{3,15},{4,0},{5,1},{6,2},{7,3},{8,4},{9,5},{1... | collective-permute-start | bytes 1572872 | tf_op jit(solution)/shard_map/ppermute | solution.py:41
  136.5 14.2 %collective-permute-start.21 = (bf16[256,1024]{1,0:T(8,128)(2,1)S(1)}, bf16[256,1024]{1,0:T(8,128)(2,1)}, u32[]{:S(2)}, u32[]{:S(2)}) collective-permute-start(bf16[256,1024]{1,0:T(8,128)(2,1)S(1)} %pad_maximum_fusion.a.ready), channel_id=1, source_target_pairs={{0,4},{1,5},{2,6},{3,7},{4,8},{5,9},{6,10},{7,11},{8,12},{9,13},{1... | collective-permute-start | bytes 1572872 | tf_op jit(solution)/shard_map/ppermute | solution.py:41
  138.5 1.4 collective-permute-start.25
  139.2 0.7 collective-permute-start.24
  140.5 7.7 %collective-permute-start.27 = (bf16[64,1024]{1,0:T(8,128)(2,1)}, bf16[64,1024]{1,0:T(8,128)(2,1)}, u32[]{:S(2)}, u32[]{:S(2)}) collective-permute-start(bf16[64,1024]{1,0:T(8,128)(2,1)} %shard_map.61.entry), channel_id=1, source_target_pairs={{176,112},{80,16},{177,113},{81,17},{178,114},{82,18},{179,115},{8... | collective-permute-start | bytes 393224 | tf_op jit(solution)/shard_map/ppermute | solution.py:47
  141.8 6.4 %collective-permute-start.26 = (bf16[64,1024]{1,0:T(8,128)(2,1)}, bf16[64,1024]{1,0:T(8,128)(2,1)}, u32[]{:S(2)}, u32[]{:S(2)}) collective-permute-start(bf16[64,1024]{1,0:T(8,128)(2,1)} %shard_map.61.entry), channel_id=1, source_target_pairs={{176,144},{80,48},{177,145},{81,49},{178,146},{82,50},{179,147},{8... | collective-permute-start | bytes 393224 | tf_op jit(solution)/shard_map/ppermute | solution.py:47
  149.3 2.9 %copy-start.4 = (bf16[64,1024]{1,0:T(8,128)(2,1)S(1)}, bf16[64,1024]{1,0:T(8,128)(2,1)}, u32[]{:S(2)}) copy-start(bf16[64,1024]{1,0:T(8,128)(2,1)} %copy-done.3) | copy-start | bytes 393220
  149.3 2.8 %collective-permute-start.28 = (bf16[64,1024]{1,0:T(8,128)(2,1)S(1)}, bf16[64,1024]{1,0:T(8,128)(2,1)S(1)}, u32[]{:S(2)}, u32[]{:S(2)}) collective-permute-start(bf16[64,1024]{1,0:T(8,128)(2,1)S(1)} %shard_map.62.entry), channel_id=1, source_target_pairs={{16,0},{48,32},{80,64},{112,96},{144,128},{176,160},{208,192},{240... | collective-permute-start | bytes 393224 | tf_op jit(solution)/shard_map/ppermute | solution.py:333

commit v8 on v7

--- a/solution.py
+++ b/solution.py
@@ -101,13 +101,18 @@
         out[cut, :] = half_product(a, d, cut).astype(BF16)
 
 
-def step_kernel(panel, part, b, c, a_right, d_right, step, bias):
+def step_kernel(part, b, c, step, token):
+    token[...] = jnp.zeros_like(token)
     wide = b.shape[1]
     for m in range(step.shape[0] // wide):
         cut = slice(m * wide, (m + 1) * wide)
         step[cut, :] = (-(part[cut, :].astype(F32) + half_product(b, c, cut))).astype(BF16)
-    total = mm(panel[:, :wide], a_right[0])
-    for f, right in ((1, b), (2, c), (3, d_right)):
+
+
+def bias_kernel(panel, a, b, c, d, bias):
+    wide = a.shape[1]
+    total = mm(panel[:, :wide], a[0])
+    for f, right in ((1, b), (2, c), (3, d)):
         total = total + mm(panel[:, f * wide : (f + 1) * wide], right[0])
     bias[...] = -total
 
@@ -125,42 +130,41 @@
 def step_terms(order, panel, blocks):
     a, b, c, d = blocks
     two, wide, width = a.shape
-    cost = pl.CostEstimate(flops=width**3, bytes_accessed=6 * width**2, transcendentals=0)
-    part, token = pl.pallas_call(
+    whole = jax.ShapeDtypeStruct((width, width), BF16)
+    token = jax.ShapeDtypeStruct((8, 128), F32)
+    part, unused = pl.pallas_call(
         part_kernel,
-        out_shape=[
-            jax.ShapeDtypeStruct((width, width), BF16),
-            jax.ShapeDtypeStruct((8, 128), F32),
-        ],
+        out_shape=[whole, token],
         in_specs=[VMEM] * 2,
         out_specs=[VMEM, VMEM],
         compiler_params=PARAMS,
-        cost_estimate=cost,
     )(a, d)
+    step, ready = pl.pallas_call(
+        step_kernel,
+        out_shape=[whole, token],
+        in_specs=[VMEM] * 3,
+        out_specs=[VMEM, VMEM],
+        compiler_params=PARAMS,
+    )(part, b, c)
+    rows = 2 * panel.shape[1]
     panel = pl.pallas_call(
         cut_kernel,
-        out_shape=jax.ShapeDtypeStruct((2 * panel.shape[1], width), BF16),
+        out_shape=jax.ShapeDtypeStruct((rows, width), BF16),
         in_specs=[SMEM, VMEM, VMEM],
         out_specs=VMEM,
         compiler_params=SMALL,
-    )(order, panel, token)
-
-    def whole(shape):
-        return pl.BlockSpec(shape, lambda i: (0,) * len(shape))
-
-    right = whole((1, wide, width))
-    return pl.pallas_call(
-        step_kernel,
-        out_shape=[
-            jax.ShapeDtypeStruct((width, width), BF16),
-            jax.ShapeDtypeStruct(panel.shape, F32),
-        ],
-        in_specs=[VMEM, VMEM, VMEM, VMEM, right, right],
-        out_specs=[VMEM, VMEM],
+    )(order, panel, ready)
+    flat = pl.BlockSpec((rows, width), lambda i: (0, 0))
+    bias = pl.pallas_call(
+        bias_kernel,
+        out_shape=jax.ShapeDtypeStruct((rows, width), F32),
+        in_specs=[flat] + [pl.BlockSpec((1, wide, width), lambda i: (0, 0, 0))] * 4,
+        out_specs=flat,
         grid=(1,),
         compiler_params=PARAMS,
-        cost_estimate=cost,
-    )(panel, part, b, c, a, d)
+        cost_estimate=pl.CostEstimate(flops=40 * width**3, bytes_accessed=6 * width**2, transcendentals=0),
+    )(panel, a, b, c, d)
+    return step, bias
 
 
 def product_kernel(core, own, got, bias, bias_got, product, odd, add_even):

time: 155 us -> 154 us (level)
  local copies, waits for them, and re-layouts: 5.96 us -> 3.04 us
  Pallas kernels: 17.5 us -> 19.6 us
    ppermute x12, waiting for transfers between devices: 10.1 us -> 19.1 us  [ring_gather(): lax.ppermute(value, BOTH, ring_moves(depths, flipped, shift))]
    all_to_all x1, waiting for transfers between devices: 8.64 us -> 0.01 us  [body(): panel_rows = lax.all_to_all(panel, 'lat', 0, 0)]
    unnamed x12 -> x8, local copies, waits for them, and re-layouts: 2.95 us -> 0.02 us
    pallas_call x3 -> x4, Pallas kernels: 7.6 us -> 9.64 us  [the longest x1 4.21 us: step_terms(): pl.pallas_call(step_kernel, out_shape=[whole, token], in_specs=[VMEM] * 3...]
  transfers between devices with their start and end apart: 30 -> 30, of which waited for: 10 -> 9; matrix products, arithmetic and copies ran while one was open for 2% -> 3% of each run, Pallas kernels for 4% -> 8%
where the time goes in v8:
time: 154 us; the launch traced here: 153 us
  starting transfers between devices  68.6 us (45%)
  waiting for transfers between devices  51.7 us (34%)
  Pallas kernels  19.6 us (13%)
  matrix products  6.37 us (4%)
  local copies, waits for them, and re-layouts  3.04 us (2%)
  other arithmetic  2.48 us (2%)
  between operations  1.63 us (1%)
    ppermute x12, starting transfers between devices, ring_gather(): lax.ppermute(value, BOTH, ring_moves(depths, flipped, shift))  38.1 us
    ppermute x9, waiting for transfers between devices, body(): v_in = v_in + lax.ppermute(v_even.astype(BF16), 'depth', pairs)  24.5 us
    ppermute x12, waiting for transfers between devices, ring_gather(): lax.ppermute(value, BOTH, ring_moves(depths, flipped, shift))  19.1 us
    ppermute x1, starting transfers between devices, body(): got = lax.ppermute(step, 'depth', swap)  7.52 us
    ppermute x9, starting transfers between devices, body(): v_in = v_in + lax.ppermute(v_even.astype(BF16), 'depth', pairs)  6.82 us
    dot_general x12, matrix products, mm(): return jnp.dot(a, b, preferred_element_type=F32)  6.37 us
    ppermute x1, starting transfers between devices, body(): lax.ppermute(jnp.where(low, v_odd.astype(BF16), edge), 'depth', swap[:2 *...  5.8 us
    ppermute x4, waiting for transfers between devices, sent_down(): lax.ppermute(value, 'depth', [(2 * a + 1, 2 * b + 1) for a, b in chip_pai...  5.02 us
  transfers between devices with their start and end apart: 30, of which 9 were waited for; matrix products, arithmetic and copies ran while one was open for 3% of the time, Pallas kernels for 8%

profile of v8, /device:TPU:1, one launch (start us, length us, event | category | flops | bytes accessed | tf_op | source)
XLA Modules:
  0.0 153.3 jit_solution(11866943736416484827)
XLA Ops:
  0.8 1.1 fusion.14
  1.9 0.9 pad_maximum_fusion.1.a
  2.8 5.7 %collective-permute-start.2 = (bf16[2,64,1024]{2,1,0:T(8,128)(2,1)S(1)}, bf16[2,64,1024]{2,1,0:T(8,128)(2,1)S(1)}, u32[]{:S(2)}, u32[]{:S(2)}) collective-permute-start(bf16[2,64,1024]{2,1,0:T(8,128)(2,1)S(1)} %pad_maximum_fusion.1.a), channel_id=1, source_target_pairs={{0,2},{1,3},{2,0},{3,1},{4,6},{5,7},{6,4},{7,5},{8,10},{9,11},{10,... | collective-permute-start | bytes 786440 | tf_op jit(solution)/shard_map/ppermute | solution.py:41
  8.5 2.7 %collective-permute-start.1 = (bf16[2,64,1024]{2,1,0:T(8,128)(2,1)S(1)}, bf16[2,64,1024]{2,1,0:T(8,128)(2,1)S(1)}, u32[]{:S(2)}, u32[]{:S(2)}) collective-permute-start(bf16[2,64,1024]{2,1,0:T(8,128)(2,1)S(1)} %pad_maximum_fusion.1.a), channel_id=1, source_target_pairs={{0,3},{1,0},{2,1},{3,2},{4,7},{5,4},{6,5},{7,6},{8,11},{9,8},{10,9... | collective-permute-start | bytes 786440 | tf_op jit(solution)/shard_map/ppermute | solution.py:41
  11.2 2.6 %collective-permute-start = (bf16[2,64,1024]{2,1,0:T(8,128)(2,1)S(1)}, bf16[2,64,1024]{2,1,0:T(8,128)(2,1)S(1)}, u32[]{:S(2)}, u32[]{:S(2)}) collective-permute-start(bf16[2,64,1024]{2,1,0:T(8,128)(2,1)S(1)} %pad_maximum_fusion.1.a), channel_id=1, source_target_pairs={{0,1},{1,2},{2,3},{3,0},{4,5},{5,6},{6,7},{7,4},{8,9},{9,10},{10,1... | collective-permute-start | bytes 786440 | tf_op jit(solution)/shard_map/ppermute | solution.py:41
  13.8 1.8 %collective-permute-done.1.c = bf16[2,64,1024]{2,1,0:T(8,128)(2,1)S(1)} collective-permute-done((bf16[2,64,1024]{2,1,0:T(8,128)(2,1)S(1)}, bf16[2,64,1024]{2,1,0:T(8,128)(2,1)S(1)}, u32[]{:S(2)}, u32[]{:S(2)}) %collective-permute-start.1) | collective-permute-done | bytes 262176 | tf_op jit(solution)/shard_map/ppermute | solution.py:41
  15.6 3.9 %collective-permute-done.b = bf16[2,64,1024]{2,1,0:T(8,128)(2,1)S(1)} collective-permute-done((bf16[2,64,1024]{2,1,0:T(8,128)(2,1)S(1)}, bf16[2,64,1024]{2,1,0:T(8,128)(2,1)S(1)}, u32[]{:S(2)}, u32[]{:S(2)}) %collective-permute-start) | collective-permute-done | bytes 262176 | tf_op jit(solution)/shard_map/ppermute | solution.py:41
  19.7 4.7 %collective-permute-start.3 = (bf16[2,256,1024]{2,1,0:T(8,128)(2,1)S(1)}, bf16[2,256,1024]{2,1,0:T(8,128)(2,1)}, u32[]{:S(2)}, u32[]{:S(2)}) collective-permute-start(bf16[2,256,1024]{2,1,0:T(8,128)(2,1)S(1)} %shard_map.55.a), channel_id=1, source_target_pairs={{0,8},{1,9},{2,10},{3,11},{4,12},{5,13},{6,14},{7,15},{8,0},{9,1},... | collective-permute-start | bytes 3145736 | tf_op jit(solution)/shard_map/ppermute | solution.py:41
  24.4 2.8 %collective-permute-start.5 = (bf16[2,256,1024]{2,1,0:T(8,128)(2,1)S(1)}, bf16[2,256,1024]{2,1,0:T(8,128)(2,1)}, u32[]{:S(2)}, u32[]{:S(2)}) collective-permute-start(bf16[2,256,1024]{2,1,0:T(8,128)(2,1)S(1)} %shard_map.55.a), channel_id=1, source_target_pairs={{0,12},{1,13},{2,14},{3,15},{4,0},{5,1},{6,2},{7,3},{8,4},{9,5},{1... | collective-permute-start | bytes 3145736 | tf_op jit(solution)/shard_map/ppermute | solution.py:41
  27.1 2.5 %collective-permute-start.4 = (bf16[2,256,1024]{2,1,0:T(8,128)(2,1)S(1)}, bf16[2,256,1024]{2,1,0:T(8,128)(2,1)}, u32[]{:S(2)}, u32[]{:S(2)}) collective-permute-start(bf16[2,256,1024]{2,1,0:T(8,128)(2,1)S(1)} %shard_map.55.a), channel_id=1, source_target_pairs={{0,4},{1,5},{2,6},{3,7},{4,8},{5,9},{6,10},{7,11},{8,12},{9,13},{1... | collective-permute-start | bytes 3145736 | tf_op jit(solution)/shard_map/ppermute | solution.py:41
  29.7 0.8 convolution_convert_fusion
  30.6 0.9 copy.8
  31.6 1.8 %reshape.11 = bf16[16,32,128]{2,1,0:T(8,128)(2,1)} reshape(bf16[16,32,2,64]{3,2,1,0:T(2,128)(2,1)} %copy.8) | data formatting | bytes 262144 | tf_op jit(solution)/shard_map/reshape | solution.py:294
  33.4 3.7 %all-to-all-start = ((bf16[16,32,128]{2,1,0:T(8,128)(2,1)}), bf16[16,32,128]{2,1,0:T(8,128)(2,1)S(1)}, u32[]{:S(2)}, u32[]{:S(2)}) async-start(bf16[16,32,128]{2,1,0:T(8,128)(2,1)} %reshape.11), calls=%async_computation | async-start | bytes 262144 | tf_op jit(solution)/shard_map/all_to_all | solution.py:295
  37.4 2.9 %shard_map.56 = (bf16[1024,1024]{1,0:T(8,128)(2,1)S(1)}, f32[8,128]{1,0:T(8,128)}) custom-call(bf16[2,256,1024]{2,1,0:T(8,128)(2,1)S(1)} %shard_map.55.a, bf16[2,256,1024]{2,1,0:T(8,128)(2,1)} %collective-permute-done.3.d), custom_call_target="tpu_custom_call" | custom-call | tf_op jit(solution)/shard_map/pallas_call | solution.py:135
  40.3 8.9 %collective-permute-done.5.c = bf16[2,256,1024]{2,1,0:T(8,128)(2,1)} collective-permute-done((bf16[2,256,1024]{2,1,0:T(8,128)(2,1)S(1)}, bf16[2,256,1024]{2,1,0:T(8,128)(2,1)}, u32[]{:S(2)}, u32[]{:S(2)}) %collective-permute-start.5) | collective-permute-done | bytes 1048608 | tf_op jit(solution)/shard_map/ppermute | solution.py:41
  49.2 4.2 %shard_map.57 = (bf16[1024,1024]{1,0:T(8,128)(2,1)}, f32[8,128]{1,0:T(8,128)S(1)}) custom-call(bf16[1024,1024]{1,0:T(8,128)(2,1)S(1)} %get-tuple-element.11.part, bf16[2,256,1024]{2,1,0:T(8,128)(2,1)} %collective-permute-done.4.b, bf16[2,256,1024]{2,1,0:T(8,128)(2,1)} %collective-permute-done.5.c), custom_call_target="tpu_custom_call" | custom-call | tf_op jit(solution)/shard_map/pallas_call | solution.py:142
  53.4 7.5 %collective-permute-start.6 = (bf16[1024,1024]{1,0:T(8,128)(2,1)}, bf16[1024,1024]{1,0:T(8,128)(2,1)}, u32[]{:S(2)}, u32[]{:S(2)}) collective-permute-start(bf16[1024,1024]{1,0:T(8,128)(2,1)} %get-tuple-element.12.own), channel_id=1, source_target_pairs={{0,16},{16,0},{32,48},{48,32},{64,80},{80,64},{96,112},{112,96},{1... | collective-permute-start | bytes 6291464 | tf_op jit(solution)/shard_map/ppermute | solution.py:302
  61.0 0.6 shard_map.58.panel
  61.6 1.8 %shard_map.59.bias = f32[64,1024]{1,0:T(8,128)S(1)} custom-call(bf16[64,1024]{1,0:T(8,128)(2,1)S(1)} %shard_map.58.panel, bf16[2,256,1024]{2,1,0:T(8,128)(2,1)S(1)} %shard_map.55.a, bf16[2,256,1024]{2,1,0:T(8,128)(2,1)} %collective-permute-done.4.b, bf16[2,256,1024]{2,1,0:T(8,128)(2,1)} %collective-permute-done.5.c, ...), custom_call_target="tpu_custom_call" | custom-call | flops 42949672960 | bytes 6291456 | tf_op jit(solution)/shard_map/pallas_call | solution.py:158
  63.5 1.3 collective-permute-start.7
  64.8 2.1 %collective-permute-done.7.bias_got = f32[64,1024]{1,0:T(8,128)S(1)} collective-permute-done((f32[64,1024]{1,0:T(8,128)S(1)}, f32[64,1024]{1,0:T(8,128)S(1)}, u32[]{:S(2)}, u32[]{:S(2)}) %collective-permute-start.7) | collective-permute-done | bytes 262176 | tf_op jit(solution)/shard_map/ppermute | solution.py:303
  66.9 4.9 %shard_map.60 = (bf16[1024,1024]{1,0:T(8,128)(2,1)S(1)}, bf16[1024,1024]{1,0:T(8,128)(2,1)S(1)}, f32[64,1024]{1,0:T(8,128)S(1)}) custom-call(s32[1]{0:T(128)} %bitcast.18.core, bf16[1024,1024]{1,0:T(8,128)(2,1)} %get-tuple-element.12.own, bf16[1024,1024]{1,0:T(8,128)(2,1)} %collective-permute-done.6.got, f32[64,1024]{1,0:T(8,128)S(1)} %shard_map.59.bias, ...), custom_call_target="tpu_custom_call" | custom-call | flops 2147483648 | bytes 6291456 | tf_op jit(solution)/shard_map/pallas_call | solution.py:193
  71.8 0.5 fusion
  72.3 0.7 collective-permute-start.8
  73.0 0.6 fusion.1
  73.6 0.7 collective-permute-start.9
  74.3 0.6 fusion.2
  74.9 0.7 collective-permute-start.10
  75.7 0.5 fusion.3
  76.2 0.7 collective-permute-start.11
  77.0 0.5 fusion.4
  77.5 1.3 collective-permute-start.12
  78.8 24.4 %collective-permute-done.12 = bf16[64,1024]{1,0:T(8,128)(2,1)S(1)} collective-permute-done((bf16[64,1024]{1,0:T(8,128)(2,1)S(1)}, bf16[64,1024]{1,0:T(8,128)(2,1)S(1)}, u32[]{:S(2)}, u32[]{:S(2)}) %collective-permute-start.12) | collective-permute-done | bytes 131104 | tf_op jit(solution)/shard_map/ppermute | solution.py:318
  103.2 0.5 fusion.5
  103.7 0.7 collective-permute-start.13
  104.5 0.5 fusion.6
  105.0 0.8 collective-permute-start.14
  105.9 0.5 fusion.7
  106.4 0.7 collective-permute-start.15
  107.1 0.5 fusion.8
  107.6 0.7 collective-permute-start.16
  108.3 0.5 convolution_add_fusion.v_odd
  108.8 0.5 convert_select_fusion
  109.3 5.8 %collective-permute-start.17 = (bf16[64,1024]{1,0:T(8,128)(2,1)S(1)}, bf16[64,1024]{1,0:T(8,128)(2,1)S(1)}, u32[]{:S(2)}, u32[]{:S(2)}) collective-permute-start(bf16[64,1024]{1,0:T(8,128)(2,1)S(1)} %get-tuple-element.17), channel_id=1, source_target_pairs={{0,16},{16,0},{32,48},{48,32},{64,80},{80,64},{96,112},{112,96},{1... | collective-permute-start | bytes 393224 | tf_op jit(solution)/shard_map/ppermute | solution.py:322
  115.1 1.0 collective-permute-done.17.other
  116.1 4.4 %collective-permute-start.20 = (bf16[64,1024]{1,0:T(8,128)(2,1)S(1)}, bf16[64,1024]{1,0:T(8,128)(2,1)S(1)}, u32[]{:S(2)}, u32[]{:S(2)}) collective-permute-start(bf16[64,1024]{1,0:T(8,128)(2,1)S(1)} %broadcast_select_fusion), channel_id=1, source_target_pairs={{0,2},{1,3},{2,0},{3,1},{4,6},{5,7},{6,4},{7,5},{8,10},{9,11},{10,... | collective-permute-start | bytes 393224 | tf_op jit(solution)/shard_map/ppermute | solution.py:41
  120.5 2.8 %collective-permute-start.19 = (bf16[64,1024]{1,0:T(8,128)(2,1)S(1)}, bf16[64,1024]{1,0:T(8,128)(2,1)S(1)}, u32[]{:S(2)}, u32[]{:S(2)}) collective-permute-start(bf16[64,1024]{1,0:T(8,128)(2,1)S(1)} %broadcast_select_fusion), channel_id=1, source_target_pairs={{0,3},{1,0},{2,1},{3,2},{4,7},{5,4},{6,5},{7,6},{8,11},{9,8},{10,9... | collective-permute-start | bytes 393224 | tf_op jit(solution)/shard_map/ppermute | solution.py:41
  123.4 2.4 %collective-permute-start.18 = (bf16[64,1024]{1,0:T(8,128)(2,1)S(1)}, bf16[64,1024]{1,0:T(8,128)(2,1)S(1)}, u32[]{:S(2)}, u32[]{:S(2)}) collective-permute-start(bf16[64,1024]{1,0:T(8,128)(2,1)S(1)} %broadcast_select_fusion), channel_id=1, source_target_pairs={{0,1},{1,2},{2,3},{3,0},{4,5},{5,6},{6,7},{7,4},{8,9},{9,10},{10,1... | collective-permute-start | bytes 393224 | tf_op jit(solution)/shard_map/ppermute | solution.py:41
  125.8 0.4 collective-permute-done.19
  126.3 4.1 %collective-permute-done.18 = bf16[64,1024]{1,0:T(8,128)(2,1)S(1)} collective-permute-done((bf16[64,1024]{1,0:T(8,128)(2,1)S(1)}, bf16[64,1024]{1,0:T(8,128)(2,1)S(1)}, u32[]{:S(2)}, u32[]{:S(2)}) %collective-permute-start.18) | collective-permute-done | bytes 131104 | tf_op jit(solution)/shard_map/ppermute | solution.py:41
  130.4 1.9 %collective-permute-start.23 = (bf16[256,1024]{1,0:T(8,128)(2,1)S(1)}, bf16[256,1024]{1,0:T(8,128)(2,1)S(1)}, u32[]{:S(2)}, u32[]{:S(2)}) collective-permute-start(bf16[256,1024]{1,0:T(8,128)(2,1)S(1)} %pad_maximum_fusion.a.ready), channel_id=1, source_target_pairs={{0,8},{1,9},{2,10},{3,11},{4,12},{5,13},{6,14},{7,15},{8,0},{9,1},... | collective-permute-start | bytes 1572872 | tf_op jit(solution)/shard_map/ppermute | solution.py:41
  132.3 3.7 %collective-permute-start.22 = (bf16[256,1024]{1,0:T(8,128)(2,1)S(1)}, bf16[256,1024]{1,0:T(8,128)(2,1)}, u32[]{:S(2)}, u32[]{:S(2)}) collective-permute-start(bf16[256,1024]{1,0:T(8,128)(2,1)S(1)} %pad_maximum_fusion.a.ready), channel_id=1, source_target_pairs={{0,12},{1,13},{2,14},{3,15},{4,0},{5,1},{6,2},{7,3},{8,4},{9,5},{1... | collective-permute-start | bytes 1572872 | tf_op jit(solution)/shard_map/ppermute | solution.py:41
  136.0 1.9 %collective-permute-start.21 = (bf16[256,1024]{1,0:T(8,128)(2,1)S(1)}, bf16[256,1024]{1,0:T(8,128)(2,1)}, u32[]{:S(2)}, u32[]{:S(2)}) collective-permute-start(bf16[256,1024]{1,0:T(8,128)(2,1)S(1)} %pad_maximum_fusion.a.ready), channel_id=1, source_target_pairs={{0,4},{1,5},{2,6},{3,7},{4,8},{5,9},{6,10},{7,11},{8,12},{9,13},{1... | collective-permute-start | bytes 1572872 | tf_op jit(solution)/shard_map/ppermute | solution.py:41
  137.9 0.7 collective-permute-start.25
  138.6 0.7 collective-permute-start.24
  139.3 0.7 shard_map.62.entry
  139.9 1.3 collective-permute-start.27
  141.2 1.3 collective-permute-start.26
  142.6 5.0 %collective-permute-done.27.last = bf16[64,1024]{1,0:T(8,128)(2,1)} collective-permute-done((bf16[64,1024]{1,0:T(8,128)(2,1)}, bf16[64,1024]{1,0:T(8,128)(2,1)}, u32[]{:S(2)}, u32[]{:S(2)}) %collective-permute-start.27) | collective-permute-done | bytes 131104 | tf_op jit(solution)/shard_map/ppermute | solution.py:47
  147.6 1.1 shard_map.63.entry
  148.7 1.4 collective-permute-start.28
  150.2 1.4 shard_map.61.maps
  151.6 1.7 %shard_map.64 = f32[64,1024]{1,0:T(8,128)} custom-call(s32[2]{0:T(128)S(1)} %add_convert_fusion.flags, bf16[1024,1024]{1,0:T(8,128)(2,1)S(1)} %shard_map.61.maps, bf16[64,1024]{1,0:T(8,128)(2,1)S(1)} %shard_map.63.entry, bf16[64,1024]{1,0:T(8,128)(2,1)S(1)} %collective-permute-done.28.across, bf16[64,1024]{1,0:T(8,128)(2,1)S(1)} %copy-done.2, ...), custom_call_target="tpu_custom_call" | custom-call | tf_op jit(solution)/shard_map/pallas_call | solution.py:262
  (42 shorter events, 1.0 us)
Async XLA Ops:
  0.0 29.7 %copy-start = (bf16[1024,1024]{1,0:T(8,128)(2,1)S(1)}, bf16[1024,1024]{1,0:T(8,128)(2,1)}, u32[]{:S(2)}) copy-start(bf16[1024,1024]{1,0:T(8,128)(2,1)} %param.8) | copy-start | bytes 6291460
  0.0 29.7 %copy-start.3 = (bf16[1,1024,64]{1,2,0:T(8,128)(2,1)S(1)}, bf16[1,1024,64]{1,2,0:T(8,128)(2,1)}, u32[]{:S(2)}) copy-start(bf16[1,1024,64]{1,2,0:T(8,128)(2,1)} %param.7) | copy-start | bytes 393220
  2.8 11.0 %collective-permute-start.2 = (bf16[2,64,1024]{2,1,0:T(8,128)(2,1)S(1)}, bf16[2,64,1024]{2,1,0:T(8,128)(2,1)S(1)}, u32[]{:S(2)}, u32[]{:S(2)}) collective-permute-start(bf16[2,64,1024]{2,1,0:T(8,128)(2,1)S(1)} %pad_maximum_fusion.1.a), channel_id=1, source_target_pairs={{0,2},{1,3},{2,0},{3,1},{4,6},{5,7},{6,4},{7,5},{8,10},{9,11},{10,... | collective-permute-start | bytes 786440 | tf_op jit(solution)/shard_map/ppermute | solution.py:41
  8.5 7.1 %collective-permute-start.1 = (bf16[2,64,1024]{2,1,0:T(8,128)(2,1)S(1)}, bf16[2,64,1024]{2,1,0:T(8,128)(2,1)S(1)}, u32[]{:S(2)}, u32[]{:S(2)}) collective-permute-start(bf16[2,64,1024]{2,1,0:T(8,128)(2,1)S(1)} %pad_maximum_fusion.1.a), channel_id=1, source_target_pairs={{0,3},{1,0},{2,1},{3,2},{4,7},{5,4},{6,5},{7,6},{8,11},{9,8},{10,9... | collective-permute-start | bytes 786440 | tf_op jit(solution)/shard_map/ppermute | solution.py:41
  11.2 8.3 %collective-permute-start = (bf16[2,64,1024]{2,1,0:T(8,128)(2,1)S(1)}, bf16[2,64,1024]{2,1,0:T(8,128)(2,1)S(1)}, u32[]{:S(2)}, u32[]{:S(2)}) collective-permute-start(bf16[2,64,1024]{2,1,0:T(8,128)(2,1)S(1)} %pad_maximum_fusion.1.a), channel_id=1, source_target_pairs={{0,1},{1,2},{2,3},{3,0},{4,5},{5,6},{6,7},{7,4},{8,9},{9,10},{10,1... | collective-permute-start | bytes 786440 | tf_op jit(solution)/shard_map/ppermute | solution.py:41
  19.7 17.7 %collective-permute-start.3 = (bf16[2,256,1024]{2,1,0:T(8,128)(2,1)S(1)}, bf16[2,256,1024]{2,1,0:T(8,128)(2,1)}, u32[]{:S(2)}, u32[]{:S(2)}) collective-permute-start(bf16[2,256,1024]{2,1,0:T(8,128)(2,1)S(1)} %shard_map.55.a), channel_id=1, source_target_pairs={{0,8},{1,9},{2,10},{3,11},{4,12},{5,13},{6,14},{7,15},{8,0},{9,1},... | collective-permute-start | bytes 3145736 | tf_op jit(solution)/shard_map/ppermute | solution.py:41
  24.4 24.9 %collective-permute-start.5 = (bf16[2,256,1024]{2,1,0:T(8,128)(2,1)S(1)}, bf16[2,256,1024]{2,1,0:T(8,128)(2,1)}, u32[]{:S(2)}, u32[]{:S(2)}) collective-permute-start(bf16[2,256,1024]{2,1,0:T(8,128)(2,1)S(1)} %shard_map.55.a), channel_id=1, source_target_pairs={{0,12},{1,13},{2,14},{3,15},{4,0},{5,1},{6,2},{7,3},{8,4},{9,5},{1... | collective-permute-start | bytes 3145736 | tf_op jit(solution)/shard_map/ppermute | solution.py:41
  27.1 22.1 %collective-permute-start.4 = (bf16[2,256,1024]{2,1,0:T(8,128)(2,1)S(1)}, bf16[2,256,1024]{2,1,0:T(8,128)(2,1)}, u32[]{:S(2)}, u32[]{:S(2)}) collective-permute-start(bf16[2,256,1024]{2,1,0:T(8,128)(2,1)S(1)} %shard_map.55.a), channel_id=1, source_target_pairs={{0,4},{1,5},{2,6},{3,7},{4,8},{5,9},{6,10},{7,11},{8,12},{9,13},{1... | collective-permute-start | bytes 3145736 | tf_op jit(solution)/shard_map/ppermute | solution.py:41
  33.4 27.6 %all-to-all-start = ((bf16[16,32,128]{2,1,0:T(8,128)(2,1)}), bf16[16,32,128]{2,1,0:T(8,128)(2,1)S(1)}, u32[]{:S(2)}, u32[]{:S(2)}) async-start(bf16[16,32,128]{2,1,0:T(8,128)(2,1)} %reshape.11), calls=%async_computation | async-start | bytes 262144 | tf_op jit(solution)/shard_map/all_to_all | solution.py:295
  53.4 13.5 %collective-permute-start.6 = (bf16[1024,1024]{1,0:T(8,128)(2,1)}, bf16[1024,1024]{1,0:T(8,128)(2,1)}, u32[]{:S(2)}, u32[]{:S(2)}) collective-permute-start(bf16[1024,1024]{1,0:T(8,128)(2,1)} %get-tuple-element.12.own), channel_id=1, source_target_pairs={{0,16},{16,0},{32,48},{48,32},{64,80},{80,64},{96,112},{112,96},{1... | collective-permute-start | bytes 6291464 | tf_op jit(solution)/shard_map/ppermute | solution.py:302
  63.5 3.4 %collective-permute-start.7 = (f32[64,1024]{1,0:T(8,128)S(1)}, f32[64,1024]{1,0:T(8,128)S(1)}, u32[]{:S(2)}, u32[]{:S(2)}) collective-permute-start(f32[64,1024]{1,0:T(8,128)S(1)} %shard_map.59.bias), channel_id=1, source_target_pairs={{0,16},{32,48},{64,80},{96,112},{128,144},{160,176},{192,208},{224... | collective-permute-start | bytes 786440 | tf_op jit(solution)/shard_map/ppermute | solution.py:303
  72.3 0.7 collective-permute-start.8
  73.6 0.7 collective-permute-start.9
  74.9 0.7 collective-permute-start.10
  76.2 0.7 collective-permute-start.11
  77.5 25.7 %collective-permute-start.12 = (bf16[64,1024]{1,0:T(8,128)(2,1)S(1)}, bf16[64,1024]{1,0:T(8,128)(2,1)S(1)}, u32[]{:S(2)}, u32[]{:S(2)}) collective-permute-start(bf16[64,1024]{1,0:T(8,128)(2,1)S(1)} %fusion.4), channel_id=1, source_target_pairs={{368,336},{32,0},{48,16},{369,337},{33,1},{49,17},{370,338},{34,2}... | collective-permute-start | bytes 393224 | tf_op jit(solution)/shard_map/ppermute | solution.py:318
  103.7 0.7 collective-permute-start.13
  105.0 0.9 collective-permute-start.14
  106.4 0.7 collective-permute-start.15
  107.6 0.7 collective-permute-start.16
  109.3 6.8 %collective-permute-start.17 = (bf16[64,1024]{1,0:T(8,128)(2,1)S(1)}, bf16[64,1024]{1,0:T(8,128)(2,1)S(1)}, u32[]{:S(2)}, u32[]{:S(2)}) collective-permute-start(bf16[64,1024]{1,0:T(8,128)(2,1)S(1)} %get-tuple-element.17), channel_id=1, source_target_pairs={{0,16},{16,0},{32,48},{48,32},{64,80},{80,64},{96,112},{112,96},{1... | collective-permute-start | bytes 393224 | tf_op jit(solution)/shard_map/ppermute | solution.py:322
  116.1 10.2 %copy-start.1 = (bf16[64,1024]{1,0:T(8,128)(2,1)}, bf16[64,1024]{1,0:T(8,128)(2,1)S(1)}, u32[]{:S(2)}) copy-start(bf16[64,1024]{1,0:T(8,128)(2,1)S(1)} %collective-permute-done.17.other) | copy-start | bytes 393220
  116.1 9.7 %collective-permute-start.20 = (bf16[64,1024]{1,0:T(8,128)(2,1)S(1)}, bf16[64,1024]{1,0:T(8,128)(2,1)S(1)}, u32[]{:S(2)}, u32[]{:S(2)}) collective-permute-start(bf16[64,1024]{1,0:T(8,128)(2,1)S(1)} %broadcast_select_fusion), channel_id=1, source_target_pairs={{0,2},{1,3},{2,0},{3,1},{4,6},{5,7},{6,4},{7,5},{8,10},{9,11},{10,... | collective-permute-start | bytes 393224 | tf_op jit(solution)/shard_map/ppermute | solution.py:41
  120.5 5.7 %collective-permute-start.19 = (bf16[64,1024]{1,0:T(8,128)(2,1)S(1)}, bf16[64,1024]{1,0:T(8,128)(2,1)S(1)}, u32[]{:S(2)}, u32[]{:S(2)}) collective-permute-start(bf16[64,1024]{1,0:T(8,128)(2,1)S(1)} %broadcast_select_fusion), channel_id=1, source_target_pairs={{0,3},{1,0},{2,1},{3,2},{4,7},{5,4},{6,5},{7,6},{8,11},{9,8},{10,9... | collective-permute-start | bytes 393224 | tf_op jit(solution)/shard_map/ppermute | solution.py:41
  123.4 6.9 %collective-permute-start.18 = (bf16[64,1024]{1,0:T(8,128)(2,1)S(1)}, bf16[64,1024]{1,0:T(8,128)(2,1)S(1)}, u32[]{:S(2)}, u32[]{:S(2)}) collective-permute-start(bf16[64,1024]{1,0:T(8,128)(2,1)S(1)} %broadcast_select_fusion), channel_id=1, source_target_pairs={{0,1},{1,2},{2,3},{3,0},{4,5},{5,6},{6,7},{7,4},{8,9},{9,10},{10,1... | collective-permute-start | bytes 393224 | tf_op jit(solution)/shard_map/ppermute | solution.py:41
  130.4 19.8 %collective-permute-start.23 = (bf16[256,1024]{1,0:T(8,128)(2,1)S(1)}, bf16[256,1024]{1,0:T(8,128)(2,1)S(1)}, u32[]{:S(2)}, u32[]{:S(2)}) collective-permute-start(bf16[256,1024]{1,0:T(8,128)(2,1)S(1)} %pad_maximum_fusion.a.ready), channel_id=1, source_target_pairs={{0,8},{1,9},{2,10},{3,11},{4,12},{5,13},{6,14},{7,15},{8,0},{9,1},... | collective-permute-start | bytes 1572872 | tf_op jit(solution)/shard_map/ppermute | solution.py:41
  132.3 17.9 %collective-permute-start.22 = (bf16[256,1024]{1,0:T(8,128)(2,1)S(1)}, bf16[256,1024]{1,0:T(8,128)(2,1)}, u32[]{:S(2)}, u32[]{:S(2)}) collective-permute-start(bf16[256,1024]{1,0:T(8,128)(2,1)S(1)} %pad_maximum_fusion.a.ready), channel_id=1, source_target_pairs={{0,12},{1,13},{2,14},{3,15},{4,0},{5,1},{6,2},{7,3},{8,4},{9,5},{1... | collective-permute-start | bytes 1572872 | tf_op jit(solution)/shard_map/ppermute | solution.py:41
  136.0 14.2 %collective-permute-start.21 = (bf16[256,1024]{1,0:T(8,128)(2,1)S(1)}, bf16[256,1024]{1,0:T(8,128)(2,1)}, u32[]{:S(2)}, u32[]{:S(2)}) collective-permute-start(bf16[256,1024]{1,0:T(8,128)(2,1)S(1)} %pad_maximum_fusion.a.ready), channel_id=1, source_target_pairs={{0,4},{1,5},{2,6},{3,7},{4,8},{5,9},{6,10},{7,11},{8,12},{9,13},{1... | collective-permute-start | bytes 1572872 | tf_op jit(solution)/shard_map/ppermute | solution.py:41
  137.9 1.4 collective-permute-start.25
  138.6 0.7 collective-permute-start.24
  139.9 7.7 %collective-permute-start.27 = (bf16[64,1024]{1,0:T(8,128)(2,1)}, bf16[64,1024]{1,0:T(8,128)(2,1)}, u32[]{:S(2)}, u32[]{:S(2)}) collective-permute-start(bf16[64,1024]{1,0:T(8,128)(2,1)} %shard_map.62.entry), channel_id=1, source_target_pairs={{176,112},{80,16},{177,113},{81,17},{178,114},{82,18},{179,115},{8... | collective-permute-start | bytes 393224 | tf_op jit(solution)/shard_map/ppermute | solution.py:47
  141.2 6.4 %collective-permute-start.26 = (bf16[64,1024]{1,0:T(8,128)(2,1)}, bf16[64,1024]{1,0:T(8,128)(2,1)}, u32[]{:S(2)}, u32[]{:S(2)}) collective-permute-start(bf16[64,1024]{1,0:T(8,128)(2,1)} %shard_map.62.entry), channel_id=1, source_target_pairs={{176,144},{80,48},{177,145},{81,49},{178,146},{82,50},{179,147},{8... | collective-permute-start | bytes 393224 | tf_op jit(solution)/shard_map/ppermute | solution.py:47
  148.7 2.9 %copy-start.2 = (bf16[64,1024]{1,0:T(8,128)(2,1)S(1)}, bf16[64,1024]{1,0:T(8,128)(2,1)}, u32[]{:S(2)}) copy-start(bf16[64,1024]{1,0:T(8,128)(2,1)} %copy-done.1) | copy-start | bytes 393220
  148.7 2.8 %collective-permute-start.28 = (bf16[64,1024]{1,0:T(8,128)(2,1)S(1)}, bf16[64,1024]{1,0:T(8,128)(2,1)S(1)}, u32[]{:S(2)}, u32[]{:S(2)}) collective-permute-start(bf16[64,1024]{1,0:T(8,128)(2,1)S(1)} %shard_map.63.entry), channel_id=1, source_target_pairs={{16,0},{48,32},{80,64},{112,96},{144,128},{176,160},{208,192},{240... | collective-permute-start | bytes 393224 | tf_op jit(solution)/shard_map/ppermute | solution.py:337

commit v9 on v8

--- a/solution.py
+++ b/solution.py
@@ -167,7 +167,8 @@
     return step, bias
 
 
-def product_kernel(core, own, got, bias, bias_got, product, odd, add_even):
+def product_kernel(core, own, got, bias, bias_got, product, odd, add_even, turn):
+    turn[...] = jnp.zeros_like(turn)
     cut = 256
     width = own.shape[0]
 
@@ -196,12 +197,27 @@
             jax.ShapeDtypeStruct(own.shape, BF16),
             jax.ShapeDtypeStruct(own.shape, BF16),
             jax.ShapeDtypeStruct(bias.shape, F32),
+            jax.ShapeDtypeStruct((8, 128), F32),
         ],
         in_specs=[SMEM] + [VMEM] * 4,
-        out_specs=[VMEM] * 3,
+        out_specs=[VMEM] * 4,
         compiler_params=PARAMS,
         cost_estimate=pl.CostEstimate(flops=2 * width**3, bytes_accessed=6 * width**2, transcendentals=0),
     )(core.reshape(1), own, got, bias, bias_got)
+
+
+def hold_kernel(value, ready, out):
+    out[...] = value[...]
+
+
+def held(value, ready):
+    return pl.pallas_call(
+        hold_kernel,
+        out_shape=jax.ShapeDtypeStruct(value.shape, value.dtype),
+        in_specs=[VMEM, VMEM],
+        out_specs=VMEM,
+        compiler_params=SMALL,
+    )(value, ready)
 
 
 def join_kernel(a, b, ready, out):
@@ -215,6 +231,7 @@
         in_specs=[VMEM, VMEM, VMEM],
         out_specs=VMEM,
         compiler_params=SMALL,
+        cost_estimate=pl.CostEstimate(flops=4 * 10**10, bytes_accessed=0, transcendentals=0),
     )(a, b, ready)
 
 
@@ -301,13 +318,15 @@
     swap = [(d, d ^ 1) for d in range(depth_count)]
     got = lax.ppermute(step, "depth", swap)
     bias_got = lax.ppermute(bias, "depth", [(2 * k, 2 * k + 1) for k in range(chips)])
-    product, step_odd, add_even = products(core, step, got, bias, bias_got)
+    product, step_odd, add_even, turn = products(core, step, got, bias, bias_got)
     add_odd = jnp.where(low, jnp.zeros_like(bias), bias)
     lower = (chips * 6) // 16
     tops = [chips - 1, lower - 1]
     sizes = [chips - lower, lower]
     start = (row == col) & ((chip == tops[0]) | (chip == tops[1])) & low
     v_in = jnp.where(start, 1.0, 0.0).astype(BF16)
+    turn = lax.ppermute(turn, "depth", [(2 * k, 2 * k + 1) for k in range(lower)])
+    v_in = held(v_in, turn)
     v_even = mm(v_in, product) + add_even
     for hop in range(1, max(sizes)):
         pairs = []

time: 154 us -> 157 us (1.019)
  starting transfers between devices: 68.6 us -> 76.2 us
  waiting for transfers between devices: 51.7 us -> 46.8 us
    ppermute x9, waiting for transfers between devices: 24.5 us -> 19.7 us  [body(): v_in = v_in + lax.ppermute(v_even.astype(BF16), 'depth', pairs)]
    ppermute x1, starting transfers between devices: 7.52 us -> 11.6 us  [body(): got = lax.ppermute(step, 'depth', swap)]
    ppermute x12, waiting for transfers between devices: 19.1 us -> 16.5 us  [ring_gather(): lax.ppermute(value, BOTH, ring_moves(depths, flipped, shift))]
    ppermute x12, starting transfers between devices: 38.1 us -> 40.2 us  [ring_gather(): lax.ppermute(value, BOTH, ring_moves(depths, flipped, shift))]
    ppermute x0 -> x1, waiting for transfers between devices: none -> 1.63 us  [body(): lax.ppermute(turn, 'depth', [(2 * k, 2 * k + 1) for k in range(lower)])]
  transfers between devices with their start and end apart: 30 -> 31, of which waited for: 9 -> 9; matrix products, arithmetic and copies ran while one was open for 3% -> 3% of each run, Pallas kernels for 8% -> 8%
where the time goes in v9:
time: 157 us; the launch traced here: 156 us
  starting transfers between devices  76.2 us (49%)
  waiting for transfers between devices  46.8 us (30%)
  Pallas kernels  19.6 us (12%)
  matrix products  6.18 us (4%)
  local copies, waits for them, and re-layouts  3.01 us (2%)
  other arithmetic  2.53 us (2%)
  between operations  1.7 us (1%)
    ppermute x12, starting transfers between devices, ring_gather(): lax.ppermute(value, BOTH, ring_moves(depths, flipped, shift))  40.2 us
    ppermute x9, waiting for transfers between devices, body(): v_in = v_in + lax.ppermute(v_even.astype(BF16), 'depth', pairs)  19.7 us
    ppermute x12, waiting for transfers between devices, ring_gather(): lax.ppermute(value, BOTH, ring_moves(depths, flipped, shift))  16.5 us
    ppermute x1, starting transfers between devices, body(): got = lax.ppermute(step, 'depth', swap)  11.6 us
    ppermute x9, starting transfers between devices, body(): v_in = v_in + lax.ppermute(v_even.astype(BF16), 'depth', pairs)  6.82 us
    dot_general x12, matrix products, mm(): return jnp.dot(a, b, preferred_element_type=F32)  6.18 us
    ppermute x1, starting transfers between devices, body(): lax.ppermute(jnp.where(low, v_odd.astype(BF16), edge), 'depth', swap[:2 *...  6.07 us
    ppermute x4, waiting for transfers between devices, sent_down(): lax.ppermute(value, 'depth', [(2 * a + 1, 2 * b + 1) for a, b in chip_pai...  5.85 us
  transfers between devices with their start and end apart: 31, of which 9 were waited for; matrix products, arithmetic and copies ran while one was open for 3% of the time, Pallas kernels for 8%

profile of v9, /device:TPU:1, one launch (start us, length us, event | category | flops | bytes accessed | tf_op | source)
XLA Modules:
  0.0 155.9 jit_solution(10914292909586242052)
XLA Ops:
  0.8 1.1 fusion.13
  1.9 0.9 pad_maximum_fusion.1.a
  2.8 4.0 %collective-permute-start = (bf16[2,64,1024]{2,1,0:T(8,128)(2,1)S(1)}, bf16[2,64,1024]{2,1,0:T(8,128)(2,1)S(1)}, u32[]{:S(2)}, u32[]{:S(2)}) collective-permute-start(bf16[2,64,1024]{2,1,0:T(8,128)(2,1)S(1)} %pad_maximum_fusion.1.a), channel_id=1, source_target_pairs={{0,1},{1,2},{2,3},{3,0},{4,5},{5,6},{6,7},{7,4},{8,9},{9,10},{10,1... | collective-permute-start | bytes 786440 | tf_op jit(solution)/shard_map/ppermute | solution.py:41
  6.8 3.4 %collective-permute-start.1 = (bf16[2,64,1024]{2,1,0:T(8,128)(2,1)S(1)}, bf16[2,64,1024]{2,1,0:T(8,128)(2,1)S(1)}, u32[]{:S(2)}, u32[]{:S(2)}) collective-permute-start(bf16[2,64,1024]{2,1,0:T(8,128)(2,1)S(1)} %pad_maximum_fusion.1.a), channel_id=1, source_target_pairs={{0,3},{1,0},{2,1},{3,2},{4,7},{5,4},{6,5},{7,6},{8,11},{9,8},{10,9... | collective-permute-start | bytes 786440 | tf_op jit(solution)/shard_map/ppermute | solution.py:41
  10.2 3.5 %collective-permute-start.2 = (bf16[2,64,1024]{2,1,0:T(8,128)(2,1)S(1)}, bf16[2,64,1024]{2,1,0:T(8,128)(2,1)S(1)}, u32[]{:S(2)}, u32[]{:S(2)}) collective-permute-start(bf16[2,64,1024]{2,1,0:T(8,128)(2,1)S(1)} %pad_maximum_fusion.1.a), channel_id=1, source_target_pairs={{0,2},{1,3},{2,0},{3,1},{4,6},{5,7},{6,4},{7,5},{8,10},{9,11},{10,... | collective-permute-start | bytes 786440 | tf_op jit(solution)/shard_map/ppermute | solution.py:41
  14.0 4.9 %collective-permute-done.2.d = bf16[2,64,1024]{2,1,0:T(8,128)(2,1)S(1)} collective-permute-done((bf16[2,64,1024]{2,1,0:T(8,128)(2,1)S(1)}, bf16[2,64,1024]{2,1,0:T(8,128)(2,1)S(1)}, u32[]{:S(2)}, u32[]{:S(2)}) %collective-permute-start.2) | collective-permute-done | bytes 262176 | tf_op jit(solution)/shard_map/ppermute | solution.py:41
  19.0 4.7 %collective-permute-start.3 = (bf16[2,256,1024]{2,1,0:T(8,128)(2,1)S(1)}, bf16[2,256,1024]{2,1,0:T(8,128)(2,1)}, u32[]{:S(2)}, u32[]{:S(2)}) collective-permute-start(bf16[2,256,1024]{2,1,0:T(8,128)(2,1)S(1)} %shard_map.55.a), channel_id=1, source_target_pairs={{0,8},{1,9},{2,10},{3,11},{4,12},{5,13},{6,14},{7,15},{8,0},{9,1},... | collective-permute-start | bytes 3145736 | tf_op jit(solution)/shard_map/ppermute | solution.py:41
  23.7 2.2 %collective-permute-start.4 = (bf16[2,256,1024]{2,1,0:T(8,128)(2,1)S(1)}, bf16[2,256,1024]{2,1,0:T(8,128)(2,1)}, u32[]{:S(2)}, u32[]{:S(2)}) collective-permute-start(bf16[2,256,1024]{2,1,0:T(8,128)(2,1)S(1)} %shard_map.55.a), channel_id=1, source_target_pairs={{0,4},{1,5},{2,6},{3,7},{4,8},{5,9},{6,10},{7,11},{8,12},{9,13},{1... | collective-permute-start | bytes 3145736 | tf_op jit(solution)/shard_map/ppermute | solution.py:41
  25.9 4.3 %collective-permute-start.5 = (bf16[2,256,1024]{2,1,0:T(8,128)(2,1)S(1)}, bf16[2,256,1024]{2,1,0:T(8,128)(2,1)}, u32[]{:S(2)}, u32[]{:S(2)}) collective-permute-start(bf16[2,256,1024]{2,1,0:T(8,128)(2,1)S(1)} %shard_map.55.a), channel_id=1, source_target_pairs={{0,12},{1,13},{2,14},{3,15},{4,0},{5,1},{6,2},{7,3},{8,4},{9,5},{1... | collective-permute-start | bytes 3145736 | tf_op jit(solution)/shard_map/ppermute | solution.py:41
  30.2 0.8 convolution_convert_fusion
  31.2 0.9 copy.8
  32.1 1.8 %reshape.11 = bf16[16,32,128]{2,1,0:T(8,128)(2,1)} reshape(bf16[16,32,2,64]{3,2,1,0:T(2,128)(2,1)} %copy.8) | data formatting | bytes 262144 | tf_op jit(solution)/shard_map/reshape | solution.py:311
  33.9 3.5 %all-to-all-start = ((bf16[16,32,128]{2,1,0:T(8,128)(2,1)}), bf16[16,32,128]{2,1,0:T(8,128)(2,1)S(1)}, u32[]{:S(2)}, u32[]{:S(2)}) async-start(bf16[16,32,128]{2,1,0:T(8,128)(2,1)} %reshape.11), calls=%async_computation | async-start | bytes 262144 | tf_op jit(solution)/shard_map/all_to_all | solution.py:312
  37.7 2.9 %shard_map.56 = (bf16[1024,1024]{1,0:T(8,128)(2,1)S(1)}, f32[8,128]{1,0:T(8,128)}) custom-call(bf16[2,256,1024]{2,1,0:T(8,128)(2,1)S(1)} %shard_map.55.a, bf16[2,256,1024]{2,1,0:T(8,128)(2,1)} %collective-permute-done.3.d), custom_call_target="tpu_custom_call" | custom-call | tf_op jit(solution)/shard_map/pallas_call | solution.py:135
  40.7 8.0 %collective-permute-done.4.b = bf16[2,256,1024]{2,1,0:T(8,128)(2,1)} collective-permute-done((bf16[2,256,1024]{2,1,0:T(8,128)(2,1)S(1)}, bf16[2,256,1024]{2,1,0:T(8,128)(2,1)}, u32[]{:S(2)}, u32[]{:S(2)}) %collective-permute-start.4) | collective-permute-done | bytes 1048608 | tf_op jit(solution)/shard_map/ppermute | solution.py:41
  48.7 4.2 %shard_map.57 = (bf16[1024,1024]{1,0:T(8,128)(2,1)}, f32[8,128]{1,0:T(8,128)S(1)}) custom-call(bf16[1024,1024]{1,0:T(8,128)(2,1)S(1)} %get-tuple-element.12.part, bf16[2,256,1024]{2,1,0:T(8,128)(2,1)} %collective-permute-done.4.b, bf16[2,256,1024]{2,1,0:T(8,128)(2,1)} %collective-permute-done.5.c), custom_call_target="tpu_custom_call" | custom-call | tf_op jit(solution)/shard_map/pallas_call | solution.py:142
  52.9 11.6 %collective-permute-start.6 = (bf16[1024,1024]{1,0:T(8,128)(2,1)}, bf16[1024,1024]{1,0:T(8,128)(2,1)}, u32[]{:S(2)}, u32[]{:S(2)}) collective-permute-start(bf16[1024,1024]{1,0:T(8,128)(2,1)} %get-tuple-element.13.own), channel_id=1, source_target_pairs={{0,16},{16,0},{32,48},{48,32},{64,80},{80,64},{96,112},{112,96},{1... | collective-permute-start | bytes 6291464 | tf_op jit(solution)/shard_map/ppermute | solution.py:319
  64.5 0.6 shard_map.58.panel
  65.2 1.8 %shard_map.59.bias = f32[64,1024]{1,0:T(8,128)S(1)} custom-call(bf16[64,1024]{1,0:T(8,128)(2,1)S(1)} %shard_map.58.panel, bf16[2,256,1024]{2,1,0:T(8,128)(2,1)S(1)} %shard_map.55.a, bf16[2,256,1024]{2,1,0:T(8,128)(2,1)} %collective-permute-done.4.b, bf16[2,256,1024]{2,1,0:T(8,128)(2,1)} %collective-permute-done.5.c, ...), custom_call_target="tpu_custom_call" | custom-call | flops 42949672960 | bytes 6291456 | tf_op jit(solution)/shard_map/pallas_call | solution.py:158
  67.0 1.3 collective-permute-start.7
  68.4 2.1 %collective-permute-done.7.bias_got = f32[64,1024]{1,0:T(8,128)S(1)} collective-permute-done((f32[64,1024]{1,0:T(8,128)S(1)}, f32[64,1024]{1,0:T(8,128)S(1)}, u32[]{:S(2)}, u32[]{:S(2)}) %collective-permute-start.7) | collective-permute-done | bytes 262176 | tf_op jit(solution)/shard_map/ppermute | solution.py:320
  70.5 4.9 %shard_map.60 = (bf16[1024,1024]{1,0:T(8,128)(2,1)S(1)}, bf16[1024,1024]{1,0:T(8,128)(2,1)S(1)}, f32[64,1024]{1,0:T(8,128)S(1)}, f32[8,128]{1,0:T(8,128)S(1)}) custom-call(s32[1]{0:T(128)} %bitcast.18.core, bf16[1024,1024]{1,0:T(8,128)(2,1)} %get-tuple-element.13.own, bf16[1024,1024]{1,0:T(8,128)(2,1)} %collective-permute-done.6.got, ...), custom_call_target="tpu_custom_call" | custom-call | flops 2147483648 | bytes 6291456 | tf_op jit(solution)/shard_map/pallas_call | solution.py:194
  75.4 1.3 collective-permute-start.8
  76.8 1.6 %collective-permute-done.8.ready = f32[8,128]{1,0:T(8,128)S(1)} collective-permute-done((f32[8,128]{1,0:T(8,128)S(1)}, f32[8,128]{1,0:T(8,128)S(1)}, u32[]{:S(2)}, u32[]{:S(2)}) %collective-permute-start.8) | collective-permute-done | bytes 4128 | tf_op jit(solution)/shard_map/ppermute | solution.py:328
  78.5 0.5 fusion
  79.0 0.7 collective-permute-start.9
  79.7 0.5 fusion.1
  80.2 0.7 collective-permute-start.10
  80.9 0.5 fusion.2
  81.4 0.7 collective-permute-start.11
  82.1 0.5 fusion.3
  82.6 0.7 collective-permute-start.12
  83.4 0.5 fusion.4
  83.9 1.3 collective-permute-start.13
  85.2 19.7 %collective-permute-done.13 = bf16[64,1024]{1,0:T(8,128)(2,1)S(1)} collective-permute-done((bf16[64,1024]{1,0:T(8,128)(2,1)S(1)}, bf16[64,1024]{1,0:T(8,128)(2,1)S(1)}, u32[]{:S(2)}, u32[]{:S(2)}) %collective-permute-start.13) | collective-permute-done | bytes 131104 | tf_op jit(solution)/shard_map/ppermute | solution.py:337
  104.9 0.5 fusion.5
  105.4 0.7 collective-permute-start.14
  106.1 0.5 fusion.6
  106.6 0.8 collective-permute-start.15
  107.5 0.5 fusion.7
  108.0 0.7 collective-permute-start.16
  108.8 0.5 fusion.8
  109.3 0.7 collective-permute-start.17
  109.9 0.5 convolution_add_fusion.v_odd
  110.5 0.5 convert_select_fusion
  111.0 6.1 %collective-permute-start.18 = (bf16[64,1024]{1,0:T(8,128)(2,1)S(1)}, bf16[64,1024]{1,0:T(8,128)(2,1)S(1)}, u32[]{:S(2)}, u32[]{:S(2)}) collective-permute-start(bf16[64,1024]{1,0:T(8,128)(2,1)S(1)} %get-tuple-element.19), channel_id=1, source_target_pairs={{0,16},{16,0},{32,48},{48,32},{64,80},{80,64},{96,112},{112,96},{1... | collective-permute-start | bytes 393224 | tf_op jit(solution)/shard_map/ppermute | solution.py:341
  117.0 1.0 collective-permute-done.18.other
  118.0 4.4 %collective-permute-start.21 = (bf16[64,1024]{1,0:T(8,128)(2,1)S(1)}, bf16[64,1024]{1,0:T(8,128)(2,1)S(1)}, u32[]{:S(2)}, u32[]{:S(2)}) collective-permute-start(bf16[64,1024]{1,0:T(8,128)(2,1)S(1)} %broadcast_select_fusion), channel_id=1, source_target_pairs={{0,2},{1,3},{2,0},{3,1},{4,6},{5,7},{6,4},{7,5},{8,10},{9,11},{10,... | collective-permute-start | bytes 393224 | tf_op jit(solution)/shard_map/ppermute | solution.py:41
  122.5 2.8 %collective-permute-start.20 = (bf16[64,1024]{1,0:T(8,128)(2,1)S(1)}, bf16[64,1024]{1,0:T(8,128)(2,1)S(1)}, u32[]{:S(2)}, u32[]{:S(2)}) collective-permute-start(bf16[64,1024]{1,0:T(8,128)(2,1)S(1)} %broadcast_select_fusion), channel_id=1, source_target_pairs={{0,3},{1,0},{2,1},{3,2},{4,7},{5,4},{6,5},{7,6},{8,11},{9,8},{10,9... | collective-permute-start | bytes 393224 | tf_op jit(solution)/shard_map/ppermute | solution.py:41
  125.3 2.4 %collective-permute-start.19 = (bf16[64,1024]{1,0:T(8,128)(2,1)S(1)}, bf16[64,1024]{1,0:T(8,128)(2,1)S(1)}, u32[]{:S(2)}, u32[]{:S(2)}) collective-permute-start(bf16[64,1024]{1,0:T(8,128)(2,1)S(1)} %broadcast_select_fusion), channel_id=1, source_target_pairs={{0,1},{1,2},{2,3},{3,0},{4,5},{5,6},{6,7},{7,4},{8,9},{9,10},{10,1... | collective-permute-start | bytes 393224 | tf_op jit(solution)/shard_map/ppermute | solution.py:41
  127.8 0.7 collective-permute-start.25
  128.5 0.7 collective-permute-start.26
  129.2 3.4 %collective-permute-done.19 = bf16[64,1024]{1,0:T(8,128)(2,1)S(1)} collective-permute-done((bf16[64,1024]{1,0:T(8,128)(2,1)S(1)}, bf16[64,1024]{1,0:T(8,128)(2,1)S(1)}, u32[]{:S(2)}, u32[]{:S(2)}) %collective-permute-start.19) | collective-permute-done | bytes 131104 | tf_op jit(solution)/shard_map/ppermute | solution.py:41
  132.6 1.9 %collective-permute-start.22 = (bf16[256,1024]{1,0:T(8,128)(2,1)S(1)}, bf16[256,1024]{1,0:T(8,128)(2,1)S(1)}, u32[]{:S(2)}, u32[]{:S(2)}) collective-permute-start(bf16[256,1024]{1,0:T(8,128)(2,1)S(1)} %pad_maximum_fusion.a.ready), channel_id=1, source_target_pairs={{0,4},{1,5},{2,6},{3,7},{4,8},{5,9},{6,10},{7,11},{8,12},{9,13},{1... | collective-permute-start | bytes 1572872 | tf_op jit(solution)/shard_map/ppermute | solution.py:41
  134.5 4.6 %collective-permute-start.23 = (bf16[256,1024]{1,0:T(8,128)(2,1)S(1)}, bf16[256,1024]{1,0:T(8,128)(2,1)}, u32[]{:S(2)}, u32[]{:S(2)}) collective-permute-start(bf16[256,1024]{1,0:T(8,128)(2,1)S(1)} %pad_maximum_fusion.a.ready), channel_id=1, source_target_pairs={{0,12},{1,13},{2,14},{3,15},{4,0},{5,1},{6,2},{7,3},{8,4},{9,5},{1... | collective-permute-start | bytes 1572872 | tf_op jit(solution)/shard_map/ppermute | solution.py:41
  139.1 1.9 %collective-permute-start.24 = (bf16[256,1024]{1,0:T(8,128)(2,1)S(1)}, bf16[256,1024]{1,0:T(8,128)(2,1)}, u32[]{:S(2)}, u32[]{:S(2)}) collective-permute-start(bf16[256,1024]{1,0:T(8,128)(2,1)S(1)} %pad_maximum_fusion.a.ready), channel_id=1, source_target_pairs={{0,8},{1,9},{2,10},{3,11},{4,12},{5,13},{6,14},{7,15},{8,0},{9,1},... | collective-permute-start | bytes 1572872 | tf_op jit(solution)/shard_map/ppermute | solution.py:41
  141.1 0.7 shard_map.63.entry
  141.7 1.3 collective-permute-start.27
  143.0 1.3 collective-permute-start.28
  144.4 5.8 %collective-permute-done.28.last = bf16[64,1024]{1,0:T(8,128)(2,1)} collective-permute-done((bf16[64,1024]{1,0:T(8,128)(2,1)}, bf16[64,1024]{1,0:T(8,128)(2,1)}, u32[]{:S(2)}, u32[]{:S(2)}) %collective-permute-start.28) | collective-permute-done | bytes 131104 | tf_op jit(solution)/shard_map/ppermute | solution.py:47
  150.2 1.1 shard_map.64.entry
  151.3 1.4 collective-permute-start.29
  152.8 1.4 shard_map.62.maps
  154.2 1.7 %shard_map.65 = f32[64,1024]{1,0:T(8,128)} custom-call(s32[2]{0:T(128)S(1)} %add_convert_fusion.flags, bf16[1024,1024]{1,0:T(8,128)(2,1)S(1)} %shard_map.62.maps, bf16[64,1024]{1,0:T(8,128)(2,1)S(1)} %shard_map.64.entry, bf16[64,1024]{1,0:T(8,128)(2,1)S(1)} %collective-permute-done.29.across, bf16[64,1024]{1,0:T(8,128)(2,1)S(1)} %copy-done.2, ...), custom_call_target="tpu_custom_call" | custom-call | tf_op jit(solution)/shard_map/pallas_call | solution.py:279
  (48 shorter events, 1.3 us)
Async XLA Ops:
  0.0 30.2 %copy-start = (bf16[1024,1024]{1,0:T(8,128)(2,1)S(1)}, bf16[1024,1024]{1,0:T(8,128)(2,1)}, u32[]{:S(2)}) copy-start(bf16[1024,1024]{1,0:T(8,128)(2,1)} %param.8) | copy-start | bytes 6291460
  0.0 30.2 %copy-start.3 = (bf16[1,1024,64]{1,2,0:T(8,128)(2,1)S(1)}, bf16[1,1024,64]{1,2,0:T(8,128)(2,1)}, u32[]{:S(2)}) copy-start(bf16[1,1024,64]{1,2,0:T(8,128)(2,1)} %param.7) | copy-start | bytes 393220
  2.8 11.0 %collective-permute-start = (bf16[2,64,1024]{2,1,0:T(8,128)(2,1)S(1)}, bf16[2,64,1024]{2,1,0:T(8,128)(2,1)S(1)}, u32[]{:S(2)}, u32[]{:S(2)}) collective-permute-start(bf16[2,64,1024]{2,1,0:T(8,128)(2,1)S(1)} %pad_maximum_fusion.1.a), channel_id=1, source_target_pairs={{0,1},{1,2},{2,3},{3,0},{4,5},{5,6},{6,7},{7,4},{8,9},{9,10},{10,1... | collective-permute-start | bytes 786440 | tf_op jit(solution)/shard_map/ppermute | solution.py:41
  6.8 7.1 %collective-permute-start.1 = (bf16[2,64,1024]{2,1,0:T(8,128)(2,1)S(1)}, bf16[2,64,1024]{2,1,0:T(8,128)(2,1)S(1)}, u32[]{:S(2)}, u32[]{:S(2)}) collective-permute-start(bf16[2,64,1024]{2,1,0:T(8,128)(2,1)S(1)} %pad_maximum_fusion.1.a), channel_id=1, source_target_pairs={{0,3},{1,0},{2,1},{3,2},{4,7},{5,4},{6,5},{7,6},{8,11},{9,8},{10,9... | collective-permute-start | bytes 786440 | tf_op jit(solution)/shard_map/ppermute | solution.py:41
  10.2 8.6 %collective-permute-start.2 = (bf16[2,64,1024]{2,1,0:T(8,128)(2,1)S(1)}, bf16[2,64,1024]{2,1,0:T(8,128)(2,1)S(1)}, u32[]{:S(2)}, u32[]{:S(2)}) collective-permute-start(bf16[2,64,1024]{2,1,0:T(8,128)(2,1)S(1)} %pad_maximum_fusion.1.a), channel_id=1, source_target_pairs={{0,2},{1,3},{2,0},{3,1},{4,6},{5,7},{6,4},{7,5},{8,10},{9,11},{10,... | collective-permute-start | bytes 786440 | tf_op jit(solution)/shard_map/ppermute | solution.py:41
  19.0 18.7 %collective-permute-start.3 = (bf16[2,256,1024]{2,1,0:T(8,128)(2,1)S(1)}, bf16[2,256,1024]{2,1,0:T(8,128)(2,1)}, u32[]{:S(2)}, u32[]{:S(2)}) collective-permute-start(bf16[2,256,1024]{2,1,0:T(8,128)(2,1)S(1)} %shard_map.55.a), channel_id=1, source_target_pairs={{0,8},{1,9},{2,10},{3,11},{4,12},{5,13},{6,14},{7,15},{8,0},{9,1},... | collective-permute-start | bytes 3145736 | tf_op jit(solution)/shard_map/ppermute | solution.py:41
  23.7 25.0 %collective-permute-start.4 = (bf16[2,256,1024]{2,1,0:T(8,128)(2,1)S(1)}, bf16[2,256,1024]{2,1,0:T(8,128)(2,1)}, u32[]{:S(2)}, u32[]{:S(2)}) collective-permute-start(bf16[2,256,1024]{2,1,0:T(8,128)(2,1)S(1)} %shard_map.55.a), channel_id=1, source_target_pairs={{0,4},{1,5},{2,6},{3,7},{4,8},{5,9},{6,10},{7,11},{8,12},{9,13},{1... | collective-permute-start | bytes 3145736 | tf_op jit(solution)/shard_map/ppermute | solution.py:41
  25.9 22.8 %collective-permute-start.5 = (bf16[2,256,1024]{2,1,0:T(8,128)(2,1)S(1)}, bf16[2,256,1024]{2,1,0:T(8,128)(2,1)}, u32[]{:S(2)}, u32[]{:S(2)}) collective-permute-start(bf16[2,256,1024]{2,1,0:T(8,128)(2,1)S(1)} %shard_map.55.a), channel_id=1, source_target_pairs={{0,12},{1,13},{2,14},{3,15},{4,0},{5,1},{6,2},{7,3},{8,4},{9,5},{1... | collective-permute-start | bytes 3145736 | tf_op jit(solution)/shard_map/ppermute | solution.py:41
  33.9 30.6 %all-to-all-start = ((bf16[16,32,128]{2,1,0:T(8,128)(2,1)}), bf16[16,32,128]{2,1,0:T(8,128)(2,1)S(1)}, u32[]{:S(2)}, u32[]{:S(2)}) async-start(bf16[16,32,128]{2,1,0:T(8,128)(2,1)} %reshape.11), calls=%async_computation | async-start | bytes 262144 | tf_op jit(solution)/shard_map/all_to_all | solution.py:312
  52.9 17.5 %collective-permute-start.6 = (bf16[1024,1024]{1,0:T(8,128)(2,1)}, bf16[1024,1024]{1,0:T(8,128)(2,1)}, u32[]{:S(2)}, u32[]{:S(2)}) collective-permute-start(bf16[1024,1024]{1,0:T(8,128)(2,1)} %get-tuple-element.13.own), channel_id=1, source_target_pairs={{0,16},{16,0},{32,48},{48,32},{64,80},{80,64},{96,112},{112,96},{1... | collective-permute-start | bytes 6291464 | tf_op jit(solution)/shard_map/ppermute | solution.py:319
  67.0 3.4 %collective-permute-start.7 = (f32[64,1024]{1,0:T(8,128)S(1)}, f32[64,1024]{1,0:T(8,128)S(1)}, u32[]{:S(2)}, u32[]{:S(2)}) collective-permute-start(f32[64,1024]{1,0:T(8,128)S(1)} %shard_map.59.bias), channel_id=1, source_target_pairs={{0,16},{32,48},{64,80},{96,112},{128,144},{160,176},{192,208},{224... | collective-permute-start | bytes 786440 | tf_op jit(solution)/shard_map/ppermute | solution.py:320
  75.4 3.1 %collective-permute-start.8 = (f32[8,128]{1,0:T(8,128)S(1)}, f32[8,128]{1,0:T(8,128)S(1)}, u32[]{:S(2)}, u32[]{:S(2)}) collective-permute-start(f32[8,128]{1,0:T(8,128)S(1)} %get-tuple-element.15), channel_id=1, source_target_pairs={{0,16},{32,48},{64,80},{96,112},{128,144},{160,176},{1,17},{33,49}... | collective-permute-start | bytes 12296 | tf_op jit(solution)/shard_map/ppermute | solution.py:328
  79.0 0.7 collective-permute-start.9
  80.2 0.7 collective-permute-start.10
  81.4 0.7 collective-permute-start.11
  82.6 0.7 collective-permute-start.12
  83.9 21.0 %collective-permute-start.13 = (bf16[64,1024]{1,0:T(8,128)(2,1)S(1)}, bf16[64,1024]{1,0:T(8,128)(2,1)S(1)}, u32[]{:S(2)}, u32[]{:S(2)}) collective-permute-start(bf16[64,1024]{1,0:T(8,128)(2,1)S(1)} %fusion.4), channel_id=1, source_target_pairs={{368,336},{32,0},{48,16},{369,337},{33,1},{49,17},{370,338},{34,2}... | collective-permute-start | bytes 393224 | tf_op jit(solution)/shard_map/ppermute | solution.py:337
  105.4 0.7 collective-permute-start.14
  106.6 0.9 collective-permute-start.15
  108.0 0.7 collective-permute-start.16
  109.3 0.7 collective-permute-start.17
  111.0 7.0 %collective-permute-start.18 = (bf16[64,1024]{1,0:T(8,128)(2,1)S(1)}, bf16[64,1024]{1,0:T(8,128)(2,1)S(1)}, u32[]{:S(2)}, u32[]{:S(2)}) collective-permute-start(bf16[64,1024]{1,0:T(8,128)(2,1)S(1)} %get-tuple-element.19), channel_id=1, source_target_pairs={{0,16},{16,0},{32,48},{48,32},{64,80},{80,64},{96,112},{112,96},{1... | collective-permute-start | bytes 393224 | tf_op jit(solution)/shard_map/ppermute | solution.py:341
  118.0 11.1 %copy-start.1 = (bf16[64,1024]{1,0:T(8,128)(2,1)}, bf16[64,1024]{1,0:T(8,128)(2,1)S(1)}, u32[]{:S(2)}) copy-start(bf16[64,1024]{1,0:T(8,128)(2,1)S(1)} %collective-permute-done.18.other) | copy-start | bytes 393220
  118.0 11.1 %collective-permute-start.21 = (bf16[64,1024]{1,0:T(8,128)(2,1)S(1)}, bf16[64,1024]{1,0:T(8,128)(2,1)S(1)}, u32[]{:S(2)}, u32[]{:S(2)}) collective-permute-start(bf16[64,1024]{1,0:T(8,128)(2,1)S(1)} %broadcast_select_fusion), channel_id=1, source_target_pairs={{0,2},{1,3},{2,0},{3,1},{4,6},{5,7},{6,4},{7,5},{8,10},{9,11},{10,... | collective-permute-start | bytes 393224 | tf_op jit(solution)/shard_map/ppermute | solution.py:41
  122.5 6.7 %collective-permute-start.20 = (bf16[64,1024]{1,0:T(8,128)(2,1)S(1)}, bf16[64,1024]{1,0:T(8,128)(2,1)S(1)}, u32[]{:S(2)}, u32[]{:S(2)}) collective-permute-start(bf16[64,1024]{1,0:T(8,128)(2,1)S(1)} %broadcast_select_fusion), channel_id=1, source_target_pairs={{0,3},{1,0},{2,1},{3,2},{4,7},{5,4},{6,5},{7,6},{8,11},{9,8},{10,9... | collective-permute-start | bytes 393224 | tf_op jit(solution)/shard_map/ppermute | solution.py:41
  125.3 7.2 %collective-permute-start.19 = (bf16[64,1024]{1,0:T(8,128)(2,1)S(1)}, bf16[64,1024]{1,0:T(8,128)(2,1)S(1)}, u32[]{:S(2)}, u32[]{:S(2)}) collective-permute-start(bf16[64,1024]{1,0:T(8,128)(2,1)S(1)} %broadcast_select_fusion), channel_id=1, source_target_pairs={{0,1},{1,2},{2,3},{3,0},{4,5},{5,6},{6,7},{7,4},{8,9},{9,10},{10,1... | collective-permute-start | bytes 393224 | tf_op jit(solution)/shard_map/ppermute | solution.py:41
  127.8 13.3 %collective-permute-start.25 = (bf16[64,1024]{1,0:T(8,128)(2,1)S(1)}, bf16[64,1024]{1,0:T(8,128)(2,1)S(1)}, u32[]{:S(2)}, u32[]{:S(2)}) collective-permute-start(bf16[64,1024]{1,0:T(8,128)(2,1)S(1)} %get-tuple-element.20.edge), channel_id=1, source_target_pairs={{208,176},{209,177},{210,178},{211,179},{212,180},{213,181},{214,1... | collective-permute-start | bytes 393224 | tf_op jit(solution)/shard_map/ppermute | solution.py:47
  128.5 12.6 %collective-permute-start.26 = (bf16[64,1024]{1,0:T(8,128)(2,1)S(1)}, bf16[64,1024]{1,0:T(8,128)(2,1)S(1)}, u32[]{:S(2)}, u32[]{:S(2)}) collective-permute-start(bf16[64,1024]{1,0:T(8,128)(2,1)S(1)} %get-tuple-element.20.edge), channel_id=1, source_target_pairs={{208,80},{209,81},{210,82},{211,83},{212,84},{213,85},{214,86},{21... | collective-permute-start | bytes 393224 | tf_op jit(solution)/shard_map/ppermute | solution.py:47
  132.6 20.2 %collective-permute-start.22 = (bf16[256,1024]{1,0:T(8,128)(2,1)S(1)}, bf16[256,1024]{1,0:T(8,128)(2,1)S(1)}, u32[]{:S(2)}, u32[]{:S(2)}) collective-permute-start(bf16[256,1024]{1,0:T(8,128)(2,1)S(1)} %pad_maximum_fusion.a.ready), channel_id=1, source_target_pairs={{0,4},{1,5},{2,6},{3,7},{4,8},{5,9},{6,10},{7,11},{8,12},{9,13},{1... | collective-permute-start | bytes 1572872 | tf_op jit(solution)/shard_map/ppermute | solution.py:41
  134.5 18.3 %collective-permute-start.23 = (bf16[256,1024]{1,0:T(8,128)(2,1)S(1)}, bf16[256,1024]{1,0:T(8,128)(2,1)}, u32[]{:S(2)}, u32[]{:S(2)}) collective-permute-start(bf16[256,1024]{1,0:T(8,128)(2,1)S(1)} %pad_maximum_fusion.a.ready), channel_id=1, source_target_pairs={{0,12},{1,13},{2,14},{3,15},{4,0},{5,1},{6,2},{7,3},{8,4},{9,5},{1... | collective-permute-start | bytes 1572872 | tf_op jit(solution)/shard_map/ppermute | solution.py:41
  139.1 13.7 %collective-permute-start.24 = (bf16[256,1024]{1,0:T(8,128)(2,1)S(1)}, bf16[256,1024]{1,0:T(8,128)(2,1)}, u32[]{:S(2)}, u32[]{:S(2)}) collective-permute-start(bf16[256,1024]{1,0:T(8,128)(2,1)S(1)} %pad_maximum_fusion.a.ready), channel_id=1, source_target_pairs={{0,8},{1,9},{2,10},{3,11},{4,12},{5,13},{6,14},{7,15},{8,0},{9,1},... | collective-permute-start | bytes 1572872 | tf_op jit(solution)/shard_map/ppermute | solution.py:41
  141.7 2.7 %collective-permute-start.27 = (bf16[64,1024]{1,0:T(8,128)(2,1)}, bf16[64,1024]{1,0:T(8,128)(2,1)}, u32[]{:S(2)}, u32[]{:S(2)}) collective-permute-start(bf16[64,1024]{1,0:T(8,128)(2,1)} %shard_map.63.entry), channel_id=1, source_target_pairs={{176,144},{80,48},{177,145},{81,49},{178,146},{82,50},{179,147},{8... | collective-permute-start | bytes 393224 | tf_op jit(solution)/shard_map/ppermute | solution.py:47
  143.0 7.2 %collective-permute-start.28 = (bf16[64,1024]{1,0:T(8,128)(2,1)}, bf16[64,1024]{1,0:T(8,128)(2,1)}, u32[]{:S(2)}, u32[]{:S(2)}) collective-permute-start(bf16[64,1024]{1,0:T(8,128)(2,1)} %shard_map.63.entry), channel_id=1, source_target_pairs={{176,112},{80,16},{177,113},{81,17},{178,114},{82,18},{179,115},{8... | collective-permute-start | bytes 393224 | tf_op jit(solution)/shard_map/ppermute | solution.py:47
  151.3 2.9 %copy-start.2 = (bf16[64,1024]{1,0:T(8,128)(2,1)S(1)}, bf16[64,1024]{1,0:T(8,128)(2,1)}, u32[]{:S(2)}) copy-start(bf16[64,1024]{1,0:T(8,128)(2,1)} %copy-done.1) | copy-start | bytes 393220
  151.3 2.8 %collective-permute-start.29 = (bf16[64,1024]{1,0:T(8,128)(2,1)S(1)}, bf16[64,1024]{1,0:T(8,128)(2,1)S(1)}, u32[]{:S(2)}, u32[]{:S(2)}) collective-permute-start(bf16[64,1024]{1,0:T(8,128)(2,1)S(1)} %shard_map.64.entry), channel_id=1, source_target_pairs={{16,0},{48,32},{80,64},{112,96},{144,128},{176,160},{208,192},{240... | collective-permute-start | bytes 393224 | tf_op jit(solution)/shard_map/ppermute | solution.py:356

commit v10 on v8

--- a/solution.py
+++ b/solution.py
@@ -47,25 +47,6 @@
     return lax.ppermute(value, "depth", [(2 * a + 1, 2 * b + 1) for a, b in chip_pairs])
 
 
-def place_kernel(order, a, b, c, d, out):
-    count = out.shape[0] // 16
-    for g, block in enumerate((a, b, c, d)):
-        for f in range(4):
-            start = pl.multiple_of(order[4 * g + f] * count, count)
-            out[pl.ds(start, count), :] = block[f * count : (f + 1) * count, :]
-
-
-def place(order, blocks):
-    rows, width = blocks[0].shape
-    return pl.pallas_call(
-        place_kernel,
-        out_shape=jax.ShapeDtypeStruct((4 * rows, width), blocks[0].dtype),
-        in_specs=[SMEM] + [VMEM] * 4,
-        out_specs=VMEM,
-        compiler_params=PARAMS,
-    )(order, *blocks)
-
-
 def pack_kernel(a, b, c, d, out):
     count = a.shape[1]
     wide = out.shape[1]
@@ -101,12 +82,11 @@
         out[cut, :] = half_product(a, d, cut).astype(BF16)
 
 
-def step_kernel(part, b, c, step, token):
+def step_kernel(part, b_left, b_right, c_left, c_right, step, token):
     token[...] = jnp.zeros_like(token)
-    wide = b.shape[1]
-    for m in range(step.shape[0] // wide):
-        cut = slice(m * wide, (m + 1) * wide)
-        step[cut, :] = (-(part[cut, :].astype(F32) + half_product(b, c, cut))).astype(BF16)
+    left = jnp.concatenate([b_left[0], c_left[0]], axis=1)
+    right = jnp.concatenate([b_right[0], c_right[0]])
+    step[...] = (-(part[...].astype(F32) + mm(left, right))).astype(BF16)
 
 
 def bias_kernel(panel, a, b, c, d, bias):
@@ -139,13 +119,17 @@
         out_specs=[VMEM, VMEM],
         compiler_params=PARAMS,
     )(a, d)
+    rows_of = pl.BlockSpec((wide, width), lambda m: (m, 0))
+    left = pl.BlockSpec((1, wide, wide), lambda m: (1, 0, m))
+    right = pl.BlockSpec((1, wide, width), lambda m: (0, 0, 0))
     step, ready = pl.pallas_call(
         step_kernel,
         out_shape=[whole, token],
-        in_specs=[VMEM] * 3,
-        out_specs=[VMEM, VMEM],
-        compiler_params=PARAMS,
-    )(part, b, c)
+        grid=(width // wide,),
+        in_specs=[rows_of, left, right, left, right],
+        out_specs=[rows_of, pl.BlockSpec((8, 128), lambda m: (0, 0))],
+        compiler_params=PARAMS,
+    )(part, b, b, c, c)
     rows = 2 * panel.shape[1]
     panel = pl.pallas_call(
         cut_kernel,
@@ -238,8 +222,27 @@
     )(flags, entry, relayed, last, edge)
 
 
-def close_kernel(flags, maps, entry, across, other, v_odd, out):
+def close_kernel(flags, order, a, b, c, d, entry, across, other, v_odd, out, maps, sems):
     low, below = flags[0] != 0, flags[1] != 0
+    count = maps.shape[0] // 16
+
+    @pl.when(below)
+    def _():
+        copies = []
+        for g, block in enumerate((a, b, c, d)):
+            for f in range(4):
+                start = pl.multiple_of(order[4 * g + f] * count, count)
+                copies.append(
+                    pltpu.make_async_copy(
+                        block.at[pl.ds(f * count, count), :],
+                        maps.at[pl.ds(start, count), :],
+                        sems.at[4 * g + f],
+                    )
+                )
+        for copy in copies:
+            copy.start()
+        for copy in copies:
+            copy.wait()
 
     @pl.when(low & below)
     def _():
@@ -258,14 +261,16 @@
         out[...] = v_odd[...]
 
 
-def closed(flags, maps, entry, across, other, v_odd):
+def closed(flags, order, blocks, entry, across, other, v_odd):
+    width = entry.shape[1]
     return pl.pallas_call(
         close_kernel,
         out_shape=jax.ShapeDtypeStruct(entry.shape, F32),
-        in_specs=[SMEM] + [VMEM] * 5,
-        out_specs=VMEM,
-        compiler_params=PARAMS,
-    )(flags, maps, entry, across, other, v_odd)
+        in_specs=[SMEM, SMEM] + [pl.BlockSpec(memory_space=pl.ANY)] * 4 + [VMEM] * 4,
+        out_specs=VMEM,
+        scratch_shapes=[pltpu.VMEM((width, width), BF16), pltpu.SemaphoreType.DMA((16,))],
+        compiler_params=PARAMS,
+    )(flags, order, *blocks, entry, across, other, v_odd)
 
 
 def body(inv_diag, couple, arrow, corner, band_offset):
@@ -330,12 +335,12 @@
     relayed = sent_down(entry, [(near, near - 1), (far, far - 1)])
     last = [(source, source - 2) for source, low_end in ((near, far), (far, -1)) if source - 2 > low_end]
     last = sent_down(entry, last)
-    maps = place(order, ring_gather(ring, depths, True))
+    blocks = ring_gather(ring, depths, True)
     below = chip < lower
     flags = jnp.stack([low, below]).astype(jnp.int32)
     entry = settled(flags, entry, relayed, last, edge)
     across = lax.ppermute(entry, "depth", [(2 * k + 1, 2 * k) for k in range(chips)])
-    return closed(flags, maps, entry, across, other, v_odd)[None]
+    return closed(flags, order, blocks, entry, across, other, v_odd)[None]
 
 
 def solution(mesh):

time: 154 us -> 155 us (level)
    pallas_call x1, Pallas kernels: 1.74 us -> 4.02 us  [closed(): pl.pallas_call(close_kernel, out_shape=jax.ShapeDtypeStruct(entry.shape,...]
    pallas_call x2 -> x1, Pallas kernels: 5.56 us -> 4.84 us  [step_terms(): pl.pallas_call(step_kernel, out_shape=[whole, token], grid=(width // wide...]
  transfers between devices with their start and end apart: 30 -> 30, of which waited for: 9 -> 10; matrix products, arithmetic and copies ran while one was open for 3% -> 2% of each run, Pallas kernels for 8% -> 7%
where the time goes in v10:
time: 155 us; the launch traced here: 154 us
  starting transfers between devices  67.8 us (44%)
  waiting for transfers between devices  53.1 us (34%)
  Pallas kernels  20 us (13%)
  matrix products  6.23 us (4%)
  local copies, waits for them, and re-layouts  3.02 us (2%)
  other arithmetic  2.48 us (2%)
  between operations  1.77 us (1%)
    ppermute x12, starting transfers between devices, ring_gather(): lax.ppermute(value, BOTH, ring_moves(depths, flipped, shift))  38.1 us
    ppermute x9, waiting for transfers between devices, body(): v_in = v_in + lax.ppermute(v_even.astype(BF16), 'depth', pairs)  24.5 us
    ppermute x12, waiting for transfers between devices, ring_gather(): lax.ppermute(value, BOTH, ring_moves(depths, flipped, shift))  19.1 us
    ppermute x1, starting transfers between devices, body(): got = lax.ppermute(step, 'depth', swap)  7.51 us
    ppermute x9, starting transfers between devices, body(): v_in = v_in + lax.ppermute(v_even.astype(BF16), 'depth', pairs)  6.82 us
    dot_general x12, matrix products, mm(): return jnp.dot(a, b, preferred_element_type=F32)  6.23 us
    ppermute x1, starting transfers between devices, body(): lax.ppermute(jnp.where(low, v_odd.astype(BF16), edge), 'depth', swap[:2 *...  5.78 us
    ppermute x4, waiting for transfers between devices, sent_down(): lax.ppermute(value, 'depth', [(2 * a + 1, 2 * b + 1) for a, b in chip_pai...  5.44 us
  transfers between devices with their start and end apart: 30, of which 10 were waited for; matrix products, arithmetic and copies ran while one was open for 2% of the time, Pallas kernels for 7%

profile of v10, /device:TPU:1, one launch (start us, length us, event | category | flops | bytes accessed | tf_op | source)
XLA Modules:
  0.0 154.3 jit_solution(8858889606360301502)
XLA Ops:
  0.8 1.1 fusion.14
  1.9 0.9 pad_maximum_fusion.1.a
  2.8 5.7 %collective-permute-start.2 = (bf16[2,64,1024]{2,1,0:T(8,128)(2,1)S(1)}, bf16[2,64,1024]{2,1,0:T(8,128)(2,1)S(1)}, u32[]{:S(2)}, u32[]{:S(2)}) collective-permute-start(bf16[2,64,1024]{2,1,0:T(8,128)(2,1)S(1)} %pad_maximum_fusion.1.a), channel_id=1, source_target_pairs={{0,2},{1,3},{2,0},{3,1},{4,6},{5,7},{6,4},{7,5},{8,10},{9,11},{10,... | collective-permute-start | bytes 786440 | tf_op jit(solution)/shard_map/ppermute | solution.py:41
  8.5 2.7 %collective-permute-start.1 = (bf16[2,64,1024]{2,1,0:T(8,128)(2,1)S(1)}, bf16[2,64,1024]{2,1,0:T(8,128)(2,1)S(1)}, u32[]{:S(2)}, u32[]{:S(2)}) collective-permute-start(bf16[2,64,1024]{2,1,0:T(8,128)(2,1)S(1)} %pad_maximum_fusion.1.a), channel_id=1, source_target_pairs={{0,3},{1,0},{2,1},{3,2},{4,7},{5,4},{6,5},{7,6},{8,11},{9,8},{10,9... | collective-permute-start | bytes 786440 | tf_op jit(solution)/shard_map/ppermute | solution.py:41
  11.2 2.6 %collective-permute-start = (bf16[2,64,1024]{2,1,0:T(8,128)(2,1)S(1)}, bf16[2,64,1024]{2,1,0:T(8,128)(2,1)S(1)}, u32[]{:S(2)}, u32[]{:S(2)}) collective-permute-start(bf16[2,64,1024]{2,1,0:T(8,128)(2,1)S(1)} %pad_maximum_fusion.1.a), channel_id=1, source_target_pairs={{0,1},{1,2},{2,3},{3,0},{4,5},{5,6},{6,7},{7,4},{8,9},{9,10},{10,1... | collective-permute-start | bytes 786440 | tf_op jit(solution)/shard_map/ppermute | solution.py:41
  13.8 1.8 %collective-permute-done.1.c = bf16[2,64,1024]{2,1,0:T(8,128)(2,1)S(1)} collective-permute-done((bf16[2,64,1024]{2,1,0:T(8,128)(2,1)S(1)}, bf16[2,64,1024]{2,1,0:T(8,128)(2,1)S(1)}, u32[]{:S(2)}, u32[]{:S(2)}) %collective-permute-start.1) | collective-permute-done | bytes 262176 | tf_op jit(solution)/shard_map/ppermute | solution.py:41
  15.6 3.9 %collective-permute-done.b = bf16[2,64,1024]{2,1,0:T(8,128)(2,1)S(1)} collective-permute-done((bf16[2,64,1024]{2,1,0:T(8,128)(2,1)S(1)}, bf16[2,64,1024]{2,1,0:T(8,128)(2,1)S(1)}, u32[]{:S(2)}, u32[]{:S(2)}) %collective-permute-start) | collective-permute-done | bytes 262176 | tf_op jit(solution)/shard_map/ppermute | solution.py:41
  19.5 0.2 shard_map.55.a
  19.7 4.7 %collective-permute-start.3 = (bf16[2,256,1024]{2,1,0:T(8,128)(2,1)S(1)}, bf16[2,256,1024]{2,1,0:T(8,128)(2,1)}, u32[]{:S(2)}, u32[]{:S(2)}) collective-permute-start(bf16[2,256,1024]{2,1,0:T(8,128)(2,1)S(1)} %shard_map.55.a), channel_id=1, source_target_pairs={{0,8},{1,9},{2,10},{3,11},{4,12},{5,13},{6,14},{7,15},{8,0},{9,1},... | collective-permute-start | bytes 3145736 | tf_op jit(solution)/shard_map/ppermute | solution.py:41
  24.4 2.8 %collective-permute-start.5 = (bf16[2,256,1024]{2,1,0:T(8,128)(2,1)S(1)}, bf16[2,256,1024]{2,1,0:T(8,128)(2,1)}, u32[]{:S(2)}, u32[]{:S(2)}) collective-permute-start(bf16[2,256,1024]{2,1,0:T(8,128)(2,1)S(1)} %shard_map.55.a), channel_id=1, source_target_pairs={{0,12},{1,13},{2,14},{3,15},{4,0},{5,1},{6,2},{7,3},{8,4},{9,5},{1... | collective-permute-start | bytes 3145736 | tf_op jit(solution)/shard_map/ppermute | solution.py:41
  27.1 2.5 %collective-permute-start.4 = (bf16[2,256,1024]{2,1,0:T(8,128)(2,1)S(1)}, bf16[2,256,1024]{2,1,0:T(8,128)(2,1)}, u32[]{:S(2)}, u32[]{:S(2)}) collective-permute-start(bf16[2,256,1024]{2,1,0:T(8,128)(2,1)S(1)} %shard_map.55.a), channel_id=1, source_target_pairs={{0,4},{1,5},{2,6},{3,7},{4,8},{5,9},{6,10},{7,11},{8,12},{9,13},{1... | collective-permute-start | bytes 3145736 | tf_op jit(solution)/shard_map/ppermute | solution.py:41
  29.7 0.8 convolution_convert_fusion
  30.6 0.9 copy.8
  31.6 1.8 %reshape.11 = bf16[16,32,128]{2,1,0:T(8,128)(2,1)} reshape(bf16[16,32,2,64]{3,2,1,0:T(2,128)(2,1)} %copy.8) | data formatting | bytes 262144 | tf_op jit(solution)/shard_map/reshape | solution.py:299
  33.4 3.7 %all-to-all-start = ((bf16[16,32,128]{2,1,0:T(8,128)(2,1)}), bf16[16,32,128]{2,1,0:T(8,128)(2,1)S(1)}, u32[]{:S(2)}, u32[]{:S(2)}) async-start(bf16[16,32,128]{2,1,0:T(8,128)(2,1)} %reshape.11), calls=%async_computation | async-start | bytes 262144 | tf_op jit(solution)/shard_map/all_to_all | solution.py:300
  37.3 2.9 %shard_map.56 = (bf16[1024,1024]{1,0:T(8,128)(2,1)S(1)}, f32[8,128]{1,0:T(8,128)}) custom-call(bf16[2,256,1024]{2,1,0:T(8,128)(2,1)S(1)} %shard_map.55.a, bf16[2,256,1024]{2,1,0:T(8,128)(2,1)} %collective-permute-done.3.d), custom_call_target="tpu_custom_call" | custom-call | tf_op jit(solution)/shard_map/pallas_call | solution.py:115
  40.3 8.9 %collective-permute-done.5.c_left.c_right.c = bf16[2,256,1024]{2,1,0:T(8,128)(2,1)} collective-permute-done((bf16[2,256,1024]{2,1,0:T(8,128)(2,1)S(1)}, bf16[2,256,1024]{2,1,0:T(8,128)(2,1)}, u32[]{:S(2)}, u32[]{:S(2)}) %collective-permute-start.5) | collective-permute-done | bytes 1048608 | tf_op jit(solution)/shard_map/ppermute | solution.py:41
  49.2 4.8 %shard_map.57 = (bf16[1024,1024]{1,0:T(8,128)(2,1)}, f32[8,128]{1,0:T(8,128)S(1)}) custom-call(bf16[1024,1024]{1,0:T(8,128)(2,1)S(1)} %get-tuple-element.11.part, bf16[2,256,1024]{2,1,0:T(8,128)(2,1)} %collective-permute-done.4.b_left.b_right.b, bf16[2,256,1024]{2,1,0:T(8,128)(2,1)} %collective-permute-done.4.b_left.b_right.b, ...), custom_call_target="tpu_custom_call" | custom-call | tf_op jit(solution)/shard_map/pallas_call | solution.py:125
  54.0 7.5 %collective-permute-start.6 = (bf16[1024,1024]{1,0:T(8,128)(2,1)}, bf16[1024,1024]{1,0:T(8,128)(2,1)}, u32[]{:S(2)}, u32[]{:S(2)}) collective-permute-start(bf16[1024,1024]{1,0:T(8,128)(2,1)} %get-tuple-element.12.own), channel_id=1, source_target_pairs={{0,16},{16,0},{32,48},{48,32},{64,80},{80,64},{96,112},{112,96},{1... | collective-permute-start | bytes 6291464 | tf_op jit(solution)/shard_map/ppermute | solution.py:307
  61.6 0.6 shard_map.58.panel
  62.2 1.8 %shard_map.59.bias = f32[64,1024]{1,0:T(8,128)S(1)} custom-call(bf16[64,1024]{1,0:T(8,128)(2,1)S(1)} %shard_map.58.panel, bf16[2,256,1024]{2,1,0:T(8,128)(2,1)S(1)} %shard_map.55.a, bf16[2,256,1024]{2,1,0:T(8,128)(2,1)} %collective-permute-done.4.b_left.b_right.b, bf16[2,256,1024]{2,1,0:T(8,128)(2,1)} %collective-permute-done.5.c_left.c_right.c, ...), custom_call_target="tpu_custom_call" | custom-call | flops 42949672960 | bytes 6291456 | tf_op jit(solution)/shard_map/pallas_call | solution.py:142
  64.1 1.3 collective-permute-start.7
  65.4 2.1 %collective-permute-done.7.bias_got = f32[64,1024]{1,0:T(8,128)S(1)} collective-permute-done((f32[64,1024]{1,0:T(8,128)S(1)}, f32[64,1024]{1,0:T(8,128)S(1)}, u32[]{:S(2)}, u32[]{:S(2)}) %collective-permute-start.7) | collective-permute-done | bytes 262176 | tf_op jit(solution)/shard_map/ppermute | solution.py:308
  67.5 4.9 %shard_map.60 = (bf16[1024,1024]{1,0:T(8,128)(2,1)S(1)}, bf16[1024,1024]{1,0:T(8,128)(2,1)S(1)}, f32[64,1024]{1,0:T(8,128)S(1)}) custom-call(s32[1]{0:T(128)} %bitcast.18.core, bf16[1024,1024]{1,0:T(8,128)(2,1)} %get-tuple-element.12.own, bf16[1024,1024]{1,0:T(8,128)(2,1)} %collective-permute-done.6.got, f32[64,1024]{1,0:T(8,128)S(1)} %shard_map.59.bias, ...), custom_call_target="tpu_custom_call" | custom-call | flops 2147483648 | bytes 6291456 | tf_op jit(solution)/shard_map/pallas_call | solution.py:177
  72.4 0.5 fusion
  73.0 0.7 collective-permute-start.8
  73.7 0.6 fusion.1
  74.2 0.7 collective-permute-start.9
  74.9 0.5 fusion.2
  75.4 0.7 collective-permute-start.10
  76.3 0.5 fusion.3
  76.8 0.7 collective-permute-start.11
  77.5 0.5 fusion.4
  78.0 1.3 collective-permute-start.12
  79.3 24.5 %collective-permute-done.12 = bf16[64,1024]{1,0:T(8,128)(2,1)S(1)} collective-permute-done((bf16[64,1024]{1,0:T(8,128)(2,1)S(1)}, bf16[64,1024]{1,0:T(8,128)(2,1)S(1)}, u32[]{:S(2)}, u32[]{:S(2)}) %collective-permute-start.12) | collective-permute-done | bytes 131104 | tf_op jit(solution)/shard_map/ppermute | solution.py:323
  103.8 0.5 fusion.5
  104.3 0.7 collective-permute-start.13
  105.1 0.5 fusion.6
  105.6 0.7 collective-permute-start.14
  106.3 0.5 fusion.7
  106.8 0.7 collective-permute-start.15
  107.5 0.5 fusion.8
  108.0 0.8 collective-permute-start.16
  108.9 0.5 convolution_add_fusion.v_odd
  109.4 0.5 convert_select_fusion
  109.9 5.8 %collective-permute-start.17 = (bf16[64,1024]{1,0:T(8,128)(2,1)S(1)}, bf16[64,1024]{1,0:T(8,128)(2,1)S(1)}, u32[]{:S(2)}, u32[]{:S(2)}) collective-permute-start(bf16[64,1024]{1,0:T(8,128)(2,1)S(1)} %get-tuple-element.17), channel_id=1, source_target_pairs={{0,16},{16,0},{32,48},{48,32},{64,80},{80,64},{96,112},{112,96},{1... | collective-permute-start | bytes 393224 | tf_op jit(solution)/shard_map/ppermute | solution.py:327
  115.6 1.0 collective-permute-done.17.other
  116.6 4.4 %collective-permute-start.20 = (bf16[64,1024]{1,0:T(8,128)(2,1)S(1)}, bf16[64,1024]{1,0:T(8,128)(2,1)S(1)}, u32[]{:S(2)}, u32[]{:S(2)}) collective-permute-start(bf16[64,1024]{1,0:T(8,128)(2,1)S(1)} %broadcast_select_fusion), channel_id=1, source_target_pairs={{0,2},{1,3},{2,0},{3,1},{4,6},{5,7},{6,4},{7,5},{8,10},{9,11},{10,... | collective-permute-start | bytes 393224 | tf_op jit(solution)/shard_map/ppermute | solution.py:41
  121.1 2.8 %collective-permute-start.19 = (bf16[64,1024]{1,0:T(8,128)(2,1)S(1)}, bf16[64,1024]{1,0:T(8,128)(2,1)S(1)}, u32[]{:S(2)}, u32[]{:S(2)}) collective-permute-start(bf16[64,1024]{1,0:T(8,128)(2,1)S(1)} %broadcast_select_fusion), channel_id=1, source_target_pairs={{0,3},{1,0},{2,1},{3,2},{4,7},{5,4},{6,5},{7,6},{8,11},{9,8},{10,9... | collective-permute-start | bytes 393224 | tf_op jit(solution)/shard_map/ppermute | solution.py:41
  123.9 2.4 %collective-permute-start.18 = (bf16[64,1024]{1,0:T(8,128)(2,1)S(1)}, bf16[64,1024]{1,0:T(8,128)(2,1)S(1)}, u32[]{:S(2)}, u32[]{:S(2)}) collective-permute-start(bf16[64,1024]{1,0:T(8,128)(2,1)S(1)} %broadcast_select_fusion), channel_id=1, source_target_pairs={{0,1},{1,2},{2,3},{3,0},{4,5},{5,6},{6,7},{7,4},{8,9},{9,10},{10,1... | collective-permute-start | bytes 393224 | tf_op jit(solution)/shard_map/ppermute | solution.py:41
  126.4 0.4 collective-permute-done.19
  126.8 4.1 %collective-permute-done.18 = bf16[64,1024]{1,0:T(8,128)(2,1)S(1)} collective-permute-done((bf16[64,1024]{1,0:T(8,128)(2,1)S(1)}, bf16[64,1024]{1,0:T(8,128)(2,1)S(1)}, u32[]{:S(2)}, u32[]{:S(2)}) %collective-permute-start.18) | collective-permute-done | bytes 131104 | tf_op jit(solution)/shard_map/ppermute | solution.py:41
  130.9 1.9 %collective-permute-start.23 = (bf16[256,1024]{1,0:T(8,128)(2,1)S(1)}, bf16[256,1024]{1,0:T(8,128)(2,1)}, u32[]{:S(2)}, u32[]{:S(2)}) collective-permute-start(bf16[256,1024]{1,0:T(8,128)(2,1)S(1)} %pad_maximum_fusion.ready.a), channel_id=1, source_target_pairs={{0,8},{1,9},{2,10},{3,11},{4,12},{5,13},{6,14},{7,15},{8,0},{9,1},... | collective-permute-start | bytes 1572872 | tf_op jit(solution)/shard_map/ppermute | solution.py:41
  132.8 3.7 %collective-permute-start.22 = (bf16[256,1024]{1,0:T(8,128)(2,1)S(1)}, bf16[256,1024]{1,0:T(8,128)(2,1)}, u32[]{:S(2)}, u32[]{:S(2)}) collective-permute-start(bf16[256,1024]{1,0:T(8,128)(2,1)S(1)} %pad_maximum_fusion.ready.a), channel_id=1, source_target_pairs={{0,12},{1,13},{2,14},{3,15},{4,0},{5,1},{6,2},{7,3},{8,4},{9,5},{1... | collective-permute-start | bytes 1572872 | tf_op jit(solution)/shard_map/ppermute | solution.py:41
  136.5 1.9 %collective-permute-start.21 = (bf16[256,1024]{1,0:T(8,128)(2,1)S(1)}, bf16[256,1024]{1,0:T(8,128)(2,1)}, u32[]{:S(2)}, u32[]{:S(2)}) collective-permute-start(bf16[256,1024]{1,0:T(8,128)(2,1)S(1)} %pad_maximum_fusion.ready.a), channel_id=1, source_target_pairs={{0,4},{1,5},{2,6},{3,7},{4,8},{5,9},{6,10},{7,11},{8,12},{9,13},{1... | collective-permute-start | bytes 1572872 | tf_op jit(solution)/shard_map/ppermute | solution.py:41
  138.4 0.7 collective-permute-start.25
  139.1 0.7 collective-permute-start.24
  139.8 1.3 collective-permute-start.27
  141.1 0.7 collective-permute-start.26
  141.9 5.4 %collective-permute-done.27.last = bf16[64,1024]{1,0:T(8,128)(2,1)S(1)} collective-permute-done((bf16[64,1024]{1,0:T(8,128)(2,1)S(1)}, bf16[64,1024]{1,0:T(8,128)(2,1)S(1)}, u32[]{:S(2)}, u32[]{:S(2)}) %collective-permute-start.27) | collective-permute-done | bytes 131104 | tf_op jit(solution)/shard_map/ppermute | solution.py:47
  147.3 0.6 shard_map.62.entry
  147.9 1.3 collective-permute-start.28
  149.2 1.0 collective-permute-done.28.across
  150.2 4.0 %shard_map.63 = f32[64,1024]{1,0:T(8,128)} custom-call(s32[2]{0:T(128)S(1)} %add_convert_fusion.flags, s32[16]{0:T(128)S(1)} %stack.85.order, bf16[256,1024]{1,0:T(8,128)(2,1)S(1)} %pad_maximum_fusion.ready.a, bf16[256,1024]{1,0:T(8,128)(2,1)} %collective-permute-done.21.b, bf16[256,1024]{1,0:T(8,128)(2,1)} %collective-permute-done.22.c, ...), custom_call_target="tpu_custom_call" | custom-call | tf_op jit(solution)/shard_map/pallas_call | solution.py:266
  (37 shorter events, 0.8 us)
Async XLA Ops:
  0.0 29.7 %copy-start = (bf16[1024,1024]{1,0:T(8,128)(2,1)S(1)}, bf16[1024,1024]{1,0:T(8,128)(2,1)}, u32[]{:S(2)}) copy-start(bf16[1024,1024]{1,0:T(8,128)(2,1)} %param.8) | copy-start | bytes 6291460
  0.0 29.7 %copy-start.1 = (bf16[1,1024,64]{1,2,0:T(8,128)(2,1)S(1)}, bf16[1,1024,64]{1,2,0:T(8,128)(2,1)}, u32[]{:S(2)}) copy-start(bf16[1,1024,64]{1,2,0:T(8,128)(2,1)} %param.7) | copy-start | bytes 393220
  2.8 11.0 %collective-permute-start.2 = (bf16[2,64,1024]{2,1,0:T(8,128)(2,1)S(1)}, bf16[2,64,1024]{2,1,0:T(8,128)(2,1)S(1)}, u32[]{:S(2)}, u32[]{:S(2)}) collective-permute-start(bf16[2,64,1024]{2,1,0:T(8,128)(2,1)S(1)} %pad_maximum_fusion.1.a), channel_id=1, source_target_pairs={{0,2},{1,3},{2,0},{3,1},{4,6},{5,7},{6,4},{7,5},{8,10},{9,11},{10,... | collective-permute-start | bytes 786440 | tf_op jit(solution)/shard_map/ppermute | solution.py:41
  8.5 7.1 %collective-permute-start.1 = (bf16[2,64,1024]{2,1,0:T(8,128)(2,1)S(1)}, bf16[2,64,1024]{2,1,0:T(8,128)(2,1)S(1)}, u32[]{:S(2)}, u32[]{:S(2)}) collective-permute-start(bf16[2,64,1024]{2,1,0:T(8,128)(2,1)S(1)} %pad_maximum_fusion.1.a), channel_id=1, source_target_pairs={{0,3},{1,0},{2,1},{3,2},{4,7},{5,4},{6,5},{7,6},{8,11},{9,8},{10,9... | collective-permute-start | bytes 786440 | tf_op jit(solution)/shard_map/ppermute | solution.py:41
  11.2 8.3 %collective-permute-start = (bf16[2,64,1024]{2,1,0:T(8,128)(2,1)S(1)}, bf16[2,64,1024]{2,1,0:T(8,128)(2,1)S(1)}, u32[]{:S(2)}, u32[]{:S(2)}) collective-permute-start(bf16[2,64,1024]{2,1,0:T(8,128)(2,1)S(1)} %pad_maximum_fusion.1.a), channel_id=1, source_target_pairs={{0,1},{1,2},{2,3},{3,0},{4,5},{5,6},{6,7},{7,4},{8,9},{9,10},{10,1... | collective-permute-start | bytes 786440 | tf_op jit(solution)/shard_map/ppermute | solution.py:41
  19.7 17.6 %collective-permute-start.3 = (bf16[2,256,1024]{2,1,0:T(8,128)(2,1)S(1)}, bf16[2,256,1024]{2,1,0:T(8,128)(2,1)}, u32[]{:S(2)}, u32[]{:S(2)}) collective-permute-start(bf16[2,256,1024]{2,1,0:T(8,128)(2,1)S(1)} %shard_map.55.a), channel_id=1, source_target_pairs={{0,8},{1,9},{2,10},{3,11},{4,12},{5,13},{6,14},{7,15},{8,0},{9,1},... | collective-permute-start | bytes 3145736 | tf_op jit(solution)/shard_map/ppermute | solution.py:41
  24.4 24.9 %collective-permute-start.5 = (bf16[2,256,1024]{2,1,0:T(8,128)(2,1)S(1)}, bf16[2,256,1024]{2,1,0:T(8,128)(2,1)}, u32[]{:S(2)}, u32[]{:S(2)}) collective-permute-start(bf16[2,256,1024]{2,1,0:T(8,128)(2,1)S(1)} %shard_map.55.a), channel_id=1, source_target_pairs={{0,12},{1,13},{2,14},{3,15},{4,0},{5,1},{6,2},{7,3},{8,4},{9,5},{1... | collective-permute-start | bytes 3145736 | tf_op jit(solution)/shard_map/ppermute | solution.py:41
  27.1 22.1 %collective-permute-start.4 = (bf16[2,256,1024]{2,1,0:T(8,128)(2,1)S(1)}, bf16[2,256,1024]{2,1,0:T(8,128)(2,1)}, u32[]{:S(2)}, u32[]{:S(2)}) collective-permute-start(bf16[2,256,1024]{2,1,0:T(8,128)(2,1)S(1)} %shard_map.55.a), channel_id=1, source_target_pairs={{0,4},{1,5},{2,6},{3,7},{4,8},{5,9},{6,10},{7,11},{8,12},{9,13},{1... | collective-permute-start | bytes 3145736 | tf_op jit(solution)/shard_map/ppermute | solution.py:41
  33.4 28.2 %all-to-all-start = ((bf16[16,32,128]{2,1,0:T(8,128)(2,1)}), bf16[16,32,128]{2,1,0:T(8,128)(2,1)S(1)}, u32[]{:S(2)}, u32[]{:S(2)}) async-start(bf16[16,32,128]{2,1,0:T(8,128)(2,1)} %reshape.11), calls=%async_computation | async-start | bytes 262144 | tf_op jit(solution)/shard_map/all_to_all | solution.py:300
  54.0 13.5 %collective-permute-start.6 = (bf16[1024,1024]{1,0:T(8,128)(2,1)}, bf16[1024,1024]{1,0:T(8,128)(2,1)}, u32[]{:S(2)}, u32[]{:S(2)}) collective-permute-start(bf16[1024,1024]{1,0:T(8,128)(2,1)} %get-tuple-element.12.own), channel_id=1, source_target_pairs={{0,16},{16,0},{32,48},{48,32},{64,80},{80,64},{96,112},{112,96},{1... | collective-permute-start | bytes 6291464 | tf_op jit(solution)/shard_map/ppermute | solution.py:307
  64.1 3.4 %collective-permute-start.7 = (f32[64,1024]{1,0:T(8,128)S(1)}, f32[64,1024]{1,0:T(8,128)S(1)}, u32[]{:S(2)}, u32[]{:S(2)}) collective-permute-start(f32[64,1024]{1,0:T(8,128)S(1)} %shard_map.59.bias), channel_id=1, source_target_pairs={{0,16},{32,48},{64,80},{96,112},{128,144},{160,176},{192,208},{224... | collective-permute-start | bytes 786440 | tf_op jit(solution)/shard_map/ppermute | solution.py:308
  73.0 0.7 collective-permute-start.8
  74.2 0.7 collective-permute-start.9
  75.4 0.7 collective-permute-start.10
  76.8 0.7 collective-permute-start.11
  78.0 25.8 %collective-permute-start.12 = (bf16[64,1024]{1,0:T(8,128)(2,1)S(1)}, bf16[64,1024]{1,0:T(8,128)(2,1)S(1)}, u32[]{:S(2)}, u32[]{:S(2)}) collective-permute-start(bf16[64,1024]{1,0:T(8,128)(2,1)S(1)} %fusion.4), channel_id=1, source_target_pairs={{368,336},{32,0},{48,16},{369,337},{33,1},{49,17},{370,338},{34,2}... | collective-permute-start | bytes 393224 | tf_op jit(solution)/shard_map/ppermute | solution.py:323
  104.3 0.7 collective-permute-start.13
  105.6 0.7 collective-permute-start.14
  106.8 0.7 collective-permute-start.15
  108.0 0.9 collective-permute-start.16
  109.9 6.8 %collective-permute-start.17 = (bf16[64,1024]{1,0:T(8,128)(2,1)S(1)}, bf16[64,1024]{1,0:T(8,128)(2,1)S(1)}, u32[]{:S(2)}, u32[]{:S(2)}) collective-permute-start(bf16[64,1024]{1,0:T(8,128)(2,1)S(1)} %get-tuple-element.17), channel_id=1, source_target_pairs={{0,16},{16,0},{32,48},{48,32},{64,80},{80,64},{96,112},{112,96},{1... | collective-permute-start | bytes 393224 | tf_op jit(solution)/shard_map/ppermute | solution.py:327
  116.6 9.7 %collective-permute-start.20 = (bf16[64,1024]{1,0:T(8,128)(2,1)S(1)}, bf16[64,1024]{1,0:T(8,128)(2,1)S(1)}, u32[]{:S(2)}, u32[]{:S(2)}) collective-permute-start(bf16[64,1024]{1,0:T(8,128)(2,1)S(1)} %broadcast_select_fusion), channel_id=1, source_target_pairs={{0,2},{1,3},{2,0},{3,1},{4,6},{5,7},{6,4},{7,5},{8,10},{9,11},{10,... | collective-permute-start | bytes 393224 | tf_op jit(solution)/shard_map/ppermute | solution.py:41
  121.1 5.7 %collective-permute-start.19 = (bf16[64,1024]{1,0:T(8,128)(2,1)S(1)}, bf16[64,1024]{1,0:T(8,128)(2,1)S(1)}, u32[]{:S(2)}, u32[]{:S(2)}) collective-permute-start(bf16[64,1024]{1,0:T(8,128)(2,1)S(1)} %broadcast_select_fusion), channel_id=1, source_target_pairs={{0,3},{1,0},{2,1},{3,2},{4,7},{5,4},{6,5},{7,6},{8,11},{9,8},{10,9... | collective-permute-start | bytes 393224 | tf_op jit(solution)/shard_map/ppermute | solution.py:41
  123.9 6.9 %collective-permute-start.18 = (bf16[64,1024]{1,0:T(8,128)(2,1)S(1)}, bf16[64,1024]{1,0:T(8,128)(2,1)S(1)}, u32[]{:S(2)}, u32[]{:S(2)}) collective-permute-start(bf16[64,1024]{1,0:T(8,128)(2,1)S(1)} %broadcast_select_fusion), channel_id=1, source_target_pairs={{0,1},{1,2},{2,3},{3,0},{4,5},{5,6},{6,7},{7,4},{8,9},{9,10},{10,1... | collective-permute-start | bytes 393224 | tf_op jit(solution)/shard_map/ppermute | solution.py:41
  130.9 19.3 %collective-permute-start.23 = (bf16[256,1024]{1,0:T(8,128)(2,1)S(1)}, bf16[256,1024]{1,0:T(8,128)(2,1)}, u32[]{:S(2)}, u32[]{:S(2)}) collective-permute-start(bf16[256,1024]{1,0:T(8,128)(2,1)S(1)} %pad_maximum_fusion.ready.a), channel_id=1, source_target_pairs={{0,8},{1,9},{2,10},{3,11},{4,12},{5,13},{6,14},{7,15},{8,0},{9,1},... | collective-permute-start | bytes 1572872 | tf_op jit(solution)/shard_map/ppermute | solution.py:41
  132.8 17.4 %collective-permute-start.22 = (bf16[256,1024]{1,0:T(8,128)(2,1)S(1)}, bf16[256,1024]{1,0:T(8,128)(2,1)}, u32[]{:S(2)}, u32[]{:S(2)}) collective-permute-start(bf16[256,1024]{1,0:T(8,128)(2,1)S(1)} %pad_maximum_fusion.ready.a), channel_id=1, source_target_pairs={{0,12},{1,13},{2,14},{3,15},{4,0},{5,1},{6,2},{7,3},{8,4},{9,5},{1... | collective-permute-start | bytes 1572872 | tf_op jit(solution)/shard_map/ppermute | solution.py:41
  136.5 13.7 %collective-permute-start.21 = (bf16[256,1024]{1,0:T(8,128)(2,1)S(1)}, bf16[256,1024]{1,0:T(8,128)(2,1)}, u32[]{:S(2)}, u32[]{:S(2)}) collective-permute-start(bf16[256,1024]{1,0:T(8,128)(2,1)S(1)} %pad_maximum_fusion.ready.a), channel_id=1, source_target_pairs={{0,4},{1,5},{2,6},{3,7},{4,8},{5,9},{6,10},{7,11},{8,12},{9,13},{1... | collective-permute-start | bytes 1572872 | tf_op jit(solution)/shard_map/ppermute | solution.py:41
  138.4 1.4 collective-permute-start.25
  139.1 0.7 collective-permute-start.24
  139.8 7.5 %collective-permute-start.27 = (bf16[64,1024]{1,0:T(8,128)(2,1)S(1)}, bf16[64,1024]{1,0:T(8,128)(2,1)S(1)}, u32[]{:S(2)}, u32[]{:S(2)}) collective-permute-start(bf16[64,1024]{1,0:T(8,128)(2,1)S(1)} %shard_map.61.entry), channel_id=1, source_target_pairs={{176,112},{80,16},{177,113},{81,17},{178,114},{82,18},{179,115},{8... | collective-permute-start | bytes 393224 | tf_op jit(solution)/shard_map/ppermute | solution.py:47
  141.1 6.2 %collective-permute-start.26 = (bf16[64,1024]{1,0:T(8,128)(2,1)S(1)}, bf16[64,1024]{1,0:T(8,128)(2,1)S(1)}, u32[]{:S(2)}, u32[]{:S(2)}) collective-permute-start(bf16[64,1024]{1,0:T(8,128)(2,1)S(1)} %shard_map.61.entry), channel_id=1, source_target_pairs={{176,144},{80,48},{177,145},{81,49},{178,146},{82,50},{179,147},{8... | collective-permute-start | bytes 393224 | tf_op jit(solution)/shard_map/ppermute | solution.py:47
  147.9 2.3 %collective-permute-start.28 = (bf16[64,1024]{1,0:T(8,128)(2,1)S(1)}, bf16[64,1024]{1,0:T(8,128)(2,1)S(1)}, u32[]{:S(2)}, u32[]{:S(2)}) collective-permute-start(bf16[64,1024]{1,0:T(8,128)(2,1)S(1)} %shard_map.62.entry), channel_id=1, source_target_pairs={{16,0},{48,32},{80,64},{112,96},{144,128},{176,160},{208,192},{240... | collective-permute-start | bytes 393224 | tf_op jit(solution)/shard_map/ppermute | solution.py:342

commit v11 on v9

--- a/solution.py
+++ b/solution.py
@@ -13,8 +13,13 @@
 VMEM = pl.BlockSpec(memory_space=pltpu.VMEM)
 SMEM = pl.BlockSpec(memory_space=pltpu.SMEM)
 MIB = 1024 * 1024
-PARAMS = pltpu.CompilerParams(vmem_limit_bytes=16 * MIB)
-SMALL = pltpu.CompilerParams(vmem_limit_bytes=4 * MIB)
+
+
+def room(mib):
+    return pltpu.CompilerParams(vmem_limit_bytes=mib * MIB)
+
+
+SMALL = pltpu.CompilerParams(vmem_limit_bytes=2 * MIB)
 
 
 def mm(a, b):
@@ -37,10 +42,11 @@
 
 
 def ring_gather(value, depths, flipped):
-    return [value] + [
+    from_right, from_left, across = [
         lax.ppermute(value, BOTH, ring_moves(depths, flipped, shift))
-        for shift in (1, -1, 2)
+        for shift in (-1, 1, 2)
     ]
+    return [value, from_left, from_right, across]
 
 
 def sent_down(value, chip_pairs):
@@ -62,7 +68,7 @@
         out_shape=jax.ShapeDtypeStruct((4 * rows, width), blocks[0].dtype),
         in_specs=[SMEM] + [VMEM] * 4,
         out_specs=VMEM,
-        compiler_params=PARAMS,
+        compiler_params=room(6),
     )(order, *blocks)
 
 
@@ -84,7 +90,7 @@
         out_shape=jax.ShapeDtypeStruct((two, 4 * count, width), BF16),
         in_specs=[VMEM] * 4,
         out_specs=VMEM,
-        compiler_params=PARAMS,
+        compiler_params=room(6),
     )(*blocks)
 
 
@@ -137,15 +143,15 @@
         out_shape=[whole, token],
         in_specs=[VMEM] * 2,
         out_specs=[VMEM, VMEM],
-        compiler_params=PARAMS,
+        compiler_params=room(10),
     )(a, d)
     step, ready = pl.pallas_call(
         step_kernel,
         out_shape=[whole, token],
         in_specs=[VMEM] * 3,
         out_specs=[VMEM, VMEM],
-        compiler_params=PARAMS,
-    )(part, b, c)
+        compiler_params=room(12),
+    )(part, c, b)
     rows = 2 * panel.shape[1]
     panel = pl.pallas_call(
         cut_kernel,
@@ -161,7 +167,7 @@
         in_specs=[flat] + [pl.BlockSpec((1, wide, width), lambda i: (0, 0, 0))] * 4,
         out_specs=flat,
         grid=(1,),
-        compiler_params=PARAMS,
+        compiler_params=room(8),
         cost_estimate=pl.CostEstimate(flops=40 * width**3, bytes_accessed=6 * width**2, transcendentals=0),
     )(panel, a, b, c, d)
     return step, bias
@@ -201,7 +207,7 @@
         ],
         in_specs=[SMEM] + [VMEM] * 4,
         out_specs=[VMEM] * 4,
-        compiler_params=PARAMS,
+        compiler_params=room(14),
         cost_estimate=pl.CostEstimate(flops=2 * width**3, bytes_accessed=6 * width**2, transcendentals=0),
     )(core.reshape(1), own, got, bias, bias_got)
 
@@ -281,7 +287,7 @@
         out_shape=jax.ShapeDtypeStruct(entry.shape, F32),
         in_specs=[SMEM] + [VMEM] * 5,
         out_specs=VMEM,
-        compiler_params=PARAMS,
+        compiler_params=room(5),
     )(flags, maps, entry, across, other, v_odd)
 
 
@@ -325,8 +331,7 @@
     sizes = [chips - lower, lower]
     start = (row == col) & ((chip == tops[0]) | (chip == tops[1])) & low
     v_in = jnp.where(start, 1.0, 0.0).astype(BF16)
-    turn = lax.ppermute(turn, "depth", [(2 * k, 2 * k + 1) for k in range(lower)])
-    v_in = held(v_in, turn)
+    v_in = held(v_in, sent_down(turn, [(k + 1, k) for k in range(lower)]))
     v_even = mm(v_in, product) + add_even
     for hop in range(1, max(sizes)):
         pairs = []
@@ -345,7 +350,8 @@
     depths = range(2 * lower)
     ring = jnp.concatenate(ring_gather(map_rows, depths, False))
     near, far = lower - 1, lower // 2 - 1
-    entry = joined(sent_down(edge, [(lower, near)]), sent_down(edge, [(lower, far)]), ring)
+    to_far = sent_down(edge, [(lower, far)])
+    entry = joined(to_far, sent_down(edge, [(lower, near)]), ring)
     relayed = sent_down(entry, [(near, near - 1), (far, far - 1)])
     last = [(source, source - 2) for source, low_end in ((near, far), (far, -1)) if source - 2 > low_end]
     last = sent_down(entry, last)

time: 157 us -> 155 us (0.987)
  starting transfers between devices: 76.2 us -> 72.9 us
  waiting for transfers between devices: 46.8 us -> 48.4 us
    ppermute x1, starting transfers between devices: 6.07 us -> 2.43 us  [body(): lax.ppermute(jnp.where(low, v_odd.astype(BF16), edge), 'depth', swap[:2 *...]
    ppermute x4 -> x5, waiting for transfers between devices: 5.85 us -> 8.76 us  [sent_down(): lax.ppermute(value, 'depth', [(2 * a + 1, 2 * b + 1) for a, b in chip_pai...]
    ppermute x1 -> x0, waiting for transfers between devices: 1.63 us -> none  [body(): lax.ppermute(turn, 'depth', [(2 * k, 2 * k + 1) for k in range(lower)])]
    all_to_all x1, starting transfers between devices: 3.51 us -> 5.09 us  [body(): panel_rows = lax.all_to_all(panel, 'lat', 0, 0)]
    ppermute x4 -> x5, starting transfers between devices: 3.91 us -> 5.21 us  [sent_down(): lax.ppermute(value, 'depth', [(2 * a + 1, 2 * b + 1) for a, b in chip_pai...]
  transfers between devices with their start and end apart: 31 -> 31, of which waited for: 9 -> 10; matrix products, arithmetic and copies ran while one was open for 3% -> 3% of each run, Pallas kernels for 8% -> 8%
where the time goes in v11:
time: 155 us; the launch traced here: 154 us
  starting transfers between devices  72.9 us (47%)
  waiting for transfers between devices  48.4 us (31%)
  Pallas kernels  19.6 us (13%)
  matrix products  6.18 us (4%)
  local copies, waits for them, and re-layouts  3.01 us (2%)
  other arithmetic  2.53 us (2%)
  between operations  1.7 us (1%)
    ppermute x12, starting transfers between devices, ring_gather(): lax.ppermute(value, BOTH, ring_moves(depths, flipped, shift))  39 us
    ppermute x9, waiting for transfers between devices, body(): v_in = v_in + lax.ppermute(v_even.astype(BF16), 'depth', pairs)  20.4 us
    ppermute x12, waiting for transfers between devices, ring_gather(): lax.ppermute(value, BOTH, ring_moves(depths, flipped, shift))  16.1 us
    ppermute x1, starting transfers between devices, body(): got = lax.ppermute(step, 'depth', swap)  11.6 us
    ppermute x5, waiting for transfers between devices, sent_down(): lax.ppermute(value, 'depth', [(2 * a + 1, 2 * b + 1) for a, b in chip_pai...  8.76 us
    ppermute x9, starting transfers between devices, body(): v_in = v_in + lax.ppermute(v_even.astype(BF16), 'depth', pairs)  6.82 us
    dot_general x12, matrix products, mm(): return jnp.dot(a, b, preferred_element_type=F32)  6.18 us
    ppermute x5, starting transfers between devices, sent_down(): lax.ppermute(value, 'depth', [(2 * a + 1, 2 * b + 1) for a, b in chip_pai...  5.21 us
  transfers between devices with their start and end apart: 31, of which 10 were waited for; matrix products, arithmetic and copies ran while one was open for 3% of the time, Pallas kernels for 8%

profile of v11, /device:TPU:1, one launch (start us, length us, event | category | flops | bytes accessed | tf_op | source)
XLA Modules:
  0.0 154.3 jit_solution(7480818032557370542)
XLA Ops:
  0.8 1.1 fusion.13
  1.9 0.9 pad_maximum_fusion.1.a
  2.8 4.0 %collective-permute-start = (bf16[2,64,1024]{2,1,0:T(8,128)(2,1)S(1)}, bf16[2,64,1024]{2,1,0:T(8,128)(2,1)S(1)}, u32[]{:S(2)}, u32[]{:S(2)}) collective-permute-start(bf16[2,64,1024]{2,1,0:T(8,128)(2,1)S(1)} %pad_maximum_fusion.1.a), channel_id=1, source_target_pairs={{0,1},{1,2},{2,3},{3,0},{4,5},{5,6},{6,7},{7,4},{8,9},{9,10},{10,1... | collective-permute-start | bytes 786440 | tf_op jit(solution)/shard_map/ppermute | solution.py:46
  6.8 3.4 %collective-permute-start.1 = (bf16[2,64,1024]{2,1,0:T(8,128)(2,1)S(1)}, bf16[2,64,1024]{2,1,0:T(8,128)(2,1)S(1)}, u32[]{:S(2)}, u32[]{:S(2)}) collective-permute-start(bf16[2,64,1024]{2,1,0:T(8,128)(2,1)S(1)} %pad_maximum_fusion.1.a), channel_id=1, source_target_pairs={{0,3},{1,0},{2,1},{3,2},{4,7},{5,4},{6,5},{7,6},{8,11},{9,8},{10,9... | collective-permute-start | bytes 786440 | tf_op jit(solution)/shard_map/ppermute | solution.py:46
  10.2 3.5 %collective-permute-start.2 = (bf16[2,64,1024]{2,1,0:T(8,128)(2,1)S(1)}, bf16[2,64,1024]{2,1,0:T(8,128)(2,1)S(1)}, u32[]{:S(2)}, u32[]{:S(2)}) collective-permute-start(bf16[2,64,1024]{2,1,0:T(8,128)(2,1)S(1)} %pad_maximum_fusion.1.a), channel_id=1, source_target_pairs={{0,2},{1,3},{2,0},{3,1},{4,6},{5,7},{6,4},{7,5},{8,10},{9,11},{10,... | collective-permute-start | bytes 786440 | tf_op jit(solution)/shard_map/ppermute | solution.py:46
  14.0 4.9 %collective-permute-done.2.d = bf16[2,64,1024]{2,1,0:T(8,128)(2,1)S(1)} collective-permute-done((bf16[2,64,1024]{2,1,0:T(8,128)(2,1)S(1)}, bf16[2,64,1024]{2,1,0:T(8,128)(2,1)S(1)}, u32[]{:S(2)}, u32[]{:S(2)}) %collective-permute-start.2) | collective-permute-done | bytes 262176 | tf_op jit(solution)/shard_map/ppermute | solution.py:46
  19.0 4.7 %collective-permute-start.3 = (bf16[2,256,1024]{2,1,0:T(8,128)(2,1)S(1)}, bf16[2,256,1024]{2,1,0:T(8,128)(2,1)}, u32[]{:S(2)}, u32[]{:S(2)}) collective-permute-start(bf16[2,256,1024]{2,1,0:T(8,128)(2,1)S(1)} %shard_map.55.a), channel_id=1, source_target_pairs={{0,8},{1,9},{2,10},{3,11},{4,12},{5,13},{6,14},{7,15},{8,0},{9,1},... | collective-permute-start | bytes 3145736 | tf_op jit(solution)/shard_map/ppermute | solution.py:46
  23.7 2.8 %collective-permute-start.4 = (bf16[2,256,1024]{2,1,0:T(8,128)(2,1)S(1)}, bf16[2,256,1024]{2,1,0:T(8,128)(2,1)}, u32[]{:S(2)}, u32[]{:S(2)}) collective-permute-start(bf16[2,256,1024]{2,1,0:T(8,128)(2,1)S(1)} %shard_map.55.a), channel_id=1, source_target_pairs={{0,12},{1,13},{2,14},{3,15},{4,0},{5,1},{6,2},{7,3},{8,4},{9,5},{1... | collective-permute-start | bytes 3145736 | tf_op jit(solution)/shard_map/ppermute | solution.py:46
  26.5 2.5 %collective-permute-start.5 = (bf16[2,256,1024]{2,1,0:T(8,128)(2,1)S(1)}, bf16[2,256,1024]{2,1,0:T(8,128)(2,1)}, u32[]{:S(2)}, u32[]{:S(2)}) collective-permute-start(bf16[2,256,1024]{2,1,0:T(8,128)(2,1)S(1)} %shard_map.55.a), channel_id=1, source_target_pairs={{0,4},{1,5},{2,6},{3,7},{4,8},{5,9},{6,10},{7,11},{8,12},{9,13},{1... | collective-permute-start | bytes 3145736 | tf_op jit(solution)/shard_map/ppermute | solution.py:46
  29.0 0.8 convolution_convert_fusion
  30.0 0.9 copy.8
  30.9 1.8 %reshape.11 = bf16[16,32,128]{2,1,0:T(8,128)(2,1)} reshape(bf16[16,32,2,64]{3,2,1,0:T(2,128)(2,1)} %copy.8) | data formatting | bytes 262144 | tf_op jit(solution)/shard_map/reshape | solution.py:317
  32.7 5.1 %all-to-all-start = ((bf16[16,32,128]{2,1,0:T(8,128)(2,1)}), bf16[16,32,128]{2,1,0:T(8,128)(2,1)S(1)}, u32[]{:S(2)}, u32[]{:S(2)}) async-start(bf16[16,32,128]{2,1,0:T(8,128)(2,1)} %reshape.11), calls=%async_computation | async-start | bytes 262144 | tf_op jit(solution)/shard_map/all_to_all | solution.py:318
  38.1 3.0 %shard_map.56 = (bf16[1024,1024]{1,0:T(8,128)(2,1)S(1)}, f32[8,128]{1,0:T(8,128)}) custom-call(bf16[2,256,1024]{2,1,0:T(8,128)(2,1)S(1)} %shard_map.55.a, bf16[2,256,1024]{2,1,0:T(8,128)(2,1)} %collective-permute-done.3.d), custom_call_target="tpu_custom_call" | custom-call | tf_op jit(solution)/shard_map/pallas_call | solution.py:141
  41.1 7.2 %collective-permute-done.4.b.c = bf16[2,256,1024]{2,1,0:T(8,128)(2,1)} collective-permute-done((bf16[2,256,1024]{2,1,0:T(8,128)(2,1)S(1)}, bf16[2,256,1024]{2,1,0:T(8,128)(2,1)}, u32[]{:S(2)}, u32[]{:S(2)}) %collective-permute-start.4) | collective-permute-done | bytes 1048608 | tf_op jit(solution)/shard_map/ppermute | solution.py:46
  48.7 4.2 %shard_map.57 = (bf16[1024,1024]{1,0:T(8,128)(2,1)}, f32[8,128]{1,0:T(8,128)S(1)}) custom-call(bf16[1024,1024]{1,0:T(8,128)(2,1)S(1)} %get-tuple-element.12.part, bf16[2,256,1024]{2,1,0:T(8,128)(2,1)} %collective-permute-done.4.b.c, bf16[2,256,1024]{2,1,0:T(8,128)(2,1)} %collective-permute-done.5.c.b), custom_call_target="tpu_custom_call" | custom-call | tf_op jit(solution)/shard_map/pallas_call | solution.py:148
  52.9 11.6 %collective-permute-start.6 = (bf16[1024,1024]{1,0:T(8,128)(2,1)}, bf16[1024,1024]{1,0:T(8,128)(2,1)}, u32[]{:S(2)}, u32[]{:S(2)}) collective-permute-start(bf16[1024,1024]{1,0:T(8,128)(2,1)} %get-tuple-element.13.own), channel_id=1, source_target_pairs={{0,16},{16,0},{32,48},{48,32},{64,80},{80,64},{96,112},{112,96},{1... | collective-permute-start | bytes 6291464 | tf_op jit(solution)/shard_map/ppermute | solution.py:325
  64.5 0.6 shard_map.58.panel
  65.2 1.8 %shard_map.59.bias = f32[64,1024]{1,0:T(8,128)S(1)} custom-call(bf16[64,1024]{1,0:T(8,128)(2,1)S(1)} %shard_map.58.panel, bf16[2,256,1024]{2,1,0:T(8,128)(2,1)S(1)} %shard_map.55.a, bf16[2,256,1024]{2,1,0:T(8,128)(2,1)} %collective-permute-done.5.c.b, bf16[2,256,1024]{2,1,0:T(8,128)(2,1)} %collective-permute-done.4.b.c, ...), custom_call_target="tpu_custom_call" | custom-call | flops 42949672960 | bytes 6291456 | tf_op jit(solution)/shard_map/pallas_call | solution.py:164
  67.0 1.3 collective-permute-start.7
  68.3 2.1 %collective-permute-done.7.bias_got = f32[64,1024]{1,0:T(8,128)S(1)} collective-permute-done((f32[64,1024]{1,0:T(8,128)S(1)}, f32[64,1024]{1,0:T(8,128)S(1)}, u32[]{:S(2)}, u32[]{:S(2)}) %collective-permute-start.7) | collective-permute-done | bytes 262176 | tf_op jit(solution)/shard_map/ppermute | solution.py:326
  70.5 4.9 %shard_map.60 = (bf16[1024,1024]{1,0:T(8,128)(2,1)S(1)}, bf16[1024,1024]{1,0:T(8,128)(2,1)S(1)}, f32[64,1024]{1,0:T(8,128)S(1)}, f32[8,128]{1,0:T(8,128)S(1)}) custom-call(s32[1]{0:T(128)} %bitcast.18.core, bf16[1024,1024]{1,0:T(8,128)(2,1)} %get-tuple-element.13.own, bf16[1024,1024]{1,0:T(8,128)(2,1)} %collective-permute-done.6.got, ...), custom_call_target="tpu_custom_call" | custom-call | flops 2147483648 | bytes 6291456 | tf_op jit(solution)/shard_map/pallas_call | solution.py:200
  75.4 1.3 collective-permute-start.8
  76.8 2.9 %collective-permute-done.8.ready = f32[8,128]{1,0:T(8,128)S(1)} collective-permute-done((f32[8,128]{1,0:T(8,128)S(1)}, f32[8,128]{1,0:T(8,128)S(1)}, u32[]{:S(2)}, u32[]{:S(2)}) %collective-permute-start.8) | collective-permute-done | bytes 4128 | tf_op jit(solution)/shard_map/ppermute | solution.py:53
  79.7 0.5 fusion
  80.2 0.7 collective-permute-start.9
  81.0 0.5 fusion.1
  81.5 0.7 collective-permute-start.10
  82.2 0.5 fusion.2
  82.7 0.7 collective-permute-start.11
  83.4 0.5 fusion.3
  83.9 0.7 collective-permute-start.12
  84.7 0.5 fusion.4
  85.2 1.3 collective-permute-start.13
  86.5 20.4 %collective-permute-done.13 = bf16[64,1024]{1,0:T(8,128)(2,1)S(1)} collective-permute-done((bf16[64,1024]{1,0:T(8,128)(2,1)S(1)}, bf16[64,1024]{1,0:T(8,128)(2,1)S(1)}, u32[]{:S(2)}, u32[]{:S(2)}) %collective-permute-start.13) | collective-permute-done | bytes 131104 | tf_op jit(solution)/shard_map/ppermute | solution.py:342
  106.9 0.5 fusion.5
  107.4 0.7 collective-permute-start.14
  108.1 0.5 fusion.6
  108.6 0.8 collective-permute-start.15
  109.5 0.5 fusion.7
  110.0 0.7 collective-permute-start.16
  110.8 0.5 fusion.8
  111.3 0.7 collective-permute-start.17
  112.0 0.5 convolution_add_fusion.v_odd
  112.5 0.5 convert_select_fusion
  113.0 2.4 %collective-permute-start.18 = (bf16[64,1024]{1,0:T(8,128)(2,1)S(1)}, bf16[64,1024]{1,0:T(8,128)(2,1)S(1)}, u32[]{:S(2)}, u32[]{:S(2)}) collective-permute-start(bf16[64,1024]{1,0:T(8,128)(2,1)S(1)} %get-tuple-element.19), channel_id=1, source_target_pairs={{0,16},{16,0},{32,48},{48,32},{64,80},{80,64},{96,112},{112,96},{1... | collective-permute-start | bytes 393224 | tf_op jit(solution)/shard_map/ppermute | solution.py:346
  115.4 1.0 collective-permute-done.18.other
  116.4 4.4 %collective-permute-start.21 = (bf16[64,1024]{1,0:T(8,128)(2,1)S(1)}, bf16[64,1024]{1,0:T(8,128)(2,1)S(1)}, u32[]{:S(2)}, u32[]{:S(2)}) collective-permute-start(bf16[64,1024]{1,0:T(8,128)(2,1)S(1)} %broadcast_select_fusion), channel_id=1, source_target_pairs={{0,2},{1,3},{2,0},{3,1},{4,6},{5,7},{6,4},{7,5},{8,10},{9,11},{10,... | collective-permute-start | bytes 393224 | tf_op jit(solution)/shard_map/ppermute | solution.py:46
  120.8 2.8 %collective-permute-start.20 = (bf16[64,1024]{1,0:T(8,128)(2,1)S(1)}, bf16[64,1024]{1,0:T(8,128)(2,1)S(1)}, u32[]{:S(2)}, u32[]{:S(2)}) collective-permute-start(bf16[64,1024]{1,0:T(8,128)(2,1)S(1)} %broadcast_select_fusion), channel_id=1, source_target_pairs={{0,3},{1,0},{2,1},{3,2},{4,7},{5,4},{6,5},{7,6},{8,11},{9,8},{10,9... | collective-permute-start | bytes 393224 | tf_op jit(solution)/shard_map/ppermute | solution.py:46
  123.7 2.4 %collective-permute-start.19 = (bf16[64,1024]{1,0:T(8,128)(2,1)S(1)}, bf16[64,1024]{1,0:T(8,128)(2,1)S(1)}, u32[]{:S(2)}, u32[]{:S(2)}) collective-permute-start(bf16[64,1024]{1,0:T(8,128)(2,1)S(1)} %broadcast_select_fusion), channel_id=1, source_target_pairs={{0,1},{1,2},{2,3},{3,0},{4,5},{5,6},{6,7},{7,4},{8,9},{9,10},{10,1... | collective-permute-start | bytes 393224 | tf_op jit(solution)/shard_map/ppermute | solution.py:46
  126.1 0.7 collective-permute-start.25
  126.8 0.7 collective-permute-start.26
  127.5 3.4 %collective-permute-done.19 = bf16[64,1024]{1,0:T(8,128)(2,1)S(1)} collective-permute-done((bf16[64,1024]{1,0:T(8,128)(2,1)S(1)}, bf16[64,1024]{1,0:T(8,128)(2,1)S(1)}, u32[]{:S(2)}, u32[]{:S(2)}) %collective-permute-start.19) | collective-permute-done | bytes 131104 | tf_op jit(solution)/shard_map/ppermute | solution.py:46
  130.9 1.9 %collective-permute-start.22 = (bf16[256,1024]{1,0:T(8,128)(2,1)S(1)}, bf16[256,1024]{1,0:T(8,128)(2,1)S(1)}, u32[]{:S(2)}, u32[]{:S(2)}) collective-permute-start(bf16[256,1024]{1,0:T(8,128)(2,1)S(1)} %pad_maximum_fusion.a.ready), channel_id=1, source_target_pairs={{0,4},{1,5},{2,6},{3,7},{4,8},{5,9},{6,10},{7,11},{8,12},{9,13},{1... | collective-permute-start | bytes 1572872 | tf_op jit(solution)/shard_map/ppermute | solution.py:46
  132.9 4.6 %collective-permute-start.23 = (bf16[256,1024]{1,0:T(8,128)(2,1)S(1)}, bf16[256,1024]{1,0:T(8,128)(2,1)}, u32[]{:S(2)}, u32[]{:S(2)}) collective-permute-start(bf16[256,1024]{1,0:T(8,128)(2,1)S(1)} %pad_maximum_fusion.a.ready), channel_id=1, source_target_pairs={{0,12},{1,13},{2,14},{3,15},{4,0},{5,1},{6,2},{7,3},{8,4},{9,5},{1... | collective-permute-start | bytes 1572872 | tf_op jit(solution)/shard_map/ppermute | solution.py:46
  137.5 1.9 %collective-permute-start.24 = (bf16[256,1024]{1,0:T(8,128)(2,1)S(1)}, bf16[256,1024]{1,0:T(8,128)(2,1)}, u32[]{:S(2)}, u32[]{:S(2)}) collective-permute-start(bf16[256,1024]{1,0:T(8,128)(2,1)S(1)} %pad_maximum_fusion.a.ready), channel_id=1, source_target_pairs={{0,8},{1,9},{2,10},{3,11},{4,12},{5,13},{6,14},{7,15},{8,0},{9,1},... | collective-permute-start | bytes 1572872 | tf_op jit(solution)/shard_map/ppermute | solution.py:46
  139.4 0.7 shard_map.63.entry
  140.1 1.3 collective-permute-start.27
  141.4 1.3 collective-permute-start.28
  142.8 5.8 %collective-permute-done.28.last = bf16[64,1024]{1,0:T(8,128)(2,1)} collective-permute-done((bf16[64,1024]{1,0:T(8,128)(2,1)}, bf16[64,1024]{1,0:T(8,128)(2,1)}, u32[]{:S(2)}, u32[]{:S(2)}) %collective-permute-start.28) | collective-permute-done | bytes 131104 | tf_op jit(solution)/shard_map/ppermute | solution.py:53
  148.6 1.1 shard_map.64.entry
  149.7 1.4 collective-permute-start.29
  151.2 1.4 shard_map.62.maps
  152.5 1.7 %shard_map.65 = f32[64,1024]{1,0:T(8,128)} custom-call(s32[2]{0:T(128)S(1)} %add_convert_fusion.flags, bf16[1024,1024]{1,0:T(8,128)(2,1)S(1)} %shard_map.62.maps, bf16[64,1024]{1,0:T(8,128)(2,1)S(1)} %shard_map.64.entry, bf16[64,1024]{1,0:T(8,128)(2,1)S(1)} %collective-permute-done.29.across, bf16[64,1024]{1,0:T(8,128)(2,1)S(1)} %copy-done.2, ...), custom_call_target="tpu_custom_call" | custom-call | tf_op jit(solution)/shard_map/pallas_call | solution.py:285
  (48 shorter events, 1.8 us)
Async XLA Ops:
  0.0 29.0 %copy-start = (bf16[1024,1024]{1,0:T(8,128)(2,1)S(1)}, bf16[1024,1024]{1,0:T(8,128)(2,1)}, u32[]{:S(2)}) copy-start(bf16[1024,1024]{1,0:T(8,128)(2,1)} %param.8) | copy-start | bytes 6291460
  0.0 29.0 %copy-start.3 = (bf16[1,1024,64]{1,2,0:T(8,128)(2,1)S(1)}, bf16[1,1024,64]{1,2,0:T(8,128)(2,1)}, u32[]{:S(2)}) copy-start(bf16[1,1024,64]{1,2,0:T(8,128)(2,1)} %param.7) | copy-start | bytes 393220
  2.8 11.0 %collective-permute-start = (bf16[2,64,1024]{2,1,0:T(8,128)(2,1)S(1)}, bf16[2,64,1024]{2,1,0:T(8,128)(2,1)S(1)}, u32[]{:S(2)}, u32[]{:S(2)}) collective-permute-start(bf16[2,64,1024]{2,1,0:T(8,128)(2,1)S(1)} %pad_maximum_fusion.1.a), channel_id=1, source_target_pairs={{0,1},{1,2},{2,3},{3,0},{4,5},{5,6},{6,7},{7,4},{8,9},{9,10},{10,1... | collective-permute-start | bytes 786440 | tf_op jit(solution)/shard_map/ppermute | solution.py:46
  6.8 7.1 %collective-permute-start.1 = (bf16[2,64,1024]{2,1,0:T(8,128)(2,1)S(1)}, bf16[2,64,1024]{2,1,0:T(8,128)(2,1)S(1)}, u32[]{:S(2)}, u32[]{:S(2)}) collective-permute-start(bf16[2,64,1024]{2,1,0:T(8,128)(2,1)S(1)} %pad_maximum_fusion.1.a), channel_id=1, source_target_pairs={{0,3},{1,0},{2,1},{3,2},{4,7},{5,4},{6,5},{7,6},{8,11},{9,8},{10,9... | collective-permute-start | bytes 786440 | tf_op jit(solution)/shard_map/ppermute | solution.py:46
  10.2 8.6 %collective-permute-start.2 = (bf16[2,64,1024]{2,1,0:T(8,128)(2,1)S(1)}, bf16[2,64,1024]{2,1,0:T(8,128)(2,1)S(1)}, u32[]{:S(2)}, u32[]{:S(2)}) collective-permute-start(bf16[2,64,1024]{2,1,0:T(8,128)(2,1)S(1)} %pad_maximum_fusion.1.a), channel_id=1, source_target_pairs={{0,2},{1,3},{2,0},{3,1},{4,6},{5,7},{6,4},{7,5},{8,10},{9,11},{10,... | collective-permute-start | bytes 786440 | tf_op jit(solution)/shard_map/ppermute | solution.py:46
  19.0 19.1 %collective-permute-start.3 = (bf16[2,256,1024]{2,1,0:T(8,128)(2,1)S(1)}, bf16[2,256,1024]{2,1,0:T(8,128)(2,1)}, u32[]{:S(2)}, u32[]{:S(2)}) collective-permute-start(bf16[2,256,1024]{2,1,0:T(8,128)(2,1)S(1)} %shard_map.55.a), channel_id=1, source_target_pairs={{0,8},{1,9},{2,10},{3,11},{4,12},{5,13},{6,14},{7,15},{8,0},{9,1},... | collective-permute-start | bytes 3145736 | tf_op jit(solution)/shard_map/ppermute | solution.py:46
  23.7 24.5 %collective-permute-start.4 = (bf16[2,256,1024]{2,1,0:T(8,128)(2,1)S(1)}, bf16[2,256,1024]{2,1,0:T(8,128)(2,1)}, u32[]{:S(2)}, u32[]{:S(2)}) collective-permute-start(bf16[2,256,1024]{2,1,0:T(8,128)(2,1)S(1)} %shard_map.55.a), channel_id=1, source_target_pairs={{0,12},{1,13},{2,14},{3,15},{4,0},{5,1},{6,2},{7,3},{8,4},{9,5},{1... | collective-permute-start | bytes 3145736 | tf_op jit(solution)/shard_map/ppermute | solution.py:46
  26.5 22.2 %collective-permute-start.5 = (bf16[2,256,1024]{2,1,0:T(8,128)(2,1)S(1)}, bf16[2,256,1024]{2,1,0:T(8,128)(2,1)}, u32[]{:S(2)}, u32[]{:S(2)}) collective-permute-start(bf16[2,256,1024]{2,1,0:T(8,128)(2,1)S(1)} %shard_map.55.a), channel_id=1, source_target_pairs={{0,4},{1,5},{2,6},{3,7},{4,8},{5,9},{6,10},{7,11},{8,12},{9,13},{1... | collective-permute-start | bytes 3145736 | tf_op jit(solution)/shard_map/ppermute | solution.py:46
  32.7 31.8 %all-to-all-start = ((bf16[16,32,128]{2,1,0:T(8,128)(2,1)}), bf16[16,32,128]{2,1,0:T(8,128)(2,1)S(1)}, u32[]{:S(2)}, u32[]{:S(2)}) async-start(bf16[16,32,128]{2,1,0:T(8,128)(2,1)} %reshape.11), calls=%async_computation | async-start | bytes 262144 | tf_op jit(solution)/shard_map/all_to_all | solution.py:318
  52.9 17.5 %collective-permute-start.6 = (bf16[1024,1024]{1,0:T(8,128)(2,1)}, bf16[1024,1024]{1,0:T(8,128)(2,1)}, u32[]{:S(2)}, u32[]{:S(2)}) collective-permute-start(bf16[1024,1024]{1,0:T(8,128)(2,1)} %get-tuple-element.13.own), channel_id=1, source_target_pairs={{0,16},{16,0},{32,48},{48,32},{64,80},{80,64},{96,112},{112,96},{1... | collective-permute-start | bytes 6291464 | tf_op jit(solution)/shard_map/ppermute | solution.py:325
  67.0 3.4 %collective-permute-start.7 = (f32[64,1024]{1,0:T(8,128)S(1)}, f32[64,1024]{1,0:T(8,128)S(1)}, u32[]{:S(2)}, u32[]{:S(2)}) collective-permute-start(f32[64,1024]{1,0:T(8,128)S(1)} %shard_map.59.bias), channel_id=1, source_target_pairs={{0,16},{32,48},{64,80},{96,112},{128,144},{160,176},{192,208},{224... | collective-permute-start | bytes 786440 | tf_op jit(solution)/shard_map/ppermute | solution.py:326
  75.4 4.4 %collective-permute-start.8 = (f32[8,128]{1,0:T(8,128)S(1)}, f32[8,128]{1,0:T(8,128)S(1)}, u32[]{:S(2)}, u32[]{:S(2)}) collective-permute-start(f32[8,128]{1,0:T(8,128)S(1)} %get-tuple-element.15), channel_id=1, source_target_pairs={{48,16},{80,48},{112,80},{144,112},{176,144},{208,176},{49,17},{81... | collective-permute-start | bytes 12296 | tf_op jit(solution)/shard_map/ppermute | solution.py:53
  80.2 0.7 collective-permute-start.9
  81.5 0.7 collective-permute-start.10
  82.7 0.7 collective-permute-start.11
  83.9 0.7 collective-permute-start.12
  85.2 21.7 %collective-permute-start.13 = (bf16[64,1024]{1,0:T(8,128)(2,1)S(1)}, bf16[64,1024]{1,0:T(8,128)(2,1)S(1)}, u32[]{:S(2)}, u32[]{:S(2)}) collective-permute-start(bf16[64,1024]{1,0:T(8,128)(2,1)S(1)} %fusion.4), channel_id=1, source_target_pairs={{368,336},{32,0},{48,16},{369,337},{33,1},{49,17},{370,338},{34,2}... | collective-permute-start | bytes 393224 | tf_op jit(solution)/shard_map/ppermute | solution.py:342
  107.4 0.7 collective-permute-start.14
  108.6 0.9 collective-permute-start.15
  110.0 0.7 collective-permute-start.16
  111.3 0.7 collective-permute-start.17
  113.0 3.4 %collective-permute-start.18 = (bf16[64,1024]{1,0:T(8,128)(2,1)S(1)}, bf16[64,1024]{1,0:T(8,128)(2,1)S(1)}, u32[]{:S(2)}, u32[]{:S(2)}) collective-permute-start(bf16[64,1024]{1,0:T(8,128)(2,1)S(1)} %get-tuple-element.19), channel_id=1, source_target_pairs={{0,16},{16,0},{32,48},{48,32},{64,80},{80,64},{96,112},{112,96},{1... | collective-permute-start | bytes 393224 | tf_op jit(solution)/shard_map/ppermute | solution.py:346
  116.4 11.1 %copy-start.1 = (bf16[64,1024]{1,0:T(8,128)(2,1)}, bf16[64,1024]{1,0:T(8,128)(2,1)S(1)}, u32[]{:S(2)}) copy-start(bf16[64,1024]{1,0:T(8,128)(2,1)S(1)} %collective-permute-done.18.other) | copy-start | bytes 393220
  116.4 11.1 %collective-permute-start.21 = (bf16[64,1024]{1,0:T(8,128)(2,1)S(1)}, bf16[64,1024]{1,0:T(8,128)(2,1)S(1)}, u32[]{:S(2)}, u32[]{:S(2)}) collective-permute-start(bf16[64,1024]{1,0:T(8,128)(2,1)S(1)} %broadcast_select_fusion), channel_id=1, source_target_pairs={{0,2},{1,3},{2,0},{3,1},{4,6},{5,7},{6,4},{7,5},{8,10},{9,11},{10,... | collective-permute-start | bytes 393224 | tf_op jit(solution)/shard_map/ppermute | solution.py:46
  120.8 6.7 %collective-permute-start.20 = (bf16[64,1024]{1,0:T(8,128)(2,1)S(1)}, bf16[64,1024]{1,0:T(8,128)(2,1)S(1)}, u32[]{:S(2)}, u32[]{:S(2)}) collective-permute-start(bf16[64,1024]{1,0:T(8,128)(2,1)S(1)} %broadcast_select_fusion), channel_id=1, source_target_pairs={{0,3},{1,0},{2,1},{3,2},{4,7},{5,4},{6,5},{7,6},{8,11},{9,8},{10,9... | collective-permute-start | bytes 393224 | tf_op jit(solution)/shard_map/ppermute | solution.py:46
  123.7 7.2 %collective-permute-start.19 = (bf16[64,1024]{1,0:T(8,128)(2,1)S(1)}, bf16[64,1024]{1,0:T(8,128)(2,1)S(1)}, u32[]{:S(2)}, u32[]{:S(2)}) collective-permute-start(bf16[64,1024]{1,0:T(8,128)(2,1)S(1)} %broadcast_select_fusion), channel_id=1, source_target_pairs={{0,1},{1,2},{2,3},{3,0},{4,5},{5,6},{6,7},{7,4},{8,9},{9,10},{10,1... | collective-permute-start | bytes 393224 | tf_op jit(solution)/shard_map/ppermute | solution.py:46
  126.1 13.3 %collective-permute-start.25 = (bf16[64,1024]{1,0:T(8,128)(2,1)S(1)}, bf16[64,1024]{1,0:T(8,128)(2,1)S(1)}, u32[]{:S(2)}, u32[]{:S(2)}) collective-permute-start(bf16[64,1024]{1,0:T(8,128)(2,1)S(1)} %get-tuple-element.20.edge), channel_id=1, source_target_pairs={{208,80},{209,81},{210,82},{211,83},{212,84},{213,85},{214,86},{21... | collective-permute-start | bytes 393224 | tf_op jit(solution)/shard_map/ppermute | solution.py:53
  126.8 12.6 %collective-permute-start.26 = (bf16[64,1024]{1,0:T(8,128)(2,1)S(1)}, bf16[64,1024]{1,0:T(8,128)(2,1)S(1)}, u32[]{:S(2)}, u32[]{:S(2)}) collective-permute-start(bf16[64,1024]{1,0:T(8,128)(2,1)S(1)} %get-tuple-element.20.edge), channel_id=1, source_target_pairs={{208,176},{209,177},{210,178},{211,179},{212,180},{213,181},{214,1... | collective-permute-start | bytes 393224 | tf_op jit(solution)/shard_map/ppermute | solution.py:53
  130.9 20.2 %collective-permute-start.22 = (bf16[256,1024]{1,0:T(8,128)(2,1)S(1)}, bf16[256,1024]{1,0:T(8,128)(2,1)S(1)}, u32[]{:S(2)}, u32[]{:S(2)}) collective-permute-start(bf16[256,1024]{1,0:T(8,128)(2,1)S(1)} %pad_maximum_fusion.a.ready), channel_id=1, source_target_pairs={{0,4},{1,5},{2,6},{3,7},{4,8},{5,9},{6,10},{7,11},{8,12},{9,13},{1... | collective-permute-start | bytes 1572872 | tf_op jit(solution)/shard_map/ppermute | solution.py:46
  132.9 18.3 %collective-permute-start.23 = (bf16[256,1024]{1,0:T(8,128)(2,1)S(1)}, bf16[256,1024]{1,0:T(8,128)(2,1)}, u32[]{:S(2)}, u32[]{:S(2)}) collective-permute-start(bf16[256,1024]{1,0:T(8,128)(2,1)S(1)} %pad_maximum_fusion.a.ready), channel_id=1, source_target_pairs={{0,12},{1,13},{2,14},{3,15},{4,0},{5,1},{6,2},{7,3},{8,4},{9,5},{1... | collective-permute-start | bytes 1572872 | tf_op jit(solution)/shard_map/ppermute | solution.py:46
  137.5 13.7 %collective-permute-start.24 = (bf16[256,1024]{1,0:T(8,128)(2,1)S(1)}, bf16[256,1024]{1,0:T(8,128)(2,1)}, u32[]{:S(2)}, u32[]{:S(2)}) collective-permute-start(bf16[256,1024]{1,0:T(8,128)(2,1)S(1)} %pad_maximum_fusion.a.ready), channel_id=1, source_target_pairs={{0,8},{1,9},{2,10},{3,11},{4,12},{5,13},{6,14},{7,15},{8,0},{9,1},... | collective-permute-start | bytes 1572872 | tf_op jit(solution)/shard_map/ppermute | solution.py:46
  140.1 2.7 %collective-permute-start.27 = (bf16[64,1024]{1,0:T(8,128)(2,1)}, bf16[64,1024]{1,0:T(8,128)(2,1)}, u32[]{:S(2)}, u32[]{:S(2)}) collective-permute-start(bf16[64,1024]{1,0:T(8,128)(2,1)} %shard_map.63.entry), channel_id=1, source_target_pairs={{176,144},{80,48},{177,145},{81,49},{178,146},{82,50},{179,147},{8... | collective-permute-start | bytes 393224 | tf_op jit(solution)/shard_map/ppermute | solution.py:53
  141.4 7.2 %collective-permute-start.28 = (bf16[64,1024]{1,0:T(8,128)(2,1)}, bf16[64,1024]{1,0:T(8,128)(2,1)}, u32[]{:S(2)}, u32[]{:S(2)}) collective-permute-start(bf16[64,1024]{1,0:T(8,128)(2,1)} %shard_map.63.entry), channel_id=1, source_target_pairs={{176,112},{80,16},{177,113},{81,17},{178,114},{82,18},{179,115},{8... | collective-permute-start | bytes 393224 | tf_op jit(solution)/shard_map/ppermute | solution.py:53
  149.7 2.9 %copy-start.2 = (bf16[64,1024]{1,0:T(8,128)(2,1)S(1)}, bf16[64,1024]{1,0:T(8,128)(2,1)}, u32[]{:S(2)}) copy-start(bf16[64,1024]{1,0:T(8,128)(2,1)} %copy-done.1) | copy-start | bytes 393220
  149.7 2.8 %collective-permute-start.29 = (bf16[64,1024]{1,0:T(8,128)(2,1)S(1)}, bf16[64,1024]{1,0:T(8,128)(2,1)S(1)}, u32[]{:S(2)}, u32[]{:S(2)}) collective-permute-start(bf16[64,1024]{1,0:T(8,128)(2,1)S(1)} %shard_map.64.entry), channel_id=1, source_target_pairs={{16,0},{48,32},{80,64},{112,96},{144,128},{176,160},{208,192},{240... | collective-permute-start | bytes 393224 | tf_op jit(solution)/shard_map/ppermute | solution.py:362

commit v12 on v11

--- a/solution.py
+++ b/solution.py
@@ -72,7 +72,7 @@
     )(order, *blocks)
 
 
-def pack_kernel(a, b, c, d, out):
+def pack_kernel(a, d, c, b, out):
     count = a.shape[1]
     wide = out.shape[1]
     for f, block in enumerate((a, b, c, d)):
@@ -91,7 +91,7 @@
         in_specs=[VMEM] * 4,
         out_specs=VMEM,
         compiler_params=room(6),
-    )(*blocks)
+    )(blocks[0], *blocks[:0:-1])
 
 
 def half_product(first, second, cut):

time: 155 us -> 156 us (level)
  waiting for transfers between devices: 48.4 us -> 54.2 us
  starting transfers between devices: 72.9 us -> 67.4 us
    ppermute x9, waiting for transfers between devices: 20.4 us -> 24.6 us  [body(): v_in = v_in + lax.ppermute(v_even.astype(BF16), 'depth', pairs)]
    ppermute x1, starting transfers between devices: 11.6 us -> 7.52 us  [body(): got = lax.ppermute(step, 'depth', swap)]
    ppermute x12, waiting for transfers between devices: 16.1 us -> 17.8 us  [ring_gather(): lax.ppermute(value, BOTH, ring_moves(depths, flipped, shift))]
  transfers between devices with their start and end apart: 31 -> 31, of which waited for: 10 -> 9; matrix products, arithmetic and copies ran while one was open for 3% -> 3% of each run, Pallas kernels for 8% -> 8%
where the time goes in v12:
time: 156 us; the launch traced here: 155 us
  starting transfers between devices  67.4 us (43%)
  waiting for transfers between devices  54.2 us (35%)
  Pallas kernels  19.6 us (13%)
  matrix products  6.18 us (4%)
  local copies, waits for them, and re-layouts  3.01 us (2%)
  other arithmetic  2.53 us (2%)
  between operations  1.7 us (1%)
    ppermute x12, starting transfers between devices, ring_gather(): lax.ppermute(value, BOTH, ring_moves(depths, flipped, shift))  39 us
    ppermute x9, waiting for transfers between devices, body(): v_in = v_in + lax.ppermute(v_even.astype(BF16), 'depth', pairs)  24.6 us
    ppermute x12, waiting for transfers between devices, ring_gather(): lax.ppermute(value, BOTH, ring_moves(depths, flipped, shift))  17.8 us
    ppermute x5, waiting for transfers between devices, sent_down(): lax.ppermute(value, 'depth', [(2 * a + 1, 2 * b + 1) for a, b in chip_pai...  8.76 us
    ppermute x1, starting transfers between devices, body(): got = lax.ppermute(step, 'depth', swap)  7.52 us
    ppermute x9, starting transfers between devices, body(): v_in = v_in + lax.ppermute(v_even.astype(BF16), 'depth', pairs)  6.82 us
    dot_general x12, matrix products, mm(): return jnp.dot(a, b, preferred_element_type=F32)  6.18 us
    ppermute x5, starting transfers between devices, sent_down(): lax.ppermute(value, 'depth', [(2 * a + 1, 2 * b + 1) for a, b in chip_pai...  5.21 us
  transfers between devices with their start and end apart: 31, of which 9 were waited for; matrix products, arithmetic and copies ran while one was open for 3% of the time, Pallas kernels for 8%

profile of v12, /device:TPU:1, one launch (start us, length us, event | category | flops | bytes accessed | tf_op | source)
XLA Modules:
  0.0 154.6 jit_solution(1923380749878050909)
XLA Ops:
  0.8 1.1 fusion.13
  1.9 0.9 pad_maximum_fusion.1.a
  2.8 5.7 %collective-permute-start = (bf16[2,64,1024]{2,1,0:T(8,128)(2,1)S(1)}, bf16[2,64,1024]{2,1,0:T(8,128)(2,1)S(1)}, u32[]{:S(2)}, u32[]{:S(2)}) collective-permute-start(bf16[2,64,1024]{2,1,0:T(8,128)(2,1)S(1)} %pad_maximum_fusion.1.a), channel_id=1, source_target_pairs={{0,2},{1,3},{2,0},{3,1},{4,6},{5,7},{6,4},{7,5},{8,10},{9,11},{10,... | collective-permute-start | bytes 786440 | tf_op jit(solution)/shard_map/ppermute | solution.py:46
  8.5 2.7 %collective-permute-start.1 = (bf16[2,64,1024]{2,1,0:T(8,128)(2,1)S(1)}, bf16[2,64,1024]{2,1,0:T(8,128)(2,1)S(1)}, u32[]{:S(2)}, u32[]{:S(2)}) collective-permute-start(bf16[2,64,1024]{2,1,0:T(8,128)(2,1)S(1)} %pad_maximum_fusion.1.a), channel_id=1, source_target_pairs={{0,3},{1,0},{2,1},{3,2},{4,7},{5,4},{6,5},{7,6},{8,11},{9,8},{10,9... | collective-permute-start | bytes 786440 | tf_op jit(solution)/shard_map/ppermute | solution.py:46
  11.2 2.6 %collective-permute-start.2 = (bf16[2,64,1024]{2,1,0:T(8,128)(2,1)S(1)}, bf16[2,64,1024]{2,1,0:T(8,128)(2,1)S(1)}, u32[]{:S(2)}, u32[]{:S(2)}) collective-permute-start(bf16[2,64,1024]{2,1,0:T(8,128)(2,1)S(1)} %pad_maximum_fusion.1.a), channel_id=1, source_target_pairs={{0,1},{1,2},{2,3},{3,0},{4,5},{5,6},{6,7},{7,4},{8,9},{9,10},{10,1... | collective-permute-start | bytes 786440 | tf_op jit(solution)/shard_map/ppermute | solution.py:46
  13.8 1.8 %collective-permute-done.1.c = bf16[2,64,1024]{2,1,0:T(8,128)(2,1)S(1)} collective-permute-done((bf16[2,64,1024]{2,1,0:T(8,128)(2,1)S(1)}, bf16[2,64,1024]{2,1,0:T(8,128)(2,1)S(1)}, u32[]{:S(2)}, u32[]{:S(2)}) %collective-permute-start.1) | collective-permute-done | bytes 262176 | tf_op jit(solution)/shard_map/ppermute | solution.py:46
  15.6 3.9 %collective-permute-done.2.b = bf16[2,64,1024]{2,1,0:T(8,128)(2,1)S(1)} collective-permute-done((bf16[2,64,1024]{2,1,0:T(8,128)(2,1)S(1)}, bf16[2,64,1024]{2,1,0:T(8,128)(2,1)S(1)}, u32[]{:S(2)}, u32[]{:S(2)}) %collective-permute-start.2) | collective-permute-done | bytes 262176 | tf_op jit(solution)/shard_map/ppermute | solution.py:46
  19.7 4.7 %collective-permute-start.3 = (bf16[2,256,1024]{2,1,0:T(8,128)(2,1)S(1)}, bf16[2,256,1024]{2,1,0:T(8,128)(2,1)}, u32[]{:S(2)}, u32[]{:S(2)}) collective-permute-start(bf16[2,256,1024]{2,1,0:T(8,128)(2,1)S(1)} %shard_map.55.a), channel_id=1, source_target_pairs={{0,8},{1,9},{2,10},{3,11},{4,12},{5,13},{6,14},{7,15},{8,0},{9,1},... | collective-permute-start | bytes 3145736 | tf_op jit(solution)/shard_map/ppermute | solution.py:46
  24.4 2.8 %collective-permute-start.4 = (bf16[2,256,1024]{2,1,0:T(8,128)(2,1)S(1)}, bf16[2,256,1024]{2,1,0:T(8,128)(2,1)}, u32[]{:S(2)}, u32[]{:S(2)}) collective-permute-start(bf16[2,256,1024]{2,1,0:T(8,128)(2,1)S(1)} %shard_map.55.a), channel_id=1, source_target_pairs={{0,12},{1,13},{2,14},{3,15},{4,0},{5,1},{6,2},{7,3},{8,4},{9,5},{1... | collective-permute-start | bytes 3145736 | tf_op jit(solution)/shard_map/ppermute | solution.py:46
  27.1 2.5 %collective-permute-start.5 = (bf16[2,256,1024]{2,1,0:T(8,128)(2,1)S(1)}, bf16[2,256,1024]{2,1,0:T(8,128)(2,1)}, u32[]{:S(2)}, u32[]{:S(2)}) collective-permute-start(bf16[2,256,1024]{2,1,0:T(8,128)(2,1)S(1)} %shard_map.55.a), channel_id=1, source_target_pairs={{0,4},{1,5},{2,6},{3,7},{4,8},{5,9},{6,10},{7,11},{8,12},{9,13},{1... | collective-permute-start | bytes 3145736 | tf_op jit(solution)/shard_map/ppermute | solution.py:46
  29.7 0.8 convolution_convert_fusion
  30.6 0.9 copy.8
  31.6 1.8 %reshape.11 = bf16[16,32,128]{2,1,0:T(8,128)(2,1)} reshape(bf16[16,32,2,64]{3,2,1,0:T(2,128)(2,1)} %copy.8) | data formatting | bytes 262144 | tf_op jit(solution)/shard_map/reshape | solution.py:317
  33.3 3.7 %all-to-all-start = ((bf16[16,32,128]{2,1,0:T(8,128)(2,1)}), bf16[16,32,128]{2,1,0:T(8,128)(2,1)S(1)}, u32[]{:S(2)}, u32[]{:S(2)}) async-start(bf16[16,32,128]{2,1,0:T(8,128)(2,1)} %reshape.11), calls=%async_computation | async-start | bytes 262144 | tf_op jit(solution)/shard_map/all_to_all | solution.py:318
  37.3 3.0 %shard_map.56 = (bf16[1024,1024]{1,0:T(8,128)(2,1)S(1)}, f32[8,128]{1,0:T(8,128)}) custom-call(bf16[2,256,1024]{2,1,0:T(8,128)(2,1)S(1)} %shard_map.55.a, bf16[2,256,1024]{2,1,0:T(8,128)(2,1)} %collective-permute-done.3.d), custom_call_target="tpu_custom_call" | custom-call | tf_op jit(solution)/shard_map/pallas_call | solution.py:141
  40.3 8.9 %collective-permute-done.4.b.c = bf16[2,256,1024]{2,1,0:T(8,128)(2,1)} collective-permute-done((bf16[2,256,1024]{2,1,0:T(8,128)(2,1)S(1)}, bf16[2,256,1024]{2,1,0:T(8,128)(2,1)}, u32[]{:S(2)}, u32[]{:S(2)}) %collective-permute-start.4) | collective-permute-done | bytes 1048608 | tf_op jit(solution)/shard_map/ppermute | solution.py:46
  49.2 4.2 %shard_map.57 = (bf16[1024,1024]{1,0:T(8,128)(2,1)}, f32[8,128]{1,0:T(8,128)S(1)}) custom-call(bf16[1024,1024]{1,0:T(8,128)(2,1)S(1)} %get-tuple-element.12.part, bf16[2,256,1024]{2,1,0:T(8,128)(2,1)} %collective-permute-done.4.b.c, bf16[2,256,1024]{2,1,0:T(8,128)(2,1)} %collective-permute-done.5.c.b), custom_call_target="tpu_custom_call" | custom-call | tf_op jit(solution)/shard_map/pallas_call | solution.py:148
  53.4 7.5 %collective-permute-start.6 = (bf16[1024,1024]{1,0:T(8,128)(2,1)}, bf16[1024,1024]{1,0:T(8,128)(2,1)}, u32[]{:S(2)}, u32[]{:S(2)}) collective-permute-start(bf16[1024,1024]{1,0:T(8,128)(2,1)} %get-tuple-element.13.own), channel_id=1, source_target_pairs={{0,16},{16,0},{32,48},{48,32},{64,80},{80,64},{96,112},{112,96},{1... | collective-permute-start | bytes 6291464 | tf_op jit(solution)/shard_map/ppermute | solution.py:325
  60.9 0.6 shard_map.58.panel
  61.6 1.8 %shard_map.59.bias = f32[64,1024]{1,0:T(8,128)S(1)} custom-call(bf16[64,1024]{1,0:T(8,128)(2,1)S(1)} %shard_map.58.panel, bf16[2,256,1024]{2,1,0:T(8,128)(2,1)S(1)} %shard_map.55.a, bf16[2,256,1024]{2,1,0:T(8,128)(2,1)} %collective-permute-done.5.c.b, bf16[2,256,1024]{2,1,0:T(8,128)(2,1)} %collective-permute-done.4.b.c, ...), custom_call_target="tpu_custom_call" | custom-call | flops 42949672960 | bytes 6291456 | tf_op jit(solution)/shard_map/pallas_call | solution.py:164
  63.4 1.3 collective-permute-start.7
  64.8 2.1 %collective-permute-done.7.bias_got = f32[64,1024]{1,0:T(8,128)S(1)} collective-permute-done((f32[64,1024]{1,0:T(8,128)S(1)}, f32[64,1024]{1,0:T(8,128)S(1)}, u32[]{:S(2)}, u32[]{:S(2)}) %collective-permute-start.7) | collective-permute-done | bytes 262176 | tf_op jit(solution)/shard_map/ppermute | solution.py:326
  66.9 4.9 %shard_map.60 = (bf16[1024,1024]{1,0:T(8,128)(2,1)S(1)}, bf16[1024,1024]{1,0:T(8,128)(2,1)S(1)}, f32[64,1024]{1,0:T(8,128)S(1)}, f32[8,128]{1,0:T(8,128)S(1)}) custom-call(s32[1]{0:T(128)} %bitcast.18.core, bf16[1024,1024]{1,0:T(8,128)(2,1)} %get-tuple-element.13.own, bf16[1024,1024]{1,0:T(8,128)(2,1)} %collective-permute-done.6.got, ...), custom_call_target="tpu_custom_call" | custom-call | flops 2147483648 | bytes 6291456 | tf_op jit(solution)/shard_map/pallas_call | solution.py:200
  71.8 1.3 collective-permute-start.8
  73.2 2.9 %collective-permute-done.8.ready = f32[8,128]{1,0:T(8,128)S(1)} collective-permute-done((f32[8,128]{1,0:T(8,128)S(1)}, f32[8,128]{1,0:T(8,128)S(1)}, u32[]{:S(2)}, u32[]{:S(2)}) %collective-permute-start.8) | collective-permute-done | bytes 4128 | tf_op jit(solution)/shard_map/ppermute | solution.py:53
  76.2 0.5 fusion
  76.7 0.7 collective-permute-start.9
  77.4 0.5 fusion.1
  77.9 0.7 collective-permute-start.10
  78.6 0.5 fusion.2
  79.1 0.7 collective-permute-start.11
  79.9 0.5 fusion.3
  80.4 0.7 collective-permute-start.12
  81.1 0.5 fusion.4
  81.6 1.3 collective-permute-start.13
  82.9 24.6 %collective-permute-done.13 = bf16[64,1024]{1,0:T(8,128)(2,1)S(1)} collective-permute-done((bf16[64,1024]{1,0:T(8,128)(2,1)S(1)}, bf16[64,1024]{1,0:T(8,128)(2,1)S(1)}, u32[]{:S(2)}, u32[]{:S(2)}) %collective-permute-start.13) | collective-permute-done | bytes 131104 | tf_op jit(solution)/shard_map/ppermute | solution.py:342
  107.5 0.5 fusion.5
  108.0 0.7 collective-permute-start.14
  108.8 0.5 fusion.6
  109.3 0.8 collective-permute-start.15
  110.7 0.7 collective-permute-start.16
  111.4 0.5 fusion.8
  111.9 0.7 collective-permute-start.17
  112.6 0.5 convolution_add_fusion.v_odd
  113.1 0.5 convert_select_fusion
  113.6 2.4 %collective-permute-start.18 = (bf16[64,1024]{1,0:T(8,128)(2,1)S(1)}, bf16[64,1024]{1,0:T(8,128)(2,1)S(1)}, u32[]{:S(2)}, u32[]{:S(2)}) collective-permute-start(bf16[64,1024]{1,0:T(8,128)(2,1)S(1)} %get-tuple-element.19), channel_id=1, source_target_pairs={{0,16},{16,0},{32,48},{48,32},{64,80},{80,64},{96,112},{112,96},{1... | collective-permute-start | bytes 393224 | tf_op jit(solution)/shard_map/ppermute | solution.py:346
  116.0 1.0 collective-permute-done.18.other
  117.0 4.4 %collective-permute-start.21 = (bf16[64,1024]{1,0:T(8,128)(2,1)S(1)}, bf16[64,1024]{1,0:T(8,128)(2,1)S(1)}, u32[]{:S(2)}, u32[]{:S(2)}) collective-permute-start(bf16[64,1024]{1,0:T(8,128)(2,1)S(1)} %broadcast_select_fusion), channel_id=1, source_target_pairs={{0,2},{1,3},{2,0},{3,1},{4,6},{5,7},{6,4},{7,5},{8,10},{9,11},{10,... | collective-permute-start | bytes 393224 | tf_op jit(solution)/shard_map/ppermute | solution.py:46
  121.5 2.8 %collective-permute-start.20 = (bf16[64,1024]{1,0:T(8,128)(2,1)S(1)}, bf16[64,1024]{1,0:T(8,128)(2,1)S(1)}, u32[]{:S(2)}, u32[]{:S(2)}) collective-permute-start(bf16[64,1024]{1,0:T(8,128)(2,1)S(1)} %broadcast_select_fusion), channel_id=1, source_target_pairs={{0,3},{1,0},{2,1},{3,2},{4,7},{5,4},{6,5},{7,6},{8,11},{9,8},{10,9... | collective-permute-start | bytes 393224 | tf_op jit(solution)/shard_map/ppermute | solution.py:46
  124.3 2.4 %collective-permute-start.19 = (bf16[64,1024]{1,0:T(8,128)(2,1)S(1)}, bf16[64,1024]{1,0:T(8,128)(2,1)S(1)}, u32[]{:S(2)}, u32[]{:S(2)}) collective-permute-start(bf16[64,1024]{1,0:T(8,128)(2,1)S(1)} %broadcast_select_fusion), channel_id=1, source_target_pairs={{0,1},{1,2},{2,3},{3,0},{4,5},{5,6},{6,7},{7,4},{8,9},{9,10},{10,1... | collective-permute-start | bytes 393224 | tf_op jit(solution)/shard_map/ppermute | solution.py:46
  126.8 0.7 collective-permute-start.25
  127.4 0.7 collective-permute-start.26
  128.2 3.1 %collective-permute-done.19 = bf16[64,1024]{1,0:T(8,128)(2,1)S(1)} collective-permute-done((bf16[64,1024]{1,0:T(8,128)(2,1)S(1)}, bf16[64,1024]{1,0:T(8,128)(2,1)S(1)}, u32[]{:S(2)}, u32[]{:S(2)}) %collective-permute-start.19) | collective-permute-done | bytes 131104 | tf_op jit(solution)/shard_map/ppermute | solution.py:46
  131.3 1.9 %collective-permute-start.22 = (bf16[256,1024]{1,0:T(8,128)(2,1)S(1)}, bf16[256,1024]{1,0:T(8,128)(2,1)S(1)}, u32[]{:S(2)}, u32[]{:S(2)}) collective-permute-start(bf16[256,1024]{1,0:T(8,128)(2,1)S(1)} %pad_maximum_fusion.a.ready), channel_id=1, source_target_pairs={{0,4},{1,5},{2,6},{3,7},{4,8},{5,9},{6,10},{7,11},{8,12},{9,13},{1... | collective-permute-start | bytes 1572872 | tf_op jit(solution)/shard_map/ppermute | solution.py:46
  133.2 4.6 %collective-permute-start.23 = (bf16[256,1024]{1,0:T(8,128)(2,1)S(1)}, bf16[256,1024]{1,0:T(8,128)(2,1)}, u32[]{:S(2)}, u32[]{:S(2)}) collective-permute-start(bf16[256,1024]{1,0:T(8,128)(2,1)S(1)} %pad_maximum_fusion.a.ready), channel_id=1, source_target_pairs={{0,12},{1,13},{2,14},{3,15},{4,0},{5,1},{6,2},{7,3},{8,4},{9,5},{1... | collective-permute-start | bytes 1572872 | tf_op jit(solution)/shard_map/ppermute | solution.py:46
  137.8 1.9 %collective-permute-start.24 = (bf16[256,1024]{1,0:T(8,128)(2,1)S(1)}, bf16[256,1024]{1,0:T(8,128)(2,1)}, u32[]{:S(2)}, u32[]{:S(2)}) collective-permute-start(bf16[256,1024]{1,0:T(8,128)(2,1)S(1)} %pad_maximum_fusion.a.ready), channel_id=1, source_target_pairs={{0,8},{1,9},{2,10},{3,11},{4,12},{5,13},{6,14},{7,15},{8,0},{9,1},... | collective-permute-start | bytes 1572872 | tf_op jit(solution)/shard_map/ppermute | solution.py:46
  139.7 0.7 shard_map.63.entry
  140.4 1.3 collective-permute-start.27
  141.7 1.3 collective-permute-start.28
  143.1 5.8 %collective-permute-done.28.last = bf16[64,1024]{1,0:T(8,128)(2,1)} collective-permute-done((bf16[64,1024]{1,0:T(8,128)(2,1)}, bf16[64,1024]{1,0:T(8,128)(2,1)}, u32[]{:S(2)}, u32[]{:S(2)}) %collective-permute-start.28) | collective-permute-done | bytes 131104 | tf_op jit(solution)/shard_map/ppermute | solution.py:53
  148.9 1.1 shard_map.64.entry
  150.0 1.4 collective-permute-start.29
  151.5 1.4 shard_map.62.maps
  152.9 1.7 %shard_map.65 = f32[64,1024]{1,0:T(8,128)} custom-call(s32[2]{0:T(128)S(1)} %add_convert_fusion.flags, bf16[1024,1024]{1,0:T(8,128)(2,1)S(1)} %shard_map.62.maps, bf16[64,1024]{1,0:T(8,128)(2,1)S(1)} %shard_map.64.entry, bf16[64,1024]{1,0:T(8,128)(2,1)S(1)} %collective-permute-done.29.across, bf16[64,1024]{1,0:T(8,128)(2,1)S(1)} %copy-done.2, ...), custom_call_target="tpu_custom_call" | custom-call | tf_op jit(solution)/shard_map/pallas_call | solution.py:285
  (48 shorter events, 1.6 us)
Async XLA Ops:
  0.0 29.7 %copy-start = (bf16[1024,1024]{1,0:T(8,128)(2,1)S(1)}, bf16[1024,1024]{1,0:T(8,128)(2,1)}, u32[]{:S(2)}) copy-start(bf16[1024,1024]{1,0:T(8,128)(2,1)} %param.8) | copy-start | bytes 6291460
  0.0 29.7 %copy-start.3 = (bf16[1,1024,64]{1,2,0:T(8,128)(2,1)S(1)}, bf16[1,1024,64]{1,2,0:T(8,128)(2,1)}, u32[]{:S(2)}) copy-start(bf16[1,1024,64]{1,2,0:T(8,128)(2,1)} %param.7) | copy-start | bytes 393220
  2.8 11.0 %collective-permute-start = (bf16[2,64,1024]{2,1,0:T(8,128)(2,1)S(1)}, bf16[2,64,1024]{2,1,0:T(8,128)(2,1)S(1)}, u32[]{:S(2)}, u32[]{:S(2)}) collective-permute-start(bf16[2,64,1024]{2,1,0:T(8,128)(2,1)S(1)} %pad_maximum_fusion.1.a), channel_id=1, source_target_pairs={{0,2},{1,3},{2,0},{3,1},{4,6},{5,7},{6,4},{7,5},{8,10},{9,11},{10,... | collective-permute-start | bytes 786440 | tf_op jit(solution)/shard_map/ppermute | solution.py:46
  8.5 7.1 %collective-permute-start.1 = (bf16[2,64,1024]{2,1,0:T(8,128)(2,1)S(1)}, bf16[2,64,1024]{2,1,0:T(8,128)(2,1)S(1)}, u32[]{:S(2)}, u32[]{:S(2)}) collective-permute-start(bf16[2,64,1024]{2,1,0:T(8,128)(2,1)S(1)} %pad_maximum_fusion.1.a), channel_id=1, source_target_pairs={{0,3},{1,0},{2,1},{3,2},{4,7},{5,4},{6,5},{7,6},{8,11},{9,8},{10,9... | collective-permute-start | bytes 786440 | tf_op jit(solution)/shard_map/ppermute | solution.py:46
  11.2 8.3 %collective-permute-start.2 = (bf16[2,64,1024]{2,1,0:T(8,128)(2,1)S(1)}, bf16[2,64,1024]{2,1,0:T(8,128)(2,1)S(1)}, u32[]{:S(2)}, u32[]{:S(2)}) collective-permute-start(bf16[2,64,1024]{2,1,0:T(8,128)(2,1)S(1)} %pad_maximum_fusion.1.a), channel_id=1, source_target_pairs={{0,1},{1,2},{2,3},{3,0},{4,5},{5,6},{6,7},{7,4},{8,9},{9,10},{10,1... | collective-permute-start | bytes 786440 | tf_op jit(solution)/shard_map/ppermute | solution.py:46
  19.7 17.6 %collective-permute-start.3 = (bf16[2,256,1024]{2,1,0:T(8,128)(2,1)S(1)}, bf16[2,256,1024]{2,1,0:T(8,128)(2,1)}, u32[]{:S(2)}, u32[]{:S(2)}) collective-permute-start(bf16[2,256,1024]{2,1,0:T(8,128)(2,1)S(1)} %shard_map.55.a), channel_id=1, source_target_pairs={{0,8},{1,9},{2,10},{3,11},{4,12},{5,13},{6,14},{7,15},{8,0},{9,1},... | collective-permute-start | bytes 3145736 | tf_op jit(solution)/shard_map/ppermute | solution.py:46
  24.4 24.9 %collective-permute-start.4 = (bf16[2,256,1024]{2,1,0:T(8,128)(2,1)S(1)}, bf16[2,256,1024]{2,1,0:T(8,128)(2,1)}, u32[]{:S(2)}, u32[]{:S(2)}) collective-permute-start(bf16[2,256,1024]{2,1,0:T(8,128)(2,1)S(1)} %shard_map.55.a), channel_id=1, source_target_pairs={{0,12},{1,13},{2,14},{3,15},{4,0},{5,1},{6,2},{7,3},{8,4},{9,5},{1... | collective-permute-start | bytes 3145736 | tf_op jit(solution)/shard_map/ppermute | solution.py:46
  27.1 22.1 %collective-permute-start.5 = (bf16[2,256,1024]{2,1,0:T(8,128)(2,1)S(1)}, bf16[2,256,1024]{2,1,0:T(8,128)(2,1)}, u32[]{:S(2)}, u32[]{:S(2)}) collective-permute-start(bf16[2,256,1024]{2,1,0:T(8,128)(2,1)S(1)} %shard_map.55.a), channel_id=1, source_target_pairs={{0,4},{1,5},{2,6},{3,7},{4,8},{5,9},{6,10},{7,11},{8,12},{9,13},{1... | collective-permute-start | bytes 3145736 | tf_op jit(solution)/shard_map/ppermute | solution.py:46
  33.3 27.6 %all-to-all-start = ((bf16[16,32,128]{2,1,0:T(8,128)(2,1)}), bf16[16,32,128]{2,1,0:T(8,128)(2,1)S(1)}, u32[]{:S(2)}, u32[]{:S(2)}) async-start(bf16[16,32,128]{2,1,0:T(8,128)(2,1)} %reshape.11), calls=%async_computation | async-start | bytes 262144 | tf_op jit(solution)/shard_map/all_to_all | solution.py:318
  53.4 13.5 %collective-permute-start.6 = (bf16[1024,1024]{1,0:T(8,128)(2,1)}, bf16[1024,1024]{1,0:T(8,128)(2,1)}, u32[]{:S(2)}, u32[]{:S(2)}) collective-permute-start(bf16[1024,1024]{1,0:T(8,128)(2,1)} %get-tuple-element.13.own), channel_id=1, source_target_pairs={{0,16},{16,0},{32,48},{48,32},{64,80},{80,64},{96,112},{112,96},{1... | collective-permute-start | bytes 6291464 | tf_op jit(solution)/shard_map/ppermute | solution.py:325
  63.4 3.4 %collective-permute-start.7 = (f32[64,1024]{1,0:T(8,128)S(1)}, f32[64,1024]{1,0:T(8,128)S(1)}, u32[]{:S(2)}, u32[]{:S(2)}) collective-permute-start(f32[64,1024]{1,0:T(8,128)S(1)} %shard_map.59.bias), channel_id=1, source_target_pairs={{0,16},{32,48},{64,80},{96,112},{128,144},{160,176},{192,208},{224... | collective-permute-start | bytes 786440 | tf_op jit(solution)/shard_map/ppermute | solution.py:326
  71.8 4.4 %collective-permute-start.8 = (f32[8,128]{1,0:T(8,128)S(1)}, f32[8,128]{1,0:T(8,128)S(1)}, u32[]{:S(2)}, u32[]{:S(2)}) collective-permute-start(f32[8,128]{1,0:T(8,128)S(1)} %get-tuple-element.15), channel_id=1, source_target_pairs={{48,16},{80,48},{112,80},{144,112},{176,144},{208,176},{49,17},{81... | collective-permute-start | bytes 12296 | tf_op jit(solution)/shard_map/ppermute | solution.py:53
  76.7 0.7 collective-permute-start.9
  77.9 0.7 collective-permute-start.10
  79.1 0.7 collective-permute-start.11
  80.4 0.7 collective-permute-start.12
  81.6 25.9 %collective-permute-start.13 = (bf16[64,1024]{1,0:T(8,128)(2,1)S(1)}, bf16[64,1024]{1,0:T(8,128)(2,1)S(1)}, u32[]{:S(2)}, u32[]{:S(2)}) collective-permute-start(bf16[64,1024]{1,0:T(8,128)(2,1)S(1)} %fusion.4), channel_id=1, source_target_pairs={{368,336},{32,0},{48,16},{369,337},{33,1},{49,17},{370,338},{34,2}... | collective-permute-start | bytes 393224 | tf_op jit(solution)/shard_map/ppermute | solution.py:342
  108.0 0.7 collective-permute-start.14
  109.3 0.9 collective-permute-start.15
  110.7 0.7 collective-permute-start.16
  111.9 0.7 collective-permute-start.17
  113.6 3.4 %collective-permute-start.18 = (bf16[64,1024]{1,0:T(8,128)(2,1)S(1)}, bf16[64,1024]{1,0:T(8,128)(2,1)S(1)}, u32[]{:S(2)}, u32[]{:S(2)}) collective-permute-start(bf16[64,1024]{1,0:T(8,128)(2,1)S(1)} %get-tuple-element.19), channel_id=1, source_target_pairs={{0,16},{16,0},{32,48},{48,32},{64,80},{80,64},{96,112},{112,96},{1... | collective-permute-start | bytes 393224 | tf_op jit(solution)/shard_map/ppermute | solution.py:346
  117.0 11.1 %copy-start.1 = (bf16[64,1024]{1,0:T(8,128)(2,1)}, bf16[64,1024]{1,0:T(8,128)(2,1)S(1)}, u32[]{:S(2)}) copy-start(bf16[64,1024]{1,0:T(8,128)(2,1)S(1)} %collective-permute-done.18.other) | copy-start | bytes 393220
  117.0 11.1 %collective-permute-start.21 = (bf16[64,1024]{1,0:T(8,128)(2,1)S(1)}, bf16[64,1024]{1,0:T(8,128)(2,1)S(1)}, u32[]{:S(2)}, u32[]{:S(2)}) collective-permute-start(bf16[64,1024]{1,0:T(8,128)(2,1)S(1)} %broadcast_select_fusion), channel_id=1, source_target_pairs={{0,2},{1,3},{2,0},{3,1},{4,6},{5,7},{6,4},{7,5},{8,10},{9,11},{10,... | collective-permute-start | bytes 393224 | tf_op jit(solution)/shard_map/ppermute | solution.py:46
  121.5 6.7 %collective-permute-start.20 = (bf16[64,1024]{1,0:T(8,128)(2,1)S(1)}, bf16[64,1024]{1,0:T(8,128)(2,1)S(1)}, u32[]{:S(2)}, u32[]{:S(2)}) collective-permute-start(bf16[64,1024]{1,0:T(8,128)(2,1)S(1)} %broadcast_select_fusion), channel_id=1, source_target_pairs={{0,3},{1,0},{2,1},{3,2},{4,7},{5,4},{6,5},{7,6},{8,11},{9,8},{10,9... | collective-permute-start | bytes 393224 | tf_op jit(solution)/shard_map/ppermute | solution.py:46
  124.3 6.9 %collective-permute-start.19 = (bf16[64,1024]{1,0:T(8,128)(2,1)S(1)}, bf16[64,1024]{1,0:T(8,128)(2,1)S(1)}, u32[]{:S(2)}, u32[]{:S(2)}) collective-permute-start(bf16[64,1024]{1,0:T(8,128)(2,1)S(1)} %broadcast_select_fusion), channel_id=1, source_target_pairs={{0,1},{1,2},{2,3},{3,0},{4,5},{5,6},{6,7},{7,4},{8,9},{9,10},{10,1... | collective-permute-start | bytes 393224 | tf_op jit(solution)/shard_map/ppermute | solution.py:46
  126.8 13.0 %collective-permute-start.25 = (bf16[64,1024]{1,0:T(8,128)(2,1)S(1)}, bf16[64,1024]{1,0:T(8,128)(2,1)S(1)}, u32[]{:S(2)}, u32[]{:S(2)}) collective-permute-start(bf16[64,1024]{1,0:T(8,128)(2,1)S(1)} %get-tuple-element.20.edge), channel_id=1, source_target_pairs={{208,80},{209,81},{210,82},{211,83},{212,84},{213,85},{214,86},{21... | collective-permute-start | bytes 393224 | tf_op jit(solution)/shard_map/ppermute | solution.py:53
  127.4 12.3 %collective-permute-start.26 = (bf16[64,1024]{1,0:T(8,128)(2,1)S(1)}, bf16[64,1024]{1,0:T(8,128)(2,1)S(1)}, u32[]{:S(2)}, u32[]{:S(2)}) collective-permute-start(bf16[64,1024]{1,0:T(8,128)(2,1)S(1)} %get-tuple-element.20.edge), channel_id=1, source_target_pairs={{208,176},{209,177},{210,178},{211,179},{212,180},{213,181},{214,1... | collective-permute-start | bytes 393224 | tf_op jit(solution)/shard_map/ppermute | solution.py:53
  131.3 20.2 %collective-permute-start.22 = (bf16[256,1024]{1,0:T(8,128)(2,1)S(1)}, bf16[256,1024]{1,0:T(8,128)(2,1)S(1)}, u32[]{:S(2)}, u32[]{:S(2)}) collective-permute-start(bf16[256,1024]{1,0:T(8,128)(2,1)S(1)} %pad_maximum_fusion.a.ready), channel_id=1, source_target_pairs={{0,4},{1,5},{2,6},{3,7},{4,8},{5,9},{6,10},{7,11},{8,12},{9,13},{1... | collective-permute-start | bytes 1572872 | tf_op jit(solution)/shard_map/ppermute | solution.py:46
  133.2 18.3 %collective-permute-start.23 = (bf16[256,1024]{1,0:T(8,128)(2,1)S(1)}, bf16[256,1024]{1,0:T(8,128)(2,1)}, u32[]{:S(2)}, u32[]{:S(2)}) collective-permute-start(bf16[256,1024]{1,0:T(8,128)(2,1)S(1)} %pad_maximum_fusion.a.ready), channel_id=1, source_target_pairs={{0,12},{1,13},{2,14},{3,15},{4,0},{5,1},{6,2},{7,3},{8,4},{9,5},{1... | collective-permute-start | bytes 1572872 | tf_op jit(solution)/shard_map/ppermute | solution.py:46
  137.8 13.7 %collective-permute-start.24 = (bf16[256,1024]{1,0:T(8,128)(2,1)S(1)}, bf16[256,1024]{1,0:T(8,128)(2,1)}, u32[]{:S(2)}, u32[]{:S(2)}) collective-permute-start(bf16[256,1024]{1,0:T(8,128)(2,1)S(1)} %pad_maximum_fusion.a.ready), channel_id=1, source_target_pairs={{0,8},{1,9},{2,10},{3,11},{4,12},{5,13},{6,14},{7,15},{8,0},{9,1},... | collective-permute-start | bytes 1572872 | tf_op jit(solution)/shard_map/ppermute | solution.py:46
  140.4 2.7 %collective-permute-start.27 = (bf16[64,1024]{1,0:T(8,128)(2,1)}, bf16[64,1024]{1,0:T(8,128)(2,1)}, u32[]{:S(2)}, u32[]{:S(2)}) collective-permute-start(bf16[64,1024]{1,0:T(8,128)(2,1)} %shard_map.63.entry), channel_id=1, source_target_pairs={{176,144},{80,48},{177,145},{81,49},{178,146},{82,50},{179,147},{8... | collective-permute-start | bytes 393224 | tf_op jit(solution)/shard_map/ppermute | solution.py:53
  141.7 7.2 %collective-permute-start.28 = (bf16[64,1024]{1,0:T(8,128)(2,1)}, bf16[64,1024]{1,0:T(8,128)(2,1)}, u32[]{:S(2)}, u32[]{:S(2)}) collective-permute-start(bf16[64,1024]{1,0:T(8,128)(2,1)} %shard_map.63.entry), channel_id=1, source_target_pairs={{176,112},{80,16},{177,113},{81,17},{178,114},{82,18},{179,115},{8... | collective-permute-start | bytes 393224 | tf_op jit(solution)/shard_map/ppermute | solution.py:53
  150.0 2.9 %copy-start.2 = (bf16[64,1024]{1,0:T(8,128)(2,1)S(1)}, bf16[64,1024]{1,0:T(8,128)(2,1)}, u32[]{:S(2)}) copy-start(bf16[64,1024]{1,0:T(8,128)(2,1)} %copy-done.1) | copy-start | bytes 393220
  150.0 2.8 %collective-permute-start.29 = (bf16[64,1024]{1,0:T(8,128)(2,1)S(1)}, bf16[64,1024]{1,0:T(8,128)(2,1)S(1)}, u32[]{:S(2)}, u32[]{:S(2)}) collective-permute-start(bf16[64,1024]{1,0:T(8,128)(2,1)S(1)} %shard_map.64.entry), channel_id=1, source_target_pairs={{16,0},{48,32},{80,64},{112,96},{144,128},{176,160},{208,192},{240... | collective-permute-start | bytes 393224 | tf_op jit(solution)/shard_map/ppermute | solution.py:362
